TPU v7x, 32 devices: a whole 2x2x4 slice. The times are simulated.
32 devices in a mesh: groups: 2 (over y), dp: 4 (over z), tensor: 4 (over x, core).
Axes of the slice: x: 2, y: 2, z: 4, core: 2. Of those that a mesh axis runs over, the one named last changes fastest.
Arguments:
- hidden: bfloat16 [16, 4, 8192], P(('groups', 'dp'), None, 'tensor'), parts along dimension 0, may hold values from -6 to 6
- norm_gain: bfloat16 [8192], P('tensor'), may hold values from 0.099609375 to 1.8984375
- queries: bfloat16 [16, 4, 8192], P(('groups', 'dp')), parts along dimension 0, may hold values from -150 to 150
- key_weight: bfloat16 [8192, 1024], P('tensor'), may hold values from -0.0625 to 0.0625
- value_weight: bfloat16 [8192, 1024], P('tensor'), may hold values from -0.0625 to 0.0625
- key_down: float32 [128, 8192], P(('groups', 'dp'), 'tensor'), parts along dimension 0, may hold values from -0.0625 to 0.0625
- key_up: float32 [2048, 64], P(('groups', 'dp')), parts along dimension 0, may hold values from -0.75 to 0.75
- value_down: float32 [128, 8192], P(('groups', 'dp'), 'tensor'), parts along dimension 0, may hold values from -0.0625 to 0.0625
- value_up: float32 [2048, 64], P(('groups', 'dp')), parts along dimension 0, may hold values from -0.75 to 0.75
- key_cache: bfloat16 [16, 2048, 1024], P(('groups', 'dp'), 'tensor'), parts along dimension 0, may hold values from -6 to 6
- value_cache: bfloat16 [16, 2048, 1024], P(('groups', 'dp'), 'tensor'), parts along dimension 0, may hold values from -6 to 6
- lengths: int32 [16], P(('groups', 'dp')), parts along dimension 0, may hold values from 1 to 2048, as said below
Outputs:
- new_keys: bfloat16 [16, 4, 1024], P(('groups', 'dp')), parts along dimension 0
- new_values: bfloat16 [16, 4, 1024], P(('groups', 'dp')), parts along dimension 0
- attended: bfloat16 [16, 4, 8192], P(('groups', 'dp')), parts along dimension 0
There are 2 independent parts, one for each index of `groups`. A program takes and returns all parts, laid end to end along the dimension named above; an argument that names none is the same for every part. Nothing has to cross between parts.
Inputs may be any that keep to these rules, and one draw needn't show every extreme that they name: `lengths`: some sequence fills all 2048 cache positions.
All inputs are finite; a program needn't handle non-finite values.
Results may differ from a plain program's by a relative error of at most 0.0078.
Values may be sent and summed in bfloat16 or wider, within the bound.
No kernel may reach another device: no remote copies, remote signals or barrier semaphores. Data moves between devices by JAX's collectives and lax.ppermute only.
A program may use at most 64 MiB of HBM per device.

v0:
```python
import math

import jax
import jax.numpy as jnp
from jax import lax
from jax.sharding import PartitionSpec as P

D = 8192
HD = 128


EPSILON = 1e-05
ROPE_BASE = 500000.0
MASKED_SCORE = -1e30


def joined(value, axis, join):
    pieces = jax.tree.map(lambda part: lax.all_gather(part, axis), value)
    head = jax.tree.map(lambda part: part[0], pieces)
    tail = jax.tree.map(lambda part: part[1:], pieces)
    so_far, _ = lax.scan(lambda so_far, piece: (join(so_far, piece), None), head, tail)
    return so_far


def rotate(vectors, positions):
    half_size = vectors.shape[-1] // 2
    frequency = ROPE_BASE ** (-(2.0 * jnp.arange(half_size, dtype=jnp.float32)) / vectors.shape[-1])
    angles = positions.astype(jnp.float32)[..., None, None] * frequency
    cosine = jnp.cos(angles)
    sine_part = jnp.sin(angles)
    front = vectors[..., :half_size]
    back = vectors[..., half_size:]
    return jnp.concatenate(
        [front * cosine - back * sine_part, back * cosine + front * sine_part], -1
    )


def combine(part_a, part_b):
    max_a, sum_a, numer_a = part_a
    max_b, sum_b, numer_b = part_b
    joint_max = jnp.maximum(max_a, max_b)
    factor_a = jnp.exp(max_a - joint_max)
    factor_b = jnp.exp(max_b - joint_max)
    return (
        joint_max,
        sum_a * factor_a + sum_b * factor_b,
        numer_a * factor_a[..., None] + numer_b * factor_b[..., None],
    )


def shards(
    hidden,
    norm_gain,
    queries,
    key_weight,
    value_weight,
    key_down,
    key_up,
    value_down,
    value_up,
    key_cache,
    value_cache,
    lengths,
):
    highest = lax.Precision.HIGHEST
    seq_count, step_count, width_part = hidden.shape
    kv_width = key_weight.shape[1]
    rows_flat = hidden.reshape(seq_count * step_count, width_part).astype(jnp.float32)
    squares = lax.psum(jnp.sum(rows_flat * rows_flat, axis=1, keepdims=True), "tensor")
    normed = (rows_flat * lax.rsqrt(squares / D + EPSILON) * norm_gain.astype(jnp.float32)).astype(
        jnp.bfloat16
    )
    up_key, up_value = (
        lax.all_gather(key_up, "dp", axis=0, tiled=True),
        lax.all_gather(value_up, "dp", axis=0, tiled=True),
    )
    merged_key = key_weight.astype(jnp.float32) + jnp.dot(
        lax.all_gather(key_down.astype(jnp.bfloat16), "dp", axis=0, tiled=True)
        .astype(jnp.float32)
        .T,
        up_key.T,
        precision=highest,
    )
    merged_value = value_weight.astype(jnp.float32) + jnp.dot(
        lax.all_gather(value_down.astype(jnp.bfloat16), "dp", axis=0, tiled=True)
        .astype(jnp.float32)
        .T,
        up_value.T,
        precision=highest,
    )
    normed_wide = normed.astype(jnp.float32)
    partial_kv = jnp.concatenate(
        [
            jnp.dot(normed_wide, merged_key, precision=highest),
            jnp.dot(normed_wide, merged_value, precision=highest),
        ],
        1,
    )
    summed = lax.psum(partial_kv, "tensor")
    raw_key = summed[:, :kv_width]
    raw_value = summed[:, kv_width:]
    kv_count = kv_width // HD
    head_count = queries.shape[2] // HD
    group_size = head_count // kv_count
    positions = lengths[:, None] + jnp.arange(step_count, dtype=jnp.int32)[None, :]
    new_keys = rotate(raw_key.reshape(seq_count, step_count, kv_count, HD), positions).astype(
        jnp.bfloat16
    )
    new_values = raw_value.reshape(seq_count, step_count, kv_count, HD).astype(jnp.bfloat16)
    rotated = rotate(
        queries.astype(jnp.float32).reshape(seq_count, step_count, head_count, HD), positions
    ).astype(jnp.bfloat16)
    rotated = rotated.reshape(seq_count, step_count, kv_count, group_size, HD)
    local_length = key_cache.shape[1]
    tensor_place = lax.axis_index("tensor")
    cache_pos = tensor_place * local_length + jnp.arange(local_length, dtype=jnp.int32)
    valid_c = (cache_pos[None, :] < lengths[:, None])[:, None, None, None, :]
    keys_c = key_cache.reshape(seq_count, local_length, kv_count, HD)
    values_c = value_cache.reshape(seq_count, local_length, kv_count, HD)
    scores_c = jnp.einsum(
        "sikgd,stkd->sikgt", rotated, keys_c, preferred_element_type=jnp.float32
    ) / math.sqrt(HD)
    scores_n = jnp.einsum(
        "sikgd,sjkd->sikgj", rotated, new_keys, preferred_element_type=jnp.float32
    ) / math.sqrt(HD)
    step_ids = jnp.arange(step_count, dtype=jnp.int32)
    valid_n = ((step_ids[None, :] <= step_ids[:, None]) & (tensor_place == 0))[
        None, :, None, None, :
    ]
    masked_c = jnp.where(valid_c, scores_c, MASKED_SCORE)
    masked_n = jnp.where(valid_n, scores_n, MASKED_SCORE)
    row_max = jnp.maximum(jnp.max(masked_c, axis=-1), jnp.max(masked_n, axis=-1))
    weights_c = jnp.where(valid_c, jnp.exp(masked_c - row_max[..., None]), 0.0).astype(jnp.bfloat16)
    weights_n = jnp.where(valid_n, jnp.exp(masked_n - row_max[..., None]), 0.0).astype(jnp.bfloat16)
    weight_sum = jnp.sum(weights_c.astype(jnp.float32), axis=-1) + jnp.sum(
        weights_n.astype(jnp.float32), axis=-1
    )
    numerator = jnp.einsum(
        "sikgt,stkd->sikgd", weights_c, values_c, preferred_element_type=jnp.float32
    )
    numerator = numerator + jnp.einsum(
        "sikgj,sjkd->sikgd", weights_n, new_values, preferred_element_type=jnp.float32
    )
    row_max, weight_sum, numerator = joined((row_max, weight_sum, numerator), "tensor", combine)
    attended = (
        (numerator / weight_sum[..., None])
        .reshape(seq_count, step_count, head_count * HD)
        .astype(jnp.bfloat16)
    )
    return (
        new_keys.reshape(seq_count, step_count, kv_width),
        new_values.reshape(seq_count, step_count, kv_width),
        attended,
    )


def solution(mesh):
    return jax.shard_map(
        shards,
        mesh=mesh,
        in_specs=(
            P(("groups", "dp"), None, "tensor"),
            P("tensor"),
            P(("groups", "dp"), None, None),
            P("tensor", None),
            P("tensor", None),
            P(("groups", "dp"), "tensor"),
            P(("groups", "dp"), None),
            P(("groups", "dp"), "tensor"),
            P(("groups", "dp"), None),
            P(("groups", "dp"), "tensor", None),
            P(("groups", "dp"), "tensor", None),
            P(("groups", "dp")),
        ),
        out_specs=(
            P(("groups", "dp"), None, None),
            P(("groups", "dp"), None, None),
            P(("groups", "dp"), None, None),
        ),
        check_vma=False,
    )
```

profile of v0, /device:TPU:0, one launch (start us, length us, event | category | flops | bytes accessed | tf_op | source)
XLA Modules:
  0.0 158.0 jit_solution(176870365684223019)
XLA Ops:
  8.0 0.9 multiply_reduce_fusion
  9.6 8.3 %psum.14 = f32[8,1]{0,1:T(1,128)S(1)} all-reduce(f32[8,1]{0,1:T(1,128)S(1)} %broadcast_in_dim.59), channel_id=1, replica_groups=mesh['groups'=2,'dp'=4,'tensor'=4] {'tensor'}, use_global_device_ids=true, to_apply=%region_1.0 | all-reduce | flops 8 | bytes 64 | tf_op jit(solution)/shard_map/psum | solution.py:69
  17.9 0.9 convert_element_type.84
  18.8 14.1 %all_gather.28 = bf16[64,2048]{1,0:T(8,128)(2,1)S(1)} all-gather(bf16[16,2048]{1,0:T(8,128)(2,1)S(1)} %convert_element_type.84), channel_id=1, replica_groups=mesh['groups'=2,'dp'=4,'tensor'=4] {'dp'}, dimensions={0}, use_global_device_ids=true | all-gather | bytes 327680 | tf_op jit(solution)/shard_map/all_gather | solution.py:85
  33.0 14.6 %all_gather.29 = f32[1024,64]{0,1:T(8,128)S(1)} all-gather(f32[256,64]{0,1:T(8,128)} %param.22), channel_id=1, replica_groups=mesh['groups'=2,'dp'=4,'tensor'=4] {'dp'}, dimensions={0}, use_global_device_ids=true | all-gather | bytes 327680 | tf_op jit(solution)/shard_map/all_gather | solution.py:75
  47.6 0.9 convert_element_type.82
  48.5 13.9 %all_gather.26 = bf16[64,2048]{1,0:T(8,128)(2,1)S(1)} all-gather(bf16[16,2048]{1,0:T(8,128)(2,1)S(1)} %convert_element_type.82), channel_id=1, replica_groups=mesh['groups'=2,'dp'=4,'tensor'=4] {'dp'}, dimensions={0}, use_global_device_ids=true | all-gather | bytes 327680 | tf_op jit(solution)/shard_map/all_gather | solution.py:78
  62.4 14.1 %all_gather.27 = f32[1024,64]{0,1:T(8,128)S(1)} all-gather(f32[256,64]{0,1:T(8,128)} %param.20), channel_id=1, replica_groups=mesh['groups'=2,'dp'=4,'tensor'=4] {'dp'}, dimensions={0}, use_global_device_ids=true | all-gather | bytes 327680 | tf_op jit(solution)/shard_map/all_gather | solution.py:74
  76.5 3.5 %fusion.44 = f32[2048,1024]{1,0:T(8,128)S(1)} fusion(bf16[64,2048]{1,0:T(8,128)(2,1)S(1)} %all_gather.28, f32[1024,64]{0,1:T(8,128)S(1)} %all_gather.29), kind=kOutput, calls=%fused_computation.67 | convolution fusion | flops 1610612736 | bytes 8912896 | tf_op jit(solution)/shard_map/dot_general | solution.py:84
  80.0 3.5 %fusion.43 = f32[2048,1024]{1,0:T(8,128)S(1)} fusion(bf16[64,2048]{1,0:T(8,128)(2,1)S(1)} %all_gather.26, f32[1024,64]{0,1:T(8,128)S(1)} %all_gather.27), kind=kOutput, calls=%fused_computation.66 | convolution fusion | flops 1610612736 | bytes 8912896 | tf_op jit(solution)/shard_map/dot_general | solution.py:77
  83.6 3.3 %fusion.3 = f32[8,1024]{1,0:T(8,128)S(1)} fusion(f32[2048,1024]{1,0:T(8,128)S(1)} %fusion.44, bf16[2048,1024]{1,0:T(8,128)(2,1)S(1)} %copy-done, f32[8,2048]{1,0:T(8,128)S(1)} %reshape.156, f32[2048]{0:T(1024)S(1)} %convert_element_type.79, f32[8]{0:T(128)S(1)} %rsqrt_bitcast_fusion), kind=kOutput, calls=%fused_computation.8 | convolution fusion | flops 205570048 | bytes 12689440 | tf_op jit(solution)/shard_map/dot_general | solution.py:95
  86.9 3.5 %fusion.6 = f32[8,1024]{1,0:T(8,128)S(1)} fusion(f32[2048,1024]{1,0:T(8,128)S(1)} %fusion.43, bf16[2048,1024]{1,0:T(8,128)(2,1)S(1)} %copy-done.1, f32[8,2048]{1,0:T(8,128)S(1)} %reshape.156, f32[2048]{0:T(1024)S(1)} %convert_element_type.79, f32[8]{0:T(128)S(1)} %rsqrt_bitcast_fusion), kind=kOutput, calls=%fused_computation.11 | convolution fusion | flops 205570048 | bytes 12689440 | tf_op jit(solution)/shard_map/dot_general | solution.py:94
  92.2 0.8 copy-done.3
  94.1 1.0 fusion.40
  95.7 26.8 %all-reduce.2.cloned.1.call-done = f32[8,2048]{1,0:T(8,128)} async-done(((f32[8,2048]{1,0:T(8,128)}), f32[8,2048]{1,0:T(8,128)}) %all-reduce.2.cloned.1.call-update) | async-done | bytes 65552 | tf_op jit(solution)/shard_map/psum | solution.py:99
  124.9 1.7 %fusion.41 = (f32[2,4,8,8]{3,1,2,0:T(4,128)S(1)}, f32[2,4,8,8,4]{3,4,1,2,0:T(4,128)S(1)}) fusion(pred[4,4]{1,0:T(4,128)(4,1)} %fusion.36, bf16[2,4,8,64]{3,1,2,0:T(4,128)(2,1)S(1)} %get-tuple-element.78, bf16[2,4,8,64]{3,1,2,0:T(4,128)(2,1)S(1)} %get-tuple-element.77, bf16[2,4,8,8,64]{4,3,2,1,0:T(8,128)(2,1)} %copy-done.4, ...), kind=kOutput, calls=%fused_computation.63 | convolution fusion | flops 824832 | bytes 157712 | tf_op jit(solution)/shard_map/sikgd,sjkd->sikgj/dot_general | solution.py:123
  126.6 1.0 convolution_bitcast_fusion
  127.6 1.3 fusion.25
  130.3 5.4 %all-gather.1 = f32[8,4,8,8]{3,2,1,0:T(8,128)S(1)} all-gather(f32[2,4,8,8]{3,2,1,0:T(8,128)S(1)} %copy.41), channel_id=3, replica_groups=mesh['groups'=2,'dp'=4,'tensor'=4] {'tensor'}, dimensions={0}, use_global_device_ids=true | all-gather | bytes 10240 | tf_op jit(solution)/shard_map/all_gather | solution.py:18
  135.7 5.9 %all-gather = f32[8,4,8,8]{3,2,1,0:T(8,128)S(1)} all-gather(f32[2,4,8,8]{3,2,1,0:T(8,128)S(1)} %copy.40), channel_id=2, replica_groups=mesh['groups'=2,'dp'=4,'tensor'=4] {'tensor'}, dimensions={0}, use_global_device_ids=true | all-gather | bytes 10240 | tf_op jit(solution)/shard_map/all_gather | solution.py:18
  143.7 3.5 %all-gather.5.cloned.1.call-done = f32[8,4,8,8,128]{4,3,2,1,0:T(8,128)} async-done(((f32[2,4,8,8,128]{4,3,2,1,0:T(8,128)}), f32[8,4,8,8,128]{4,3,2,1,0:T(8,128)}) %all-gather.5.cloned.1.call-update) | async-done | bytes 1048592 | tf_op jit(solution)/shard_map/all_gather | solution.py:18
  147.1 1.2 slice.65
  148.3 1.0 slice.62
  149.3 1.0 while.14
  (72 shorter events, 12.4 us)
Async XLA Ops:
  7.2 115.3 %all-reduce.2.cloned.1.call-start = ((), (), s32[]{:S(2)}) async-start(), calls=%async_computation | async-start | bytes 131072 | tf_op jit(solution)/shard_map/psum | solution.py:99
  80.0 3.6 %copy-start = (bf16[2048,1024]{1,0:T(8,128)(2,1)S(1)}, bf16[2048,1024]{1,0:T(8,128)(2,1)}, u32[]{:S(2)}) copy-start(bf16[2048,1024]{1,0:T(8,128)(2,1)} %param.18) | copy-start | bytes 12582916
  83.6 3.3 %copy-start.1 = (bf16[2048,1024]{1,0:T(8,128)(2,1)S(1)}, bf16[2048,1024]{1,0:T(8,128)(2,1)}, u32[]{:S(2)}) copy-start(bf16[2048,1024]{1,0:T(8,128)(2,1)} %param.17) | copy-start | bytes 12582916
  86.9 4.2 %copy-start.11 = (s32[2]{0:T(128)S(1)}, s32[2]{0:T(128)}, u32[]{:S(2)}) copy-start(s32[2]{0:T(128)} %param.25) | copy-start | bytes 28
  86.9 4.3 %copy-start.5 = (bf16[2,4,8192]{2,1,0:T(4,128)(2,1)S(1)}, bf16[2,4,8192]{2,1,0:T(4,128)(2,1)}, u32[]{:S(2)}) copy-start(bf16[2,4,8192]{2,1,0:T(4,128)(2,1)} %param.16) | copy-start | bytes 393220
  86.9 4.5 %copy-start.2 = (bf16[2,512,1024]{2,1,0:T(8,128)(2,1)S(1)}, bf16[2,512,1024]{2,1,0:T(8,128)(2,1)}, u32[]{:S(2)}) copy-start(bf16[2,512,1024]{2,1,0:T(8,128)(2,1)} %param.23) | copy-start | bytes 6291460
  91.0 56.1 %all-gather.5.cloned.1.call-start = ((), (), s32[]{:S(2)}) async-start(), calls=%async_computation.1 | async-start | bytes 1310720 | tf_op jit(solution)/shard_map/all_gather | solution.py:18
  91.4 2.7 %copy-start.8 = (pred[2,512]{1,0:T(4,128)(4,1)}, pred[2,512]{1,0:T(4,128)(4,1)S(1)}, u32[]{:S(2)}) copy-start(pred[2,512]{1,0:T(4,128)(4,1)S(1)} %broadcast_compare_fusion) | copy-start | bytes 3076
  91.4 1.6 %copy-start.3 = (bf16[2,512,1024]{2,1,0:T(8,128)(2,1)S(1)}, bf16[2,512,1024]{2,1,0:T(8,128)(2,1)}, u32[]{:S(2)}) copy-start(bf16[2,512,1024]{2,1,0:T(8,128)(2,1)} %param.24) | copy-start | bytes 6291460
  93.9 1.2 copy-start.6
  93.9 1.2 copy-start.7
  94.1 1.0 copy-start.4
  126.6 3.1 %copy-start.10 = (pred[4,4]{1,0:T(4,128)(4,1)S(1)}, pred[4,4]{1,0:T(4,128)(4,1)}, u32[]{:S(2)}) copy-start(pred[4,4]{1,0:T(4,128)(4,1)} %fusion.36) | copy-start | bytes 52
  126.6 3.3 %copy-start.9 = (pred[2,512]{1,0:T(4,128)(4,1)S(1)}, pred[2,512]{1,0:T(4,128)(4,1)}, u32[]{:S(2)}) copy-start(pred[2,512]{1,0:T(4,128)(4,1)} %copy-done.8) | copy-start | bytes 3076
Sparse Core Ops, SparseCore 0:
  91.2 31.3 all-reduce.1
  129.8 17.2 all-gather.4
where the time goes:
time: 159 us; the launch traced here: 158 us
  blocking collectives  76.3 us (48%)
  waiting for transfers between devices  30.3 us (19%)
  matrix products  18.8 us (12%)
  between operations  14.4 us (9%)
  local copies, waits for them, and re-layouts  9.95 us (6%)
  other arithmetic  8.02 us (5%)
    psum x1, waiting for transfers between devices, shards(): summed = lax.psum(partial_kv, 'tensor')  26.8 us
    all_gather x1, blocking collectives, shards(): lax.all_gather(value_up, 'dp', axis=0, tiled=True)  14.6 us
    all_gather x1, blocking collectives, shards(): lax.all_gather(value_down.astype(jnp.bfloat16), 'dp', axis=0, tiled=True)  14.1 us
    all_gather x1, blocking collectives, shards(): lax.all_gather(key_up, 'dp', axis=0, tiled=True)  14.1 us
    all_gather x1, blocking collectives, shards(): lax.all_gather(key_down.astype(jnp.bfloat16), 'dp', axis=0, tiled=True)  13.9 us
    all_gather x2, blocking collectives, joined(): pieces = jax.tree.map(lambda part: lax.all_gather(part, axis), value)  11.3 us
    psum x1, blocking collectives, shards(): lax.psum(jnp.sum(rows_flat * rows_flat, axis=1, keepdims=True), 'tensor')  8.31 us
    unnamed x30, local copies, waits for them, and re-layouts  3.66 us
  transfers between devices with their start and end apart: 2, of which 2 were waited for; matrix products, arithmetic and copies ran while one was open for 4% of the time, Pallas kernels for 0%

commit v1 on v0

v1 whole, which is shorter than its diff:
```python
import functools
import math

import jax
import jax.numpy as jnp
from jax import lax
from jax.experimental import pallas as pl
from jax.experimental.pallas import tpu as pltpu
from jax.sharding import PartitionSpec as P

HD = 128
GROUP = 8
STEPS = 4
EPSILON = 1e-05
ROPE_BASE = 500000.0
MASKED_SCORE = -1e30
SCALE = 1.0 / math.sqrt(HD)
PAIR = GROUP * HD + 128

F32 = jnp.float32
BF16 = jnp.bfloat16
NT = (((1,), (1,)), ((), ()))


def rotated(tile, cosine, sine):
    return tile * cosine + pltpu.roll(tile, HD // 2, 1) * sine


def tokens(ref):
    return jnp.concatenate([ref[0].astype(F32), ref[1].astype(F32)], 0)


def rounded(value):
    return value.astype(BF16).astype(F32)


def cache_kernel(limit_ref, q_ref, k_ref, v_ref, cos_ref, sin_ref, out_ref, qrot_ref):
    cosine, sine = cos_ref[...], sin_ref[...]
    q = tokens(q_ref)
    rows = [[], []]
    for g in range(GROUP):
        for e in range(2):
            at = (e * GROUP + g) * HD
            rows[e].append(rotated(q[:, at : at + HD], cosine, sine))
        qrot_ref[:, g * HD : (g + 1) * HD] = jnp.concatenate([rows[0][g], rows[1][g]], 0).astype(BF16)
    zero = jnp.zeros((GROUP * 8, HD), F32)
    upper = jnp.concatenate([jnp.concatenate(rows[0], 0), zero], 1)
    lower = jnp.concatenate([zero, jnp.concatenate(rows[1], 0)], 1)
    queries = jnp.concatenate([upper, lower], 0).astype(BF16)
    scores = [
        lax.dot_general(queries, k_ref[s], NT, preferred_element_type=F32) for s in range(2)
    ]
    shape = scores[0].shape
    first = lax.broadcasted_iota(jnp.int32, shape, 0) % 8 < STEPS
    place = lax.broadcasted_iota(jnp.int32, shape, 1)
    valid = place < jnp.where(first, limit_ref[0], limit_ref[1])
    masked = jnp.where(valid, jnp.where(first, scores[0], scores[1]) * SCALE, MASKED_SCORE)
    top = rounded(jnp.max(masked, 1, keepdims=True))
    weights = rounded(jnp.where(valid, jnp.exp(masked - top), 0.0))
    total = jnp.sum(weights, 1, keepdims=True)
    numer = jnp.dot(
        jnp.where(first, weights, 0.0).astype(BF16), v_ref[0], preferred_element_type=F32
    ) + jnp.dot(jnp.where(first, 0.0, weights).astype(BF16), v_ref[1], preferred_element_type=F32)
    high = rounded(total)
    low = total - high
    lane = lax.broadcasted_iota(jnp.int32, (16, 128), 1)
    stats = jnp.zeros((16, 128), F32)
    for g in range(GROUP):
        a, b = slice(g * 8, g * 8 + 8), slice(64 + g * 8, 64 + g * 8 + 8)
        out_ref[:, g * HD : (g + 1) * HD] = jnp.concatenate(
            [numer[a, :HD], numer[b, HD:]], 0
        ).astype(BF16)
        for slot, value in enumerate((top, high, low)):
            column = jnp.concatenate([value[a], value[b]], 0)
            stats = jnp.where(lane == slot * GROUP + g, column, stats)
    out_ref[:, GROUP * HD :] = stats.astype(BF16)


def cache_attention(limits, queries, key_cache, value_cache, cosine, sine):
    seqs, length, width = key_cache.shape
    pairs = width // (2 * HD)
    table = pl.BlockSpec((8, HD), lambda p: (0, 0))
    cache = pl.BlockSpec((seqs, length, 2 * HD), lambda p: (0, 0, p))
    return pl.pallas_call(
        cache_kernel,
        grid=(pairs,),
        in_specs=[
            pl.BlockSpec(memory_space=pltpu.SMEM),
            pl.BlockSpec((seqs, STEPS, 2 * GROUP * HD), lambda p: (0, 0, p)),
            cache,
            cache,
            table,
            table,
        ],
        out_specs=[
            pl.BlockSpec((16, PAIR), lambda p: (0, p)),
            pl.BlockSpec((16, GROUP * HD), lambda p: (0, p)),
        ],
        out_shape=[
            jax.ShapeDtypeStruct((16, pairs * PAIR), BF16),
            jax.ShapeDtypeStruct((16, pairs * GROUP * HD), BF16),
        ],
        compiler_params=pltpu.CompilerParams(vmem_limit_bytes=32 * 2**20),
        cost_estimate=pl.CostEstimate(
            flops=4 * 128 * 256 * seqs * length * pairs,
            bytes_accessed=4 * seqs * length * width,
            transcendentals=128 * length * pairs,
        ),
        name="cache_attention",
    )(limits, queries, key_cache, value_cache, cosine, sine)


def base_kernel(x_ref, gain_ref, wk_ref, wv_ref, out_ref, acc_ref, sq_ref):
    step = pl.program_id(0)
    x = tokens(x_ref)
    scaled = (x * gain_ref[...].astype(F32)).astype(BF16)
    part = jnp.concatenate(
        [
            jnp.dot(scaled, wk_ref[...], preferred_element_type=F32),
            jnp.dot(scaled, wv_ref[...], preferred_element_type=F32),
        ],
        0,
    )
    squares = jnp.broadcast_to(jnp.sum(x * x, 1, keepdims=True), (8, 128))

    @pl.when(step == 0)
    def _():
        acc_ref[...] = part
        sq_ref[...] = squares

    @pl.when(step > 0)
    def _():
        acc_ref[...] += part
        sq_ref[...] += squares

    @pl.when(step == pl.num_programs(0) - 1)
    def _():
        width = acc_ref.shape[1]
        out_ref[:, :width] = acc_ref[...].astype(BF16)
        total = sq_ref[...]
        high = rounded(total)
        out_ref[:, width:] = jnp.concatenate([high, total - high], 0).astype(BF16)


def base_projection(hidden, gain, key_weight, value_weight):
    depth, width = key_weight.shape
    chunk = 512
    weight = pl.BlockSpec((chunk, width), lambda c: (c, 0))
    return pl.pallas_call(
        base_kernel,
        grid=(depth // chunk,),
        in_specs=[
            pl.BlockSpec((2, STEPS, chunk), lambda c: (0, 0, c)),
            pl.BlockSpec((1, chunk), lambda c: (0, c)),
            weight,
            weight,
        ],
        out_specs=pl.BlockSpec((16, width + 128), lambda c: (0, 0)),
        out_shape=jax.ShapeDtypeStruct((16, width + 128), BF16),
        scratch_shapes=[pltpu.VMEM((16, width), F32), pltpu.VMEM((8, 128), F32)],
        compiler_params=pltpu.CompilerParams(vmem_limit_bytes=32 * 2**20),
        cost_estimate=pl.CostEstimate(
            flops=4 * 16 * depth * width, bytes_accessed=4 * depth * width, transcendentals=0
        ),
        name="base_projection",
    )(hidden, gain, key_weight, value_weight)


def rank_kernel(n, place_ref, gain_ref, kd_ref, vd_ref, *refs):
    gain = gain_ref[...].astype(F32)
    x = jnp.concatenate([tokens(ref) for ref in refs[:n]], 0)
    own = kd_ref.shape[0]
    fill = jnp.zeros((64 - own, x.shape[1]), F32)
    down = jnp.concatenate([kd_ref[...], fill, vd_ref[...], fill], 0).astype(BF16)
    z = lax.dot_general((x * gain).astype(BF16), down, NT, preferred_element_type=F32)
    z = pltpu.roll(z, place_ref[0] * own, 1)
    for i in range(n):
        refs[n + i][...] = z[8 * i : 8 * i + 8]


def rank_products(place, gain, key_down, value_down, hiddens):
    n = len(hiddens)
    whole = pl.BlockSpec(memory_space=pltpu.VMEM)
    return pl.pallas_call(
        functools.partial(rank_kernel, n),
        in_specs=[pl.BlockSpec(memory_space=pltpu.SMEM)] + [whole] * (3 + n),
        out_specs=[whole] * n,
        out_shape=[jax.ShapeDtypeStruct((8, 128), F32)] * n,
        compiler_params=pltpu.CompilerParams(vmem_limit_bytes=32 * 2**20),
        cost_estimate=pl.CostEstimate(
            flops=2 * 8 * n * 128 * key_down.shape[1],
            bytes_accessed=8 * key_down.size + 2 * n * hiddens[0].size,
            transcendentals=0,
        ),
        name="rank_products",
    )(place, gain, key_down, value_down, *hiddens)


def final_kernel(counts, width_all, place_ref, cos_ref, sin_ref, qrot_ref, *refs):
    nz, nu, nt = counts
    zs, refs = refs[:nz], refs[nz:]
    ups, refs = refs[:nu], refs[nu:]
    bases, refs = refs[:nt], refs[nt:]
    caches, refs = refs[:nt], refs[nt:]
    keys_out, values_out, out_ref, kv_ref = refs
    width = kv_ref.shape[1]
    cosine, sine = cos_ref[...], sin_ref[...]
    z = zs[0][...]
    for ref in zs[1:]:
        z = z + ref[...]
    lane8 = lax.broadcasted_iota(jnp.int32, (8, 128), 1)
    z = jnp.concatenate([jnp.where(lane8 < 64, z, 0.0), jnp.where(lane8 < 64, 0.0, z)], 0).astype(BF16)
    for d, ref in enumerate(ups):
        rows = ref.shape[0]
        at = pl.multiple_of((place_ref[0] ^ d) * rows, rows) if nu > 1 else 0
        kv_ref[:, pl.ds(at, rows)] = lax.dot_general(z, ref[...], NT, preferred_element_type=F32)
    total = kv_ref[...]
    squares = jnp.zeros((8, 128), F32)
    for ref in bases:
        total = total + ref[:, :width].astype(F32)
        tail = ref[:, width:].astype(F32)
        squares = squares + tail[:8] + tail[8:]
    scale = lax.rsqrt(squares / width_all + EPSILON)
    row16 = lax.broadcasted_iota(jnp.int32, (16, 128), 0)
    row8 = lax.broadcasted_iota(jnp.int32, (8, 128), 0)
    lane = lax.broadcasted_iota(jnp.int32, (16, 128), 1)
    step = row16 % STEPS

    def of_step(tile, j):
        return jnp.where(row8 < STEPS, tile[j : j + 1], tile[STEPS + j : STEPS + j + 1])

    for p in range(width // (2 * HD)):
        new_keys, new_values = [], []
        for e in range(2):
            at = slice((2 * p + e) * HD, (2 * p + e + 1) * HD)
            new_keys.append(rounded(rotated(total[:8, at] * scale, cosine, sine)))
            new_values.append(rounded(total[8:, at] * scale))
        at = slice(2 * p * HD, 2 * (p + 1) * HD)
        for out, parts in ((keys_out, new_keys), (values_out, new_values)):
            both = jnp.concatenate(parts, 1).astype(BF16)
            out[0, :, at] = both[:STEPS]
            out[1, :, at] = both[STEPS:]
        keys = [
            jnp.concatenate([of_step(new_keys[0], j), of_step(new_keys[1], j)], 0)
            for j in range(STEPS)
        ]
        values = [
            jnp.concatenate([of_step(new_values[0], j), of_step(new_values[1], j)], 0)
            for j in range(STEPS)
        ]
        scores = [jnp.zeros((16, 128), F32) for _ in range(STEPS)]
        for g in range(GROUP):
            q = qrot_ref[:, (p * GROUP + g) * HD : (p * GROUP + g + 1) * HD].astype(F32)
            for j in range(STEPS):
                dot = jnp.sum(q * keys[j], 1, keepdims=True) * SCALE
                scores[j] = jnp.where(lane == g, dot, scores[j])
        scores = [jnp.where(j <= step, scores[j], MASKED_SCORE) for j in range(STEPS)]
        stats = [
            ref[:, p * PAIR + GROUP * HD : (p + 1) * PAIR].astype(F32) for ref in caches
        ]
        top = functools.reduce(jnp.maximum, scores + stats)
        fresh = [rounded(jnp.where(j <= step, jnp.exp(scores[j] - top), 0.0)) for j in range(STEPS)]
        factors = [jnp.exp(jnp.minimum(s - top, 0.0)) for s in stats]
        denom = functools.reduce(jnp.add, fresh)
        for factor, s in zip(factors, stats):
            denom = denom + factor * (
                pltpu.roll(s, 128 - GROUP, 1) + pltpu.roll(s, 128 - 2 * GROUP, 1)
            )
        inverse = 1.0 / denom
        coefficients = [c * inverse for c in fresh + factors]
        tiles = []
        for g in range(GROUP):
            at = slice(p * PAIR + g * HD, p * PAIR + (g + 1) * HD)
            terms = values + [ref[:, at].astype(F32) for ref in caches]
            tile = jnp.zeros((16, 128), F32)
            for c, term in zip(coefficients, terms):
                tile = tile + c[:, g : g + 1] * term
            tiles.append(tile)
        both = jnp.concatenate(tiles, 1)
        for e in range(2):
            at = slice((2 * p + e) * GROUP * HD, (2 * p + e + 1) * GROUP * HD)
            for s in range(2):
                out_ref[s, :, at] = both[8 * e + 4 * s : 8 * e + 4 * s + 4].astype(BF16)


def final(place, cosine, sine, qrot, zs, ups, bases, caches, width_all):
    width = bases[0].shape[1] - 128
    whole = pl.BlockSpec(memory_space=pltpu.VMEM)
    operands = [cosine, sine, qrot, *zs, *ups, *bases, *caches]
    return pl.pallas_call(
        functools.partial(final_kernel, (len(zs), len(ups), len(bases)), width_all),
        in_specs=[pl.BlockSpec(memory_space=pltpu.SMEM)] + [whole] * len(operands),
        out_specs=[whole] * 3,
        out_shape=[
            jax.ShapeDtypeStruct((2, STEPS, width), BF16),
            jax.ShapeDtypeStruct((2, STEPS, width), BF16),
            jax.ShapeDtypeStruct((2, STEPS, GROUP * width), BF16),
        ],
        scratch_shapes=[pltpu.VMEM((16, width), F32)],
        compiler_params=pltpu.CompilerParams(vmem_limit_bytes=32 * 2**20),
        name="final",
    )(place, *operands)


def swaps(value, axis, n):
    return [value] + [
        lax.ppermute(value, axis, [(i, i ^ d) for i in range(n)]) for d in range(1, n)
    ]


def shards(
    n_dp,
    n_tensor,
    hidden,
    norm_gain,
    queries,
    key_weight,
    value_weight,
    key_down,
    key_up,
    value_down,
    value_up,
    key_cache,
    value_cache,
    lengths,
):
    dp_place = lax.axis_index("dp").astype(jnp.int32).reshape(1)
    tensor_place = lax.axis_index("tensor").astype(jnp.int32)
    gain = norm_gain.reshape(1, -1)
    hiddens = swaps(hidden, "dp", n_dp)
    ups = jnp.concatenate([key_up, value_up], 1).astype(BF16)
    if n_dp <= 4:
        ups = swaps(ups, "dp", n_dp)
    else:
        ups = [lax.all_gather(ups, "dp", axis=0, tiled=True)]

    positions = (lengths[:, None] + jnp.arange(STEPS, dtype=jnp.int32)[None, :]).reshape(-1, 1)
    half = HD // 2
    frequency = ROPE_BASE ** (-(2.0 * jnp.arange(half, dtype=F32)) / HD)
    angles = positions.astype(F32) * frequency
    cosine = jnp.cos(angles)
    sine = jnp.sin(angles)
    cosine = jnp.concatenate([cosine, cosine], 1)
    sine = jnp.concatenate([-sine, sine], 1)
    limits = lengths - tensor_place * key_cache.shape[1]

    base = base_projection(hidden, gain, key_weight, value_weight)
    bases = swaps(base, "tensor", n_tensor)
    cache, qrot = cache_attention(limits, queries, key_cache, value_cache, cosine, sine)
    caches = swaps(cache, "tensor", n_tensor)

    ranks = rank_products(dp_place, gain, key_down, value_down, hiddens)
    if n_dp <= 4:
        zs = []
        for d in range(n_dp):
            for e in range(n_tensor):
                if d == 0 and e == 0:
                    zs.append(ranks[0])
                    continue
                perm = [
                    (a * n_tensor + b, (a ^ d) * n_tensor + (b ^ e))
                    for a in range(n_dp)
                    for b in range(n_tensor)
                ]
                zs.append(lax.ppermute(ranks[d], ("dp", "tensor"), perm))
    else:
        total = ranks[0]
        for d in range(1, n_dp):
            total = total + lax.ppermute(ranks[d], "dp", [(i, i ^ d) for i in range(n_dp)])
        zs = [lax.psum(total, "tensor")]
    return final(
        dp_place, cosine, sine, qrot, zs, ups, bases, caches, float(hidden.shape[2] * n_tensor)
    )


def solution(mesh):
    body = functools.partial(shards, mesh.shape["dp"], mesh.shape["tensor"])
    return jax.shard_map(
        body,
        mesh=mesh,
        in_specs=(
            P(("groups", "dp"), None, "tensor"),
            P("tensor"),
            P(("groups", "dp"), None, None),
            P("tensor", None),
            P("tensor", None),
            P(("groups", "dp"), "tensor"),
            P(("groups", "dp"), None),
            P(("groups", "dp"), "tensor"),
            P(("groups", "dp"), None),
            P(("groups", "dp"), "tensor", None),
            P(("groups", "dp"), "tensor", None),
            P(("groups", "dp")),
        ),
        out_specs=(
            P(("groups", "dp"), None, None),
            P(("groups", "dp"), None, None),
            P(("groups", "dp"), None, None),
        ),
        check_vma=False,
    )
```

time: 159 us -> 63.9 us (0.40)
  blocking collectives: 76.3 us -> 0 us
  starting transfers between devices: 0.08 us -> 32.2 us
  waiting for transfers between devices: 30.3 us -> 10.3 us
  matrix products: 18.8 us -> 0 us
  between operations: 14.4 us -> 0.79 us
  Pallas kernels: 0 us -> 8.53 us
  other arithmetic: 8.02 us -> 1.7 us
    all_gather x6 -> x0, blocking collectives: 68 us -> none  [the longest x1 14.6 us: shards(): lax.all_gather(value_up, 'dp', axis=0, tiled=True)]
    ppermute x0 -> x27, starting transfers between devices: none -> 32.2 us  [the longest x15 20.5 us: shards(): zs.append(lax.ppermute(ranks[d], ('dp', 'tensor'), perm))]
    psum x1 -> x0, waiting for transfers between devices: 26.8 us -> none  [shards(): summed = lax.psum(partial_kv, 'tensor')]
    dot_general x8 -> x0, matrix products: 18.8 us -> none  [the longest x1 3.54 us: shards(): jnp.dot(lax.all_gather(key_down.astype(jnp.bfloat16), 'dp', axis=0, tiled...]
    ppermute x0 -> x27, waiting for transfers between devices: none -> 10.3 us  [the longest x12 10.3 us: swaps(): lax.ppermute(value, axis, [(i, i ^ d) for i in range(n)])]
    pallas_call x0 -> x4, Pallas kernels: none -> 8.53 us  [the longest x1 3.98 us: cache_attention(): pl.pallas_call(cache_kernel, grid=(pairs,), in_specs=[pl.BlockSpec(memory...]
    psum x1 -> x0, blocking collectives: 8.31 us -> none  [shards(): lax.psum(jnp.sum(rows_flat * rows_flat, axis=1, keepdims=True), 'tensor')]
    unnamed x30 -> x22, local copies, waits for them, and re-layouts: 3.66 us -> 8.86 us
  transfers between devices with their start and end apart: 2 -> 27, of which waited for: 2 -> 5; matrix products, arithmetic and copies ran while one was open for 4% -> 4% of each run, Pallas kernels for 0% -> 9%
where the time goes in v1:
time: 63.9 us; the launch traced here: 63.5 us
  starting transfers between devices  32.2 us (50%)
  waiting for transfers between devices  10.3 us (16%)
  local copies, waits for them, and re-layouts  10 us (16%)
  Pallas kernels  8.53 us (13%)
  other arithmetic  1.7 us (3%)
  between operations  0.79 us (1%)
    ppermute x15, starting transfers between devices, shards(): zs.append(lax.ppermute(ranks[d], ('dp', 'tensor'), perm))  20.5 us
    ppermute x12, starting transfers between devices, swaps(): lax.ppermute(value, axis, [(i, i ^ d) for i in range(n)])  11.7 us
    ppermute x12, waiting for transfers between devices, swaps(): lax.ppermute(value, axis, [(i, i ^ d) for i in range(n)])  10.3 us
    unnamed x22, local copies, waits for them, and re-layouts  8.86 us
    pallas_call x1, Pallas kernels, cache_attention(): pl.pallas_call(cache_kernel, grid=(pairs,), in_specs=[pl.BlockSpec(memory...  3.98 us
    pallas_call x1, Pallas kernels, final(): pl.pallas_call(functools.partial(final_kernel, (len(zs), len(ups), len(ba...  2.66 us
    pallas_call x1, Pallas kernels, base_projection(): pl.pallas_call(base_kernel, grid=(depth // chunk,), in_specs=[pl.BlockSpe...  1.62 us
  transfers between devices with their start and end apart: 27, of which 5 were waited for; matrix products, arithmetic and copies ran while one was open for 4% of the time, Pallas kernels for 9%

profile of v1, /device:TPU:0, one launch (start us, length us, event | category | flops | bytes accessed | tf_op | source)
XLA Modules:
  0.0 63.5 jit_solution(7394522955375150369)
XLA Ops:
  0.6 5.1 %collective-permute-start.2 = (bf16[2,4,2048]{2,1,0:T(4,128)(2,1)}, bf16[2,4,2048]{2,1,0:T(4,128)(2,1)S(1)}, u32[]{:S(2)}, u32[]{:S(2)}) collective-permute-start(bf16[2,4,2048]{2,1,0:T(4,128)(2,1)} %x_ref.1), channel_id=1, source_target_pairs={{0,12},{4,8},{8,4},{12,0},{1,13},{5,9},{9,5},{13,1},{2,14},{6,10},... | collective-permute-start | bytes 98312 | tf_op jit(solution)/shard_map/ppermute | solution.py:307
  8.9 1.9 %collective-permute-done.1.refs_2_ = bf16[2,4,2048]{2,1,0:T(4,128)(2,1)S(1)} collective-permute-done((bf16[2,4,2048]{2,1,0:T(4,128)(2,1)}, bf16[2,4,2048]{2,1,0:T(4,128)(2,1)S(1)}, u32[]{:S(2)}, u32[]{:S(2)}) %collective-permute-start.1) | collective-permute-done | bytes 32800 | tf_op jit(solution)/shard_map/ppermute | solution.py:307
  13.7 1.6 %collective-permute-start.4 = (f32[8,128]{1,0:T(8,128)S(1)}, f32[8,128]{1,0:T(8,128)S(1)}, u32[]{:S(2)}, u32[]{:S(2)}) collective-permute-start(f32[8,128]{1,0:T(8,128)S(1)} %get-tuple-element.10.refs_0_), channel_id=1, source_target_pairs={{0,2},{1,3},{2,0},{3,1},{4,6},{5,7},{6,4},{7,5},{8,10},{9,11},{10,... | collective-permute-start | bytes 12296 | tf_op jit(solution)/shard_map/ppermute | solution.py:365
  15.9 2.3 %collective-permute-start.8 = (f32[8,128]{1,0:T(8,128)S(1)}, f32[8,128]{1,0:T(8,128)S(1)}, u32[]{:S(2)}, u32[]{:S(2)}) collective-permute-start(f32[8,128]{1,0:T(8,128)S(1)} %get-tuple-element.11), channel_id=1, source_target_pairs={{0,6},{1,7},{2,4},{3,5},{4,2},{5,3},{6,0},{7,1},{8,14},{9,15},{10,... | collective-permute-start | bytes 12296 | tf_op jit(solution)/shard_map/ppermute | solution.py:365
  18.4 1.6 %collective-permute-start.6 = (f32[8,128]{1,0:T(8,128)S(1)}, f32[8,128]{1,0:T(8,128)S(1)}, u32[]{:S(2)}, u32[]{:S(2)}) collective-permute-start(f32[8,128]{1,0:T(8,128)S(1)} %get-tuple-element.11), channel_id=1, source_target_pairs={{0,4},{1,5},{2,6},{3,7},{4,0},{5,1},{6,2},{7,3},{8,12},{9,13},{10,... | collective-permute-start | bytes 12296 | tf_op jit(solution)/shard_map/ppermute | solution.py:365
  20.0 2.6 %collective-permute-start.13 = (f32[8,128]{1,0:T(8,128)S(1)}, f32[8,128]{1,0:T(8,128)S(1)}, u32[]{:S(2)}, u32[]{:S(2)}) collective-permute-start(f32[8,128]{1,0:T(8,128)S(1)} %get-tuple-element.12), channel_id=1, source_target_pairs={{0,11},{1,10},{2,9},{3,8},{4,15},{5,14},{6,13},{7,12},{8,3},{9,2},... | collective-permute-start | bytes 12296 | tf_op jit(solution)/shard_map/ppermute | solution.py:365
  22.6 1.1 %collective-permute-start.12 = (f32[8,128]{1,0:T(8,128)S(1)}, f32[8,128]{1,0:T(8,128)S(1)}, u32[]{:S(2)}, u32[]{:S(2)}) collective-permute-start(f32[8,128]{1,0:T(8,128)S(1)} %get-tuple-element.12), channel_id=1, source_target_pairs={{0,10},{1,11},{2,8},{3,9},{4,14},{5,15},{6,12},{7,13},{8,2},{9,3},... | collective-permute-start | bytes 12296 | tf_op jit(solution)/shard_map/ppermute | solution.py:365
  23.7 1.6 %collective-permute-start.11 = (f32[8,128]{1,0:T(8,128)S(1)}, f32[8,128]{1,0:T(8,128)S(1)}, u32[]{:S(2)}, u32[]{:S(2)}) collective-permute-start(f32[8,128]{1,0:T(8,128)S(1)} %get-tuple-element.12), channel_id=1, source_target_pairs={{0,9},{1,8},{2,11},{3,10},{4,13},{5,12},{6,15},{7,14},{8,1},{9,0},... | collective-permute-start | bytes 12296 | tf_op jit(solution)/shard_map/ppermute | solution.py:365
  25.3 1.6 %copy-done.2 = bf16[2,512,1024]{2,1,0:T(8,128)(2,1)S(1)} copy-done((bf16[2,512,1024]{2,1,0:T(8,128)(2,1)S(1)}, bf16[2,512,1024]{2,1,0:T(8,128)(2,1)}, u32[]{:S(2)}) %copy-start.2) | copy-done | bytes 2097176
  26.9 1.6 %copy-done.3 = bf16[2,512,1024]{2,1,0:T(8,128)(2,1)S(1)} copy-done((bf16[2,512,1024]{2,1,0:T(8,128)(2,1)S(1)}, bf16[2,512,1024]{2,1,0:T(8,128)(2,1)}, u32[]{:S(2)}) %copy-start.3) | copy-done | bytes 2097176
  29.4 4.0 %cache_attention.1 = (bf16[16,4608]{1,0:T(8,128)(2,1)S(1)}, bf16[16,4096]{1,0:T(8,128)(2,1)S(1)}) custom-call(s32[2]{0:T(128)S(1)} %broadcast_subtract_fusion.limit_ref, bf16[2,4,8192]{2,1,0:T(4,128)(2,1)S(1)} %copy-done.6, bf16[2,512,1024]{2,1,0:T(8,128)(2,1)S(1)} %copy-done.2, bf16[2,512,1024]{2,1,0:T(8,128)(2,1)S(1)} %copy-done.3, ...), custom_call_target="tpu_custom_call" | custom-call | flops 536870912 | bytes 4194304 | tf_op jit(solution)/shard_map/cache_attention/pallas_call | solution.py:84
  34.4 2.6 %collective-permute-start.17 = (f32[8,128]{1,0:T(8,128)S(1)}, f32[8,128]{1,0:T(8,128)S(1)}, u32[]{:S(2)}, u32[]{:S(2)}) collective-permute-start(f32[8,128]{1,0:T(8,128)S(1)} %get-tuple-element.13), channel_id=1, source_target_pairs={{0,15},{1,14},{2,13},{3,12},{4,11},{5,10},{6,9},{7,8},{8,7},{9,6},... | collective-permute-start | bytes 12296 | tf_op jit(solution)/shard_map/ppermute | solution.py:365
  36.9 2.0 %collective-permute-start.16 = (f32[8,128]{1,0:T(8,128)S(1)}, f32[8,128]{1,0:T(8,128)S(1)}, u32[]{:S(2)}, u32[]{:S(2)}) collective-permute-start(f32[8,128]{1,0:T(8,128)S(1)} %get-tuple-element.13), channel_id=1, source_target_pairs={{0,14},{1,15},{2,12},{3,13},{4,10},{5,11},{6,8},{7,9},{8,6},{9,7},... | collective-permute-start | bytes 12296 | tf_op jit(solution)/shard_map/ppermute | solution.py:365
  38.9 1.6 %collective-permute-start.15 = (f32[8,128]{1,0:T(8,128)S(1)}, f32[8,128]{1,0:T(8,128)S(1)}, u32[]{:S(2)}, u32[]{:S(2)}) collective-permute-start(f32[8,128]{1,0:T(8,128)S(1)} %get-tuple-element.13), channel_id=1, source_target_pairs={{0,13},{1,12},{2,15},{3,14},{4,9},{5,8},{6,11},{7,10},{8,5},{9,4},... | collective-permute-start | bytes 12296 | tf_op jit(solution)/shard_map/ppermute | solution.py:365
  40.6 1.8 %collective-permute-start.14 = (f32[8,128]{1,0:T(8,128)S(1)}, f32[8,128]{1,0:T(8,128)S(1)}, u32[]{:S(2)}, u32[]{:S(2)}) collective-permute-start(f32[8,128]{1,0:T(8,128)S(1)} %get-tuple-element.13), channel_id=1, source_target_pairs={{0,12},{1,13},{2,14},{3,15},{4,8},{5,9},{6,10},{7,11},{8,4},{9,5},... | collective-permute-start | bytes 12296 | tf_op jit(solution)/shard_map/ppermute | solution.py:365
  42.4 2.2 %copy-done.1 = bf16[2048,1024]{1,0:T(8,128)(2,1)S(1)} copy-done((bf16[2048,1024]{1,0:T(8,128)(2,1)S(1)}, bf16[2048,1024]{1,0:T(8,128)(2,1)}, u32[]{:S(2)}) %copy-start.1) | copy-done | bytes 4194328
  44.5 1.6 %base_projection.1.refs_20_ = bf16[16,1152]{1,0:T(8,128)(2,1)S(1)} custom-call(bf16[2,4,2048]{2,1,0:T(4,128)(2,1)S(1)} %copy-done.5, bf16[1,2048]{1,0:T(2,128)(2,1)S(1)} %reshape.38.gain_ref, bf16[2048,1024]{1,0:T(8,128)(2,1)S(1)} %copy-done, bf16[2048,1024]{1,0:T(8,128)(2,1)S(1)} %copy-done.1), custom_call_target="tpu_custom_call" | custom-call | flops 134217728 | bytes 8388608 | tf_op jit(solution)/shard_map/base_projection/pallas_call | solution.py:149
  46.5 1.2 %collective-permute-start.23 = (bf16[16,1152]{1,0:T(8,128)(2,1)S(1)}, bf16[16,1152]{1,0:T(8,128)(2,1)S(1)}, u32[]{:S(2)}, u32[]{:S(2)}) collective-permute-start(bf16[16,1152]{1,0:T(8,128)(2,1)S(1)} %base_projection.1.refs_20_), channel_id=1, source_target_pairs={{0,3},{1,2},{2,1},{3,0},{4,7},{5,6},{6,5},{7,4},{8,11},{9,10},{10,... | collective-permute-start | bytes 110600 | tf_op jit(solution)/shard_map/ppermute | solution.py:307
  50.4 2.1 %collective-permute-start.20 = (bf16[256,128]{1,0:T(8,128)(2,1)S(1)}, bf16[256,128]{1,0:T(8,128)(2,1)S(1)}, u32[]{:S(2)}, u32[]{:S(2)}) collective-permute-start(bf16[256,128]{1,0:T(8,128)(2,1)S(1)} %pad_maximum_fusion.refs_16_), channel_id=1, source_target_pairs={{0,12},{4,8},{8,4},{12,0},{1,13},{5,9},{9,5},{13,1},{2,14},{6,10},... | collective-permute-start | bytes 196616 | tf_op jit(solution)/shard_map/ppermute | solution.py:307
  52.5 1.2 %collective-permute-done.21.refs_21_ = bf16[16,1152]{1,0:T(8,128)(2,1)S(1)} collective-permute-done((bf16[16,1152]{1,0:T(8,128)(2,1)S(1)}, bf16[16,1152]{1,0:T(8,128)(2,1)S(1)}, u32[]{:S(2)}, u32[]{:S(2)}) %collective-permute-start.21) | collective-permute-done | bytes 36896 | tf_op jit(solution)/shard_map/ppermute | solution.py:307
  53.7 2.9 %collective-permute-done.20.refs_19_ = bf16[256,128]{1,0:T(8,128)(2,1)S(1)} collective-permute-done((bf16[256,128]{1,0:T(8,128)(2,1)S(1)}, bf16[256,128]{1,0:T(8,128)(2,1)S(1)}, u32[]{:S(2)}, u32[]{:S(2)}) %collective-permute-start.20) | collective-permute-done | bytes 65568 | tf_op jit(solution)/shard_map/ppermute | solution.py:307
  56.6 2.9 %collective-permute-done.19.refs_18_ = bf16[256,128]{1,0:T(8,128)(2,1)S(1)} collective-permute-done((bf16[256,128]{1,0:T(8,128)(2,1)S(1)}, bf16[256,128]{1,0:T(8,128)(2,1)S(1)}, u32[]{:S(2)}, u32[]{:S(2)}) %collective-permute-start.19) | collective-permute-done | bytes 65568 | tf_op jit(solution)/shard_map/ppermute | solution.py:307
  59.4 1.4 %collective-permute-done.18.refs_17_ = bf16[256,128]{1,0:T(8,128)(2,1)S(1)} collective-permute-done((bf16[256,128]{1,0:T(8,128)(2,1)S(1)}, bf16[256,128]{1,0:T(8,128)(2,1)S(1)}, u32[]{:S(2)}, u32[]{:S(2)}) %collective-permute-start.18) | collective-permute-done | bytes 65568 | tf_op jit(solution)/shard_map/ppermute | solution.py:307
  60.9 2.7 %final.1 = (bf16[2,4,1024]{2,1,0:T(4,128)(2,1)}, bf16[2,4,1024]{2,1,0:T(4,128)(2,1)}, bf16[2,4,8192]{2,1,0:T(4,128)(2,1)}) custom-call(s32[1]{0:T(128)} %bitcast.place_ref, f32[8,128]{1,0:T(8,128)S(1)} %get-tuple-element.18.cos_ref, f32[8,128]{1,0:T(8,128)S(1)} %get-tuple-element.19.sin_ref, bf16[16,4096]{1,0:T(8,128)(2,1)S(1)} %get-tuple-element.9.qrot_ref, ...), custom_call_target="tpu_custom_call" | custom-call | tf_op jit(solution)/shard_map/final/pallas_call | solution.py:290
  (68 shorter events, 11.7 us)
Async XLA Ops:
  0.6 8.2 %collective-permute-start.2 = (bf16[2,4,2048]{2,1,0:T(4,128)(2,1)}, bf16[2,4,2048]{2,1,0:T(4,128)(2,1)S(1)}, u32[]{:S(2)}, u32[]{:S(2)}) collective-permute-start(bf16[2,4,2048]{2,1,0:T(4,128)(2,1)} %x_ref.1), channel_id=1, source_target_pairs={{0,12},{4,8},{8,4},{12,0},{1,13},{5,9},{9,5},{13,1},{2,14},{6,10},... | collective-permute-start | bytes 98312 | tf_op jit(solution)/shard_map/ppermute | solution.py:307
  5.8 5.0 %collective-permute-start.1 = (bf16[2,4,2048]{2,1,0:T(4,128)(2,1)}, bf16[2,4,2048]{2,1,0:T(4,128)(2,1)S(1)}, u32[]{:S(2)}, u32[]{:S(2)}) collective-permute-start(bf16[2,4,2048]{2,1,0:T(4,128)(2,1)} %x_ref.1), channel_id=1, source_target_pairs={{0,8},{4,12},{8,0},{12,4},{1,9},{5,13},{9,1},{13,5},{2,10},{6,14},... | collective-permute-start | bytes 98312 | tf_op jit(solution)/shard_map/ppermute | solution.py:307
  5.8 5.0 %collective-permute-start = (bf16[2,4,2048]{2,1,0:T(4,128)(2,1)}, bf16[2,4,2048]{2,1,0:T(4,128)(2,1)S(1)}, u32[]{:S(2)}, u32[]{:S(2)}) collective-permute-start(bf16[2,4,2048]{2,1,0:T(4,128)(2,1)} %x_ref.1), channel_id=1, source_target_pairs={{0,4},{4,0},{8,12},{12,8},{1,5},{5,1},{9,13},{13,9},{2,6},{6,2},{1... | collective-permute-start | bytes 98312 | tf_op jit(solution)/shard_map/ppermute | solution.py:307
  13.6 4.7 %collective-permute-start.5 = (f32[8,128]{1,0:T(8,128)S(1)}, f32[8,128]{1,0:T(8,128)S(1)}, u32[]{:S(2)}, u32[]{:S(2)}) collective-permute-start(f32[8,128]{1,0:T(8,128)S(1)} %get-tuple-element.10.refs_0_), channel_id=1, source_target_pairs={{0,3},{1,2},{2,1},{3,0},{4,7},{5,6},{6,5},{7,4},{8,11},{9,10},{10,... | collective-permute-start | bytes 12296 | tf_op jit(solution)/shard_map/ppermute | solution.py:365
  13.7 4.7 %collective-permute-start.4 = (f32[8,128]{1,0:T(8,128)S(1)}, f32[8,128]{1,0:T(8,128)S(1)}, u32[]{:S(2)}, u32[]{:S(2)}) collective-permute-start(f32[8,128]{1,0:T(8,128)S(1)} %get-tuple-element.10.refs_0_), channel_id=1, source_target_pairs={{0,2},{1,3},{2,0},{3,1},{4,6},{5,7},{6,4},{7,5},{8,10},{9,11},{10,... | collective-permute-start | bytes 12296 | tf_op jit(solution)/shard_map/ppermute | solution.py:365
  15.2 4.8 %collective-permute-start.3 = (f32[8,128]{1,0:T(8,128)S(1)}, f32[8,128]{1,0:T(8,128)S(1)}, u32[]{:S(2)}, u32[]{:S(2)}) collective-permute-start(f32[8,128]{1,0:T(8,128)S(1)} %get-tuple-element.10.refs_0_), channel_id=1, source_target_pairs={{0,1},{1,0},{2,3},{3,2},{4,5},{5,4},{6,7},{7,6},{8,9},{9,8},{10,11... | collective-permute-start | bytes 12296 | tf_op jit(solution)/shard_map/ppermute | solution.py:365
  15.5 7.1 %collective-permute-start.9 = (f32[8,128]{1,0:T(8,128)S(1)}, f32[8,128]{1,0:T(8,128)S(1)}, u32[]{:S(2)}, u32[]{:S(2)}) collective-permute-start(f32[8,128]{1,0:T(8,128)S(1)} %get-tuple-element.11), channel_id=1, source_target_pairs={{0,7},{1,6},{2,5},{3,4},{4,3},{5,2},{6,1},{7,0},{8,15},{9,14},{10,... | collective-permute-start | bytes 12296 | tf_op jit(solution)/shard_map/ppermute | solution.py:365
  15.9 7.7 %collective-permute-start.8 = (f32[8,128]{1,0:T(8,128)S(1)}, f32[8,128]{1,0:T(8,128)S(1)}, u32[]{:S(2)}, u32[]{:S(2)}) collective-permute-start(f32[8,128]{1,0:T(8,128)S(1)} %get-tuple-element.11), channel_id=1, source_target_pairs={{0,6},{1,7},{2,4},{3,5},{4,2},{5,3},{6,0},{7,1},{8,14},{9,15},{10,... | collective-permute-start | bytes 12296 | tf_op jit(solution)/shard_map/ppermute | solution.py:365
  18.3 15.0 %collective-permute-start.7 = (f32[8,128]{1,0:T(8,128)S(1)}, f32[8,128]{1,0:T(8,128)S(1)}, u32[]{:S(2)}, u32[]{:S(2)}) collective-permute-start(f32[8,128]{1,0:T(8,128)S(1)} %get-tuple-element.11), channel_id=1, source_target_pairs={{0,5},{1,4},{2,7},{3,6},{4,1},{5,0},{6,3},{7,2},{8,13},{9,12},{10,... | collective-permute-start | bytes 12296 | tf_op jit(solution)/shard_map/ppermute | solution.py:365
  18.4 16.0 %collective-permute-start.6 = (f32[8,128]{1,0:T(8,128)S(1)}, f32[8,128]{1,0:T(8,128)S(1)}, u32[]{:S(2)}, u32[]{:S(2)}) collective-permute-start(f32[8,128]{1,0:T(8,128)S(1)} %get-tuple-element.11), channel_id=1, source_target_pairs={{0,4},{1,5},{2,6},{3,7},{4,0},{5,1},{6,2},{7,3},{8,12},{9,13},{10,... | collective-permute-start | bytes 12296 | tf_op jit(solution)/shard_map/ppermute | solution.py:365
  20.0 16.9 %collective-permute-start.13 = (f32[8,128]{1,0:T(8,128)S(1)}, f32[8,128]{1,0:T(8,128)S(1)}, u32[]{:S(2)}, u32[]{:S(2)}) collective-permute-start(f32[8,128]{1,0:T(8,128)S(1)} %get-tuple-element.12), channel_id=1, source_target_pairs={{0,11},{1,10},{2,9},{3,8},{4,15},{5,14},{6,13},{7,12},{8,3},{9,2},... | collective-permute-start | bytes 12296 | tf_op jit(solution)/shard_map/ppermute | solution.py:365
  22.6 16.4 %collective-permute-start.12 = (f32[8,128]{1,0:T(8,128)S(1)}, f32[8,128]{1,0:T(8,128)S(1)}, u32[]{:S(2)}, u32[]{:S(2)}) collective-permute-start(f32[8,128]{1,0:T(8,128)S(1)} %get-tuple-element.12), channel_id=1, source_target_pairs={{0,10},{1,11},{2,8},{3,9},{4,14},{5,15},{6,12},{7,13},{8,2},{9,3},... | collective-permute-start | bytes 12296 | tf_op jit(solution)/shard_map/ppermute | solution.py:365
  23.7 16.9 %collective-permute-start.11 = (f32[8,128]{1,0:T(8,128)S(1)}, f32[8,128]{1,0:T(8,128)S(1)}, u32[]{:S(2)}, u32[]{:S(2)}) collective-permute-start(f32[8,128]{1,0:T(8,128)S(1)} %get-tuple-element.12), channel_id=1, source_target_pairs={{0,9},{1,8},{2,11},{3,10},{4,13},{5,12},{6,15},{7,14},{8,1},{9,0},... | collective-permute-start | bytes 12296 | tf_op jit(solution)/shard_map/ppermute | solution.py:365
  33.4 13.1 %collective-permute-start.10 = (f32[8,128]{1,0:T(8,128)S(1)}, f32[8,128]{1,0:T(8,128)S(1)}, u32[]{:S(2)}, u32[]{:S(2)}) collective-permute-start(f32[8,128]{1,0:T(8,128)S(1)} %get-tuple-element.12), channel_id=1, source_target_pairs={{0,8},{1,9},{2,10},{3,11},{4,12},{5,13},{6,14},{7,15},{8,0},{9,1},... | collective-permute-start | bytes 12296 | tf_op jit(solution)/shard_map/ppermute | solution.py:365
  34.4 13.3 %collective-permute-start.17 = (f32[8,128]{1,0:T(8,128)S(1)}, f32[8,128]{1,0:T(8,128)S(1)}, u32[]{:S(2)}, u32[]{:S(2)}) collective-permute-start(f32[8,128]{1,0:T(8,128)S(1)} %get-tuple-element.13), channel_id=1, source_target_pairs={{0,15},{1,14},{2,13},{3,12},{4,11},{5,10},{6,9},{7,8},{8,7},{9,6},... | collective-permute-start | bytes 12296 | tf_op jit(solution)/shard_map/ppermute | solution.py:365
  36.9 11.5 %collective-permute-start.16 = (f32[8,128]{1,0:T(8,128)S(1)}, f32[8,128]{1,0:T(8,128)S(1)}, u32[]{:S(2)}, u32[]{:S(2)}) collective-permute-start(f32[8,128]{1,0:T(8,128)S(1)} %get-tuple-element.13), channel_id=1, source_target_pairs={{0,14},{1,15},{2,12},{3,13},{4,10},{5,11},{6,8},{7,9},{8,6},{9,7},... | collective-permute-start | bytes 12296 | tf_op jit(solution)/shard_map/ppermute | solution.py:365
  38.9 10.6 %collective-permute-start.15 = (f32[8,128]{1,0:T(8,128)S(1)}, f32[8,128]{1,0:T(8,128)S(1)}, u32[]{:S(2)}, u32[]{:S(2)}) collective-permute-start(f32[8,128]{1,0:T(8,128)S(1)} %get-tuple-element.13), channel_id=1, source_target_pairs={{0,13},{1,12},{2,15},{3,14},{4,9},{5,8},{6,11},{7,10},{8,5},{9,4},... | collective-permute-start | bytes 12296 | tf_op jit(solution)/shard_map/ppermute | solution.py:365
  40.6 9.5 %collective-permute-start.14 = (f32[8,128]{1,0:T(8,128)S(1)}, f32[8,128]{1,0:T(8,128)S(1)}, u32[]{:S(2)}, u32[]{:S(2)}) collective-permute-start(f32[8,128]{1,0:T(8,128)S(1)} %get-tuple-element.13), channel_id=1, source_target_pairs={{0,12},{1,13},{2,14},{3,15},{4,8},{5,9},{6,10},{7,11},{8,4},{9,5},... | collective-permute-start | bytes 12296 | tf_op jit(solution)/shard_map/ppermute | solution.py:365
  47.6 4.8 %collective-permute-start.22 = (bf16[16,1152]{1,0:T(8,128)(2,1)S(1)}, bf16[16,1152]{1,0:T(8,128)(2,1)S(1)}, u32[]{:S(2)}, u32[]{:S(2)}) collective-permute-start(bf16[16,1152]{1,0:T(8,128)(2,1)S(1)} %base_projection.1.refs_20_), channel_id=1, source_target_pairs={{0,2},{1,3},{2,0},{3,1},{4,6},{5,7},{6,4},{7,5},{8,10},{9,11},{10,... | collective-permute-start | bytes 110600 | tf_op jit(solution)/shard_map/ppermute | solution.py:307
  48.4 12.4 %collective-permute-start.26 = (bf16[16,4608]{1,0:T(8,128)(2,1)S(1)}, bf16[16,4608]{1,0:T(8,128)(2,1)S(1)}, u32[]{:S(2)}, u32[]{:S(2)}) collective-permute-start(bf16[16,4608]{1,0:T(8,128)(2,1)S(1)} %get-tuple-element.14.refs_24_), channel_id=1, source_target_pairs={{0,3},{1,2},{2,1},{3,0},{4,7},{5,6},{6,5},{7,4},{8,11},{9,10},{10,... | collective-permute-start | bytes 442376 | tf_op jit(solution)/shard_map/ppermute | solution.py:307
  49.5 11.3 %collective-permute-start.25 = (bf16[16,4608]{1,0:T(8,128)(2,1)S(1)}, bf16[16,4608]{1,0:T(8,128)(2,1)S(1)}, u32[]{:S(2)}, u32[]{:S(2)}) collective-permute-start(bf16[16,4608]{1,0:T(8,128)(2,1)S(1)} %get-tuple-element.14.refs_24_), channel_id=1, source_target_pairs={{0,2},{1,3},{2,0},{3,1},{4,6},{5,7},{6,4},{7,5},{8,10},{9,11},{10,... | collective-permute-start | bytes 442376 | tf_op jit(solution)/shard_map/ppermute | solution.py:307
  50.0 10.8 %collective-permute-start.24 = (bf16[16,4608]{1,0:T(8,128)(2,1)S(1)}, bf16[16,4608]{1,0:T(8,128)(2,1)S(1)}, u32[]{:S(2)}, u32[]{:S(2)}) collective-permute-start(bf16[16,4608]{1,0:T(8,128)(2,1)S(1)} %get-tuple-element.14.refs_24_), channel_id=1, source_target_pairs={{0,1},{1,0},{2,3},{3,2},{4,5},{5,4},{6,7},{7,6},{8,9},{9,8},{10,11... | collective-permute-start | bytes 442376 | tf_op jit(solution)/shard_map/ppermute | solution.py:307
  50.4 6.2 %collective-permute-start.20 = (bf16[256,128]{1,0:T(8,128)(2,1)S(1)}, bf16[256,128]{1,0:T(8,128)(2,1)S(1)}, u32[]{:S(2)}, u32[]{:S(2)}) collective-permute-start(bf16[256,128]{1,0:T(8,128)(2,1)S(1)} %pad_maximum_fusion.refs_16_), channel_id=1, source_target_pairs={{0,12},{4,8},{8,4},{12,0},{1,13},{5,9},{9,5},{13,1},{2,14},{6,10},... | collective-permute-start | bytes 196616 | tf_op jit(solution)/shard_map/ppermute | solution.py:307
  53.7 5.7 %collective-permute-start.19 = (bf16[256,128]{1,0:T(8,128)(2,1)S(1)}, bf16[256,128]{1,0:T(8,128)(2,1)S(1)}, u32[]{:S(2)}, u32[]{:S(2)}) collective-permute-start(bf16[256,128]{1,0:T(8,128)(2,1)S(1)} %pad_maximum_fusion.refs_16_), channel_id=1, source_target_pairs={{0,8},{4,12},{8,0},{12,4},{1,9},{5,13},{9,1},{13,5},{2,10},{6,14},... | collective-permute-start | bytes 196616 | tf_op jit(solution)/shard_map/ppermute | solution.py:307
  (14 other events, 128.0 us)

commit v2 on v0

v2 whole, which is shorter than its diff:
```python
import functools
import math

import jax
import jax.numpy as jnp
from jax import lax
from jax.experimental import pallas as pl
from jax.experimental.pallas import tpu as pltpu
from jax.sharding import PartitionSpec as P

HD = 128
GROUP = 8
STEPS = 4
RANK = 64
EPSILON = 1e-05
ROPE_BASE = 500000.0
MASKED_SCORE = -1e30
LOWEST_TOP = -1e20
EXPONENT = math.log2(math.e) / math.sqrt(HD)
PAIR = GROUP * HD + 128
CHUNK = 512

F32 = jnp.float32
BF16 = jnp.bfloat16
NT = (((1,), (1,)), ((), ()))
VMEM = pl.BlockSpec(memory_space=pltpu.VMEM)
HBM = pl.BlockSpec(memory_space=pltpu.HBM)
MEBI = 2**20
WHOLE_VMEM = 65000 * 1024
HINT = 40 * MEBI


def rounded(value):
    return value.astype(BF16).astype(F32)


def split(value):
    high = rounded(value)
    return jnp.concatenate([high, value - high], 0).astype(BF16)


def joined(tile):
    wide = tile.astype(F32)
    return wide[:8] + wide[8:]


def rotated(tile, cosine, sine):
    return tile * cosine + pltpu.roll(tile, HD // 2, 1) * sine


def first_rows(shape):
    return lax.broadcasted_iota(jnp.int32, shape, 0) % 8 < STEPS


def exchanged(a, b):
    first = first_rows(a.shape)
    return (
        jnp.where(first, a, pltpu.roll(b, STEPS, 0)),
        jnp.where(first, pltpu.roll(a, STEPS, 0), b),
    )


def flat(matrix):
    return jnp.concatenate([matrix[i : i + 16] for i in range(0, matrix.shape[0], 16)], 1)


def pack_kernel(*refs):
    sources, (a_ref, b_ref, sq_ref), held, sems = refs[:6], refs[6:9], refs[9:15], refs[15]
    copies = [
        pltpu.make_async_copy(source, target, sems.at[i])
        for i, (source, target) in enumerate(zip(sources, held))
    ]
    for copy in copies:
        copy.start()
    x_ref, gain_ref, kd_ref, vd_ref, ku_ref, vu_ref = held
    for copy in copies:
        copy.wait()
    x = jnp.concatenate([x_ref[0].astype(F32), x_ref[1].astype(F32)], 0)
    depth = x.shape[1]
    sq_ref[...] = jnp.broadcast_to(jnp.sum(x * x, 1, keepdims=True), sq_ref.shape)
    scaled = x * gain_ref[...].astype(F32).reshape(1, depth)
    b_ref[:, : depth // 2] = jnp.concatenate(
        [scaled[:, : depth // 2], scaled[:, depth // 2 :]], 0
    ).astype(BF16)
    ups = flat(jnp.concatenate([ku_ref[...], vu_ref[...]], 0).T.astype(BF16))
    b_ref[:, depth // 2 :] = ups
    own = kd_ref.shape[0]
    for slot, ref in enumerate((kd_ref, vd_ref)):
        down = ref[...]
        if own < 16:
            down = jnp.concatenate([down, jnp.zeros((16 - own, depth), F32)], 0)
        a_ref[:, slot * depth : (slot + 1) * depth] = down.astype(BF16)
    a_ref[:, 2 * depth :] = ups


def pack(hidden, gain, key_down, value_down, key_up, value_up):
    operands = [hidden, gain, key_down, value_down, key_up.T, value_up.T]
    depth = hidden.shape[2]
    ups = key_up.shape[0] * 8
    return pl.pallas_call(
        pack_kernel,
        in_specs=[HBM] * len(operands),
        out_specs=[VMEM] * 3,
        out_shape=[
            jax.ShapeDtypeStruct((16, 2 * depth + ups), BF16),
            jax.ShapeDtypeStruct((16, depth // 2 + ups), BF16),
            jax.ShapeDtypeStruct((8, 128), F32),
        ],
        scratch_shapes=[pltpu.VMEM(o.shape, o.dtype) for o in operands]
        + [pltpu.SemaphoreType.DMA((len(operands),))],
        compiler_params=pltpu.CompilerParams(vmem_limit_bytes=WHOLE_VMEM),
        name="pack",
    )(*operands)


def tables(lengths_ref):
    shape = (8, HD)
    row = lax.broadcasted_iota(jnp.int32, shape, 0)
    lane = lax.broadcasted_iota(jnp.int32, shape, 1)
    step = row % STEPS
    position = (jnp.where(row < STEPS, lengths_ref[0], lengths_ref[1]) + step).astype(F32)
    pair = lane % (HD // 2)
    frequency = jnp.ones(shape, F32)
    for bit in range(6):
        factor = ROPE_BASE ** (-(2.0 * 2**bit) / HD)
        frequency = jnp.where((pair >> bit) & 1 == 1, frequency * factor, frequency)
    angle = position * frequency
    sine = jnp.sin(angle)
    return jnp.cos(angle), jnp.where(lane < HD // 2, -sine, sine)


def attend(p, limits, cosine, sine, q_ref, k_ref, v_ref, out_ref, qrot_ref):
    halves = [[], []]
    for e in range(2):
        tiles = []
        for g in range(GROUP):
            at = slice(((2 * p + e) * GROUP + g) * HD, ((2 * p + e) * GROUP + g + 1) * HD)
            q = jnp.concatenate([q_ref[0, :, at].astype(F32), q_ref[1, :, at].astype(F32)], 0)
            tiles.append(rotated(q, cosine, sine))
        halves[e] = tiles
    for g in range(GROUP):
        at = slice((p * GROUP + g) * HD, (p * GROUP + g + 1) * HD)
        qrot_ref[:, at] = jnp.concatenate([halves[0][g], halves[1][g]], 0).astype(BF16)
    mixed = [[exchanged(halves[e][g], halves[e][g + 4]) for g in range(4)] for e in range(2)]
    zero = jnp.zeros((32, HD), F32)
    numers, stats = [], []
    lane8 = lax.broadcasted_iota(jnp.int32, (8, 128), 1)
    pair = slice(2 * p * HD, 2 * (p + 1) * HD)
    for s in range(2):
        rows = [jnp.concatenate([mixed[e][g][s] for g in range(4)], 0) for e in range(2)]
        queries = jnp.concatenate(
            [jnp.concatenate([rows[0], zero], 1), jnp.concatenate([zero, rows[1]], 1)], 0
        ).astype(BF16)
        scores = lax.dot_general(queries, k_ref[s, :, pair], NT, preferred_element_type=F32)
        place = lax.broadcasted_iota(jnp.int32, scores.shape, 1)
        masked = jnp.where(place < limits[s], scores, MASKED_SCORE)
        top = rounded(jnp.maximum(jnp.max(masked, 1, keepdims=True), LOWEST_TOP))
        weights = jnp.exp2((masked - top) * EXPONENT).astype(BF16)
        total = jnp.sum(weights.astype(F32), 1, keepdims=True)
        numers.append(jnp.dot(weights, v_ref[s, :, pair], preferred_element_type=F32))
        high = rounded(total)
        compact = []
        for e in range(2):
            tile = jnp.zeros((8, 128), F32)
            for g in range(4):
                at = slice(32 * e + 8 * g, 32 * e + 8 * g + 8)
                for slot, value in enumerate((top, high, total - high)):
                    tile = jnp.where(lane8 == slot * GROUP + g, value[at], tile)
            compact.append(tile)
        stats.append(compact)
    outs, ends = [[], []], []
    for e in range(2):
        back = []
        for g in range(4):
            at = slice(32 * e + 8 * g, 32 * e + 8 * g + 8)
            cols = slice(e * HD, (e + 1) * HD)
            back.append(exchanged(numers[0][at, cols], numers[1][at, cols]))
        outs[e] = [b[0] for b in back] + [b[1] for b in back]
        a, b = exchanged(stats[0][e], stats[1][e])
        ends.append(jnp.where(lane8 % 8 < 4, a, pltpu.roll(b, 4, 1)))
    for g in range(GROUP):
        at = slice(p * PAIR + g * HD, p * PAIR + (g + 1) * HD)
        out_ref[:, at] = jnp.concatenate([outs[0][g], outs[1][g]], 0).astype(BF16)
    out_ref[:, p * PAIR + GROUP * HD : (p + 1) * PAIR] = jnp.concatenate(ends, 0).astype(BF16)


def local_kernel(
    x_ref, lengths_hbm, q_hbm, k_hbm, v_hbm, wk_hbm, wv_hbm,
    out_ref, qrot_ref, base_ref, trig_ref,
    lengths_ref, q_ref, k_ref, v_ref, wk_ref, wv_ref, length_sem, q_sem, cache_sem, weight_sem,
):
    pairs = k_hbm.shape[2] // (2 * HD)
    chunks = wk_hbm.shape[0] // CHUNK
    length_copy = pltpu.make_async_copy(lengths_hbm, lengths_ref, length_sem)
    length_copy.start()
    q_copy = pltpu.make_async_copy(q_hbm, q_ref, q_sem)
    q_copy.start()
    cache_copies, weight_copies = [], []
    for p in range(pairs):
        at = (slice(None), slice(None), pl.ds(2 * p * HD, 2 * HD))
        for i, (source, target) in enumerate(((k_hbm, k_ref), (v_hbm, v_ref))):
            copy = pltpu.make_async_copy(source.at[at], target.at[at], cache_sem.at[p, i])
            copy.start()
            cache_copies.append(copy)
    for c in range(chunks):
        at = pl.ds(c * CHUNK, CHUNK)
        for i, (source, target) in enumerate(((wk_hbm, wk_ref), (wv_hbm, wv_ref))):
            copy = pltpu.make_async_copy(source.at[at], target.at[at], weight_sem.at[c, i])
            copy.start()
            weight_copies.append(copy)
    length_copy.wait()
    cosine, sine = tables(lengths_ref)
    trig_ref[...] = jnp.concatenate([cosine, sine], 0)
    start = lax.axis_index("tensor") * k_hbm.shape[1]
    limits = [lengths_ref[s] - start for s in range(2)]
    q_copy.wait()
    for p in range(pairs):
        cache_copies[2 * p].wait()
        cache_copies[2 * p + 1].wait()
        attend(p, limits, cosine, sine, q_ref, k_ref, v_ref, out_ref, qrot_ref)
    half = wk_hbm.shape[0] // 2
    x = x_ref[:, :half].astype(F32)
    x = jnp.concatenate([x[:8], x[8:]], 1).astype(BF16)
    total = None
    for c in range(chunks):
        weight_copies[2 * c].wait()
        weight_copies[2 * c + 1].wait()
        rows = x[:, c * CHUNK : (c + 1) * CHUNK]
        part = jnp.concatenate(
            [
                jnp.dot(rows, ref[c * CHUNK : (c + 1) * CHUNK], preferred_element_type=F32)
                for ref in (wk_ref, wv_ref)
            ],
            0,
        )
        total = part if total is None else total + part
    base_ref[...] = total


def local(lengths, message, queries, key_cache, value_cache, key_weight, value_weight):
    seqs, length, width = key_cache.shape
    depth = key_weight.shape[0]
    pairs = width // (2 * HD)
    return pl.pallas_call(
        local_kernel,
        in_specs=[VMEM] + [HBM] * 6,
        out_specs=[VMEM] * 4,
        out_shape=[
            jax.ShapeDtypeStruct((16, pairs * PAIR), BF16),
            jax.ShapeDtypeStruct((16, pairs * GROUP * HD), BF16),
            jax.ShapeDtypeStruct((16, width), F32),
            jax.ShapeDtypeStruct((16, HD), F32),
        ],
        scratch_shapes=[
            pltpu.SMEM(lengths.shape, jnp.int32),
            pltpu.VMEM(queries.shape, BF16),
            pltpu.VMEM(key_cache.shape, BF16),
            pltpu.VMEM(value_cache.shape, BF16),
            pltpu.VMEM(key_weight.shape, BF16),
            pltpu.VMEM(value_weight.shape, BF16),
            pltpu.SemaphoreType.DMA,
            pltpu.SemaphoreType.DMA,
            pltpu.SemaphoreType.DMA((pairs, 2)),
            pltpu.SemaphoreType.DMA((depth // CHUNK, 2)),
        ],
        compiler_params=pltpu.CompilerParams(vmem_limit_bytes=WHOLE_VMEM),
        cost_estimate=pl.CostEstimate(
            flops=4 * 64 * 256 * seqs * length * pairs + 4 * 16 * depth * width,
            bytes_accessed=4 * seqs * length * width + 4 * depth * width,
            transcendentals=64 * seqs * length * pairs,
        ),
        name="local",
    )(message, lengths, queries, key_cache, value_cache, key_weight, value_weight)


def rank_kernel(n, rows, depth, *refs):
    base_ref, sq_ref, own_ref, near_ref = refs[:4]
    tokens, out_ref = refs[4 : 4 + n], refs[4 + n]
    width = base_ref.shape[1]
    place = lax.axis_index("dp")
    x = []
    for ref in tokens:
        part = ref[:, : depth // 2].astype(F32)
        x.append(jnp.concatenate([part[:8], part[8:]], 1))
    x = jnp.concatenate(x, 0).astype(BF16)
    fill = jnp.zeros((RANK - 16, depth), BF16)
    z = None
    for ref, at in ((own_ref, place), (near_ref, place ^ 1)):
        down = jnp.concatenate([ref[:, :depth], fill, ref[:, depth : 2 * depth], fill], 0)
        part = lax.dot_general(x, down, NT, preferred_element_type=F32)
        part = pltpu.roll(part, at * rows, 1)
        z = part if z is None else z + part
    out_ref[:, :width] = base_ref[...].astype(BF16)
    out_ref[:, width : width + 128] = split(sq_ref[...])
    for i in range(n):
        at = width + 128 * (i + 1)
        out_ref[:, at : at + 128] = split(z[8 * i : 8 * i + 8])


def rank_products(rows, depth, base, squares, own, near, tokens):
    n = len(tokens)
    return pl.pallas_call(
        functools.partial(rank_kernel, n, rows, depth),
        in_specs=[VMEM] * (4 + n),
        out_specs=VMEM,
        out_shape=jax.ShapeDtypeStruct((16, base.shape[1] + 128 * (n + 1)), BF16),
        compiler_params=pltpu.CompilerParams(vmem_limit_bytes=32 * MEBI),
        cost_estimate=pl.CostEstimate(flops=0, bytes_accessed=HINT, transcendentals=0),
        name="rank_products",
    )(base, squares, own, near, *tokens)


def broadcast_lane(tile, lane):
    return jnp.broadcast_to(tile[:, lane : lane + 1], tile.shape)


def combine_kernel(ca_ref, cb_ref, pa_ref, pb_ref, c_ref, p_ref):
    width = p_ref.shape[1]
    sums = pa_ref[...].astype(F32) + pb_ref[...].astype(F32)
    tail = c_ref.shape[1] // PAIR * 2 * HD
    p_ref[:, :tail] = sums[:, :tail].astype(BF16)
    p_ref[:, tail:] = split(sums[:8, tail:] + sums[8:, tail:])
    lane = lax.broadcasted_iota(jnp.int32, (16, 128), 1)
    for p in range(c_ref.shape[1] // PAIR):
        end = slice(p * PAIR + GROUP * HD, (p + 1) * PAIR)
        a, b = ca_ref[:, end].astype(F32), cb_ref[:, end].astype(F32)
        top = jnp.maximum(a, b)
        fa = jnp.exp2(jnp.minimum(a - top, 0.0) * EXPONENT)
        fb = jnp.exp2(jnp.minimum(b - top, 0.0) * EXPONENT)
        total = fa * totals(a) + fb * totals(b)
        high = rounded(total)
        stats = jnp.where(lane < GROUP, top, 0.0)
        stats = jnp.where(lane // GROUP == 1, pltpu.roll(high, GROUP, 1), stats)
        stats = jnp.where(lane // GROUP == 2, pltpu.roll(total - high, 2 * GROUP, 1), stats)
        c_ref[:, end] = stats.astype(BF16)
        for g in range(GROUP):
            at = slice(p * PAIR + g * HD, p * PAIR + (g + 1) * HD)
            c_ref[:, at] = (
                broadcast_lane(fa, g) * ca_ref[:, at].astype(F32)
                + broadcast_lane(fb, g) * cb_ref[:, at].astype(F32)
            ).astype(BF16)


def totals(stats):
    return pltpu.roll(stats, 128 - GROUP, 1) + pltpu.roll(stats, 128 - 2 * GROUP, 1)


def combine(cache_a, cache_b, part_a, part_b):
    return pl.pallas_call(
        combine_kernel,
        in_specs=[VMEM] * 4,
        out_specs=[VMEM] * 2,
        out_shape=[
            jax.ShapeDtypeStruct(cache_a.shape, BF16),
            jax.ShapeDtypeStruct(part_a.shape, BF16),
        ],
        compiler_params=pltpu.CompilerParams(vmem_limit_bytes=32 * MEBI),
        name="combine",
    )(cache_a, cache_b, part_a, part_b)


def answer_kernel(n, at, pa_ref, pb_ref, near_ref, *outs):
    ups = near_ref.shape[1] - outs[0].shape[1] + 128
    z = pa_ref[:, at:].astype(F32) + pb_ref[:, at:].astype(F32)
    for i, ref in enumerate(outs):
        part = z[:, 128 * (i + 1) : 128 * (i + 2)]
        ref[:, :128] = split(part[:8] + part[8:])
        ref[:, 128:] = near_ref[:, ups:]


def answers(n, part_a, part_b, near, up_columns):
    at = part_a.shape[1] - 128 * (n + 1)
    return pl.pallas_call(
        functools.partial(answer_kernel, n, at),
        in_specs=[VMEM] * 3,
        out_specs=[VMEM] * n,
        out_shape=[jax.ShapeDtypeStruct((16, 128 + up_columns), BF16)] * n,
        compiler_params=pltpu.CompilerParams(vmem_limit_bytes=32 * MEBI),
        name="answers",
    )(part_a, part_b, near)


def final_kernel(n, width_all, trig_ref, qrot_ref, ca_ref, cb_ref, pa_ref, pb_ref, *refs):
    own_ref, near_ref = refs[:2]
    sent, back = refs[2 : 2 + n], refs[2 + n : 2 + 2 * n]
    keys_out, values_out, out_ref, up_ref = refs[2 + 2 * n :]
    width = keys_out.shape[2]
    place = lax.axis_index("dp")
    columns = back[0].shape[1] - 128
    rows = columns // 8
    blocks = [(own_ref, 0), (near_ref, 1)]
    for i in range(n):
        blocks += [(sent[i], 2 * i + 2), (back[i], 2 * i + 3)]
    for ref, distance in blocks:
        start = ref.shape[1] - columns
        at = (place ^ distance) * rows
        for i in range(rows // 16):
            up_ref[pl.ds(pl.multiple_of(at + 16 * i, 16), 16), :] = ref[
                :, start + 128 * i : start + 128 * (i + 1)
            ]
    cosine, sine = trig_ref[:8], trig_ref[8:]
    sums = pa_ref[...].astype(F32) + pb_ref[...].astype(F32)
    tail = sums[:8, width : width + 256] + sums[8:, width : width + 256]
    squares, z = tail[:, :128], tail[:, 128:]
    for ref in back:
        z = z + joined(ref[:, :128])
    lane8 = lax.broadcasted_iota(jnp.int32, (8, 128), 1)
    z = jnp.concatenate(
        [jnp.where(lane8 < RANK, z, 0.0), jnp.where(lane8 < RANK, 0.0, z)], 0
    ).astype(BF16)
    total = sums[:, :width] + lax.dot_general(z, up_ref[...], NT, preferred_element_type=F32)
    scale = lax.rsqrt(squares / width_all + EPSILON)
    lane = lax.broadcasted_iota(jnp.int32, (16, 128), 1)
    step = lax.broadcasted_iota(jnp.int32, (16, 128), 0) % STEPS
    first = first_rows((8, 128))

    def of_step(tiles, j):
        return jnp.concatenate(
            [
                jnp.where(first, tile[j : j + 1], tile[STEPS + j : STEPS + j + 1])
                for tile in tiles
            ],
            0,
        )

    for p in range(width // (2 * HD)):
        new_keys, new_values = [], []
        for e in range(2):
            at = slice((2 * p + e) * HD, (2 * p + e + 1) * HD)
            new_keys.append(rounded(rotated(total[:8, at] * scale, cosine, sine)))
            new_values.append(rounded(total[8:, at] * scale))
        at = slice(2 * p * HD, 2 * (p + 1) * HD)
        for out, parts in ((keys_out, new_keys), (values_out, new_values)):
            both = jnp.concatenate(parts, 1).astype(BF16)
            out[0, :, at] = both[:STEPS]
            out[1, :, at] = both[STEPS:]
        keys = [of_step(new_keys, j) for j in range(STEPS)]
        values = [of_step(new_values, j) for j in range(STEPS)]
        scores = [jnp.zeros((16, 128), F32) for _ in range(STEPS)]
        for g in range(GROUP):
            q = qrot_ref[:, (p * GROUP + g) * HD : (p * GROUP + g + 1) * HD].astype(F32)
            for j in range(STEPS):
                dot = jnp.sum(q * keys[j], 1, keepdims=True)
                scores[j] = jnp.where(lane == g, dot, scores[j])
        scores = [jnp.where(j <= step, scores[j], MASKED_SCORE) for j in range(STEPS)]
        end = slice(p * PAIR + GROUP * HD, (p + 1) * PAIR)
        stats = [ref[:, end].astype(F32) for ref in (ca_ref, cb_ref)]
        top = functools.reduce(jnp.maximum, scores + stats)
        fresh = [rounded(jnp.exp2((scores[j] - top) * EXPONENT)) for j in range(STEPS)]
        factors = [jnp.exp2(jnp.minimum(s - top, 0.0) * EXPONENT) for s in stats]
        denom = functools.reduce(jnp.add, fresh)
        for factor, s in zip(factors, stats):
            denom = denom + factor * totals(s)
        inverse = 1.0 / denom
        coefficients = [c * inverse for c in fresh + factors]
        tiles = []
        for g in range(GROUP):
            at = slice(p * PAIR + g * HD, p * PAIR + (g + 1) * HD)
            terms = values + [ref[:, at].astype(F32) for ref in (ca_ref, cb_ref)]
            tile = jnp.zeros((16, 128), F32)
            for c, term in zip(coefficients, terms):
                tile = tile + broadcast_lane(c, g) * term
            tiles.append(tile)
        both = jnp.concatenate(tiles, 1)
        for e in range(2):
            at = slice((2 * p + e) * GROUP * HD, (2 * p + e + 1) * GROUP * HD)
            for s in range(2):
                out_ref[s, :, at] = both[8 * e + 4 * s : 8 * e + 4 * s + 4].astype(BF16)


def final(width, width_all, trig, qrot, caches, parts, own, near, sent, back):
    n = len(sent)
    operands = [trig, qrot, *caches, *parts, own, near, *sent, *back]
    return pl.pallas_call(
        functools.partial(final_kernel, n, width_all),
        in_specs=[VMEM] * len(operands),
        out_specs=[VMEM] * 3,
        out_shape=[
            jax.ShapeDtypeStruct((2, STEPS, width), BF16),
            jax.ShapeDtypeStruct((2, STEPS, width), BF16),
            jax.ShapeDtypeStruct((2, STEPS, GROUP * width), BF16),
        ],
        scratch_shapes=[pltpu.VMEM((width, 128), BF16)],
        compiler_params=pltpu.CompilerParams(vmem_limit_bytes=32 * MEBI),
        name="final",
    )(*operands)


def swap(value, axis, n, distance):
    return lax.ppermute(value, axis, [(i, i ^ distance) for i in range(n)])


def shards(
    n_dp,
    n_tensor,
    hidden,
    norm_gain,
    queries,
    key_weight,
    value_weight,
    key_down,
    key_up,
    value_down,
    value_up,
    key_cache,
    value_cache,
    lengths,
):
    depth, width = key_weight.shape
    rows, up_columns = key_down.shape[0], key_up.shape[0] * 8
    to_dp = lambda value, distance: swap(value, "dp", n_dp, distance)
    to_tensor = lambda value, distance: swap(value, "tensor", n_tensor, distance)
    partners = range(2, n_dp, 2)

    own, tokens, squares = pack(
        hidden, norm_gain, key_down, value_down, key_up, value_up
    )
    near = to_dp(own, 1)
    sent = [to_dp(tokens, d) for d in partners]
    cache, qrot, base, trig = local(
        lengths, tokens, queries, key_cache, value_cache, key_weight, value_weight
    )
    part = rank_products(rows, depth, base, squares, own, near, [tokens, *sent])
    cache, part = combine(cache, to_tensor(cache, 1), part, to_tensor(part, 1))
    part_far = to_tensor(part, 2)
    cache_far = to_tensor(cache, 2)
    replies = answers(len(sent), part, part_far, near, up_columns)
    back = [to_dp(reply, d) for reply, d in zip(replies, partners)]
    return final(
        width,
        float(depth * n_tensor),
        trig,
        qrot,
        (cache, cache_far),
        (part, part_far),
        own,
        near,
        sent,
        back,
    )


def solution(mesh):
    body = functools.partial(shards, mesh.shape["dp"], mesh.shape["tensor"])
    return jax.shard_map(
        body,
        mesh=mesh,
        in_specs=(
            P(("groups", "dp"), None, "tensor"),
            P("tensor"),
            P(("groups", "dp"), None, None),
            P("tensor", None),
            P("tensor", None),
            P(("groups", "dp"), "tensor"),
            P(("groups", "dp"), None),
            P(("groups", "dp"), "tensor"),
            P(("groups", "dp"), None),
            P(("groups", "dp"), "tensor", None),
            P(("groups", "dp"), "tensor", None),
            P(("groups", "dp")),
        ),
        out_specs=(
            P(("groups", "dp"), None, None),
            P(("groups", "dp"), None, None),
            P(("groups", "dp"), None, None),
        ),
        check_vma=False,
    )
```

time: 159 us -> 46.2 us (0.29)
  blocking collectives: 76.3 us -> 0 us
  matrix products: 18.8 us -> 0 us
  Pallas kernels: 0 us -> 15.5 us
  between operations: 14.4 us -> 0.69 us
  waiting for transfers between devices: 30.3 us -> 16.6 us
  starting transfers between devices: 0.08 us -> 8.82 us
  other arithmetic: 8.02 us -> 0 us
  local copies, waits for them, and re-layouts: 9.95 us -> 4.24 us
    all_gather x6 -> x0, blocking collectives: 68 us -> none  [the longest x1 14.6 us: shards(): lax.all_gather(value_up, 'dp', axis=0, tiled=True)]
    psum x1 -> x0, waiting for transfers between devices: 26.8 us -> none  [shards(): summed = lax.psum(partial_kv, 'tensor')]
    dot_general x8 -> x0, matrix products: 18.8 us -> none  [the longest x1 3.54 us: shards(): jnp.dot(lax.all_gather(key_down.astype(jnp.bfloat16), 'dp', axis=0, tiled...]
    ppermute x0 -> x7, waiting for transfers between devices: none -> 16.6 us  [swap(): return lax.ppermute(value, axis, [(i, i ^ distance) for i in range(n)])]
    pallas_call x0 -> x6, Pallas kernels: none -> 15.5 us  [the longest x1 10.3 us: local(): pl.pallas_call(local_kernel, in_specs=[VMEM] + [HBM] * 6, out_specs=[VMEM...]
    ppermute x0 -> x7, starting transfers between devices: none -> 8.82 us  [swap(): return lax.ppermute(value, axis, [(i, i ^ distance) for i in range(n)])]
    psum x1 -> x0, blocking collectives: 8.31 us -> none  [shards(): lax.psum(jnp.sum(rows_flat * rows_flat, axis=1, keepdims=True), 'tensor')]
    all_gather x1 -> x0, waiting for transfers between devices: 3.47 us -> none  [joined(): pieces = jax.tree.map(lambda part: lax.all_gather(part, axis), value)]
  transfers between devices with their start and end apart: 2 -> 7, of which waited for: 2 -> 4; matrix products, arithmetic and copies ran while one was open for 4% -> 0% of each run, Pallas kernels for 0% -> 23%
where the time goes in v2:
time: 46.2 us; the launch traced here: 45.9 us
  waiting for transfers between devices  16.6 us (36%)
  Pallas kernels  15.5 us (34%)
  starting transfers between devices  8.82 us (19%)
  local copies, waits for them, and re-layouts  4.24 us (9%)
  between operations  0.69 us (1%)
    ppermute x7, waiting for transfers between devices, swap(): return lax.ppermute(value, axis, [(i, i ^ distance) for i in range(n)])  16.6 us
    pallas_call x1, Pallas kernels, local(): pl.pallas_call(local_kernel, in_specs=[VMEM] + [HBM] * 6, out_specs=[VMEM...  10.3 us
    ppermute x7, starting transfers between devices, swap(): return lax.ppermute(value, axis, [(i, i ^ distance) for i in range(n)])  8.82 us
    unnamed x14, local copies, waits for them, and re-layouts  4.24 us
    pallas_call x1, Pallas kernels, final(): pl.pallas_call(functools.partial(final_kernel, n, width_all), in_specs=[V...  2.36 us
    pallas_call x1, Pallas kernels, pack(): pl.pallas_call(pack_kernel, in_specs=[HBM] * len(operands), out_specs=[VM...  1.94 us
  transfers between devices with their start and end apart: 7, of which 4 were waited for; matrix products, arithmetic and copies ran while one was open for 0% of the time, Pallas kernels for 23%

profile of v2, /device:TPU:0, one launch (start us, length us, event | category | flops | bytes accessed | tf_op | source)
XLA Modules:
  0.0 45.9 jit_solution(2227884555617875691)
XLA Ops:
  0.6 1.9 %pack.1 = (bf16[16,6144]{1,0:T(8,128)(2,1)}, bf16[16,3072]{1,0:T(8,128)(2,1)}, f32[8,128]{1,0:T(8,128)}) custom-call(bf16[2,4,2048]{2,1,0:T(4,128)(2,1)} %refs_0_.1, bf16[2048]{0:T(1024)(128)(2,1)} %refs_1_.1, f32[16,2048]{1,0:T(8,128)} %refs_2_.1, f32[16,2048]{1,0:T(8,128)} %refs_3_.1, f32[64,256]{1,0:T(8,128)} %bitcast.2, f32[64,256]{1,0:T(8,128)} %bitcast.3), custom_call_target="tpu_custom_call" | custom-call | tf_op jit(solution)/shard_map/pack/pallas_call | solution.py:100
  2.6 3.1 %collective-permute-start.1 = (bf16[16,6144]{1,0:T(8,128)(2,1)}, bf16[16,6144]{1,0:T(8,128)(2,1)S(1)}, u32[]{:S(2)}, u32[]{:S(2)}) collective-permute-start(bf16[16,6144]{1,0:T(8,128)(2,1)} %get-tuple-element.18.refs_2_.refs_0_), channel_id=1, source_target_pairs={{0,4},{4,0},{8,12},{12,8},{1,5},{5,1},{9,13},{13,9},{2,6},{6,2},{1... | collective-permute-start | bytes 589832 | tf_op jit(solution)/shard_map/ppermute | solution.py:490
  5.7 10.3 %local.1 = (bf16[16,4608]{1,0:T(8,128)(2,1)}, bf16[16,4096]{1,0:T(8,128)(2,1)}, f32[16,1024]{1,0:T(8,128)}, f32[16,128]{1,0:T(8,128)}) custom-call(bf16[16,3072]{1,0:T(8,128)(2,1)} %get-tuple-element.12.x_ref.refs_4_, s32[2]{0:T(128)} %lengths_hbm.1, bf16[2,4,8192]{2,1,0:T(4,128)(2,1)} %q_hbm.1, bf16[2,512,1024]{2,1,0:T(8,128)(2,1)} %k_hbm.1, ...), custom_call_target="tpu_custom_call" | custom-call | flops 402653184 | bytes 12582912 | tf_op jit(solution)/shard_map/local/pallas_call | solution.py:244
  16.0 0.1 collective-permute-start
  16.0 2.7 %collective-permute-start.2 = (bf16[16,3072]{1,0:T(8,128)(2,1)}, bf16[16,3072]{1,0:T(8,128)(2,1)S(1)}, u32[]{:S(2)}, u32[]{:S(2)}) collective-permute-start(bf16[16,3072]{1,0:T(8,128)(2,1)} %get-tuple-element.12.x_ref.refs_4_), channel_id=1, source_target_pairs={{0,8},{4,12},{8,0},{12,4},{1,9},{5,13},{9,1},{13,5},{2,10},{6,14},... | collective-permute-start | bytes 294920 | tf_op jit(solution)/shard_map/ppermute | solution.py:490
  18.7 5.6 %collective-permute-done.2.refs_5_.refs_2_ = bf16[16,3072]{1,0:T(8,128)(2,1)S(1)} collective-permute-done((bf16[16,3072]{1,0:T(8,128)(2,1)}, bf16[16,3072]{1,0:T(8,128)(2,1)S(1)}, u32[]{:S(2)}, u32[]{:S(2)}) %collective-permute-start.2) | collective-permute-done | bytes 98336 | tf_op jit(solution)/shard_map/ppermute | solution.py:490
  24.3 0.0 collective-permute-done.1.refs_3_.near_ref.refs_1_
  24.3 0.9 %copy-done.1 = bf16[16,3072]{1,0:T(8,128)(2,1)S(1)} copy-done((bf16[16,3072]{1,0:T(8,128)(2,1)S(1)}, bf16[16,3072]{1,0:T(8,128)(2,1)}, u32[]{:S(2)}) %copy-start.1) | copy-done | bytes 98328
  25.2 0.8 %copy-done.4 = f32[16,1024]{1,0:T(8,128)S(1)} copy-done((f32[16,1024]{1,0:T(8,128)S(1)}, f32[16,1024]{1,0:T(8,128)}, u32[]{:S(2)}) %copy-start.4) | copy-done | bytes 65560
  26.0 0.3 rank_products.1.pa_ref
  26.4 0.1 collective-permute-start.3
  26.5 0.0 collective-permute-done.cb_ref
  26.5 1.2 %collective-permute-done.3.pb_ref = bf16[16,1408]{1,0:T(8,128)(2,1)S(1)} collective-permute-done((bf16[16,1408]{1,0:T(8,128)(2,1)S(1)}, bf16[16,1408]{1,0:T(8,128)(2,1)S(1)}, u32[]{:S(2)}, u32[]{:S(2)}) %collective-permute-start.3) | collective-permute-done | bytes 45088 | tf_op jit(solution)/shard_map/ppermute | solution.py:490
  27.6 0.9 %copy-done.2 = bf16[16,4608]{1,0:T(8,128)(2,1)S(1)} copy-done((bf16[16,4608]{1,0:T(8,128)(2,1)S(1)}, bf16[16,4608]{1,0:T(8,128)(2,1)}, u32[]{:S(2)}) %copy-start.2) | copy-done | bytes 147480
  28.5 0.5 %combine.1 = (bf16[16,4608]{1,0:T(8,128)(2,1)S(1)}, bf16[16,1408]{1,0:T(8,128)(2,1)S(1)}) custom-call(bf16[16,4608]{1,0:T(8,128)(2,1)S(1)} %copy-done.2, bf16[16,4608]{1,0:T(8,128)(2,1)S(1)} %collective-permute-done.cb_ref, bf16[16,1408]{1,0:T(8,128)(2,1)S(1)} %rank_products.1.pa_ref, bf16[16,1408]{1,0:T(8,128)(2,1)S(1)} %collective-permute-done.3.pb_ref), custom_call_target="tpu_custom_call" | custom-call | tf_op jit(solution)/shard_map/combine/pallas_call | solution.py:349
  29.1 1.6 %collective-permute-start.4 = (bf16[16,4608]{1,0:T(8,128)(2,1)S(1)}, bf16[16,4608]{1,0:T(8,128)(2,1)S(1)}, u32[]{:S(2)}, u32[]{:S(2)}) collective-permute-start(bf16[16,4608]{1,0:T(8,128)(2,1)S(1)} %get-tuple-element.19.ca_ref), channel_id=1, source_target_pairs={{0,2},{1,3},{2,0},{3,1},{4,6},{5,7},{6,4},{7,5},{8,10},{9,11},{10,... | collective-permute-start | bytes 442376 | tf_op jit(solution)/shard_map/ppermute | solution.py:490
  30.7 0.5 %collective-permute-start.5 = (bf16[16,1408]{1,0:T(8,128)(2,1)S(1)}, bf16[16,1408]{1,0:T(8,128)(2,1)S(1)}, u32[]{:S(2)}, u32[]{:S(2)}) collective-permute-start(bf16[16,1408]{1,0:T(8,128)(2,1)S(1)} %get-tuple-element.20.pa_ref), channel_id=1, source_target_pairs={{0,2},{1,3},{2,0},{3,1},{4,6},{5,7},{6,4},{7,5},{8,10},{9,11},{10,... | collective-permute-start | bytes 135176 | tf_op jit(solution)/shard_map/ppermute | solution.py:490
  31.2 4.9 %collective-permute-done.5.pb_ref = bf16[16,1408]{1,0:T(8,128)(2,1)S(1)} collective-permute-done((bf16[16,1408]{1,0:T(8,128)(2,1)S(1)}, bf16[16,1408]{1,0:T(8,128)(2,1)S(1)}, u32[]{:S(2)}, u32[]{:S(2)}) %collective-permute-start.5) | collective-permute-done | bytes 45088 | tf_op jit(solution)/shard_map/ppermute | solution.py:490
  36.0 0.8 %collective-permute-start.6 = (bf16[16,2176]{1,0:T(8,128)(2,1)S(1)}, bf16[16,2176]{1,0:T(8,128)(2,1)S(1)}, u32[]{:S(2)}, u32[]{:S(2)}) collective-permute-start(bf16[16,2176]{1,0:T(8,128)(2,1)S(1)} %answers.1), channel_id=1, source_target_pairs={{0,8},{4,12},{8,0},{12,4},{1,9},{5,13},{9,1},{13,5},{2,10},{6,14},... | collective-permute-start | bytes 208904 | tf_op jit(solution)/shard_map/ppermute | solution.py:490
  36.9 5.0 %collective-permute-done.6.refs_3_ = bf16[16,2176]{1,0:T(8,128)(2,1)S(1)} collective-permute-done((bf16[16,2176]{1,0:T(8,128)(2,1)S(1)}, bf16[16,2176]{1,0:T(8,128)(2,1)S(1)}, u32[]{:S(2)}, u32[]{:S(2)}) %collective-permute-start.6) | collective-permute-done | bytes 69664 | tf_op jit(solution)/shard_map/ppermute | solution.py:490
  41.9 0.0 collective-permute-done.4.cb_ref
  41.9 0.9 %copy-done.3 = bf16[16,4096]{1,0:T(8,128)(2,1)S(1)} copy-done((bf16[16,4096]{1,0:T(8,128)(2,1)S(1)}, bf16[16,4096]{1,0:T(8,128)(2,1)}, u32[]{:S(2)}) %copy-start.3) | copy-done | bytes 131096
  42.8 0.7 %copy-done.5 = f32[16,128]{1,0:T(8,128)S(1)} copy-done((f32[16,128]{1,0:T(8,128)S(1)}, f32[16,128]{1,0:T(8,128)}, u32[]{:S(2)}) %copy-start.5) | copy-done | bytes 8216
  43.5 2.4 %final.1 = (bf16[2,4,1024]{2,1,0:T(4,128)(2,1)}, bf16[2,4,1024]{2,1,0:T(4,128)(2,1)}, bf16[2,4,8192]{2,1,0:T(4,128)(2,1)}) custom-call(f32[16,128]{1,0:T(8,128)S(1)} %copy-done.5, bf16[16,4096]{1,0:T(8,128)(2,1)S(1)} %copy-done.3, bf16[16,4608]{1,0:T(8,128)(2,1)S(1)} %get-tuple-element.19.ca_ref, bf16[16,4608]{1,0:T(8,128)(2,1)S(1)} %collective-permute-done.4.cb_ref, ...), custom_call_target="tpu_custom_call" | custom-call | tf_op jit(solution)/shard_map/final/pallas_call | solution.py:474
  (10 shorter events, 0.0 us)
Async XLA Ops:
  2.6 21.7 %collective-permute-start.1 = (bf16[16,6144]{1,0:T(8,128)(2,1)}, bf16[16,6144]{1,0:T(8,128)(2,1)S(1)}, u32[]{:S(2)}, u32[]{:S(2)}) collective-permute-start(bf16[16,6144]{1,0:T(8,128)(2,1)} %get-tuple-element.18.refs_2_.refs_0_), channel_id=1, source_target_pairs={{0,4},{4,0},{8,12},{12,8},{1,5},{5,1},{9,13},{13,9},{2,6},{6,2},{1... | collective-permute-start | bytes 589832 | tf_op jit(solution)/shard_map/ppermute | solution.py:490
  5.7 18.6 %copy-start = (bf16[16,6144]{1,0:T(8,128)(2,1)S(1)}, bf16[16,6144]{1,0:T(8,128)(2,1)}, u32[]{:S(2)}) copy-start(bf16[16,6144]{1,0:T(8,128)(2,1)} %get-tuple-element.18.refs_2_.refs_0_) | copy-start | bytes 589828
  5.7 18.6 %copy-start.6 = (f32[8,128]{1,0:T(8,128)S(1)}, f32[8,128]{1,0:T(8,128)}, u32[]{:S(2)}) copy-start(f32[8,128]{1,0:T(8,128)} %get-tuple-element.17.refs_1_) | copy-start | bytes 12292
  16.0 10.5 %collective-permute-start = (bf16[16,4608]{1,0:T(8,128)(2,1)}, bf16[16,4608]{1,0:T(8,128)(2,1)S(1)}, u32[]{:S(2)}, u32[]{:S(2)}) collective-permute-start(bf16[16,4608]{1,0:T(8,128)(2,1)} %get-tuple-element.15.ca_ref), channel_id=1, source_target_pairs={{0,1},{1,0},{2,3},{3,2},{4,5},{5,4},{6,7},{7,6},{8,9},{9,8},{10,11... | collective-permute-start | bytes 442376 | tf_op jit(solution)/shard_map/ppermute | solution.py:490
  16.0 8.2 %collective-permute-start.2 = (bf16[16,3072]{1,0:T(8,128)(2,1)}, bf16[16,3072]{1,0:T(8,128)(2,1)S(1)}, u32[]{:S(2)}, u32[]{:S(2)}) collective-permute-start(bf16[16,3072]{1,0:T(8,128)(2,1)} %get-tuple-element.12.x_ref.refs_4_), channel_id=1, source_target_pairs={{0,8},{4,12},{8,0},{12,4},{1,9},{5,13},{9,1},{13,5},{2,10},{6,14},... | collective-permute-start | bytes 294920 | tf_op jit(solution)/shard_map/ppermute | solution.py:490
  24.3 0.9 %copy-start.1 = (bf16[16,3072]{1,0:T(8,128)(2,1)S(1)}, bf16[16,3072]{1,0:T(8,128)(2,1)}, u32[]{:S(2)}) copy-start(bf16[16,3072]{1,0:T(8,128)(2,1)} %get-tuple-element.12.x_ref.refs_4_) | copy-start | bytes 294916
  25.2 0.8 %copy-start.4 = (f32[16,1024]{1,0:T(8,128)S(1)}, f32[16,1024]{1,0:T(8,128)}, u32[]{:S(2)}) copy-start(f32[16,1024]{1,0:T(8,128)} %get-tuple-element.16.refs_0_) | copy-start | bytes 196612
  26.4 1.2 %collective-permute-start.3 = (bf16[16,1408]{1,0:T(8,128)(2,1)S(1)}, bf16[16,1408]{1,0:T(8,128)(2,1)S(1)}, u32[]{:S(2)}, u32[]{:S(2)}) collective-permute-start(bf16[16,1408]{1,0:T(8,128)(2,1)S(1)} %rank_products.1.pa_ref), channel_id=1, source_target_pairs={{0,1},{1,0},{2,3},{3,2},{4,5},{5,4},{6,7},{7,6},{8,9},{9,8},{10,11... | collective-permute-start | bytes 135176 | tf_op jit(solution)/shard_map/ppermute | solution.py:490
  27.6 0.9 %copy-start.2 = (bf16[16,4608]{1,0:T(8,128)(2,1)S(1)}, bf16[16,4608]{1,0:T(8,128)(2,1)}, u32[]{:S(2)}) copy-start(bf16[16,4608]{1,0:T(8,128)(2,1)} %get-tuple-element.15.ca_ref) | copy-start | bytes 442372
  29.1 12.8 %collective-permute-start.4 = (bf16[16,4608]{1,0:T(8,128)(2,1)S(1)}, bf16[16,4608]{1,0:T(8,128)(2,1)S(1)}, u32[]{:S(2)}, u32[]{:S(2)}) collective-permute-start(bf16[16,4608]{1,0:T(8,128)(2,1)S(1)} %get-tuple-element.19.ca_ref), channel_id=1, source_target_pairs={{0,2},{1,3},{2,0},{3,1},{4,6},{5,7},{6,4},{7,5},{8,10},{9,11},{10,... | collective-permute-start | bytes 442376 | tf_op jit(solution)/shard_map/ppermute | solution.py:490
  30.7 5.3 %collective-permute-start.5 = (bf16[16,1408]{1,0:T(8,128)(2,1)S(1)}, bf16[16,1408]{1,0:T(8,128)(2,1)S(1)}, u32[]{:S(2)}, u32[]{:S(2)}) collective-permute-start(bf16[16,1408]{1,0:T(8,128)(2,1)S(1)} %get-tuple-element.20.pa_ref), channel_id=1, source_target_pairs={{0,2},{1,3},{2,0},{3,1},{4,6},{5,7},{6,4},{7,5},{8,10},{9,11},{10,... | collective-permute-start | bytes 135176 | tf_op jit(solution)/shard_map/ppermute | solution.py:490
  36.0 5.9 %collective-permute-start.6 = (bf16[16,2176]{1,0:T(8,128)(2,1)S(1)}, bf16[16,2176]{1,0:T(8,128)(2,1)S(1)}, u32[]{:S(2)}, u32[]{:S(2)}) collective-permute-start(bf16[16,2176]{1,0:T(8,128)(2,1)S(1)} %answers.1), channel_id=1, source_target_pairs={{0,8},{4,12},{8,0},{12,4},{1,9},{5,13},{9,1},{13,5},{2,10},{6,14},... | collective-permute-start | bytes 208904 | tf_op jit(solution)/shard_map/ppermute | solution.py:490
  41.9 0.9 %copy-start.3 = (bf16[16,4096]{1,0:T(8,128)(2,1)S(1)}, bf16[16,4096]{1,0:T(8,128)(2,1)}, u32[]{:S(2)}) copy-start(bf16[16,4096]{1,0:T(8,128)(2,1)} %get-tuple-element.14.qrot_ref) | copy-start | bytes 393220
  42.8 0.7 %copy-start.5 = (f32[16,128]{1,0:T(8,128)S(1)}, f32[16,128]{1,0:T(8,128)}, u32[]{:S(2)}) copy-start(f32[16,128]{1,0:T(8,128)} %get-tuple-element.13.trig_ref) | copy-start | bytes 24580

commit v3 on v2

v3 whole, which is shorter than its diff:
```python
import functools
import math

import jax
import jax.numpy as jnp
from jax import lax
from jax.experimental import pallas as pl
from jax.experimental.pallas import tpu as pltpu
from jax.sharding import PartitionSpec as P

HD = 128
GROUP = 8
STEPS = 4
RANK = 64
EPSILON = 1e-05
ROPE_BASE = 500000.0
MASKED_SCORE = -1e30
LOWEST_TOP = -1e20
EXPONENT = math.log2(math.e) / math.sqrt(HD)
PAIR = GROUP * HD + 128
CHUNK = 512
AHEAD = 3

F32 = jnp.float32
BF16 = jnp.bfloat16
NT = (((1,), (1,)), ((), ()))
VMEM = pl.BlockSpec(memory_space=pltpu.VMEM)
HBM = pl.BlockSpec(memory_space=pltpu.HBM)
MEBI = 2**20
WHOLE_VMEM = 65000 * 1024
LOCAL_VMEM = 54900 * 1024


def rounded(value):
    return value.astype(BF16).astype(F32)


def split(value):
    high = rounded(value)
    return jnp.concatenate([high, value - high], 0).astype(BF16)


def joined(tile):
    wide = tile.astype(F32)
    return wide[:8] + wide[8:]


def rotated(tile, cosine, sine):
    return tile * cosine + pltpu.roll(tile, HD // 2, 1) * sine


def first_rows(shape):
    return lax.broadcasted_iota(jnp.int32, shape, 0) % 8 < STEPS


def exchanged(a, b):
    first = first_rows(a.shape)
    return (
        jnp.where(first, a, pltpu.roll(b, STEPS, 0)),
        jnp.where(first, pltpu.roll(a, STEPS, 0), b),
    )


def flat(matrix):
    return jnp.concatenate([matrix[i : i + 16] for i in range(0, matrix.shape[0], 16)], 1)


def pack_kernel(*refs):
    sources, (a_ref, b_ref, up_ref, qrot_ref, table_ref) = refs[:8], refs[8:13]
    held, rows_ref, sems = refs[13:21], refs[21], refs[22]
    copies = [
        pltpu.make_async_copy(source, target, sems.at[i])
        for i, (source, target) in enumerate(zip(sources, held))
    ]
    for copy in copies:
        copy.start()
    lengths_ref, x_ref, gain_ref, kd_ref, vd_ref, ku_ref, vu_ref, q_ref = held
    for copy in copies:
        copy.wait()
    x = jnp.concatenate([x_ref[0].astype(F32), x_ref[1].astype(F32)], 0)
    depth = x.shape[1]
    scaled = x * gain_ref[...].astype(F32).reshape(1, depth)
    b_ref[:, : depth // 2] = jnp.concatenate(
        [scaled[:, : depth // 2], scaled[:, depth // 2 :]], 0
    ).astype(BF16)
    row = lax.broadcasted_iota(jnp.int32, (16, 128), 0)
    length = jnp.where(row % 8 < STEPS, lengths_ref[0], lengths_ref[1])
    length = jnp.where(row < 8, length // 64 * 64, length % 64)
    b_ref[:, depth // 2 : depth // 2 + 128] = length.astype(F32).astype(BF16)
    ups = jnp.concatenate([ku_ref[...], vu_ref[...]], 0).T.astype(BF16)
    half = ups.shape[0] // 2
    rows_ref[...] = ups
    up_ref[...] = flat(ups)
    start = pl.multiple_of(lax.axis_index("tensor") % 2 * half, half)
    b_ref[:, depth // 2 + 128 :] = flat(rows_ref[pl.ds(start, half), :])
    own = kd_ref.shape[0]
    for slot, ref in enumerate((kd_ref, vd_ref)):
        down = ref[...]
        if own < 16:
            down = jnp.concatenate([down, jnp.zeros((16 - own, depth), F32)], 0)
        a_ref[:, slot * depth : (slot + 1) * depth] = down.astype(BF16)
    cosine, sine = tables(lengths_ref)
    squares = jnp.broadcast_to(jnp.sum(x * x, 1, keepdims=True), (8, 128))
    table_ref[...] = jnp.concatenate([squares, cosine, sine], 0)
    size = 2 * GROUP * HD
    for p in range(q_ref.shape[2] // size):
        at = pl.ds(pl.multiple_of(pair_at(p) * size, size), size)
        q = jnp.concatenate([q_ref[0, :, at].astype(F32), q_ref[1, :, at].astype(F32)], 0)
        for g in range(GROUP):
            tiles = [
                rotated(q[:, (e * GROUP + g) * HD : (e * GROUP + g + 1) * HD], cosine, sine)
                for e in range(2)
            ]
            at = slice((p * GROUP + g) * HD, (p * GROUP + g + 1) * HD)
            qrot_ref[:, at] = jnp.concatenate(tiles, 0).astype(BF16)


def pack(lengths, hidden, gain, key_down, value_down, key_up, value_up, queries):
    operands = [lengths, hidden, gain, key_down, value_down, key_up.T, value_up.T, queries]
    depth = hidden.shape[2]
    ups = key_up.shape[0] * 8
    return pl.pallas_call(
        pack_kernel,
        in_specs=[HBM] * len(operands),
        out_specs=[VMEM] * 5,
        out_shape=[
            jax.ShapeDtypeStruct((16, 2 * depth), BF16),
            jax.ShapeDtypeStruct((16, depth // 2 + 128 + ups // 2), BF16),
            jax.ShapeDtypeStruct((16, ups), BF16),
            jax.ShapeDtypeStruct((16, queries.shape[2] // 2), BF16),
            jax.ShapeDtypeStruct((24, 128), F32),
        ],
        scratch_shapes=[pltpu.SMEM(lengths.shape, jnp.int32)]
        + [pltpu.VMEM(o.shape, o.dtype) for o in operands[1:]]
        + [
            pltpu.VMEM((key_up.shape[0], 128), BF16),
            pltpu.SemaphoreType.DMA((len(operands),)),
        ],
        compiler_params=pltpu.CompilerParams(vmem_limit_bytes=WHOLE_VMEM),
        name="pack",
    )(*operands)


def tables(lengths_ref):
    shape = (8, HD)
    row = lax.broadcasted_iota(jnp.int32, shape, 0)
    lane = lax.broadcasted_iota(jnp.int32, shape, 1)
    step = row % STEPS
    position = (jnp.where(row < STEPS, lengths_ref[0], lengths_ref[1]) + step).astype(F32)
    pair = lane % (HD // 2)
    frequency = jnp.ones(shape, F32)
    for bit in range(6):
        factor = ROPE_BASE ** (-(2.0 * 2**bit) / HD)
        frequency = jnp.where((pair >> bit) & 1 == 1, frequency * factor, frequency)
    angle = position * frequency
    sine = jnp.sin(angle)
    return jnp.cos(angle), jnp.where(lane < HD // 2, -sine, sine)


def attend(p, limit, q_ref, k_ref, v_ref, out_ref):
    halves = [[], []]
    for g in range(GROUP):
        tile = q_ref[:, (p * GROUP + g) * HD : (p * GROUP + g + 1) * HD].astype(F32)
        halves[0].append(tile[:8])
        halves[1].append(tile[8:])
    mixed = [[exchanged(halves[e][g], halves[e][g + 4]) for g in range(4)] for e in range(2)]
    zero = jnp.zeros((32, HD), F32)
    numers, stats = [], []
    lane8 = lax.broadcasted_iota(jnp.int32, (8, 128), 1)
    pair = slice(2 * p * HD, 2 * (p + 1) * HD)
    for s in range(2):
        rows = [jnp.concatenate([mixed[e][g][s] for g in range(4)], 0) for e in range(2)]
        queries = jnp.concatenate(
            [jnp.concatenate([rows[0], zero], 1), jnp.concatenate([zero, rows[1]], 1)], 0
        ).astype(BF16)
        scores = lax.dot_general(queries, k_ref[s, :, pair], NT, preferred_element_type=F32)
        place = lax.broadcasted_iota(jnp.int32, scores.shape, 1)
        bound = limit[STEPS * s : STEPS * s + 1, :1].astype(jnp.int32)
        masked = jnp.where(place < bound, scores, MASKED_SCORE)
        top = rounded(jnp.maximum(jnp.max(masked, 1, keepdims=True), LOWEST_TOP))
        weights = jnp.exp2((masked - top) * EXPONENT).astype(BF16)
        total = jnp.sum(weights.astype(F32), 1, keepdims=True)
        numers.append(jnp.dot(weights, v_ref[s, :, pair], preferred_element_type=F32))
        high = rounded(total)
        compact = []
        for e in range(2):
            tile = jnp.zeros((8, 128), F32)
            for g in range(4):
                at = slice(32 * e + 8 * g, 32 * e + 8 * g + 8)
                for slot, value in enumerate((top, high, total - high)):
                    tile = jnp.where(lane8 == slot * GROUP + g, value[at], tile)
            compact.append(tile)
        stats.append(compact)
    outs, ends = [[], []], []
    for e in range(2):
        back = []
        for g in range(4):
            at = slice(32 * e + 8 * g, 32 * e + 8 * g + 8)
            cols = slice(e * HD, (e + 1) * HD)
            back.append(exchanged(numers[0][at, cols], numers[1][at, cols]))
        outs[e] = [b[0] for b in back] + [b[1] for b in back]
        a, b = exchanged(stats[0][e], stats[1][e])
        ends.append(jnp.where(lane8 % 8 < 4, a, pltpu.roll(b, 4, 1)))
    p = p % (out_ref.shape[1] // PAIR)
    for g in range(GROUP):
        at = slice(p * PAIR + g * HD, p * PAIR + (g + 1) * HD)
        out_ref[:, at] = jnp.concatenate([outs[0][g], outs[1][g]], 0).astype(BF16)
    out_ref[:, p * PAIR + GROUP * HD : (p + 1) * PAIR] = jnp.concatenate(ends, 0).astype(BF16)


def pair_at(i):
    return i ^ (lax.axis_index("tensor") % 2 * 2)


def local_kernel(
    x_hbm, q_hbm, k_hbm, v_hbm, wk_hbm, wv_hbm,
    keep_ref, send_ref, base_ref,
    x_ref, q_ref, k_ref, v_ref, wk_ref, wv_ref, x_sem, q_sem, cache_sem, weight_sem,
):
    pairs = k_hbm.shape[2] // (2 * HD)
    chunks = wk_hbm.shape[0] // CHUNK
    width = wk_hbm.shape[1]
    x_copy = pltpu.make_async_copy(x_hbm, x_ref, x_sem)
    x_copy.start()
    q_copy = pltpu.make_async_copy(q_hbm, q_ref, q_sem)
    q_copy.start()
    steps = []
    for p in range(pairs):
        size = 2 * HD
        start = pl.multiple_of(pair_at(p) * size, size)
        steps.append(
            [
                pltpu.make_async_copy(
                    source.at[:, :, pl.ds(start, size)],
                    target.at[:, :, pl.ds(p * size, size)],
                    cache_sem.at[p, i],
                )
                for i, (source, target) in enumerate(((k_hbm, k_ref), (v_hbm, v_ref)))
            ]
        )
    core = lax.axis_index("tensor") % 2
    for c in range(chunks):
        copies = []
        for i, (source, target) in enumerate(((wk_hbm, wk_ref), (wv_hbm, wv_ref))):
            for h in range(2):
                start = pl.multiple_of((core ^ h) * (width // 2), width // 2)
                copies.append(
                    pltpu.make_async_copy(
                        source.at[pl.ds(c * CHUNK, CHUNK), pl.ds(start, width // 2)],
                        target.at[pl.ds(c * CHUNK, CHUNK), pl.ds(h * (width // 2), width // 2)],
                        weight_sem.at[c, 2 * i + h],
                    )
                )
        steps.append(copies)
    for copies in steps[:AHEAD]:
        for copy in copies:
            copy.start()

    def arrive(i):
        for copy in steps[i]:
            copy.wait()
        if i + AHEAD < len(steps):
            for copy in steps[i + AHEAD]:
                copy.start()

    x_copy.wait()
    half = wk_hbm.shape[0] // 2
    x = x_ref[:, :half].astype(F32)
    x = jnp.concatenate([x[:8], x[8:]], 1).astype(BF16)
    first = lax.axis_index("tensor") * k_hbm.shape[1]
    limit = joined(x_ref[:, half : half + 128]) - first.astype(F32)
    q_copy.wait()
    for p in range(pairs):
        arrive(p)
        attend(p, limit, q_ref, k_ref, v_ref, keep_ref if p < pairs // 2 else send_ref)
    total = None
    for c in range(chunks):
        arrive(pairs + c)
        rows = x[:, c * CHUNK : (c + 1) * CHUNK]
        part = jnp.concatenate(
            [
                jnp.dot(rows, ref[c * CHUNK : (c + 1) * CHUNK], preferred_element_type=F32)
                for ref in (wk_ref, wv_ref)
            ],
            0,
        )
        total = part if total is None else total + part
    base_ref[...] = total


def local(message, queries, key_cache, value_cache, key_weight, value_weight):
    seqs, length, width = key_cache.shape
    depth = key_weight.shape[0]
    pairs = width // (2 * HD)
    operands = [message, queries, key_cache, value_cache, key_weight, value_weight]
    return pl.pallas_call(
        local_kernel,
        in_specs=[HBM] * 6,
        out_specs=[VMEM] * 3,
        out_shape=[
            jax.ShapeDtypeStruct((16, pairs // 2 * PAIR), BF16),
            jax.ShapeDtypeStruct((16, pairs // 2 * PAIR), BF16),
            jax.ShapeDtypeStruct((16, width), F32),
        ],
        scratch_shapes=[pltpu.VMEM(o.shape, BF16) for o in operands]
        + [
            pltpu.SemaphoreType.DMA,
            pltpu.SemaphoreType.DMA,
            pltpu.SemaphoreType.DMA((pairs, 2)),
            pltpu.SemaphoreType.DMA((depth // CHUNK, 4)),
        ],
        compiler_params=pltpu.CompilerParams(vmem_limit_bytes=LOCAL_VMEM),
        cost_estimate=pl.CostEstimate(
            flops=4 * 64 * 256 * seqs * length * pairs + 4 * 16 * depth * width,
            bytes_accessed=4 * seqs * length * width + 4 * depth * width,
            transcendentals=64 * seqs * length * pairs,
        ),
        name="local",
    )(*operands)


def rank_kernel(n, rows, depth, columns, *refs):
    base_ref, table_ref, own_ref, near_ref = refs[:4]
    tokens, out_ref = refs[4 : 4 + n], refs[4 + n]
    half = base_ref.shape[1] // 2
    place = lax.axis_index("dp")
    x = []
    for ref in tokens:
        part = ref[:, : depth // 2].astype(F32)
        x.append(jnp.concatenate([part[:8], part[8:]], 1))
    x = jnp.concatenate(x, 0).astype(BF16)
    fill = jnp.zeros((RANK - 16, depth), BF16)
    z = None
    for ref, at in ((own_ref, place), (near_ref, place ^ 1)):
        down = jnp.concatenate([ref[:, :depth], fill, ref[:, depth:], fill], 0)
        part = lax.dot_general(x, down, NT, preferred_element_type=F32)
        part = pltpu.roll(part, at * rows, 1)
        z = part if z is None else z + part
    out_ref[:, :half] = base_ref[:, half:].astype(BF16)
    out_ref[:, half : half + 128] = split(table_ref[:8])
    for i in range(n):
        at = half + 128 * (i + 1)
        out_ref[:, at : at + 128] = split(z[8 * i : 8 * i + 8])
    if columns:
        out_ref[:, half + 128 * (n + 1) :] = tokens[1][:, depth // 2 + 128 :]


def rank_products(rows, depth, columns, base, table, own, near, tokens):
    n = len(tokens)
    return pl.pallas_call(
        functools.partial(rank_kernel, n, rows, depth, columns),
        in_specs=[VMEM] * (4 + n),
        out_specs=VMEM,
        out_shape=jax.ShapeDtypeStruct((16, base.shape[1] // 2 + 128 * (n + 1) + columns), BF16),
        compiler_params=pltpu.CompilerParams(vmem_limit_bytes=32 * MEBI),
        name="rank_products",
    )(base, table, own, near, *tokens)


def broadcast_lane(tile, lane):
    return jnp.broadcast_to(tile[:, lane : lane + 1], tile.shape)


def combine_part_kernel(n, *refs):
    base_ref, mine_ref, theirs_ref, out_ref = (*refs[:3], refs[-1])
    if len(refs) > 4:
        up_ref, sent_ref, out_ref, has_ref = refs[3:]
        core = lax.axis_index("tensor") % 2
        columns = up_ref.shape[1] // 2
        mine = sent_ref[:, sent_ref.shape[1] - columns :].astype(F32)
        theirs = theirs_ref[:, theirs_ref.shape[1] - columns :].astype(F32)
        here = lax.axis_index("dp") // 2 == core
        for h in range(2):
            at = slice(h * columns, (h + 1) * columns)
            far = jnp.where(core == h, mine, theirs)
            has_ref[:, at] = jnp.where(here, up_ref[:, at].astype(F32), far).astype(BF16)
    half = base_ref.shape[1] // 2
    own = base_ref[:, :half] + theirs_ref[:, :half].astype(F32)
    out_ref[:, :half] = own.astype(BF16)
    at = slice(half, half + 128 * (n + 2))
    sums = mine_ref[:, at].astype(F32) + theirs_ref[:, at].astype(F32)
    out_ref[:, half:] = split(sums[:8] + sums[8:])


def combine_part(n, base, mine, theirs, extra):
    half = base.shape[1] // 2
    out_shape = [jax.ShapeDtypeStruct((16, half + 128 * (n + 2)), BF16)]
    if extra:
        out_shape.append(jax.ShapeDtypeStruct(extra[0].shape, BF16))
    return pl.pallas_call(
        functools.partial(combine_part_kernel, n),
        in_specs=[VMEM] * (3 + len(extra)),
        out_specs=[VMEM] * len(out_shape),
        out_shape=out_shape,
        compiler_params=pltpu.CompilerParams(vmem_limit_bytes=32 * MEBI),
        name="combine_part",
    )(base, mine, theirs, *extra)


def combine_cache_kernel(a_ref, b_ref, out_ref):
    lane = lax.broadcasted_iota(jnp.int32, (16, 128), 1)
    for p in range(out_ref.shape[1] // PAIR):
        end = slice(p * PAIR + GROUP * HD, (p + 1) * PAIR)
        a, b = a_ref[:, end].astype(F32), b_ref[:, end].astype(F32)
        top = jnp.maximum(a, b)
        fa = jnp.exp2(jnp.minimum(a - top, 0.0) * EXPONENT)
        fb = jnp.exp2(jnp.minimum(b - top, 0.0) * EXPONENT)
        total = fa * totals(a) + fb * totals(b)
        high = rounded(total)
        stats = jnp.where(lane < GROUP, top, 0.0)
        stats = jnp.where(lane // GROUP == 1, pltpu.roll(high, GROUP, 1), stats)
        stats = jnp.where(lane // GROUP == 2, pltpu.roll(total - high, 2 * GROUP, 1), stats)
        out_ref[:, end] = stats.astype(BF16)
        for g in range(GROUP):
            at = slice(p * PAIR + g * HD, p * PAIR + (g + 1) * HD)
            out_ref[:, at] = (
                broadcast_lane(fa, g) * a_ref[:, at].astype(F32)
                + broadcast_lane(fb, g) * b_ref[:, at].astype(F32)
            ).astype(BF16)


def totals(stats):
    return pltpu.roll(stats, 128 - GROUP, 1) + pltpu.roll(stats, 128 - 2 * GROUP, 1)


def combine_cache(a, b):
    return pl.pallas_call(
        combine_cache_kernel,
        in_specs=[VMEM] * 2,
        out_specs=VMEM,
        out_shape=jax.ShapeDtypeStruct(a.shape, BF16),
        compiler_params=pltpu.CompilerParams(vmem_limit_bytes=32 * MEBI),
        name="combine_cache",
    )(a, b)


def answer_kernel(at, pa_ref, pb_ref, *outs):
    z = pa_ref[:, at:].astype(F32) + pb_ref[:, at:].astype(F32)
    for i, ref in enumerate(outs):
        part = z[:, 128 * (i + 1) : 128 * (i + 2)]
        ref[...] = split(part[:8] + part[8:])


def answers(n, part_a, part_b):
    at = part_a.shape[1] - 128 * (n + 1)
    return pl.pallas_call(
        functools.partial(answer_kernel, at),
        in_specs=[VMEM] * 2,
        out_specs=[VMEM] * n,
        out_shape=[jax.ShapeDtypeStruct((16, 128), BF16)] * n,
        compiler_params=pltpu.CompilerParams(vmem_limit_bytes=32 * MEBI),
        name="answers",
    )(part_a, part_b)


def merge_kernel(n, paired, width_all, *refs):
    table_ref, qrot_ref, pa_ref, pb_ref, ca_ref, cb_ref = refs[:6]
    backs, (ua_ref, ub_ref, out_ref) = refs[6 : 6 + n], refs[6 + n :]
    pairs = ca_ref.shape[1] // PAIR
    width = pairs * 2 * HD
    cosine, sine = table_ref[8:16], table_ref[16:]
    sums = pa_ref[...].astype(F32) + pb_ref[...].astype(F32)
    tail = sums[:8, width : width + 256] + sums[8:, width : width + 256]
    squares, z = tail[:, :128], tail[:, 128:]
    for ref in backs:
        z = z + joined(ref[...])
    lane8 = lax.broadcasted_iota(jnp.int32, (8, 128), 1)
    z = jnp.concatenate(
        [jnp.where(lane8 < RANK, z, 0.0), jnp.where(lane8 < RANK, 0.0, z)], 0
    ).astype(BF16)
    adapted = []
    for ref in (ua_ref, ub_ref):
        ups = jnp.concatenate([ref[:, i : i + 128] for i in range(0, ref.shape[1], 128)], 0)
        adapted.append(lax.dot_general(z, ups, NT, preferred_element_type=F32))
    if paired:
        even = lax.axis_index("dp") % 2 == 0
        a, b = adapted
        adapted = [jnp.where(even, a, b), jnp.where(even, b, a)]
    total = sums[:, :width] + jnp.concatenate(adapted, 1)
    scale = lax.rsqrt(squares / width_all + EPSILON)
    lane = lax.broadcasted_iota(jnp.int32, (16, 128), 1)
    step = lax.broadcasted_iota(jnp.int32, (16, 128), 0) % STEPS
    first = first_rows((8, 128))

    def of_step(tiles, j):
        return jnp.concatenate(
            [
                jnp.where(first, tile[j : j + 1], tile[STEPS + j : STEPS + j + 1])
                for tile in tiles
            ],
            0,
        )

    for p in range(pairs):
        new_keys, new_values = [], []
        for e in range(2):
            at = slice((2 * p + e) * HD, (2 * p + e + 1) * HD)
            new_keys.append(rounded(rotated(total[:8, at] * scale, cosine, sine)))
            new_values.append(rounded(total[8:, at] * scale))
            fresh = jnp.concatenate([new_keys[e], new_values[e]], 0)
            start = pairs * GROUP * HD + (2 * p + e) * HD
            out_ref[:, start : start + HD] = fresh.astype(BF16)
        keys = [of_step(new_keys, j) for j in range(STEPS)]
        values = [of_step(new_values, j) for j in range(STEPS)]
        scores = [jnp.zeros((16, 128), F32) for _ in range(STEPS)]
        for g in range(GROUP):
            q = qrot_ref[:, (p * GROUP + g) * HD : (p * GROUP + g + 1) * HD].astype(F32)
            for j in range(STEPS):
                dot = jnp.sum(q * keys[j], 1, keepdims=True)
                scores[j] = jnp.where(lane == g, dot, scores[j])
        scores = [jnp.where(j <= step, scores[j], MASKED_SCORE) for j in range(STEPS)]
        end = slice(p * PAIR + GROUP * HD, (p + 1) * PAIR)
        stats = [ref[:, end].astype(F32) for ref in (ca_ref, cb_ref)]
        top = functools.reduce(jnp.maximum, scores + stats)
        fresh = [rounded(jnp.exp2((scores[j] - top) * EXPONENT)) for j in range(STEPS)]
        factors = [jnp.exp2(jnp.minimum(s - top, 0.0) * EXPONENT) for s in stats]
        denom = functools.reduce(jnp.add, fresh)
        for factor, s in zip(factors, stats):
            denom = denom + factor * totals(s)
        inverse = 1.0 / denom
        coefficients = [c * inverse for c in fresh + factors]
        for g in range(GROUP):
            at = slice(p * PAIR + g * HD, p * PAIR + (g + 1) * HD)
            terms = values + [ref[:, at].astype(F32) for ref in (ca_ref, cb_ref)]
            tile = jnp.zeros((16, 128), F32)
            for c, term in zip(coefficients, terms):
                tile = tile + broadcast_lane(c, g) * term
            out_ref[:, (p * GROUP + g) * HD : (p * GROUP + g + 1) * HD] = tile.astype(BF16)


def merge(paired, width_all, table, qrot, parts, caches, backs, ups):
    operands = [table, qrot, *parts, *caches, *backs, *ups]
    pairs = caches[0].shape[1] // PAIR
    return pl.pallas_call(
        functools.partial(merge_kernel, len(backs), paired, width_all),
        in_specs=[VMEM] * len(operands),
        out_specs=VMEM,
        out_shape=jax.ShapeDtypeStruct((16, pairs * (GROUP + 2) * HD), BF16),
        compiler_params=pltpu.CompilerParams(vmem_limit_bytes=32 * MEBI),
        name="merge",
    )(*operands)


def place_kernel(mine_ref, theirs_ref, keys_out, values_out, out_ref):
    pairs = mine_ref.shape[1] // ((GROUP + 2) * HD)
    for c, ref in enumerate((mine_ref, theirs_ref)):
        for p in range(pairs):
            pair = pair_at(c * pairs + p)
            tiles = ref[:, p * GROUP * HD : (p + 1) * GROUP * HD].astype(F32)
            size = GROUP * HD
            for e in range(2):
                at = pl.ds(pl.multiple_of((2 * pair + e) * size, size), size)
                for s in range(2):
                    rows = slice(8 * e + 4 * s, 8 * e + 4 * s + 4)
                    out_ref[s, :, at] = tiles[rows].astype(BF16)
            start = pairs * GROUP * HD + p * 2 * HD
            fresh = ref[:, start : start + 2 * HD].astype(F32)
            at = pl.ds(pl.multiple_of(pair * 2 * HD, 2 * HD), 2 * HD)
            for i, out in enumerate((keys_out, values_out)):
                for s in range(2):
                    rows = slice(8 * i + 4 * s, 8 * i + 4 * s + 4)
                    out[s, :, at] = fresh[rows].astype(BF16)


def place(width, mine, theirs):
    return pl.pallas_call(
        place_kernel,
        in_specs=[VMEM] * 2,
        out_specs=[VMEM] * 3,
        out_shape=[
            jax.ShapeDtypeStruct((2, STEPS, width), BF16),
            jax.ShapeDtypeStruct((2, STEPS, width), BF16),
            jax.ShapeDtypeStruct((2, STEPS, GROUP * width), BF16),
        ],
        compiler_params=pltpu.CompilerParams(vmem_limit_bytes=32 * MEBI),
        name="place",
    )(mine, theirs)


def swap(value, axis, n, distance):
    return lax.ppermute(value, axis, [(i, i ^ distance) for i in range(n)])


def shards(
    n_dp,
    n_tensor,
    hidden,
    norm_gain,
    queries,
    key_weight,
    value_weight,
    key_down,
    key_up,
    value_down,
    value_up,
    key_cache,
    value_cache,
    lengths,
):
    depth, width = key_weight.shape
    rows = key_down.shape[0]
    to_dp = lambda value, distance: swap(value, "dp", n_dp, distance)
    to_tensor = lambda value, distance: swap(value, "tensor", n_tensor, distance)
    partners = range(2, n_dp, 2)
    n = len(partners)
    paired = n_dp == 4

    own, tokens, ups, qrot, table = pack(
        lengths, hidden, norm_gain, key_down, value_down, key_up, value_up, queries
    )
    near = to_dp(own, 1)
    sent = [to_dp(tokens, d) for d in partners]
    keep, send, base = local(tokens, qrot, key_cache, value_cache, key_weight, value_weight)
    received = to_tensor(send, 1)
    columns = ups.shape[1] // 2 if paired else 0
    part = rank_products(rows, depth, columns, base, table, own, near, [tokens, *sent])
    extra = [ups, sent[0]] if paired else []
    part, *has = combine_part(n, base, part, to_tensor(part, 1), extra)
    if paired:
        ups = [has[0], to_dp(has[0], 1)]
    else:
        ups = lax.all_gather(ups, "dp").reshape(n_dp, 16, -1, 128).transpose(0, 2, 1, 3)
        ups = ups.reshape(2, 2, 16, 16, 128).transpose(0, 1, 3, 2, 4).reshape(2, 2, 16, -1)
        ups = lax.dynamic_index_in_dim(ups, lax.axis_index("tensor") % 2, 0, keepdims=False)
        ups = [ups[0], ups[1]]
    cache = combine_cache(keep, received)
    part_far = to_tensor(part, 2)
    cache_far = to_tensor(cache, 2)
    backs = [to_dp(reply, d) for reply, d in zip(answers(n, part, part_far), partners)]
    merged = merge(
        paired,
        float(depth * n_tensor),
        table,
        qrot,
        (part, part_far),
        (cache, cache_far),
        backs,
        ups,
    )
    return place(width, merged, to_tensor(merged, 1))


def solution(mesh):
    body = functools.partial(shards, mesh.shape["dp"], mesh.shape["tensor"])
    return jax.shard_map(
        body,
        mesh=mesh,
        in_specs=(
            P(("groups", "dp"), None, "tensor"),
            P("tensor"),
            P(("groups", "dp"), None, None),
            P("tensor", None),
            P("tensor", None),
            P(("groups", "dp"), "tensor"),
            P(("groups", "dp"), None),
            P(("groups", "dp"), "tensor"),
            P(("groups", "dp"), None),
            P(("groups", "dp"), "tensor", None),
            P(("groups", "dp"), "tensor", None),
            P(("groups", "dp")),
        ),
        out_specs=(
            P(("groups", "dp"), None, None),
            P(("groups", "dp"), None, None),
            P(("groups", "dp"), None, None),
        ),
        check_vma=False,
    )
```

time: 46.2 us -> 31.5 us (0.68)
  waiting for transfers between devices: 16.6 us -> 9.15 us
  Pallas kernels: 15.5 us -> 11.2 us
  local copies, waits for them, and re-layouts: 4.24 us -> 0.93 us
  starting transfers between devices: 8.82 us -> 9.32 us
    ppermute x7 -> x9, waiting for transfers between devices: 16.6 us -> 9.15 us  [swap(): return lax.ppermute(value, axis, [(i, i ^ distance) for i in range(n)])]
    pallas_call x5 -> x7, Pallas kernels: 13.5 us -> 9.09 us  [the longest x1 6.97 us: local(): pl.pallas_call(local_kernel, in_specs=[HBM] * 6, out_specs=[VMEM] * 3, ou...]
    unnamed x14 -> x10, local copies, waits for them, and re-layouts: 4.24 us -> 0.93 us
    ppermute x7 -> x9, starting transfers between devices: 8.82 us -> 9.32 us  [swap(): return lax.ppermute(value, axis, [(i, i ^ distance) for i in range(n)])]
  transfers between devices with their start and end apart: 7 -> 9, of which waited for: 4 -> 4; matrix products, arithmetic and copies ran while one was open for 0% -> 0% of each run, Pallas kernels for 23% -> 24%
where the time goes in v3:
time: 31.5 us; the launch traced here: 31.3 us
  Pallas kernels  11.2 us (36%)
  starting transfers between devices  9.32 us (30%)
  waiting for transfers between devices  9.15 us (29%)
  local copies, waits for them, and re-layouts  0.93 us (3%)
  between operations  0.73 us (2%)
    ppermute x9, starting transfers between devices, swap(): return lax.ppermute(value, axis, [(i, i ^ distance) for i in range(n)])  9.32 us
    ppermute x9, waiting for transfers between devices, swap(): return lax.ppermute(value, axis, [(i, i ^ distance) for i in range(n)])  9.15 us
    pallas_call x1, Pallas kernels, local(): pl.pallas_call(local_kernel, in_specs=[HBM] * 6, out_specs=[VMEM] * 3, ou...  6.97 us
    pallas_call x1, Pallas kernels, pack(): pl.pallas_call(pack_kernel, in_specs=[HBM] * len(operands), out_specs=[VM...  2.08 us
    unnamed x10, local copies, waits for them, and re-layouts  0.93 us
    pallas_call x1, Pallas kernels, merge(): pl.pallas_call(functools.partial(merge_kernel, len(backs), paired, width_...  0.81 us
    pallas_call x1, Pallas kernels, place(): pl.pallas_call(place_kernel, in_specs=[VMEM] * 2, out_specs=[VMEM] * 3, o...  0.69 us
  transfers between devices with their start and end apart: 9, of which 4 were waited for; matrix products, arithmetic and copies ran while one was open for 0% of the time, Pallas kernels for 24%

profile of v3, /device:TPU:0, one launch (start us, length us, event | category | flops | bytes accessed | tf_op | source)
XLA Modules:
  0.0 31.3 jit_solution(13417133990076188235)
XLA Ops:
  0.6 2.1 %pack.1 = (bf16[16,4096]{1,0:T(8,128)(2,1)}, bf16[16,2176]{1,0:T(8,128)(2,1)}, bf16[16,2048]{1,0:T(8,128)(2,1)}, bf16[16,4096]{1,0:T(8,128)(2,1)}, f32[24,128]{1,0:T(8,128)}) custom-call(s32[2]{0:T(128)} %refs_0_.1, bf16[2,4,2048]{2,1,0:T(4,128)(2,1)} %refs_1_.1, bf16[2048]{0:T(1024)(128)(2,1)} %refs_2_.1, f32[16,2048]{1,0:T(8,128)} %refs_3_.1, ...), custom_call_target="tpu_custom_call" | custom-call | tf_op jit(solution)/shard_map/pack/pallas_call | solution.py:122
  2.7 3.1 %collective-permute-start = (bf16[16,4096]{1,0:T(8,128)(2,1)}, bf16[16,4096]{1,0:T(8,128)(2,1)S(1)}, u32[]{:S(2)}, u32[]{:S(2)}) collective-permute-start(bf16[16,4096]{1,0:T(8,128)(2,1)} %get-tuple-element.17.refs_2_), channel_id=1, source_target_pairs={{0,4},{4,0},{8,12},{12,8},{1,5},{5,1},{9,13},{13,9},{2,6},{6,2},{1... | collective-permute-start | bytes 393224 | tf_op jit(solution)/shard_map/ppermute | solution.py:581
  5.8 2.6 %collective-permute-start.1 = (bf16[16,2176]{1,0:T(8,128)(2,1)}, bf16[16,2176]{1,0:T(8,128)(2,1)S(1)}, u32[]{:S(2)}, u32[]{:S(2)}) collective-permute-start(bf16[16,2176]{1,0:T(8,128)(2,1)} %get-tuple-element.15.x_hbm.refs_4_), channel_id=1, source_target_pairs={{0,8},{4,12},{8,0},{12,4},{1,9},{5,13},{9,1},{13,5},{2,10},{6,14},... | collective-permute-start | bytes 208904 | tf_op jit(solution)/shard_map/ppermute | solution.py:581
  8.4 0.9 %copy-done.1 = bf16[16,2176]{1,0:T(8,128)(2,1)S(1)} copy-done((bf16[16,2176]{1,0:T(8,128)(2,1)S(1)}, bf16[16,2176]{1,0:T(8,128)(2,1)}, u32[]{:S(2)}) %copy-start.1) | copy-done | bytes 69656
  9.3 7.0 %local.1 = (bf16[16,2304]{1,0:T(8,128)(2,1)S(1)}, bf16[16,2304]{1,0:T(8,128)(2,1)S(1)}, f32[16,1024]{1,0:T(8,128)S(1)}) custom-call(bf16[16,2176]{1,0:T(8,128)(2,1)S(1)} %copy-done.1, bf16[16,4096]{1,0:T(8,128)(2,1)} %get-tuple-element.14.q_hbm.refs_1_, bf16[2,512,1024]{2,1,0:T(8,128)(2,1)} %k_hbm.1, bf16[2,512,1024]{2,1,0:T(8,128)(2,1)} %v_hbm.1, ...), custom_call_target="tpu_custom_call" | custom-call | flops 402653184 | bytes 12582912 | tf_op jit(solution)/shard_map/local/pallas_call | solution.py:296
  16.3 0.1 collective-permute-start.4
  16.4 0.0 collective-permute-done.1.refs_5_.refs_4_
  16.4 0.0 collective-permute-done.refs_3_
  16.4 0.3 %rank_products.1.refs_1_ = bf16[16,1920]{1,0:T(8,128)(2,1)S(1)} custom-call(f32[16,1024]{1,0:T(8,128)S(1)} %get-tuple-element.16.refs_0_, f32[24,128]{1,0:T(8,128)S(1)} %copy-done.4, bf16[16,4096]{1,0:T(8,128)(2,1)S(1)} %copy-done.2, bf16[16,4096]{1,0:T(8,128)(2,1)S(1)} %collective-permute-done.refs_3_, bf16[16,2176]{1,0:T(8,128)(2,1)S(1)} %copy-done.1, ...), custom_call_target="tpu_custom_call" | custom-call | tf_op jit(solution)/shard_map/rank_products/pallas_call | solution.py:350
  16.8 0.5 %collective-permute-start.2 = (bf16[16,1920]{1,0:T(8,128)(2,1)S(1)}, bf16[16,1920]{1,0:T(8,128)(2,1)S(1)}, u32[]{:S(2)}, u32[]{:S(2)}) collective-permute-start(bf16[16,1920]{1,0:T(8,128)(2,1)S(1)} %rank_products.1.refs_1_), channel_id=1, source_target_pairs={{0,1},{1,0},{2,3},{3,2},{4,5},{5,4},{6,7},{7,6},{8,9},{9,8},{10,11... | collective-permute-start | bytes 184328 | tf_op jit(solution)/shard_map/ppermute | solution.py:581
  17.3 0.4 %collective-permute-done.4.b_ref = bf16[16,2304]{1,0:T(8,128)(2,1)S(1)} collective-permute-done((bf16[16,2304]{1,0:T(8,128)(2,1)S(1)}, bf16[16,2304]{1,0:T(8,128)(2,1)S(1)}, u32[]{:S(2)}, u32[]{:S(2)}) %collective-permute-start.4) | collective-permute-done | bytes 73760 | tf_op jit(solution)/shard_map/ppermute | solution.py:581
  17.6 0.2 combine_cache.1.refs_4_
  17.9 1.6 %collective-permute-start.5 = (bf16[16,2304]{1,0:T(8,128)(2,1)S(1)}, bf16[16,2304]{1,0:T(8,128)(2,1)S(1)}, u32[]{:S(2)}, u32[]{:S(2)}) collective-permute-start(bf16[16,2304]{1,0:T(8,128)(2,1)S(1)} %combine_cache.1.refs_4_), channel_id=1, source_target_pairs={{0,2},{1,3},{2,0},{3,1},{4,6},{5,7},{6,4},{7,5},{8,10},{9,11},{10,... | collective-permute-start | bytes 221192 | tf_op jit(solution)/shard_map/ppermute | solution.py:581
  19.5 0.5 %collective-permute-start.7 = (bf16[16,2048]{1,0:T(8,128)(2,1)S(1)}, bf16[16,2048]{1,0:T(8,128)(2,1)S(1)}, u32[]{:S(2)}, u32[]{:S(2)}) collective-permute-start(bf16[16,2048]{1,0:T(8,128)(2,1)S(1)} %get-tuple-element.22.refs_7_), channel_id=1, source_target_pairs={{0,4},{4,0},{8,12},{12,8},{1,5},{5,1},{9,13},{13,9},{2,6},{6,2},{1... | collective-permute-start | bytes 196616 | tf_op jit(solution)/shard_map/ppermute | solution.py:581
  20.0 0.5 %collective-permute-start.3 = (bf16[16,896]{1,0:T(8,128)(2,1)S(1)}, bf16[16,896]{1,0:T(8,128)(2,1)S(1)}, u32[]{:S(2)}, u32[]{:S(2)}) collective-permute-start(bf16[16,896]{1,0:T(8,128)(2,1)S(1)} %get-tuple-element.19.pa_ref.refs_2_), channel_id=1, source_target_pairs={{0,2},{1,3},{2,0},{3,1},{4,6},{5,7},{6,4},{7,5},{8,10},{9,11},{10,... | collective-permute-start | bytes 86024 | tf_op jit(solution)/shard_map/ppermute | solution.py:581
  20.5 3.3 %collective-permute-done.3.pb_ref.refs_3_ = bf16[16,896]{1,0:T(8,128)(2,1)S(1)} collective-permute-done((bf16[16,896]{1,0:T(8,128)(2,1)S(1)}, bf16[16,896]{1,0:T(8,128)(2,1)S(1)}, u32[]{:S(2)}, u32[]{:S(2)}) %collective-permute-start.3) | collective-permute-done | bytes 28704 | tf_op jit(solution)/shard_map/ppermute | solution.py:581
  23.9 0.4 %collective-permute-start.6 = (bf16[16,128]{1,0:T(8,128)(2,1)S(1)}, bf16[16,128]{1,0:T(8,128)(2,1)S(1)}, u32[]{:S(2)}, u32[]{:S(2)}) collective-permute-start(bf16[16,128]{1,0:T(8,128)(2,1)S(1)} %answers.1), channel_id=1, source_target_pairs={{0,8},{4,12},{8,0},{12,4},{1,9},{5,13},{9,1},{13,5},{2,10},{6,14},... | collective-permute-start | bytes 12296 | tf_op jit(solution)/shard_map/ppermute | solution.py:581
  24.3 0.0 collective-permute-done.5.refs_5_
  24.3 4.2 %collective-permute-done.6.refs_6_ = bf16[16,128]{1,0:T(8,128)(2,1)S(1)} collective-permute-done((bf16[16,128]{1,0:T(8,128)(2,1)S(1)}, bf16[16,128]{1,0:T(8,128)(2,1)S(1)}, u32[]{:S(2)}, u32[]{:S(2)}) %collective-permute-start.6) | collective-permute-done | bytes 4128 | tf_op jit(solution)/shard_map/ppermute | solution.py:581
  28.4 0.0 collective-permute-done.7.refs_8_
  28.5 0.8 %merge.1.mine_ref = bf16[16,2560]{1,0:T(8,128)(2,1)S(1)} custom-call(f32[24,128]{1,0:T(8,128)S(1)} %copy-done.4, bf16[16,4096]{1,0:T(8,128)(2,1)S(1)} %copy-done, bf16[16,896]{1,0:T(8,128)(2,1)S(1)} %get-tuple-element.19.pa_ref.refs_2_, bf16[16,896]{1,0:T(8,128)(2,1)S(1)} %collective-permute-done.3.pb_ref.refs_3_, ...), custom_call_target="tpu_custom_call" | custom-call | tf_op jit(solution)/shard_map/merge/pallas_call | solution.py:534
  29.3 0.1 collective-permute-start.8
  29.3 1.3 %collective-permute-done.8.theirs_ref = bf16[16,2560]{1,0:T(8,128)(2,1)S(1)} collective-permute-done((bf16[16,2560]{1,0:T(8,128)(2,1)S(1)}, bf16[16,2560]{1,0:T(8,128)(2,1)S(1)}, u32[]{:S(2)}, u32[]{:S(2)}) %collective-permute-start.8) | collective-permute-done | bytes 81952 | tf_op jit(solution)/shard_map/ppermute | solution.py:581
  30.6 0.7 %place.1 = (bf16[2,4,1024]{2,1,0:T(4,128)(2,1)}, bf16[2,4,1024]{2,1,0:T(4,128)(2,1)}, bf16[2,4,8192]{2,1,0:T(4,128)(2,1)}) custom-call(bf16[16,2560]{1,0:T(8,128)(2,1)S(1)} %merge.1.mine_ref, bf16[16,2560]{1,0:T(8,128)(2,1)S(1)} %collective-permute-done.8.theirs_ref), custom_call_target="tpu_custom_call" | custom-call | tf_op jit(solution)/shard_map/place/pallas_call | solution.py:566
  (12 shorter events, 0.1 us)
Async XLA Ops:
  2.7 13.7 %collective-permute-start = (bf16[16,4096]{1,0:T(8,128)(2,1)}, bf16[16,4096]{1,0:T(8,128)(2,1)S(1)}, u32[]{:S(2)}, u32[]{:S(2)}) collective-permute-start(bf16[16,4096]{1,0:T(8,128)(2,1)} %get-tuple-element.17.refs_2_), channel_id=1, source_target_pairs={{0,4},{4,0},{8,12},{12,8},{1,5},{5,1},{9,13},{13,9},{2,6},{6,2},{1... | collective-permute-start | bytes 393224 | tf_op jit(solution)/shard_map/ppermute | solution.py:581
  5.8 10.6 %collective-permute-start.1 = (bf16[16,2176]{1,0:T(8,128)(2,1)}, bf16[16,2176]{1,0:T(8,128)(2,1)S(1)}, u32[]{:S(2)}, u32[]{:S(2)}) collective-permute-start(bf16[16,2176]{1,0:T(8,128)(2,1)} %get-tuple-element.15.x_hbm.refs_4_), channel_id=1, source_target_pairs={{0,8},{4,12},{8,0},{12,4},{1,9},{5,13},{9,1},{13,5},{2,10},{6,14},... | collective-permute-start | bytes 208904 | tf_op jit(solution)/shard_map/ppermute | solution.py:581
  8.4 0.9 %copy-start.1 = (bf16[16,2176]{1,0:T(8,128)(2,1)S(1)}, bf16[16,2176]{1,0:T(8,128)(2,1)}, u32[]{:S(2)}) copy-start(bf16[16,2176]{1,0:T(8,128)(2,1)} %get-tuple-element.15.x_hbm.refs_4_) | copy-start | bytes 208900
  9.3 7.1 %copy-start.2 = (bf16[16,4096]{1,0:T(8,128)(2,1)S(1)}, bf16[16,4096]{1,0:T(8,128)(2,1)}, u32[]{:S(2)}) copy-start(bf16[16,4096]{1,0:T(8,128)(2,1)} %get-tuple-element.17.refs_2_) | copy-start | bytes 393220
  9.3 7.1 %copy-start.4 = (f32[24,128]{1,0:T(8,128)S(1)}, f32[24,128]{1,0:T(8,128)}, u32[]{:S(2)}) copy-start(f32[24,128]{1,0:T(8,128)} %get-tuple-element.13.refs_1_.refs_0_) | copy-start | bytes 36868
  9.3 10.1 %copy-start.3 = (bf16[16,2048]{1,0:T(8,128)(2,1)S(1)}, bf16[16,2048]{1,0:T(8,128)(2,1)}, u32[]{:S(2)}) copy-start(bf16[16,2048]{1,0:T(8,128)(2,1)} %get-tuple-element.18.refs_3_) | copy-start | bytes 196612
  9.3 19.1 %copy-start = (bf16[16,4096]{1,0:T(8,128)(2,1)S(1)}, bf16[16,4096]{1,0:T(8,128)(2,1)}, u32[]{:S(2)}) copy-start(bf16[16,4096]{1,0:T(8,128)(2,1)} %get-tuple-element.14.q_hbm.refs_1_) | copy-start | bytes 393220
  16.3 1.3 %collective-permute-start.4 = (bf16[16,2304]{1,0:T(8,128)(2,1)S(1)}, bf16[16,2304]{1,0:T(8,128)(2,1)S(1)}, u32[]{:S(2)}, u32[]{:S(2)}) collective-permute-start(bf16[16,2304]{1,0:T(8,128)(2,1)S(1)} %get-tuple-element.21), channel_id=1, source_target_pairs={{0,1},{1,0},{2,3},{3,2},{4,5},{5,4},{6,7},{7,6},{8,9},{9,8},{10,11... | collective-permute-start | bytes 221192 | tf_op jit(solution)/shard_map/ppermute | solution.py:581
  16.8 2.7 %collective-permute-start.2 = (bf16[16,1920]{1,0:T(8,128)(2,1)S(1)}, bf16[16,1920]{1,0:T(8,128)(2,1)S(1)}, u32[]{:S(2)}, u32[]{:S(2)}) collective-permute-start(bf16[16,1920]{1,0:T(8,128)(2,1)S(1)} %rank_products.1.refs_1_), channel_id=1, source_target_pairs={{0,1},{1,0},{2,3},{3,2},{4,5},{5,4},{6,7},{7,6},{8,9},{9,8},{10,11... | collective-permute-start | bytes 184328 | tf_op jit(solution)/shard_map/ppermute | solution.py:581
  17.9 6.4 %collective-permute-start.5 = (bf16[16,2304]{1,0:T(8,128)(2,1)S(1)}, bf16[16,2304]{1,0:T(8,128)(2,1)S(1)}, u32[]{:S(2)}, u32[]{:S(2)}) collective-permute-start(bf16[16,2304]{1,0:T(8,128)(2,1)S(1)} %combine_cache.1.refs_4_), channel_id=1, source_target_pairs={{0,2},{1,3},{2,0},{3,1},{4,6},{5,7},{6,4},{7,5},{8,10},{9,11},{10,... | collective-permute-start | bytes 221192 | tf_op jit(solution)/shard_map/ppermute | solution.py:581
  19.5 9.0 %collective-permute-start.7 = (bf16[16,2048]{1,0:T(8,128)(2,1)S(1)}, bf16[16,2048]{1,0:T(8,128)(2,1)S(1)}, u32[]{:S(2)}, u32[]{:S(2)}) collective-permute-start(bf16[16,2048]{1,0:T(8,128)(2,1)S(1)} %get-tuple-element.22.refs_7_), channel_id=1, source_target_pairs={{0,4},{4,0},{8,12},{12,8},{1,5},{5,1},{9,13},{13,9},{2,6},{6,2},{1... | collective-permute-start | bytes 196616 | tf_op jit(solution)/shard_map/ppermute | solution.py:581
  20.0 3.9 %collective-permute-start.3 = (bf16[16,896]{1,0:T(8,128)(2,1)S(1)}, bf16[16,896]{1,0:T(8,128)(2,1)S(1)}, u32[]{:S(2)}, u32[]{:S(2)}) collective-permute-start(bf16[16,896]{1,0:T(8,128)(2,1)S(1)} %get-tuple-element.19.pa_ref.refs_2_), channel_id=1, source_target_pairs={{0,2},{1,3},{2,0},{3,1},{4,6},{5,7},{6,4},{7,5},{8,10},{9,11},{10,... | collective-permute-start | bytes 86024 | tf_op jit(solution)/shard_map/ppermute | solution.py:581
  23.9 4.6 %collective-permute-start.6 = (bf16[16,128]{1,0:T(8,128)(2,1)S(1)}, bf16[16,128]{1,0:T(8,128)(2,1)S(1)}, u32[]{:S(2)}, u32[]{:S(2)}) collective-permute-start(bf16[16,128]{1,0:T(8,128)(2,1)S(1)} %answers.1), channel_id=1, source_target_pairs={{0,8},{4,12},{8,0},{12,4},{1,9},{5,13},{9,1},{13,5},{2,10},{6,14},... | collective-permute-start | bytes 12296 | tf_op jit(solution)/shard_map/ppermute | solution.py:581
  29.3 1.3 %collective-permute-start.8 = (bf16[16,2560]{1,0:T(8,128)(2,1)S(1)}, bf16[16,2560]{1,0:T(8,128)(2,1)S(1)}, u32[]{:S(2)}, u32[]{:S(2)}) collective-permute-start(bf16[16,2560]{1,0:T(8,128)(2,1)S(1)} %merge.1.mine_ref), channel_id=1, source_target_pairs={{0,1},{1,0},{2,3},{3,2},{4,5},{5,4},{6,7},{7,6},{8,9},{9,8},{10,11... | collective-permute-start | bytes 245768 | tf_op jit(solution)/shard_map/ppermute | solution.py:581

commit v4 on v3

--- a/solution.py
+++ b/solution.py
@@ -28,7 +28,7 @@
 HBM = pl.BlockSpec(memory_space=pltpu.HBM)
 MEBI = 2**20
 WHOLE_VMEM = 65000 * 1024
-LOCAL_VMEM = 54900 * 1024
+LOCAL_VMEM = 54800 * 1024
 
 
 def rounded(value):
@@ -66,15 +66,14 @@
 
 
 def pack_kernel(*refs):
-    sources, (a_ref, b_ref, up_ref, qrot_ref, table_ref) = refs[:8], refs[8:13]
-    held, rows_ref, sems = refs[13:21], refs[21], refs[22]
+    sources, (a_ref, b_ref), held, sems = refs[:7], refs[7:9], refs[9:16], refs[16]
     copies = [
         pltpu.make_async_copy(source, target, sems.at[i])
         for i, (source, target) in enumerate(zip(sources, held))
     ]
     for copy in copies:
         copy.start()
-    lengths_ref, x_ref, gain_ref, kd_ref, vd_ref, ku_ref, vu_ref, q_ref = held
+    lengths_ref, x_ref, gain_ref, kd_ref, vd_ref, ku_ref, vu_ref = held
     for copy in copies:
         copy.wait()
     x = jnp.concatenate([x_ref[0].astype(F32), x_ref[1].astype(F32)], 0)
@@ -87,66 +86,43 @@
     length = jnp.where(row % 8 < STEPS, lengths_ref[0], lengths_ref[1])
     length = jnp.where(row < 8, length // 64 * 64, length % 64)
     b_ref[:, depth // 2 : depth // 2 + 128] = length.astype(F32).astype(BF16)
+    squares = jnp.broadcast_to(jnp.sum(x * x, 1, keepdims=True), (8, 128))
+    b_ref[:, depth // 2 + 128 : depth // 2 + 256] = split(squares)
     ups = jnp.concatenate([ku_ref[...], vu_ref[...]], 0).T.astype(BF16)
-    half = ups.shape[0] // 2
-    rows_ref[...] = ups
-    up_ref[...] = flat(ups)
-    start = pl.multiple_of(lax.axis_index("tensor") % 2 * half, half)
-    b_ref[:, depth // 2 + 128 :] = flat(rows_ref[pl.ds(start, half), :])
+    b_ref[:, depth // 2 + 256 :] = flat(ups)
     own = kd_ref.shape[0]
     for slot, ref in enumerate((kd_ref, vd_ref)):
         down = ref[...]
         if own < 16:
             down = jnp.concatenate([down, jnp.zeros((16 - own, depth), F32)], 0)
         a_ref[:, slot * depth : (slot + 1) * depth] = down.astype(BF16)
-    cosine, sine = tables(lengths_ref)
-    squares = jnp.broadcast_to(jnp.sum(x * x, 1, keepdims=True), (8, 128))
-    table_ref[...] = jnp.concatenate([squares, cosine, sine], 0)
-    size = 2 * GROUP * HD
-    for p in range(q_ref.shape[2] // size):
-        at = pl.ds(pl.multiple_of(pair_at(p) * size, size), size)
-        q = jnp.concatenate([q_ref[0, :, at].astype(F32), q_ref[1, :, at].astype(F32)], 0)
-        for g in range(GROUP):
-            tiles = [
-                rotated(q[:, (e * GROUP + g) * HD : (e * GROUP + g + 1) * HD], cosine, sine)
-                for e in range(2)
-            ]
-            at = slice((p * GROUP + g) * HD, (p * GROUP + g + 1) * HD)
-            qrot_ref[:, at] = jnp.concatenate(tiles, 0).astype(BF16)
-
-
-def pack(lengths, hidden, gain, key_down, value_down, key_up, value_up, queries):
-    operands = [lengths, hidden, gain, key_down, value_down, key_up.T, value_up.T, queries]
+
+
+def pack(lengths, hidden, gain, key_down, value_down, key_up, value_up):
+    operands = [lengths, hidden, gain, key_down, value_down, key_up.T, value_up.T]
     depth = hidden.shape[2]
     ups = key_up.shape[0] * 8
     return pl.pallas_call(
         pack_kernel,
         in_specs=[HBM] * len(operands),
-        out_specs=[VMEM] * 5,
+        out_specs=[VMEM] * 2,
         out_shape=[
             jax.ShapeDtypeStruct((16, 2 * depth), BF16),
-            jax.ShapeDtypeStruct((16, depth // 2 + 128 + ups // 2), BF16),
-            jax.ShapeDtypeStruct((16, ups), BF16),
-            jax.ShapeDtypeStruct((16, queries.shape[2] // 2), BF16),
-            jax.ShapeDtypeStruct((24, 128), F32),
+            jax.ShapeDtypeStruct((16, depth // 2 + 256 + ups), BF16),
         ],
         scratch_shapes=[pltpu.SMEM(lengths.shape, jnp.int32)]
         + [pltpu.VMEM(o.shape, o.dtype) for o in operands[1:]]
-        + [
-            pltpu.VMEM((key_up.shape[0], 128), BF16),
-            pltpu.SemaphoreType.DMA((len(operands),)),
-        ],
+        + [pltpu.SemaphoreType.DMA((len(operands),))],
         compiler_params=pltpu.CompilerParams(vmem_limit_bytes=WHOLE_VMEM),
         name="pack",
     )(*operands)
 
 
-def tables(lengths_ref):
-    shape = (8, HD)
+def tables(length):
+    shape = length.shape
     row = lax.broadcasted_iota(jnp.int32, shape, 0)
     lane = lax.broadcasted_iota(jnp.int32, shape, 1)
-    step = row % STEPS
-    position = (jnp.where(row < STEPS, lengths_ref[0], lengths_ref[1]) + step).astype(F32)
+    position = length + (row % STEPS).astype(F32)
     pair = lane % (HD // 2)
     frequency = jnp.ones(shape, F32)
     for bit in range(6):
@@ -157,12 +133,17 @@
     return jnp.cos(angle), jnp.where(lane < HD // 2, -sine, sine)
 
 
-def attend(p, limit, q_ref, k_ref, v_ref, out_ref):
+def attend(p, limit, cosine, sine, q_ref, k_ref, v_ref, out_ref, qrot_ref):
     halves = [[], []]
-    for g in range(GROUP):
-        tile = q_ref[:, (p * GROUP + g) * HD : (p * GROUP + g + 1) * HD].astype(F32)
-        halves[0].append(tile[:8])
-        halves[1].append(tile[8:])
+    for e in range(2):
+        for g in range(GROUP):
+            at = slice(((2 * p + e) * GROUP + g) * HD, ((2 * p + e) * GROUP + g + 1) * HD)
+            q = jnp.concatenate([q_ref[0, :, at].astype(F32), q_ref[1, :, at].astype(F32)], 0)
+            halves[e].append(rotated(q, cosine, sine))
+    if qrot_ref is not None:
+        for g in range(GROUP):
+            at = slice((p * GROUP + g) * HD, (p * GROUP + g + 1) * HD)
+            qrot_ref[:, at] = jnp.concatenate([halves[0][g], halves[1][g]], 0).astype(BF16)
     mixed = [[exchanged(halves[e][g], halves[e][g + 4]) for g in range(4)] for e in range(2)]
     zero = jnp.zeros((32, HD), F32)
     numers, stats = [], []
@@ -214,7 +195,7 @@
 
 def local_kernel(
     x_hbm, q_hbm, k_hbm, v_hbm, wk_hbm, wv_hbm,
-    keep_ref, send_ref, base_ref,
+    keep_ref, send_ref, base_ref, qrot_ref, table_ref,
     x_ref, q_ref, k_ref, v_ref, wk_ref, wv_ref, x_sem, q_sem, cache_sem, weight_sem,
 ):
     pairs = k_hbm.shape[2] // (2 * HD)
@@ -222,13 +203,23 @@
     width = wk_hbm.shape[1]
     x_copy = pltpu.make_async_copy(x_hbm, x_ref, x_sem)
     x_copy.start()
-    q_copy = pltpu.make_async_copy(q_hbm, q_ref, q_sem)
-    q_copy.start()
-    steps = []
+    q_copies = []
+    for p in range(pairs):
+        size = 2 * GROUP * HD
+        start = pl.multiple_of(pair_at(p) * size, size)
+        q_copies.append(
+            pltpu.make_async_copy(
+                q_hbm.at[:, :, pl.ds(start, size)],
+                q_ref.at[:, :, pl.ds(p * size, size)],
+                q_sem.at[p],
+            )
+        )
+        q_copies[p].start()
+    caches, weights = [], []
     for p in range(pairs):
         size = 2 * HD
         start = pl.multiple_of(pair_at(p) * size, size)
-        steps.append(
+        caches.append(
             [
                 pltpu.make_async_copy(
                     source.at[:, :, pl.ds(start, size)],
@@ -251,40 +242,45 @@
                         weight_sem.at[c, 2 * i + h],
                     )
                 )
-        steps.append(copies)
+        weights.append(copies)
+    steps = caches[:1] + [k + w for k, w in zip(caches[1:], weights)] + weights[pairs - 1 :]
     for copies in steps[:AHEAD]:
         for copy in copies:
             copy.start()
 
-    def arrive(i):
-        for copy in steps[i]:
+    x_copy.wait()
+    half = wk_hbm.shape[0] // 2
+    x = x_ref[:, :half].astype(F32)
+    x = jnp.concatenate([x[:8], x[8:]], 1).astype(BF16)
+    length = joined(x_ref[:, half : half + 128])
+    cosine, sine = tables(length)
+    table_ref[...] = jnp.concatenate([joined(x_ref[:, half + 128 : half + 256]), cosine, sine], 0)
+    limit = length - (lax.axis_index("tensor") * k_hbm.shape[1]).astype(F32)
+    for copy in q_copies:
+        copy.wait()
+    total = None
+    for i, copies in enumerate(steps):
+        for copy in copies:
             copy.wait()
         if i + AHEAD < len(steps):
             for copy in steps[i + AHEAD]:
                 copy.start()
-
-    x_copy.wait()
-    half = wk_hbm.shape[0] // 2
-    x = x_ref[:, :half].astype(F32)
-    x = jnp.concatenate([x[:8], x[8:]], 1).astype(BF16)
-    first = lax.axis_index("tensor") * k_hbm.shape[1]
-    limit = joined(x_ref[:, half : half + 128]) - first.astype(F32)
-    q_copy.wait()
-    for p in range(pairs):
-        arrive(p)
-        attend(p, limit, q_ref, k_ref, v_ref, keep_ref if p < pairs // 2 else send_ref)
-    total = None
-    for c in range(chunks):
-        arrive(pairs + c)
-        rows = x[:, c * CHUNK : (c + 1) * CHUNK]
-        part = jnp.concatenate(
-            [
-                jnp.dot(rows, ref[c * CHUNK : (c + 1) * CHUNK], preferred_element_type=F32)
-                for ref in (wk_ref, wv_ref)
-            ],
-            0,
-        )
-        total = part if total is None else total + part
+        if i >= 1:
+            at = slice((i - 1) * CHUNK, i * CHUNK)
+            part = jnp.concatenate(
+                [
+                    jnp.dot(x[:, at], ref[at], preferred_element_type=F32)
+                    for ref in (wk_ref, wv_ref)
+                ],
+                0,
+            )
+            total = part if total is None else total + part
+        if i < pairs:
+            kept = i < pairs // 2
+            out_ref = keep_ref if kept else send_ref
+            attend(
+                i, limit, cosine, sine, q_ref, k_ref, v_ref, out_ref, qrot_ref if kept else None
+            )
     base_ref[...] = total
 
 
@@ -296,16 +292,18 @@
     return pl.pallas_call(
         local_kernel,
         in_specs=[HBM] * 6,
-        out_specs=[VMEM] * 3,
+        out_specs=[VMEM] * 5,
         out_shape=[
             jax.ShapeDtypeStruct((16, pairs // 2 * PAIR), BF16),
             jax.ShapeDtypeStruct((16, pairs // 2 * PAIR), BF16),
             jax.ShapeDtypeStruct((16, width), F32),
+            jax.ShapeDtypeStruct((16, pairs // 2 * GROUP * HD), BF16),
+            jax.ShapeDtypeStruct((24, 128), F32),
         ],
         scratch_shapes=[pltpu.VMEM(o.shape, BF16) for o in operands]
         + [
             pltpu.SemaphoreType.DMA,
-            pltpu.SemaphoreType.DMA,
+            pltpu.SemaphoreType.DMA((pairs,)),
             pltpu.SemaphoreType.DMA((pairs, 2)),
             pltpu.SemaphoreType.DMA((depth // CHUNK, 4)),
         ],
@@ -319,9 +317,9 @@
     )(*operands)
 
 
-def rank_kernel(n, rows, depth, columns, *refs):
+def rank_kernel(n, rows, depth, *refs):
     base_ref, table_ref, own_ref, near_ref = refs[:4]
-    tokens, out_ref = refs[4 : 4 + n], refs[4 + n]
+    tokens, (out_ref, *has) = refs[4 : 4 + n], refs[4 + n :]
     half = base_ref.shape[1] // 2
     place = lax.axis_index("dp")
     x = []
@@ -341,17 +339,22 @@
     for i in range(n):
         at = half + 128 * (i + 1)
         out_ref[:, at : at + 128] = split(z[8 * i : 8 * i + 8])
-    if columns:
-        out_ref[:, half + 128 * (n + 1) :] = tokens[1][:, depth // 2 + 128 :]
+    for ref in has:
+        here = place // 2 == lax.axis_index("tensor") % 2
+        mine, far = (token[:, depth // 2 + 256 :].astype(F32) for token in tokens[:2])
+        ref[...] = jnp.where(here, mine, far).astype(BF16)
 
 
 def rank_products(rows, depth, columns, base, table, own, near, tokens):
     n = len(tokens)
-    return pl.pallas_call(
-        functools.partial(rank_kernel, n, rows, depth, columns),
+    out_shape = [jax.ShapeDtypeStruct((16, base.shape[1] // 2 + 128 * (n + 1)), BF16)]
+    if columns:
+        out_shape.append(jax.ShapeDtypeStruct((16, columns), BF16))
+    return pl.pallas_call(
+        functools.partial(rank_kernel, n, rows, depth),
         in_specs=[VMEM] * (4 + n),
-        out_specs=VMEM,
-        out_shape=jax.ShapeDtypeStruct((16, base.shape[1] // 2 + 128 * (n + 1) + columns), BF16),
+        out_specs=[VMEM] * len(out_shape),
+        out_shape=out_shape,
         compiler_params=pltpu.CompilerParams(vmem_limit_bytes=32 * MEBI),
         name="rank_products",
     )(base, table, own, near, *tokens)
@@ -361,43 +364,27 @@
     return jnp.broadcast_to(tile[:, lane : lane + 1], tile.shape)
 
 
-def combine_part_kernel(n, *refs):
-    base_ref, mine_ref, theirs_ref, out_ref = (*refs[:3], refs[-1])
-    if len(refs) > 4:
-        up_ref, sent_ref, out_ref, has_ref = refs[3:]
-        core = lax.axis_index("tensor") % 2
-        columns = up_ref.shape[1] // 2
-        mine = sent_ref[:, sent_ref.shape[1] - columns :].astype(F32)
-        theirs = theirs_ref[:, theirs_ref.shape[1] - columns :].astype(F32)
-        here = lax.axis_index("dp") // 2 == core
-        for h in range(2):
-            at = slice(h * columns, (h + 1) * columns)
-            far = jnp.where(core == h, mine, theirs)
-            has_ref[:, at] = jnp.where(here, up_ref[:, at].astype(F32), far).astype(BF16)
+def combine_part_kernel(base_ref, mine_ref, theirs_ref, out_ref):
     half = base_ref.shape[1] // 2
     own = base_ref[:, :half] + theirs_ref[:, :half].astype(F32)
     out_ref[:, :half] = own.astype(BF16)
-    at = slice(half, half + 128 * (n + 2))
-    sums = mine_ref[:, at].astype(F32) + theirs_ref[:, at].astype(F32)
+    sums = mine_ref[:, half:].astype(F32) + theirs_ref[:, half:].astype(F32)
     out_ref[:, half:] = split(sums[:8] + sums[8:])
 
 
-def combine_part(n, base, mine, theirs, extra):
-    half = base.shape[1] // 2
-    out_shape = [jax.ShapeDtypeStruct((16, half + 128 * (n + 2)), BF16)]
-    if extra:
-        out_shape.append(jax.ShapeDtypeStruct(extra[0].shape, BF16))
-    return pl.pallas_call(
-        functools.partial(combine_part_kernel, n),
-        in_specs=[VMEM] * (3 + len(extra)),
-        out_specs=[VMEM] * len(out_shape),
-        out_shape=out_shape,
+def combine_part(base, mine, theirs):
+    return pl.pallas_call(
+        combine_part_kernel,
+        in_specs=[VMEM] * 3,
+        out_specs=VMEM,
+        out_shape=jax.ShapeDtypeStruct(mine.shape, BF16),
         compiler_params=pltpu.CompilerParams(vmem_limit_bytes=32 * MEBI),
         name="combine_part",
-    )(base, mine, theirs, *extra)
-
-
-def combine_cache_kernel(a_ref, b_ref, out_ref):
+    )(base, mine, theirs)
+
+
+def combine_cache_kernel(a_ref, b_ref, *refs):
+    out_ref = refs[-1]
     lane = lax.broadcasted_iota(jnp.int32, (16, 128), 1)
     for p in range(out_ref.shape[1] // PAIR):
         end = slice(p * PAIR + GROUP * HD, (p + 1) * PAIR)
@@ -423,15 +410,15 @@
     return pltpu.roll(stats, 128 - GROUP, 1) + pltpu.roll(stats, 128 - 2 * GROUP, 1)
 
 
-def combine_cache(a, b):
+def combine_cache(a, b, *earlier):
     return pl.pallas_call(
         combine_cache_kernel,
-        in_specs=[VMEM] * 2,
+        in_specs=[VMEM] * (2 + len(earlier)),
         out_specs=VMEM,
         out_shape=jax.ShapeDtypeStruct(a.shape, BF16),
         compiler_params=pltpu.CompilerParams(vmem_limit_bytes=32 * MEBI),
         name="combine_cache",
-    )(a, b)
+    )(a, b, *earlier)
 
 
 def answer_kernel(at, pa_ref, pb_ref, *outs):
@@ -605,28 +592,29 @@
     n = len(partners)
     paired = n_dp == 4
 
-    own, tokens, ups, qrot, table = pack(
-        lengths, hidden, norm_gain, key_down, value_down, key_up, value_up, queries
-    )
+    own, tokens = pack(lengths, hidden, norm_gain, key_down, value_down, key_up, value_up)
     near = to_dp(own, 1)
     sent = [to_dp(tokens, d) for d in partners]
-    keep, send, base = local(tokens, qrot, key_cache, value_cache, key_weight, value_weight)
+    keep, send, base, qrot, table = local(
+        tokens, queries, key_cache, value_cache, key_weight, value_weight
+    )
     received = to_tensor(send, 1)
-    columns = ups.shape[1] // 2 if paired else 0
-    part = rank_products(rows, depth, columns, base, table, own, near, [tokens, *sent])
-    extra = [ups, sent[0]] if paired else []
-    part, *has = combine_part(n, base, part, to_tensor(part, 1), extra)
+    columns = key_up.shape[0] * 8 if paired else 0
+    part, *has = rank_products(rows, depth, columns, base, table, own, near, [tokens, *sent])
     if paired:
         ups = [has[0], to_dp(has[0], 1)]
     else:
-        ups = lax.all_gather(ups, "dp").reshape(n_dp, 16, -1, 128).transpose(0, 2, 1, 3)
+        ups = lax.all_gather(tokens[:, depth // 2 + 256 :], "dp")
+        ups = ups.reshape(n_dp, 16, -1, 128).transpose(0, 2, 1, 3)
         ups = ups.reshape(2, 2, 16, 16, 128).transpose(0, 1, 3, 2, 4).reshape(2, 2, 16, -1)
         ups = lax.dynamic_index_in_dim(ups, lax.axis_index("tensor") % 2, 0, keepdims=False)
         ups = [ups[0], ups[1]]
-    cache = combine_cache(keep, received)
+    part = combine_part(base, part, to_tensor(part, 1))
     part_far = to_tensor(part, 2)
+    cache = combine_cache(keep, received, part_far, ups[1])
     cache_far = to_tensor(cache, 2)
-    backs = [to_dp(reply, d) for reply, d in zip(answers(n, part, part_far), partners)]
+    replies = answers(n, part, part_far)
+    backs = [to_dp(reply, d) for reply, d in zip(replies, partners)]
     merged = merge(
         paired,
         float(depth * n_tensor),

time: 31.5 us -> 32.1 us (1.019)
  starting transfers between devices: 9.32 us -> 9.97 us
    ppermute x9, starting transfers between devices: 9.32 us -> 9.97 us  [swap(): return lax.ppermute(value, axis, [(i, i ^ distance) for i in range(n)])]
    pallas_call x4, Pallas kernels: 7.58 us -> 8.08 us  [the longest x1 7.48 us: local(): pl.pallas_call(local_kernel, in_specs=[HBM] * 6, out_specs=[VMEM] * 5, ou...]
    unnamed x10 -> x4, local copies, waits for them, and re-layouts: 0.93 us -> 0.93 us
  transfers between devices with their start and end apart: 9 -> 9, of which waited for: 4 -> 4; matrix products, arithmetic and copies ran while one was open for 0% -> 0% of each run, Pallas kernels for 24% -> 25%
where the time goes in v4:
time: 32.1 us; the launch traced here: 31.9 us
  Pallas kernels  11.5 us (36%)
  starting transfers between devices  9.97 us (31%)
  waiting for transfers between devices  8.83 us (28%)
  local copies, waits for them, and re-layouts  0.93 us (3%)
  between operations  0.71 us (2%)
    ppermute x9, starting transfers between devices, swap(): return lax.ppermute(value, axis, [(i, i ^ distance) for i in range(n)])  9.97 us
    ppermute x9, waiting for transfers between devices, swap(): return lax.ppermute(value, axis, [(i, i ^ distance) for i in range(n)])  8.83 us
    pallas_call x1, Pallas kernels, local(): pl.pallas_call(local_kernel, in_specs=[HBM] * 6, out_specs=[VMEM] * 5, ou...  7.48 us
    pallas_call x1, Pallas kernels, pack(): pl.pallas_call(pack_kernel, in_specs=[HBM] * len(operands), out_specs=[VM...  1.89 us
    unnamed x4, local copies, waits for them, and re-layouts  0.93 us
    pallas_call x1, Pallas kernels, merge(): pl.pallas_call(functools.partial(merge_kernel, len(backs), paired, width_...  0.8 us
    pallas_call x1, Pallas kernels, place(): pl.pallas_call(place_kernel, in_specs=[VMEM] * 2, out_specs=[VMEM] * 3, o...  0.69 us
  transfers between devices with their start and end apart: 9, of which 4 were waited for; matrix products, arithmetic and copies ran while one was open for 0% of the time, Pallas kernels for 25%

profile of v4, /device:TPU:0, one launch (start us, length us, event | category | flops | bytes accessed | tf_op | source)
XLA Modules:
  0.0 31.9 jit_solution(15417230059161519282)
XLA Ops:
  0.6 1.9 %pack.1 = (bf16[16,4096]{1,0:T(8,128)(2,1)}, bf16[16,3328]{1,0:T(8,128)(2,1)}) custom-call(s32[2]{0:T(128)} %refs_0_.1, bf16[2,4,2048]{2,1,0:T(4,128)(2,1)} %refs_1_.1, bf16[2048]{0:T(1024)(128)(2,1)} %refs_2_.1, f32[16,2048]{1,0:T(8,128)} %refs_3_.1, f32[16,2048]{1,0:T(8,128)} %refs_4_.1, f32[64,256]{1,0:T(8,128)} %bitcast.2, f32[64,256]{1,0:T(8,128)} %bitcast.3), custom_call_target="tpu_custom_call" | custom-call | tf_op jit(solution)/shard_map/pack/pallas_call | solution.py:105
  2.5 3.1 %collective-permute-start = (bf16[16,4096]{1,0:T(8,128)(2,1)}, bf16[16,4096]{1,0:T(8,128)(2,1)S(1)}, u32[]{:S(2)}, u32[]{:S(2)}) collective-permute-start(bf16[16,4096]{1,0:T(8,128)(2,1)} %get-tuple-element.16.refs_2_), channel_id=1, source_target_pairs={{0,4},{4,0},{8,12},{12,8},{1,5},{5,1},{9,13},{13,9},{2,6},{6,2},{1... | collective-permute-start | bytes 393224 | tf_op jit(solution)/shard_map/ppermute | solution.py:568
  5.6 2.6 %collective-permute-start.1 = (bf16[16,3328]{1,0:T(8,128)(2,1)}, bf16[16,3328]{1,0:T(8,128)(2,1)S(1)}, u32[]{:S(2)}, u32[]{:S(2)}) collective-permute-start(bf16[16,3328]{1,0:T(8,128)(2,1)} %get-tuple-element.12.x_hbm.refs_4_), channel_id=1, source_target_pairs={{0,8},{4,12},{8,0},{12,4},{1,9},{5,13},{9,1},{13,5},{2,10},{6,14},... | collective-permute-start | bytes 319496 | tf_op jit(solution)/shard_map/ppermute | solution.py:568
  8.2 0.9 %copy-done = bf16[16,3328]{1,0:T(8,128)(2,1)S(1)} copy-done((bf16[16,3328]{1,0:T(8,128)(2,1)S(1)}, bf16[16,3328]{1,0:T(8,128)(2,1)}, u32[]{:S(2)}) %copy-start) | copy-done | bytes 106520
  9.1 7.5 %local.1 = (bf16[16,2304]{1,0:T(8,128)(2,1)S(1)}, bf16[16,2304]{1,0:T(8,128)(2,1)S(1)}, f32[16,1024]{1,0:T(8,128)S(1)}, bf16[16,2048]{1,0:T(8,128)(2,1)S(1)}, f32[24,128]{1,0:T(8,128)S(1)}) custom-call(bf16[16,3328]{1,0:T(8,128)(2,1)S(1)} %copy-done, bf16[2,4,8192]{2,1,0:T(4,128)(2,1)} %q_hbm.1, bf16[2,512,1024]{2,1,0:T(8,128)(2,1)} %k_hbm.1, ...), custom_call_target="tpu_custom_call" | custom-call | flops 402653184 | bytes 12582912 | tf_op jit(solution)/shard_map/local/pallas_call | solution.py:292
  16.6 0.1 collective-permute-start.4
  16.7 0.0 collective-permute-done.1.refs_5_
  16.7 0.0 collective-permute-done.refs_3_
  16.7 0.4 %rank_products.1 = (bf16[16,896]{1,0:T(8,128)(2,1)S(1)}, bf16[16,2048]{1,0:T(8,128)(2,1)S(1)}) custom-call(f32[16,1024]{1,0:T(8,128)S(1)} %get-tuple-element.15.refs_0_.base_ref, f32[24,128]{1,0:T(8,128)S(1)} %get-tuple-element.13.refs_1_.refs_0_, bf16[16,4096]{1,0:T(8,128)(2,1)S(1)} %copy-done.1, bf16[16,4096]{1,0:T(8,128)(2,1)S(1)} %collective-permute-done.refs_3_, ...), custom_call_target="tpu_custom_call" | custom-call | tf_op jit(solution)/shard_map/rank_products/pallas_call | solution.py:353
  17.1 0.5 %collective-permute-start.5 = (bf16[16,2048]{1,0:T(8,128)(2,1)S(1)}, bf16[16,2048]{1,0:T(8,128)(2,1)S(1)}, u32[]{:S(2)}, u32[]{:S(2)}) collective-permute-start(bf16[16,2048]{1,0:T(8,128)(2,1)S(1)} %get-tuple-element.20.refs_7_), channel_id=1, source_target_pairs={{0,4},{4,0},{8,12},{12,8},{1,5},{5,1},{9,13},{13,9},{2,6},{6,2},{1... | collective-permute-start | bytes 196616 | tf_op jit(solution)/shard_map/ppermute | solution.py:568
  17.6 0.2 collective-permute-start.2
  17.8 1.0 %collective-permute-done.2.theirs_ref = bf16[16,896]{1,0:T(8,128)(2,1)S(1)} collective-permute-done((bf16[16,896]{1,0:T(8,128)(2,1)S(1)}, bf16[16,896]{1,0:T(8,128)(2,1)S(1)}, u32[]{:S(2)}, u32[]{:S(2)}) %collective-permute-start.2) | collective-permute-done | bytes 28704 | tf_op jit(solution)/shard_map/ppermute | solution.py:568
  18.8 1.6 %collective-permute-start.3 = (bf16[16,896]{1,0:T(8,128)(2,1)S(1)}, bf16[16,896]{1,0:T(8,128)(2,1)S(1)}, u32[]{:S(2)}, u32[]{:S(2)}) collective-permute-start(bf16[16,896]{1,0:T(8,128)(2,1)S(1)} %combine_part.1.pa_ref.refs_2_), channel_id=1, source_target_pairs={{0,2},{1,3},{2,0},{3,1},{4,6},{5,7},{6,4},{7,5},{8,10},{9,11},{10,... | collective-permute-start | bytes 86024 | tf_op jit(solution)/shard_map/ppermute | solution.py:568
  20.3 0.0 collective-permute-done.4.b_ref
  20.3 2.4 %collective-permute-done.3.refs_0_.pb_ref.refs_3_ = bf16[16,896]{1,0:T(8,128)(2,1)S(1)} collective-permute-done((bf16[16,896]{1,0:T(8,128)(2,1)S(1)}, bf16[16,896]{1,0:T(8,128)(2,1)S(1)}, u32[]{:S(2)}, u32[]{:S(2)}) %collective-permute-start.3) | collective-permute-done | bytes 28704 | tf_op jit(solution)/shard_map/ppermute | solution.py:568
  22.7 0.2 combine_cache.1.refs_4_
  22.9 1.6 %collective-permute-start.6 = (bf16[16,2304]{1,0:T(8,128)(2,1)S(1)}, bf16[16,2304]{1,0:T(8,128)(2,1)S(1)}, u32[]{:S(2)}, u32[]{:S(2)}) collective-permute-start(bf16[16,2304]{1,0:T(8,128)(2,1)S(1)} %combine_cache.1.refs_4_), channel_id=1, source_target_pairs={{0,2},{1,3},{2,0},{3,1},{4,6},{5,7},{6,4},{7,5},{8,10},{9,11},{10,... | collective-permute-start | bytes 221192 | tf_op jit(solution)/shard_map/ppermute | solution.py:568
  24.5 0.4 %collective-permute-start.7 = (bf16[16,128]{1,0:T(8,128)(2,1)S(1)}, bf16[16,128]{1,0:T(8,128)(2,1)S(1)}, u32[]{:S(2)}, u32[]{:S(2)}) collective-permute-start(bf16[16,128]{1,0:T(8,128)(2,1)S(1)} %answers.1), channel_id=1, source_target_pairs={{0,8},{4,12},{8,0},{12,4},{1,9},{5,13},{9,1},{13,5},{2,10},{6,14},... | collective-permute-start | bytes 12296 | tf_op jit(solution)/shard_map/ppermute | solution.py:568
  24.9 4.2 %collective-permute-done.7.refs_6_ = bf16[16,128]{1,0:T(8,128)(2,1)S(1)} collective-permute-done((bf16[16,128]{1,0:T(8,128)(2,1)S(1)}, bf16[16,128]{1,0:T(8,128)(2,1)S(1)}, u32[]{:S(2)}, u32[]{:S(2)}) %collective-permute-start.7) | collective-permute-done | bytes 4128 | tf_op jit(solution)/shard_map/ppermute | solution.py:568
  29.1 0.0 collective-permute-done.6.refs_5_
  29.1 0.8 %merge.1.mine_ref = bf16[16,2560]{1,0:T(8,128)(2,1)S(1)} custom-call(f32[24,128]{1,0:T(8,128)S(1)} %get-tuple-element.13.refs_1_.refs_0_, bf16[16,2048]{1,0:T(8,128)(2,1)S(1)} %get-tuple-element.14.refs_1_, bf16[16,896]{1,0:T(8,128)(2,1)S(1)} %combine_part.1.pa_ref.refs_2_, bf16[16,896]{1,0:T(8,128)(2,1)S(1)} %collective-permute-done.3.refs_0_.pb_ref.refs_3_, ...), custom_call_target="tpu_custom_call" | custom-call | tf_op jit(solution)/shard_map/merge/pallas_call | solution.py:521
  29.9 0.1 collective-permute-start.8
  30.0 1.3 %collective-permute-done.8.theirs_ref = bf16[16,2560]{1,0:T(8,128)(2,1)S(1)} collective-permute-done((bf16[16,2560]{1,0:T(8,128)(2,1)S(1)}, bf16[16,2560]{1,0:T(8,128)(2,1)S(1)}, u32[]{:S(2)}, u32[]{:S(2)}) %collective-permute-start.8) | collective-permute-done | bytes 81952 | tf_op jit(solution)/shard_map/ppermute | solution.py:568
  31.2 0.7 %place.1 = (bf16[2,4,1024]{2,1,0:T(4,128)(2,1)}, bf16[2,4,1024]{2,1,0:T(4,128)(2,1)}, bf16[2,4,8192]{2,1,0:T(4,128)(2,1)}) custom-call(bf16[16,2560]{1,0:T(8,128)(2,1)S(1)} %merge.1.mine_ref, bf16[16,2560]{1,0:T(8,128)(2,1)S(1)} %collective-permute-done.8.theirs_ref), custom_call_target="tpu_custom_call" | custom-call | tf_op jit(solution)/shard_map/place/pallas_call | solution.py:553
  (6 shorter events, 0.0 us)
Async XLA Ops:
  2.5 14.2 %collective-permute-start = (bf16[16,4096]{1,0:T(8,128)(2,1)}, bf16[16,4096]{1,0:T(8,128)(2,1)S(1)}, u32[]{:S(2)}, u32[]{:S(2)}) collective-permute-start(bf16[16,4096]{1,0:T(8,128)(2,1)} %get-tuple-element.16.refs_2_), channel_id=1, source_target_pairs={{0,4},{4,0},{8,12},{12,8},{1,5},{5,1},{9,13},{13,9},{2,6},{6,2},{1... | collective-permute-start | bytes 393224 | tf_op jit(solution)/shard_map/ppermute | solution.py:568
  5.6 11.1 %collective-permute-start.1 = (bf16[16,3328]{1,0:T(8,128)(2,1)}, bf16[16,3328]{1,0:T(8,128)(2,1)S(1)}, u32[]{:S(2)}, u32[]{:S(2)}) collective-permute-start(bf16[16,3328]{1,0:T(8,128)(2,1)} %get-tuple-element.12.x_hbm.refs_4_), channel_id=1, source_target_pairs={{0,8},{4,12},{8,0},{12,4},{1,9},{5,13},{9,1},{13,5},{2,10},{6,14},... | collective-permute-start | bytes 319496 | tf_op jit(solution)/shard_map/ppermute | solution.py:568
  8.2 0.9 %copy-start = (bf16[16,3328]{1,0:T(8,128)(2,1)S(1)}, bf16[16,3328]{1,0:T(8,128)(2,1)}, u32[]{:S(2)}) copy-start(bf16[16,3328]{1,0:T(8,128)(2,1)} %get-tuple-element.12.x_hbm.refs_4_) | copy-start | bytes 319492
  9.1 7.6 %copy-start.1 = (bf16[16,4096]{1,0:T(8,128)(2,1)S(1)}, bf16[16,4096]{1,0:T(8,128)(2,1)}, u32[]{:S(2)}) copy-start(bf16[16,4096]{1,0:T(8,128)(2,1)} %get-tuple-element.16.refs_2_) | copy-start | bytes 393220
  16.6 3.7 %collective-permute-start.4 = (bf16[16,2304]{1,0:T(8,128)(2,1)S(1)}, bf16[16,2304]{1,0:T(8,128)(2,1)S(1)}, u32[]{:S(2)}, u32[]{:S(2)}) collective-permute-start(bf16[16,2304]{1,0:T(8,128)(2,1)S(1)} %get-tuple-element.19), channel_id=1, source_target_pairs={{0,1},{1,0},{2,3},{3,2},{4,5},{5,4},{6,7},{7,6},{8,9},{9,8},{10,11... | collective-permute-start | bytes 221192 | tf_op jit(solution)/shard_map/ppermute | solution.py:568
  17.1 5.6 %collective-permute-start.5 = (bf16[16,2048]{1,0:T(8,128)(2,1)S(1)}, bf16[16,2048]{1,0:T(8,128)(2,1)S(1)}, u32[]{:S(2)}, u32[]{:S(2)}) collective-permute-start(bf16[16,2048]{1,0:T(8,128)(2,1)S(1)} %get-tuple-element.20.refs_7_), channel_id=1, source_target_pairs={{0,4},{4,0},{8,12},{12,8},{1,5},{5,1},{9,13},{13,9},{2,6},{6,2},{1... | collective-permute-start | bytes 196616 | tf_op jit(solution)/shard_map/ppermute | solution.py:568
  17.6 1.2 %collective-permute-start.2 = (bf16[16,896]{1,0:T(8,128)(2,1)S(1)}, bf16[16,896]{1,0:T(8,128)(2,1)S(1)}, u32[]{:S(2)}, u32[]{:S(2)}) collective-permute-start(bf16[16,896]{1,0:T(8,128)(2,1)S(1)} %get-tuple-element.17.mine_ref), channel_id=1, source_target_pairs={{0,1},{1,0},{2,3},{3,2},{4,5},{5,4},{6,7},{7,6},{8,9},{9,8},{10,11... | collective-permute-start | bytes 86024 | tf_op jit(solution)/shard_map/ppermute | solution.py:568
  18.8 3.9 %collective-permute-start.3 = (bf16[16,896]{1,0:T(8,128)(2,1)S(1)}, bf16[16,896]{1,0:T(8,128)(2,1)S(1)}, u32[]{:S(2)}, u32[]{:S(2)}) collective-permute-start(bf16[16,896]{1,0:T(8,128)(2,1)S(1)} %combine_part.1.pa_ref.refs_2_), channel_id=1, source_target_pairs={{0,2},{1,3},{2,0},{3,1},{4,6},{5,7},{6,4},{7,5},{8,10},{9,11},{10,... | collective-permute-start | bytes 86024 | tf_op jit(solution)/shard_map/ppermute | solution.py:568
  22.9 6.1 %collective-permute-start.6 = (bf16[16,2304]{1,0:T(8,128)(2,1)S(1)}, bf16[16,2304]{1,0:T(8,128)(2,1)S(1)}, u32[]{:S(2)}, u32[]{:S(2)}) collective-permute-start(bf16[16,2304]{1,0:T(8,128)(2,1)S(1)} %combine_cache.1.refs_4_), channel_id=1, source_target_pairs={{0,2},{1,3},{2,0},{3,1},{4,6},{5,7},{6,4},{7,5},{8,10},{9,11},{10,... | collective-permute-start | bytes 221192 | tf_op jit(solution)/shard_map/ppermute | solution.py:568
  24.5 4.6 %collective-permute-start.7 = (bf16[16,128]{1,0:T(8,128)(2,1)S(1)}, bf16[16,128]{1,0:T(8,128)(2,1)S(1)}, u32[]{:S(2)}, u32[]{:S(2)}) collective-permute-start(bf16[16,128]{1,0:T(8,128)(2,1)S(1)} %answers.1), channel_id=1, source_target_pairs={{0,8},{4,12},{8,0},{12,4},{1,9},{5,13},{9,1},{13,5},{2,10},{6,14},... | collective-permute-start | bytes 12296 | tf_op jit(solution)/shard_map/ppermute | solution.py:568
  29.9 1.3 %collective-permute-start.8 = (bf16[16,2560]{1,0:T(8,128)(2,1)S(1)}, bf16[16,2560]{1,0:T(8,128)(2,1)S(1)}, u32[]{:S(2)}, u32[]{:S(2)}) collective-permute-start(bf16[16,2560]{1,0:T(8,128)(2,1)S(1)} %merge.1.mine_ref), channel_id=1, source_target_pairs={{0,1},{1,0},{2,3},{3,2},{4,5},{5,4},{6,7},{7,6},{8,9},{9,8},{10,11... | collective-permute-start | bytes 245768 | tf_op jit(solution)/shard_map/ppermute | solution.py:568

commit v5 on v4

--- a/solution.py
+++ b/solution.py
@@ -19,7 +19,6 @@
 EXPONENT = math.log2(math.e) / math.sqrt(HD)
 PAIR = GROUP * HD + 128
 CHUNK = 512
-AHEAD = 3
 
 F32 = jnp.float32
 BF16 = jnp.bfloat16
@@ -28,7 +27,7 @@
 HBM = pl.BlockSpec(memory_space=pltpu.HBM)
 MEBI = 2**20
 WHOLE_VMEM = 65000 * 1024
-LOCAL_VMEM = 54800 * 1024
+LOCAL_VMEM = 54900 * 1024
 
 
 def rounded(value):
@@ -66,7 +65,7 @@
 
 
 def pack_kernel(*refs):
-    sources, (a_ref, b_ref), held, sems = refs[:7], refs[7:9], refs[9:16], refs[16]
+    sources, (a_ref, b_ref, up_ref), held, sems = refs[:7], refs[7:10], refs[10:17], refs[17]
     copies = [
         pltpu.make_async_copy(source, target, sems.at[i])
         for i, (source, target) in enumerate(zip(sources, held))
@@ -90,6 +89,7 @@
     b_ref[:, depth // 2 + 128 : depth // 2 + 256] = split(squares)
     ups = jnp.concatenate([ku_ref[...], vu_ref[...]], 0).T.astype(BF16)
     b_ref[:, depth // 2 + 256 :] = flat(ups)
+    up_ref[...] = flat(ups)
     own = kd_ref.shape[0]
     for slot, ref in enumerate((kd_ref, vd_ref)):
         down = ref[...]
@@ -105,10 +105,11 @@
     return pl.pallas_call(
         pack_kernel,
         in_specs=[HBM] * len(operands),
-        out_specs=[VMEM] * 2,
+        out_specs=[VMEM] * 3,
         out_shape=[
             jax.ShapeDtypeStruct((16, 2 * depth), BF16),
             jax.ShapeDtypeStruct((16, depth // 2 + 256 + ups), BF16),
+            jax.ShapeDtypeStruct((16, ups), BF16),
         ],
         scratch_shapes=[pltpu.SMEM(lengths.shape, jnp.int32)]
         + [pltpu.VMEM(o.shape, o.dtype) for o in operands[1:]]
@@ -201,53 +202,46 @@
     pairs = k_hbm.shape[2] // (2 * HD)
     chunks = wk_hbm.shape[0] // CHUNK
     width = wk_hbm.shape[1]
+    core = lax.axis_index("tensor") % 2
     x_copy = pltpu.make_async_copy(x_hbm, x_ref, x_sem)
     x_copy.start()
-    q_copies = []
-    for p in range(pairs):
-        size = 2 * GROUP * HD
-        start = pl.multiple_of(pair_at(p) * size, size)
-        q_copies.append(
-            pltpu.make_async_copy(
-                q_hbm.at[:, :, pl.ds(start, size)],
-                q_ref.at[:, :, pl.ds(p * size, size)],
-                q_sem.at[p],
-            )
-        )
-        q_copies[p].start()
-    caches, weights = [], []
-    for p in range(pairs):
-        size = 2 * HD
-        start = pl.multiple_of(pair_at(p) * size, size)
-        caches.append(
-            [
+    groups = []
+    for h in range(2):
+        copies = []
+        trio = ((q_hbm, q_ref, q_sem.at[h]), (k_hbm, k_ref, cache_sem.at[h, 0]))
+        for source, target, sem in (*trio, (v_hbm, v_ref, cache_sem.at[h, 1])):
+            size = source.shape[2] // 2
+            start = pl.multiple_of((core ^ h) * size, size)
+            copies.append(
                 pltpu.make_async_copy(
                     source.at[:, :, pl.ds(start, size)],
-                    target.at[:, :, pl.ds(p * size, size)],
-                    cache_sem.at[p, i],
+                    target.at[:, :, pl.ds(h * size, size)],
+                    sem,
                 )
-                for i, (source, target) in enumerate(((k_hbm, k_ref), (v_hbm, v_ref)))
+            )
+        groups.append(copies)
+    weights = []
+    for c in range(chunks):
+        at = pl.ds(c * CHUNK, CHUNK)
+        weights.append(
+            [
+                pltpu.make_async_copy(source.at[at], target.at[at], weight_sem.at[c, i])
+                for i, (source, target) in enumerate(((wk_hbm, wk_ref), (wv_hbm, wv_ref)))
             ]
         )
-    core = lax.axis_index("tensor") % 2
-    for c in range(chunks):
-        copies = []
-        for i, (source, target) in enumerate(((wk_hbm, wk_ref), (wv_hbm, wv_ref))):
-            for h in range(2):
-                start = pl.multiple_of((core ^ h) * (width // 2), width // 2)
-                copies.append(
-                    pltpu.make_async_copy(
-                        source.at[pl.ds(c * CHUNK, CHUNK), pl.ds(start, width // 2)],
-                        target.at[pl.ds(c * CHUNK, CHUNK), pl.ds(h * (width // 2), width // 2)],
-                        weight_sem.at[c, 2 * i + h],
-                    )
-                )
-        weights.append(copies)
-    steps = caches[:1] + [k + w for k, w in zip(caches[1:], weights)] + weights[pairs - 1 :]
-    for copies in steps[:AHEAD]:
+    steps = groups + weights
+    later = [[] for _ in steps]
+    later[0] = weights[:1]
+    later[1] = weights[1:3]
+    for c in range(3, chunks):
+        later[c - 1].append(weights[c])
+
+    def start(copies):
         for copy in copies:
             copy.start()
 
+    start(groups[0])
+    start(groups[1])
     x_copy.wait()
     half = wk_hbm.shape[0] // 2
     x = x_ref[:, :half].astype(F32)
@@ -256,17 +250,20 @@
     cosine, sine = tables(length)
     table_ref[...] = jnp.concatenate([joined(x_ref[:, half + 128 : half + 256]), cosine, sine], 0)
     limit = length - (lax.axis_index("tensor") * k_hbm.shape[1]).astype(F32)
-    for copy in q_copies:
-        copy.wait()
     total = None
     for i, copies in enumerate(steps):
         for copy in copies:
             copy.wait()
-        if i + AHEAD < len(steps):
-            for copy in steps[i + AHEAD]:
-                copy.start()
-        if i >= 1:
-            at = slice((i - 1) * CHUNK, i * CHUNK)
+        for ahead in later[i]:
+            start(ahead)
+        if i < 2:
+            for p in range(i * pairs // 2, (i + 1) * pairs // 2):
+                attend(
+                    p, limit, cosine, sine, q_ref, k_ref, v_ref,
+                    send_ref if i else keep_ref, None if i else qrot_ref,
+                )
+        else:
+            at = slice((i - 2) * CHUNK, (i - 1) * CHUNK)
             part = jnp.concatenate(
                 [
                     jnp.dot(x[:, at], ref[at], preferred_element_type=F32)
@@ -275,13 +272,9 @@
                 0,
             )
             total = part if total is None else total + part
-        if i < pairs:
-            kept = i < pairs // 2
-            out_ref = keep_ref if kept else send_ref
-            attend(
-                i, limit, cosine, sine, q_ref, k_ref, v_ref, out_ref, qrot_ref if kept else None
-            )
-    base_ref[...] = total
+    lower, upper = total[:, : width // 2], total[:, width // 2 :]
+    base_ref[:, : width // 2] = jnp.where(core == 0, lower, upper)
+    base_ref[:, width // 2 :] = jnp.where(core == 0, upper, lower)
 
 
 def local(message, queries, key_cache, value_cache, key_weight, value_weight):
@@ -303,9 +296,9 @@
         scratch_shapes=[pltpu.VMEM(o.shape, BF16) for o in operands]
         + [
             pltpu.SemaphoreType.DMA,
-            pltpu.SemaphoreType.DMA((pairs,)),
-            pltpu.SemaphoreType.DMA((pairs, 2)),
-            pltpu.SemaphoreType.DMA((depth // CHUNK, 4)),
+            pltpu.SemaphoreType.DMA((2,)),
+            pltpu.SemaphoreType.DMA((2, 2)),
+            pltpu.SemaphoreType.DMA((depth // CHUNK, 2)),
         ],
         compiler_params=pltpu.CompilerParams(vmem_limit_bytes=LOCAL_VMEM),
         cost_estimate=pl.CostEstimate(
@@ -364,7 +357,7 @@
     return jnp.broadcast_to(tile[:, lane : lane + 1], tile.shape)
 
 
-def combine_part_kernel(base_ref, mine_ref, theirs_ref, out_ref):
+def combine_part_kernel(base_ref, mine_ref, theirs_ref, _, out_ref):
     half = base_ref.shape[1] // 2
     own = base_ref[:, :half] + theirs_ref[:, :half].astype(F32)
     out_ref[:, :half] = own.astype(BF16)
@@ -372,19 +365,18 @@
     out_ref[:, half:] = split(sums[:8] + sums[8:])
 
 
-def combine_part(base, mine, theirs):
+def combine_part(base, mine, theirs, earlier):
     return pl.pallas_call(
         combine_part_kernel,
-        in_specs=[VMEM] * 3,
+        in_specs=[VMEM] * 4,
         out_specs=VMEM,
         out_shape=jax.ShapeDtypeStruct(mine.shape, BF16),
         compiler_params=pltpu.CompilerParams(vmem_limit_bytes=32 * MEBI),
         name="combine_part",
-    )(base, mine, theirs)
-
-
-def combine_cache_kernel(a_ref, b_ref, *refs):
-    out_ref = refs[-1]
+    )(base, mine, theirs, earlier)
+
+
+def combine_cache_kernel(a_ref, b_ref, out_ref):
     lane = lax.broadcasted_iota(jnp.int32, (16, 128), 1)
     for p in range(out_ref.shape[1] // PAIR):
         end = slice(p * PAIR + GROUP * HD, (p + 1) * PAIR)
@@ -410,15 +402,15 @@
     return pltpu.roll(stats, 128 - GROUP, 1) + pltpu.roll(stats, 128 - 2 * GROUP, 1)
 
 
-def combine_cache(a, b, *earlier):
+def combine_cache(a, b):
     return pl.pallas_call(
         combine_cache_kernel,
-        in_specs=[VMEM] * (2 + len(earlier)),
+        in_specs=[VMEM] * 2,
         out_specs=VMEM,
         out_shape=jax.ShapeDtypeStruct(a.shape, BF16),
         compiler_params=pltpu.CompilerParams(vmem_limit_bytes=32 * MEBI),
         name="combine_cache",
-    )(a, b, *earlier)
+    )(a, b)
 
 
 def answer_kernel(at, pa_ref, pb_ref, *outs):
@@ -592,7 +584,7 @@
     n = len(partners)
     paired = n_dp == 4
 
-    own, tokens = pack(lengths, hidden, norm_gain, key_down, value_down, key_up, value_up)
+    own, tokens, own_ups = pack(lengths, hidden, norm_gain, key_down, value_down, key_up, value_up)
     near = to_dp(own, 1)
     sent = [to_dp(tokens, d) for d in partners]
     keep, send, base, qrot, table = local(
@@ -602,16 +594,21 @@
     columns = key_up.shape[0] * 8 if paired else 0
     part, *has = rank_products(rows, depth, columns, base, table, own, near, [tokens, *sent])
     if paired:
-        ups = [has[0], to_dp(has[0], 1)]
+        places = [(s, t) for s in range(n_dp) for t in range(n_tensor)]
+        perm = [
+            (s * n_tensor + t, (s ^ 1) * n_tensor + t if t % 2 == s // 2 else (s ^ 3) * n_tensor + (t ^ 1))
+            for s, t in places
+        ]
+        ups = [has[0], lax.ppermute(own_ups, ("dp", "tensor"), perm)]
     else:
-        ups = lax.all_gather(tokens[:, depth // 2 + 256 :], "dp")
+        ups = lax.all_gather(own_ups, "dp")
         ups = ups.reshape(n_dp, 16, -1, 128).transpose(0, 2, 1, 3)
         ups = ups.reshape(2, 2, 16, 16, 128).transpose(0, 1, 3, 2, 4).reshape(2, 2, 16, -1)
         ups = lax.dynamic_index_in_dim(ups, lax.axis_index("tensor") % 2, 0, keepdims=False)
         ups = [ups[0], ups[1]]
-    part = combine_part(base, part, to_tensor(part, 1))
+    part = combine_part(base, part, to_tensor(part, 1), ups[1])
     part_far = to_tensor(part, 2)
-    cache = combine_cache(keep, received, part_far, ups[1])
+    cache = combine_cache(keep, received)
     cache_far = to_tensor(cache, 2)
     replies = answers(n, part, part_far)
     backs = [to_dp(reply, d) for reply, d in zip(replies, partners)]

time: 32.1 us -> 31.7 us (0.988)
  local copies, waits for them, and re-layouts: 0.93 us -> 0.01 us
  waiting for transfers between devices: 8.83 us -> 9.59 us
    unnamed x4 -> x6, local copies, waits for them, and re-layouts: 0.93 us -> 0.01 us
    ppermute x0 -> x1, waiting for transfers between devices: none -> 0.9 us  [shards(): ups = [has[0], lax.ppermute(own_ups, ('dp', 'tensor'), perm)]]
    ppermute x0 -> x1, starting transfers between devices: none -> 0.51 us  [shards(): ups = [has[0], lax.ppermute(own_ups, ('dp', 'tensor'), perm)]]
    ppermute x9 -> x8, starting transfers between devices: 9.97 us -> 9.49 us  [swap(): return lax.ppermute(value, axis, [(i, i ^ distance) for i in range(n)])]
    ppermute x9 -> x8, waiting for transfers between devices: 8.83 us -> 8.68 us  [swap(): return lax.ppermute(value, axis, [(i, i ^ distance) for i in range(n)])]
  transfers between devices with their start and end apart: 9 -> 9, of which waited for: 4 -> 6; matrix products, arithmetic and copies ran while one was open for 0% -> 0% of each run, Pallas kernels for 25% -> 25%
where the time goes in v5:
time: 31.7 us; the launch traced here: 31.5 us
  Pallas kernels  11.2 us (35%)
  starting transfers between devices  10 us (32%)
  waiting for transfers between devices  9.59 us (30%)
  between operations  0.71 us (2%)
    ppermute x8, starting transfers between devices, swap(): return lax.ppermute(value, axis, [(i, i ^ distance) for i in range(n)])  9.49 us
    ppermute x8, waiting for transfers between devices, swap(): return lax.ppermute(value, axis, [(i, i ^ distance) for i in range(n)])  8.68 us
    pallas_call x1, Pallas kernels, local(): pl.pallas_call(local_kernel, in_specs=[HBM] * 6, out_specs=[VMEM] * 5, ou...  7.18 us
    pallas_call x1, Pallas kernels, pack(): pl.pallas_call(pack_kernel, in_specs=[HBM] * len(operands), out_specs=[VM...  1.92 us
    ppermute x1, waiting for transfers between devices, shards(): ups = [has[0], lax.ppermute(own_ups, ('dp', 'tensor'), perm)]  0.9 us
    pallas_call x1, Pallas kernels, merge(): pl.pallas_call(functools.partial(merge_kernel, len(backs), paired, width_...  0.8 us
    pallas_call x1, Pallas kernels, place(): pl.pallas_call(place_kernel, in_specs=[VMEM] * 2, out_specs=[VMEM] * 3, o...  0.69 us
  transfers between devices with their start and end apart: 9, of which 6 were waited for; matrix products, arithmetic and copies ran while one was open for 0% of the time, Pallas kernels for 25%

profile of v5, /device:TPU:0, one launch (start us, length us, event | category | flops | bytes accessed | tf_op | source)
XLA Modules:
  0.0 31.5 jit_solution(6035992695887638981)
XLA Ops:
  0.6 1.9 %pack.1 = (bf16[16,4096]{1,0:T(8,128)(2,1)}, bf16[16,3328]{1,0:T(8,128)(2,1)}, bf16[16,2048]{1,0:T(8,128)(2,1)}) custom-call(s32[2]{0:T(128)} %refs_0_.1, bf16[2,4,2048]{2,1,0:T(4,128)(2,1)} %refs_1_.1, bf16[2048]{0:T(1024)(128)(2,1)} %refs_2_.1, f32[16,2048]{1,0:T(8,128)} %refs_3_.1, f32[16,2048]{1,0:T(8,128)} %refs_4_.1, f32[64,256]{1,0:T(8,128)} %bitcast.2, ...), custom_call_target="tpu_custom_call" | custom-call | tf_op jit(solution)/shard_map/pack/pallas_call | solution.py:105
  2.6 3.1 %collective-permute-start = (bf16[16,4096]{1,0:T(8,128)(2,1)}, bf16[16,4096]{1,0:T(8,128)(2,1)S(1)}, u32[]{:S(2)}, u32[]{:S(2)}) collective-permute-start(bf16[16,4096]{1,0:T(8,128)(2,1)} %get-tuple-element.17.refs_2_), channel_id=1, source_target_pairs={{0,4},{4,0},{8,12},{12,8},{1,5},{5,1},{9,13},{13,9},{2,6},{6,2},{1... | collective-permute-start | bytes 393224 | tf_op jit(solution)/shard_map/ppermute | solution.py:560
  5.7 2.6 %collective-permute-start.1 = (bf16[16,3328]{1,0:T(8,128)(2,1)}, bf16[16,3328]{1,0:T(8,128)(2,1)S(1)}, u32[]{:S(2)}, u32[]{:S(2)}) collective-permute-start(bf16[16,3328]{1,0:T(8,128)(2,1)} %get-tuple-element.13.x_hbm.refs_4_), channel_id=1, source_target_pairs={{0,8},{4,12},{8,0},{12,4},{1,9},{5,13},{9,1},{13,5},{2,10},{6,14},... | collective-permute-start | bytes 319496 | tf_op jit(solution)/shard_map/ppermute | solution.py:560
  8.2 7.2 %local.1 = (bf16[16,2304]{1,0:T(8,128)(2,1)S(1)}, bf16[16,2304]{1,0:T(8,128)(2,1)S(1)}, f32[16,1024]{1,0:T(8,128)S(1)}, bf16[16,2048]{1,0:T(8,128)(2,1)S(1)}, f32[24,128]{1,0:T(8,128)S(1)}) custom-call(bf16[16,3328]{1,0:T(8,128)(2,1)} %get-tuple-element.13.x_hbm.refs_4_, bf16[2,4,8192]{2,1,0:T(4,128)(2,1)} %q_hbm.1, bf16[2,512,1024]{2,1,0:T(8,128)(2,1)} %k_hbm.1, ...), custom_call_target="tpu_custom_call" | custom-call | flops 402653184 | bytes 12582912 | tf_op jit(solution)/shard_map/local/pallas_call | solution.py:285
  15.4 0.1 collective-permute-start.5
  15.5 0.5 %collective-permute-start.3 = (bf16[16,2048]{1,0:T(8,128)(2,1)S(1)}, bf16[16,2048]{1,0:T(8,128)(2,1)S(1)}, u32[]{:S(2)}, u32[]{:S(2)}) collective-permute-start(bf16[16,2048]{1,0:T(8,128)(2,1)S(1)} %copy-done.2), channel_id=1, source_target_pairs={{0,4},{1,12},{2,6},{3,14},{4,0},{5,8},{6,2},{7,10},{8,5},{9,13},{1... | collective-permute-start | bytes 196616 | tf_op jit(solution)/shard_map/ppermute | solution.py:602
  16.0 0.7 %collective-permute-done.5.b_ref = bf16[16,2304]{1,0:T(8,128)(2,1)S(1)} collective-permute-done((bf16[16,2304]{1,0:T(8,128)(2,1)S(1)}, bf16[16,2304]{1,0:T(8,128)(2,1)S(1)}, u32[]{:S(2)}, u32[]{:S(2)}) %collective-permute-start.5) | collective-permute-done | bytes 73760 | tf_op jit(solution)/shard_map/ppermute | solution.py:560
  16.8 0.2 combine_cache.1.refs_4_
  17.0 1.6 %collective-permute-start.6 = (bf16[16,2304]{1,0:T(8,128)(2,1)S(1)}, bf16[16,2304]{1,0:T(8,128)(2,1)S(1)}, u32[]{:S(2)}, u32[]{:S(2)}) collective-permute-start(bf16[16,2304]{1,0:T(8,128)(2,1)S(1)} %combine_cache.1.refs_4_), channel_id=1, source_target_pairs={{0,2},{1,3},{2,0},{3,1},{4,6},{5,7},{6,4},{7,5},{8,10},{9,11},{10,... | collective-permute-start | bytes 221192 | tf_op jit(solution)/shard_map/ppermute | solution.py:560
  18.5 0.0 collective-permute-done.1.refs_5_
  18.6 0.0 collective-permute-done.refs_3_
  18.6 0.4 %rank_products.1 = (bf16[16,896]{1,0:T(8,128)(2,1)S(1)}, bf16[16,2048]{1,0:T(8,128)(2,1)S(1)}) custom-call(f32[16,1024]{1,0:T(8,128)S(1)} %get-tuple-element.16.refs_0_.base_ref, f32[24,128]{1,0:T(8,128)S(1)} %get-tuple-element.14.refs_1_.refs_0_, bf16[16,4096]{1,0:T(8,128)(2,1)S(1)} %copy-done.1, bf16[16,4096]{1,0:T(8,128)(2,1)S(1)} %collective-permute-done.refs_3_, ...), custom_call_target="tpu_custom_call" | custom-call | tf_op jit(solution)/shard_map/rank_products/pallas_call | solution.py:346
  18.9 0.0 collective-permute-start.2
  18.9 0.9 %collective-permute-done.3._.refs_8_ = bf16[16,2048]{1,0:T(8,128)(2,1)S(1)} collective-permute-done((bf16[16,2048]{1,0:T(8,128)(2,1)S(1)}, bf16[16,2048]{1,0:T(8,128)(2,1)S(1)}, u32[]{:S(2)}, u32[]{:S(2)}) %collective-permute-start.3) | collective-permute-done | bytes 65568 | tf_op jit(solution)/shard_map/ppermute | solution.py:602
  19.9 0.3 collective-permute-done.2.theirs_ref
  20.2 1.3 %collective-permute-start.4 = (bf16[16,896]{1,0:T(8,128)(2,1)S(1)}, bf16[16,896]{1,0:T(8,128)(2,1)S(1)}, u32[]{:S(2)}, u32[]{:S(2)}) collective-permute-start(bf16[16,896]{1,0:T(8,128)(2,1)S(1)} %combine_part.1.pa_ref.refs_2_), channel_id=1, source_target_pairs={{0,2},{1,3},{2,0},{3,1},{4,6},{5,7},{6,4},{7,5},{8,10},{9,11},{10,... | collective-permute-start | bytes 86024 | tf_op jit(solution)/shard_map/ppermute | solution.py:560
  21.4 2.7 %collective-permute-done.4.pb_ref.refs_3_ = bf16[16,896]{1,0:T(8,128)(2,1)S(1)} collective-permute-done((bf16[16,896]{1,0:T(8,128)(2,1)S(1)}, bf16[16,896]{1,0:T(8,128)(2,1)S(1)}, u32[]{:S(2)}, u32[]{:S(2)}) %collective-permute-start.4) | collective-permute-done | bytes 28704 | tf_op jit(solution)/shard_map/ppermute | solution.py:560
  24.1 0.8 %collective-permute-start.7 = (bf16[16,128]{1,0:T(8,128)(2,1)S(1)}, bf16[16,128]{1,0:T(8,128)(2,1)S(1)}, u32[]{:S(2)}, u32[]{:S(2)}) collective-permute-start(bf16[16,128]{1,0:T(8,128)(2,1)S(1)} %answers.1), channel_id=1, source_target_pairs={{0,8},{4,12},{8,0},{12,4},{1,9},{5,13},{9,1},{13,5},{2,10},{6,14},... | collective-permute-start | bytes 12296 | tf_op jit(solution)/shard_map/ppermute | solution.py:560
  24.9 0.0 collective-permute-done.6.refs_5_
  24.9 3.7 %collective-permute-done.7.refs_6_ = bf16[16,128]{1,0:T(8,128)(2,1)S(1)} collective-permute-done((bf16[16,128]{1,0:T(8,128)(2,1)S(1)}, bf16[16,128]{1,0:T(8,128)(2,1)S(1)}, u32[]{:S(2)}, u32[]{:S(2)}) %collective-permute-start.7) | collective-permute-done | bytes 4128 | tf_op jit(solution)/shard_map/ppermute | solution.py:560
  28.7 0.8 %merge.1.mine_ref = bf16[16,2560]{1,0:T(8,128)(2,1)S(1)} custom-call(f32[24,128]{1,0:T(8,128)S(1)} %get-tuple-element.14.refs_1_.refs_0_, bf16[16,2048]{1,0:T(8,128)(2,1)S(1)} %get-tuple-element.15.refs_1_, bf16[16,896]{1,0:T(8,128)(2,1)S(1)} %combine_part.1.pa_ref.refs_2_, bf16[16,896]{1,0:T(8,128)(2,1)S(1)} %collective-permute-done.4.pb_ref.refs_3_, ...), custom_call_target="tpu_custom_call" | custom-call | tf_op jit(solution)/shard_map/merge/pallas_call | solution.py:513
  29.5 0.1 collective-permute-start.8
  29.6 1.3 %collective-permute-done.8.theirs_ref = bf16[16,2560]{1,0:T(8,128)(2,1)S(1)} collective-permute-done((bf16[16,2560]{1,0:T(8,128)(2,1)S(1)}, bf16[16,2560]{1,0:T(8,128)(2,1)S(1)}, u32[]{:S(2)}, u32[]{:S(2)}) %collective-permute-start.8) | collective-permute-done | bytes 81952 | tf_op jit(solution)/shard_map/ppermute | solution.py:560
  30.8 0.7 %place.1 = (bf16[2,4,1024]{2,1,0:T(4,128)(2,1)}, bf16[2,4,1024]{2,1,0:T(4,128)(2,1)}, bf16[2,4,8192]{2,1,0:T(4,128)(2,1)}) custom-call(bf16[16,2560]{1,0:T(8,128)(2,1)S(1)} %merge.1.mine_ref, bf16[16,2560]{1,0:T(8,128)(2,1)S(1)} %collective-permute-done.8.theirs_ref), custom_call_target="tpu_custom_call" | custom-call | tf_op jit(solution)/shard_map/place/pallas_call | solution.py:545
  (8 shorter events, 0.0 us)
Async XLA Ops:
  2.6 16.0 %collective-permute-start = (bf16[16,4096]{1,0:T(8,128)(2,1)}, bf16[16,4096]{1,0:T(8,128)(2,1)S(1)}, u32[]{:S(2)}, u32[]{:S(2)}) collective-permute-start(bf16[16,4096]{1,0:T(8,128)(2,1)} %get-tuple-element.17.refs_2_), channel_id=1, source_target_pairs={{0,4},{4,0},{8,12},{12,8},{1,5},{5,1},{9,13},{13,9},{2,6},{6,2},{1... | collective-permute-start | bytes 393224 | tf_op jit(solution)/shard_map/ppermute | solution.py:560
  5.6 9.9 %copy-start.2 = (bf16[16,2048]{1,0:T(8,128)(2,1)S(1)}, bf16[16,2048]{1,0:T(8,128)(2,1)}, u32[]{:S(2)}) copy-start(bf16[16,2048]{1,0:T(8,128)(2,1)} %get-tuple-element.19) | copy-start | bytes 196612
  5.6 12.9 %copy-start = (bf16[16,3328]{1,0:T(8,128)(2,1)S(1)}, bf16[16,3328]{1,0:T(8,128)(2,1)}, u32[]{:S(2)}) copy-start(bf16[16,3328]{1,0:T(8,128)(2,1)} %get-tuple-element.13.x_hbm.refs_4_) | copy-start | bytes 319492
  5.7 12.9 %copy-start.1 = (bf16[16,4096]{1,0:T(8,128)(2,1)S(1)}, bf16[16,4096]{1,0:T(8,128)(2,1)}, u32[]{:S(2)}) copy-start(bf16[16,4096]{1,0:T(8,128)(2,1)} %get-tuple-element.17.refs_2_) | copy-start | bytes 393220
  5.7 12.9 %collective-permute-start.1 = (bf16[16,3328]{1,0:T(8,128)(2,1)}, bf16[16,3328]{1,0:T(8,128)(2,1)S(1)}, u32[]{:S(2)}, u32[]{:S(2)}) collective-permute-start(bf16[16,3328]{1,0:T(8,128)(2,1)} %get-tuple-element.13.x_hbm.refs_4_), channel_id=1, source_target_pairs={{0,8},{4,12},{8,0},{12,4},{1,9},{5,13},{9,1},{13,5},{2,10},{6,14},... | collective-permute-start | bytes 319496 | tf_op jit(solution)/shard_map/ppermute | solution.py:560
  15.4 1.3 %collective-permute-start.5 = (bf16[16,2304]{1,0:T(8,128)(2,1)S(1)}, bf16[16,2304]{1,0:T(8,128)(2,1)S(1)}, u32[]{:S(2)}, u32[]{:S(2)}) collective-permute-start(bf16[16,2304]{1,0:T(8,128)(2,1)S(1)} %get-tuple-element.21), channel_id=1, source_target_pairs={{0,1},{1,0},{2,3},{3,2},{4,5},{5,4},{6,7},{7,6},{8,9},{9,8},{10,11... | collective-permute-start | bytes 221192 | tf_op jit(solution)/shard_map/ppermute | solution.py:560
  15.5 4.3 %collective-permute-start.3 = (bf16[16,2048]{1,0:T(8,128)(2,1)S(1)}, bf16[16,2048]{1,0:T(8,128)(2,1)S(1)}, u32[]{:S(2)}, u32[]{:S(2)}) collective-permute-start(bf16[16,2048]{1,0:T(8,128)(2,1)S(1)} %copy-done.2), channel_id=1, source_target_pairs={{0,4},{1,12},{2,6},{3,14},{4,0},{5,8},{6,2},{7,10},{8,5},{9,13},{1... | collective-permute-start | bytes 196616 | tf_op jit(solution)/shard_map/ppermute | solution.py:602
  17.0 7.9 %collective-permute-start.6 = (bf16[16,2304]{1,0:T(8,128)(2,1)S(1)}, bf16[16,2304]{1,0:T(8,128)(2,1)S(1)}, u32[]{:S(2)}, u32[]{:S(2)}) collective-permute-start(bf16[16,2304]{1,0:T(8,128)(2,1)S(1)} %combine_cache.1.refs_4_), channel_id=1, source_target_pairs={{0,2},{1,3},{2,0},{3,1},{4,6},{5,7},{6,4},{7,5},{8,10},{9,11},{10,... | collective-permute-start | bytes 221192 | tf_op jit(solution)/shard_map/ppermute | solution.py:560
  18.9 1.2 %collective-permute-start.2 = (bf16[16,896]{1,0:T(8,128)(2,1)S(1)}, bf16[16,896]{1,0:T(8,128)(2,1)S(1)}, u32[]{:S(2)}, u32[]{:S(2)}) collective-permute-start(bf16[16,896]{1,0:T(8,128)(2,1)S(1)} %get-tuple-element.18.mine_ref), channel_id=1, source_target_pairs={{0,1},{1,0},{2,3},{3,2},{4,5},{5,4},{6,7},{7,6},{8,9},{9,8},{10,11... | collective-permute-start | bytes 86024 | tf_op jit(solution)/shard_map/ppermute | solution.py:560
  20.2 3.9 %collective-permute-start.4 = (bf16[16,896]{1,0:T(8,128)(2,1)S(1)}, bf16[16,896]{1,0:T(8,128)(2,1)S(1)}, u32[]{:S(2)}, u32[]{:S(2)}) collective-permute-start(bf16[16,896]{1,0:T(8,128)(2,1)S(1)} %combine_part.1.pa_ref.refs_2_), channel_id=1, source_target_pairs={{0,2},{1,3},{2,0},{3,1},{4,6},{5,7},{6,4},{7,5},{8,10},{9,11},{10,... | collective-permute-start | bytes 86024 | tf_op jit(solution)/shard_map/ppermute | solution.py:560
  24.1 4.6 %collective-permute-start.7 = (bf16[16,128]{1,0:T(8,128)(2,1)S(1)}, bf16[16,128]{1,0:T(8,128)(2,1)S(1)}, u32[]{:S(2)}, u32[]{:S(2)}) collective-permute-start(bf16[16,128]{1,0:T(8,128)(2,1)S(1)} %answers.1), channel_id=1, source_target_pairs={{0,8},{4,12},{8,0},{12,4},{1,9},{5,13},{9,1},{13,5},{2,10},{6,14},... | collective-permute-start | bytes 12296 | tf_op jit(solution)/shard_map/ppermute | solution.py:560
  29.5 1.3 %collective-permute-start.8 = (bf16[16,2560]{1,0:T(8,128)(2,1)S(1)}, bf16[16,2560]{1,0:T(8,128)(2,1)S(1)}, u32[]{:S(2)}, u32[]{:S(2)}) collective-permute-start(bf16[16,2560]{1,0:T(8,128)(2,1)S(1)} %merge.1.mine_ref), channel_id=1, source_target_pairs={{0,1},{1,0},{2,3},{3,2},{4,5},{5,4},{6,7},{7,6},{8,9},{9,8},{10,11... | collective-permute-start | bytes 245768 | tf_op jit(solution)/shard_map/ppermute | solution.py:560

commit v6 on v5

--- a/solution.py
+++ b/solution.py
@@ -134,60 +134,66 @@
     return jnp.cos(angle), jnp.where(lane < HD // 2, -sine, sine)
 
 
-def attend(p, limit, cosine, sine, q_ref, k_ref, v_ref, out_ref, qrot_ref):
-    halves = [[], []]
-    for e in range(2):
-        for g in range(GROUP):
-            at = slice(((2 * p + e) * GROUP + g) * HD, ((2 * p + e) * GROUP + g + 1) * HD)
-            q = jnp.concatenate([q_ref[0, :, at].astype(F32), q_ref[1, :, at].astype(F32)], 0)
-            halves[e].append(rotated(q, cosine, sine))
-    if qrot_ref is not None:
-        for g in range(GROUP):
-            at = slice((p * GROUP + g) * HD, (p * GROUP + g + 1) * HD)
-            qrot_ref[:, at] = jnp.concatenate([halves[0][g], halves[1][g]], 0).astype(BF16)
-    mixed = [[exchanged(halves[e][g], halves[e][g + 4]) for g in range(4)] for e in range(2)]
+def attend(pairs, limit, cosine, sine, q_ref, k_ref, v_ref, out_ref, qrot_ref):
     zero = jnp.zeros((32, HD), F32)
-    numers, stats = [], []
+    scores = []
+    for p in pairs:
+        halves = [[], []]
+        for e in range(2):
+            for g in range(GROUP):
+                at = slice(((2 * p + e) * GROUP + g) * HD, ((2 * p + e) * GROUP + g + 1) * HD)
+                q = jnp.concatenate([q_ref[0, :, at].astype(F32), q_ref[1, :, at].astype(F32)], 0)
+                halves[e].append(rotated(q, cosine, sine))
+        if qrot_ref is not None:
+            for g in range(GROUP):
+                at = slice((p * GROUP + g) * HD, (p * GROUP + g + 1) * HD)
+                qrot_ref[:, at] = jnp.concatenate([halves[0][g], halves[1][g]], 0).astype(BF16)
+        mixed = [[exchanged(halves[e][g], halves[e][g + 4]) for g in range(4)] for e in range(2)]
+        for s in range(2):
+            rows = [jnp.concatenate([mixed[e][g][s] for g in range(4)], 0) for e in range(2)]
+            queries = jnp.concatenate(
+                [jnp.concatenate([rows[0], zero], 1), jnp.concatenate([zero, rows[1]], 1)], 0
+            ).astype(BF16)
+            keys = k_ref[s, :, 2 * p * HD : 2 * (p + 1) * HD]
+            score = lax.dot_general(queries, keys, NT, preferred_element_type=F32)
+            place = lax.broadcasted_iota(jnp.int32, score.shape, 1)
+            bound = limit[STEPS * s : STEPS * s + 1, :1].astype(jnp.int32)
+            scores.append(jnp.where(place < bound, score, MASKED_SCORE))
+    scores = jnp.concatenate(scores, 0)
+    top = rounded(jnp.maximum(jnp.max(scores, 1, keepdims=True), LOWEST_TOP))
+    weights = jnp.exp2((scores - top) * EXPONENT).astype(BF16)
+    total = jnp.sum(weights.astype(F32), 1, keepdims=True)
+    high = rounded(total)
+    columns = (top, high, total - high)
     lane8 = lax.broadcasted_iota(jnp.int32, (8, 128), 1)
-    pair = slice(2 * p * HD, 2 * (p + 1) * HD)
-    for s in range(2):
-        rows = [jnp.concatenate([mixed[e][g][s] for g in range(4)], 0) for e in range(2)]
-        queries = jnp.concatenate(
-            [jnp.concatenate([rows[0], zero], 1), jnp.concatenate([zero, rows[1]], 1)], 0
-        ).astype(BF16)
-        scores = lax.dot_general(queries, k_ref[s, :, pair], NT, preferred_element_type=F32)
-        place = lax.broadcasted_iota(jnp.int32, scores.shape, 1)
-        bound = limit[STEPS * s : STEPS * s + 1, :1].astype(jnp.int32)
-        masked = jnp.where(place < bound, scores, MASKED_SCORE)
-        top = rounded(jnp.maximum(jnp.max(masked, 1, keepdims=True), LOWEST_TOP))
-        weights = jnp.exp2((masked - top) * EXPONENT).astype(BF16)
-        total = jnp.sum(weights.astype(F32), 1, keepdims=True)
-        numers.append(jnp.dot(weights, v_ref[s, :, pair], preferred_element_type=F32))
-        high = rounded(total)
-        compact = []
+    numers = []
+    for i, p in enumerate(pairs):
+        for s in range(2):
+            at = slice(64 * (2 * i + s), 64 * (2 * i + s + 1))
+            values = v_ref[s, :, 2 * p * HD : 2 * (p + 1) * HD]
+            numers.append(jnp.dot(weights[at], values, preferred_element_type=F32))
+    for i, p in enumerate(pairs):
+        outs, ends = [[], []], []
         for e in range(2):
-            tile = jnp.zeros((8, 128), F32)
+            back, stats = [], []
+            for s in range(2):
+                tile = jnp.zeros((8, 128), F32)
+                for g in range(4):
+                    row = 64 * (2 * i + s) + 32 * e + 8 * g
+                    for slot, value in enumerate(columns):
+                        tile = jnp.where(lane8 == slot * GROUP + g, value[row : row + 8], tile)
+                stats.append(tile)
             for g in range(4):
                 at = slice(32 * e + 8 * g, 32 * e + 8 * g + 8)
-                for slot, value in enumerate((top, high, total - high)):
-                    tile = jnp.where(lane8 == slot * GROUP + g, value[at], tile)
-            compact.append(tile)
-        stats.append(compact)
-    outs, ends = [[], []], []
-    for e in range(2):
-        back = []
-        for g in range(4):
-            at = slice(32 * e + 8 * g, 32 * e + 8 * g + 8)
-            cols = slice(e * HD, (e + 1) * HD)
-            back.append(exchanged(numers[0][at, cols], numers[1][at, cols]))
-        outs[e] = [b[0] for b in back] + [b[1] for b in back]
-        a, b = exchanged(stats[0][e], stats[1][e])
-        ends.append(jnp.where(lane8 % 8 < 4, a, pltpu.roll(b, 4, 1)))
-    p = p % (out_ref.shape[1] // PAIR)
-    for g in range(GROUP):
-        at = slice(p * PAIR + g * HD, p * PAIR + (g + 1) * HD)
-        out_ref[:, at] = jnp.concatenate([outs[0][g], outs[1][g]], 0).astype(BF16)
-    out_ref[:, p * PAIR + GROUP * HD : (p + 1) * PAIR] = jnp.concatenate(ends, 0).astype(BF16)
+                cols = slice(e * HD, (e + 1) * HD)
+                back.append(exchanged(numers[2 * i][at, cols], numers[2 * i + 1][at, cols]))
+            outs[e] = [b[0] for b in back] + [b[1] for b in back]
+            a, b = exchanged(*stats)
+            ends.append(jnp.where(lane8 % 8 < 4, a, pltpu.roll(b, 4, 1)))
+        for g in range(GROUP):
+            at = slice(i * PAIR + g * HD, i * PAIR + (g + 1) * HD)
+            out_ref[:, at] = jnp.concatenate([outs[0][g], outs[1][g]], 0).astype(BF16)
+        out_ref[:, i * PAIR + GROUP * HD : (i + 1) * PAIR] = jnp.concatenate(ends, 0).astype(BF16)
 
 
 def pair_at(i):
@@ -257,11 +263,10 @@
         for ahead in later[i]:
             start(ahead)
         if i < 2:
-            for p in range(i * pairs // 2, (i + 1) * pairs // 2):
-                attend(
-                    p, limit, cosine, sine, q_ref, k_ref, v_ref,
-                    send_ref if i else keep_ref, None if i else qrot_ref,
-                )
+            attend(
+                range(i * pairs // 2, (i + 1) * pairs // 2), limit, cosine, sine,
+                q_ref, k_ref, v_ref, send_ref if i else keep_ref, None if i else qrot_ref,
+            )
         else:
             at = slice((i - 2) * CHUNK, (i - 1) * CHUNK)
             part = jnp.concatenate(
@@ -357,7 +362,10 @@
     return jnp.broadcast_to(tile[:, lane : lane + 1], tile.shape)
 
 
-def combine_part_kernel(base_ref, mine_ref, theirs_ref, _, out_ref):
+def combine_part_kernel(base_ref, mine_ref, theirs_ref, *refs):
+    (*passed, out_ref), through = refs[: len(refs) // 2 + 1], refs[len(refs) // 2 + 1 :]
+    for source, target in zip(passed, through):
+        target[...] = source[...]
     half = base_ref.shape[1] // 2
     own = base_ref[:, :half] + theirs_ref[:, :half].astype(F32)
     out_ref[:, :half] = own.astype(BF16)
@@ -365,18 +373,19 @@
     out_ref[:, half:] = split(sums[:8] + sums[8:])
 
 
-def combine_part(base, mine, theirs, earlier):
+def combine_part(base, mine, theirs, *passed):
+    shapes = [mine.shape] + [p.shape for p in passed]
     return pl.pallas_call(
         combine_part_kernel,
-        in_specs=[VMEM] * 4,
-        out_specs=VMEM,
-        out_shape=jax.ShapeDtypeStruct(mine.shape, BF16),
+        in_specs=[VMEM] * (3 + len(passed)),
+        out_specs=[VMEM] * len(shapes),
+        out_shape=[jax.ShapeDtypeStruct(shape, BF16) for shape in shapes],
         compiler_params=pltpu.CompilerParams(vmem_limit_bytes=32 * MEBI),
         name="combine_part",
-    )(base, mine, theirs, earlier)
-
-
-def combine_cache_kernel(a_ref, b_ref, out_ref):
+    )(base, mine, theirs, *passed)
+
+
+def combine_cache_kernel(a_ref, b_ref, _, out_ref):
     lane = lax.broadcasted_iota(jnp.int32, (16, 128), 1)
     for p in range(out_ref.shape[1] // PAIR):
         end = slice(p * PAIR + GROUP * HD, (p + 1) * PAIR)
@@ -402,15 +411,15 @@
     return pltpu.roll(stats, 128 - GROUP, 1) + pltpu.roll(stats, 128 - 2 * GROUP, 1)
 
 
-def combine_cache(a, b):
+def combine_cache(a, b, earlier):
     return pl.pallas_call(
         combine_cache_kernel,
-        in_specs=[VMEM] * 2,
+        in_specs=[VMEM] * 3,
         out_specs=VMEM,
         out_shape=jax.ShapeDtypeStruct(a.shape, BF16),
         compiler_params=pltpu.CompilerParams(vmem_limit_bytes=32 * MEBI),
         name="combine_cache",
-    )(a, b)
+    )(a, b, earlier)
 
 
 def answer_kernel(at, pa_ref, pb_ref, *outs):
@@ -592,7 +601,8 @@
     )
     received = to_tensor(send, 1)
     columns = key_up.shape[0] * 8 if paired else 0
-    part, *has = rank_products(rows, depth, columns, base, table, own, near, [tokens, *sent])
+    message, *has = rank_products(rows, depth, columns, base, table, own, near, [tokens, *sent])
+    part, own_ups = combine_part(base, message, to_tensor(message, 1), own_ups)
     if paired:
         places = [(s, t) for s in range(n_dp) for t in range(n_tensor)]
         perm = [
@@ -606,9 +616,8 @@
         ups = ups.reshape(2, 2, 16, 16, 128).transpose(0, 1, 3, 2, 4).reshape(2, 2, 16, -1)
         ups = lax.dynamic_index_in_dim(ups, lax.axis_index("tensor") % 2, 0, keepdims=False)
         ups = [ups[0], ups[1]]
-    part = combine_part(base, part, to_tensor(part, 1), ups[1])
     part_far = to_tensor(part, 2)
-    cache = combine_cache(keep, received)
+    cache = combine_cache(keep, received, message)
     cache_far = to_tensor(cache, 2)
     replies = answers(n, part, part_far)
     backs = [to_dp(reply, d) for reply, d in zip(replies, partners)]

time: 31.7 us -> 29.3 us (0.924)
  Pallas kernels: 11.2 us -> 9.95 us
  waiting for transfers between devices: 9.59 us -> 8.55 us
    pallas_call x1, Pallas kernels: 7.18 us -> 5.92 us  [local(): pl.pallas_call(local_kernel, in_specs=[HBM] * 6, out_specs=[VMEM] * 5, ou...]
    ppermute x1, waiting for transfers between devices: 0.9 us -> 0.01 us  [shards(): ups = [has[0], lax.ppermute(own_ups, ('dp', 'tensor'), perm)]]
  transfers between devices with their start and end apart: 9 -> 9, of which waited for: 6 -> 4; matrix products, arithmetic and copies ran while one was open for 0% -> 0% of each run, Pallas kernels for 25% -> 22%
where the time goes in v6:
time: 29.3 us; the launch traced here: 29.1 us
  Pallas kernels  9.95 us (34%)
  starting transfers between devices  9.92 us (34%)
  waiting for transfers between devices  8.55 us (29%)
  between operations  0.72 us (2%)
    ppermute x8, starting transfers between devices, swap(): return lax.ppermute(value, axis, [(i, i ^ distance) for i in range(n)])  9.4 us
    ppermute x8, waiting for transfers between devices, swap(): return lax.ppermute(value, axis, [(i, i ^ distance) for i in range(n)])  8.54 us
    pallas_call x1, Pallas kernels, local(): pl.pallas_call(local_kernel, in_specs=[HBM] * 6, out_specs=[VMEM] * 5, ou...  5.92 us
    pallas_call x1, Pallas kernels, pack(): pl.pallas_call(pack_kernel, in_specs=[HBM] * len(operands), out_specs=[VM...  1.92 us
    pallas_call x1, Pallas kernels, merge(): pl.pallas_call(functools.partial(merge_kernel, len(backs), paired, width_...  0.81 us
    pallas_call x1, Pallas kernels, place(): pl.pallas_call(place_kernel, in_specs=[VMEM] * 2, out_specs=[VMEM] * 3, o...  0.69 us
  transfers between devices with their start and end apart: 9, of which 4 were waited for; matrix products, arithmetic and copies ran while one was open for 0% of the time, Pallas kernels for 22%

profile of v6, /device:TPU:0, one launch (start us, length us, event | category | flops | bytes accessed | tf_op | source)
XLA Modules:
  0.0 29.1 jit_solution(2939253300039693984)
XLA Ops:
  0.6 1.9 %pack.1 = (bf16[16,4096]{1,0:T(8,128)(2,1)}, bf16[16,3328]{1,0:T(8,128)(2,1)}, bf16[16,2048]{1,0:T(8,128)(2,1)}) custom-call(s32[2]{0:T(128)} %refs_0_.1, bf16[2,4,2048]{2,1,0:T(4,128)(2,1)} %refs_1_.1, bf16[2048]{0:T(1024)(128)(2,1)} %refs_2_.1, f32[16,2048]{1,0:T(8,128)} %refs_3_.1, f32[16,2048]{1,0:T(8,128)} %refs_4_.1, f32[64,256]{1,0:T(8,128)} %bitcast.2, ...), custom_call_target="tpu_custom_call" | custom-call | tf_op jit(solution)/shard_map/pack/pallas_call | solution.py:105
  2.6 3.1 %collective-permute-start = (bf16[16,4096]{1,0:T(8,128)(2,1)}, bf16[16,4096]{1,0:T(8,128)(2,1)S(1)}, u32[]{:S(2)}, u32[]{:S(2)}) collective-permute-start(bf16[16,4096]{1,0:T(8,128)(2,1)} %get-tuple-element.19.refs_2_), channel_id=1, source_target_pairs={{0,4},{4,0},{8,12},{12,8},{1,5},{5,1},{9,13},{13,9},{2,6},{6,2},{1... | collective-permute-start | bytes 393224 | tf_op jit(solution)/shard_map/ppermute | solution.py:569
  5.7 2.6 %collective-permute-start.1 = (bf16[16,3328]{1,0:T(8,128)(2,1)}, bf16[16,3328]{1,0:T(8,128)(2,1)S(1)}, u32[]{:S(2)}, u32[]{:S(2)}) collective-permute-start(bf16[16,3328]{1,0:T(8,128)(2,1)} %get-tuple-element.15.x_hbm.refs_4_), channel_id=1, source_target_pairs={{0,8},{4,12},{8,0},{12,4},{1,9},{5,13},{9,1},{13,5},{2,10},{6,14},... | collective-permute-start | bytes 319496 | tf_op jit(solution)/shard_map/ppermute | solution.py:569
  8.2 5.9 %local.1 = (bf16[16,2304]{1,0:T(8,128)(2,1)S(1)}, bf16[16,2304]{1,0:T(8,128)(2,1)S(1)}, f32[16,1024]{1,0:T(8,128)S(1)}, bf16[16,2048]{1,0:T(8,128)(2,1)S(1)}, f32[24,128]{1,0:T(8,128)S(1)}) custom-call(bf16[16,3328]{1,0:T(8,128)(2,1)} %get-tuple-element.15.x_hbm.refs_4_, bf16[2,4,8192]{2,1,0:T(4,128)(2,1)} %q_hbm.1, bf16[2,512,1024]{2,1,0:T(8,128)(2,1)} %k_hbm.1, ...), custom_call_target="tpu_custom_call" | custom-call | flops 402653184 | bytes 12582912 | tf_op jit(solution)/shard_map/local/pallas_call | solution.py:290
  14.2 0.1 collective-permute-start.4
  14.3 0.0 collective-permute-done.1.refs_5_
  14.3 0.0 collective-permute-done.refs_3_
  14.3 0.4 %rank_products.1 = (bf16[16,896]{1,0:T(8,128)(2,1)S(1)}, bf16[16,2048]{1,0:T(8,128)(2,1)S(1)}) custom-call(f32[16,1024]{1,0:T(8,128)S(1)} %get-tuple-element.18.refs_0_.base_ref, f32[24,128]{1,0:T(8,128)S(1)} %get-tuple-element.16.refs_1_.refs_0_, bf16[16,4096]{1,0:T(8,128)(2,1)S(1)} %copy-done.1, bf16[16,4096]{1,0:T(8,128)(2,1)S(1)} %collective-permute-done.refs_3_, ...), custom_call_target="tpu_custom_call" | custom-call | tf_op jit(solution)/shard_map/rank_products/pallas_call | solution.py:351
  14.6 0.5 %collective-permute-start.2 = (bf16[16,896]{1,0:T(8,128)(2,1)S(1)}, bf16[16,896]{1,0:T(8,128)(2,1)S(1)}, u32[]{:S(2)}, u32[]{:S(2)}) collective-permute-start(bf16[16,896]{1,0:T(8,128)(2,1)S(1)} %get-tuple-element.20.mine_ref._), channel_id=1, source_target_pairs={{0,1},{1,0},{2,3},{3,2},{4,5},{5,4},{6,7},{7,6},{8,9},{9,8},{10,11... | collective-permute-start | bytes 86024 | tf_op jit(solution)/shard_map/ppermute | solution.py:569
  15.1 0.4 %collective-permute-done.4.b_ref = bf16[16,2304]{1,0:T(8,128)(2,1)S(1)} collective-permute-done((bf16[16,2304]{1,0:T(8,128)(2,1)S(1)}, bf16[16,2304]{1,0:T(8,128)(2,1)S(1)}, u32[]{:S(2)}, u32[]{:S(2)}) %collective-permute-start.4) | collective-permute-done | bytes 73760 | tf_op jit(solution)/shard_map/ppermute | solution.py:569
  15.5 0.2 combine_cache.1.refs_4_
  15.7 1.6 %collective-permute-start.5 = (bf16[16,2304]{1,0:T(8,128)(2,1)S(1)}, bf16[16,2304]{1,0:T(8,128)(2,1)S(1)}, u32[]{:S(2)}, u32[]{:S(2)}) collective-permute-start(bf16[16,2304]{1,0:T(8,128)(2,1)S(1)} %combine_cache.1.refs_4_), channel_id=1, source_target_pairs={{0,2},{1,3},{2,0},{3,1},{4,6},{5,7},{6,4},{7,5},{8,10},{9,11},{10,... | collective-permute-start | bytes 221192 | tf_op jit(solution)/shard_map/ppermute | solution.py:569
  17.3 0.0 collective-permute-done.2.theirs_ref
  17.3 0.5 %collective-permute-start.7 = (bf16[16,2048]{1,0:T(8,128)(2,1)S(1)}, bf16[16,2048]{1,0:T(8,128)(2,1)S(1)}, u32[]{:S(2)}, u32[]{:S(2)}) collective-permute-start(bf16[16,2048]{1,0:T(8,128)(2,1)S(1)} %get-tuple-element.26), channel_id=1, source_target_pairs={{0,4},{1,12},{2,6},{3,14},{4,0},{5,8},{6,2},{7,10},{8,5},{9,13},{1... | collective-permute-start | bytes 196616 | tf_op jit(solution)/shard_map/ppermute | solution.py:612
  17.8 0.5 %collective-permute-start.3 = (bf16[16,896]{1,0:T(8,128)(2,1)S(1)}, bf16[16,896]{1,0:T(8,128)(2,1)S(1)}, u32[]{:S(2)}, u32[]{:S(2)}) collective-permute-start(bf16[16,896]{1,0:T(8,128)(2,1)S(1)} %get-tuple-element.22.pa_ref.refs_2_), channel_id=1, source_target_pairs={{0,2},{1,3},{2,0},{3,1},{4,6},{5,7},{6,4},{7,5},{8,10},{9,11},{10,... | collective-permute-start | bytes 86024 | tf_op jit(solution)/shard_map/ppermute | solution.py:569
  18.4 3.3 %collective-permute-done.3.pb_ref.refs_3_ = bf16[16,896]{1,0:T(8,128)(2,1)S(1)} collective-permute-done((bf16[16,896]{1,0:T(8,128)(2,1)S(1)}, bf16[16,896]{1,0:T(8,128)(2,1)S(1)}, u32[]{:S(2)}, u32[]{:S(2)}) %collective-permute-start.3) | collective-permute-done | bytes 28704 | tf_op jit(solution)/shard_map/ppermute | solution.py:569
  21.7 1.0 %collective-permute-start.6 = (bf16[16,128]{1,0:T(8,128)(2,1)S(1)}, bf16[16,128]{1,0:T(8,128)(2,1)S(1)}, u32[]{:S(2)}, u32[]{:S(2)}) collective-permute-start(bf16[16,128]{1,0:T(8,128)(2,1)S(1)} %answers.1), channel_id=1, source_target_pairs={{0,8},{4,12},{8,0},{12,4},{1,9},{5,13},{9,1},{13,5},{2,10},{6,14},... | collective-permute-start | bytes 12296 | tf_op jit(solution)/shard_map/ppermute | solution.py:569
  22.7 3.6 %collective-permute-done.6.refs_6_ = bf16[16,128]{1,0:T(8,128)(2,1)S(1)} collective-permute-done((bf16[16,128]{1,0:T(8,128)(2,1)S(1)}, bf16[16,128]{1,0:T(8,128)(2,1)S(1)}, u32[]{:S(2)}, u32[]{:S(2)}) %collective-permute-start.6) | collective-permute-done | bytes 4128 | tf_op jit(solution)/shard_map/ppermute | solution.py:569
  26.3 0.0 collective-permute-done.5.refs_5_
  26.3 0.0 collective-permute-done.7.refs_8_
  26.3 0.8 %merge.1.mine_ref = bf16[16,2560]{1,0:T(8,128)(2,1)S(1)} custom-call(f32[24,128]{1,0:T(8,128)S(1)} %get-tuple-element.16.refs_1_.refs_0_, bf16[16,2048]{1,0:T(8,128)(2,1)S(1)} %get-tuple-element.17.refs_1_, bf16[16,896]{1,0:T(8,128)(2,1)S(1)} %get-tuple-element.22.pa_ref.refs_2_, bf16[16,896]{1,0:T(8,128)(2,1)S(1)} %collective-permute-done.3.pb_ref.refs_3_, ...), custom_call_target="tpu_custom_call" | custom-call | tf_op jit(solution)/shard_map/merge/pallas_call | solution.py:522
  27.1 0.1 collective-permute-start.8
  27.2 1.3 %collective-permute-done.8.theirs_ref = bf16[16,2560]{1,0:T(8,128)(2,1)S(1)} collective-permute-done((bf16[16,2560]{1,0:T(8,128)(2,1)S(1)}, bf16[16,2560]{1,0:T(8,128)(2,1)S(1)}, u32[]{:S(2)}, u32[]{:S(2)}) %collective-permute-start.8) | collective-permute-done | bytes 81952 | tf_op jit(solution)/shard_map/ppermute | solution.py:569
  28.5 0.7 %place.1 = (bf16[2,4,1024]{2,1,0:T(4,128)(2,1)}, bf16[2,4,1024]{2,1,0:T(4,128)(2,1)}, bf16[2,4,8192]{2,1,0:T(4,128)(2,1)}) custom-call(bf16[16,2560]{1,0:T(8,128)(2,1)S(1)} %merge.1.mine_ref, bf16[16,2560]{1,0:T(8,128)(2,1)S(1)} %collective-permute-done.8.theirs_ref), custom_call_target="tpu_custom_call" | custom-call | tf_op jit(solution)/shard_map/place/pallas_call | solution.py:554
  (8 shorter events, 0.0 us)
Async XLA Ops:
  2.6 11.7 %collective-permute-start = (bf16[16,4096]{1,0:T(8,128)(2,1)}, bf16[16,4096]{1,0:T(8,128)(2,1)S(1)}, u32[]{:S(2)}, u32[]{:S(2)}) collective-permute-start(bf16[16,4096]{1,0:T(8,128)(2,1)} %get-tuple-element.19.refs_2_), channel_id=1, source_target_pairs={{0,4},{4,0},{8,12},{12,8},{1,5},{5,1},{9,13},{13,9},{2,6},{6,2},{1... | collective-permute-start | bytes 393224 | tf_op jit(solution)/shard_map/ppermute | solution.py:569
  5.6 8.6 %copy-start = (bf16[16,3328]{1,0:T(8,128)(2,1)S(1)}, bf16[16,3328]{1,0:T(8,128)(2,1)}, u32[]{:S(2)}) copy-start(bf16[16,3328]{1,0:T(8,128)(2,1)} %get-tuple-element.15.x_hbm.refs_4_) | copy-start | bytes 319492
  5.6 8.6 %copy-start.1 = (bf16[16,4096]{1,0:T(8,128)(2,1)S(1)}, bf16[16,4096]{1,0:T(8,128)(2,1)}, u32[]{:S(2)}) copy-start(bf16[16,4096]{1,0:T(8,128)(2,1)} %get-tuple-element.19.refs_2_) | copy-start | bytes 393220
  5.7 11.6 %copy-start.2 = (bf16[16,2048]{1,0:T(8,128)(2,1)S(1)}, bf16[16,2048]{1,0:T(8,128)(2,1)}, u32[]{:S(2)}) copy-start(bf16[16,2048]{1,0:T(8,128)(2,1)} %get-tuple-element.21.refs_0_) | copy-start | bytes 196612
  5.7 8.6 %collective-permute-start.1 = (bf16[16,3328]{1,0:T(8,128)(2,1)}, bf16[16,3328]{1,0:T(8,128)(2,1)S(1)}, u32[]{:S(2)}, u32[]{:S(2)}) collective-permute-start(bf16[16,3328]{1,0:T(8,128)(2,1)} %get-tuple-element.15.x_hbm.refs_4_), channel_id=1, source_target_pairs={{0,8},{4,12},{8,0},{12,4},{1,9},{5,13},{9,1},{13,5},{2,10},{6,14},... | collective-permute-start | bytes 319496 | tf_op jit(solution)/shard_map/ppermute | solution.py:569
  14.2 1.3 %collective-permute-start.4 = (bf16[16,2304]{1,0:T(8,128)(2,1)S(1)}, bf16[16,2304]{1,0:T(8,128)(2,1)S(1)}, u32[]{:S(2)}, u32[]{:S(2)}) collective-permute-start(bf16[16,2304]{1,0:T(8,128)(2,1)S(1)} %get-tuple-element.24), channel_id=1, source_target_pairs={{0,1},{1,0},{2,3},{3,2},{4,5},{5,4},{6,7},{7,6},{8,9},{9,8},{10,11... | collective-permute-start | bytes 221192 | tf_op jit(solution)/shard_map/ppermute | solution.py:569
  14.6 2.6 %collective-permute-start.2 = (bf16[16,896]{1,0:T(8,128)(2,1)S(1)}, bf16[16,896]{1,0:T(8,128)(2,1)S(1)}, u32[]{:S(2)}, u32[]{:S(2)}) collective-permute-start(bf16[16,896]{1,0:T(8,128)(2,1)S(1)} %get-tuple-element.20.mine_ref._), channel_id=1, source_target_pairs={{0,1},{1,0},{2,3},{3,2},{4,5},{5,4},{6,7},{7,6},{8,9},{9,8},{10,11... | collective-permute-start | bytes 86024 | tf_op jit(solution)/shard_map/ppermute | solution.py:569
  15.7 10.6 %collective-permute-start.5 = (bf16[16,2304]{1,0:T(8,128)(2,1)S(1)}, bf16[16,2304]{1,0:T(8,128)(2,1)S(1)}, u32[]{:S(2)}, u32[]{:S(2)}) collective-permute-start(bf16[16,2304]{1,0:T(8,128)(2,1)S(1)} %combine_cache.1.refs_4_), channel_id=1, source_target_pairs={{0,2},{1,3},{2,0},{3,1},{4,6},{5,7},{6,4},{7,5},{8,10},{9,11},{10,... | collective-permute-start | bytes 221192 | tf_op jit(solution)/shard_map/ppermute | solution.py:569
  17.3 9.0 %collective-permute-start.7 = (bf16[16,2048]{1,0:T(8,128)(2,1)S(1)}, bf16[16,2048]{1,0:T(8,128)(2,1)S(1)}, u32[]{:S(2)}, u32[]{:S(2)}) collective-permute-start(bf16[16,2048]{1,0:T(8,128)(2,1)S(1)} %get-tuple-element.26), channel_id=1, source_target_pairs={{0,4},{1,12},{2,6},{3,14},{4,0},{5,8},{6,2},{7,10},{8,5},{9,13},{1... | collective-permute-start | bytes 196616 | tf_op jit(solution)/shard_map/ppermute | solution.py:612
  17.8 3.9 %collective-permute-start.3 = (bf16[16,896]{1,0:T(8,128)(2,1)S(1)}, bf16[16,896]{1,0:T(8,128)(2,1)S(1)}, u32[]{:S(2)}, u32[]{:S(2)}) collective-permute-start(bf16[16,896]{1,0:T(8,128)(2,1)S(1)} %get-tuple-element.22.pa_ref.refs_2_), channel_id=1, source_target_pairs={{0,2},{1,3},{2,0},{3,1},{4,6},{5,7},{6,4},{7,5},{8,10},{9,11},{10,... | collective-permute-start | bytes 86024 | tf_op jit(solution)/shard_map/ppermute | solution.py:569
  21.7 4.6 %collective-permute-start.6 = (bf16[16,128]{1,0:T(8,128)(2,1)S(1)}, bf16[16,128]{1,0:T(8,128)(2,1)S(1)}, u32[]{:S(2)}, u32[]{:S(2)}) collective-permute-start(bf16[16,128]{1,0:T(8,128)(2,1)S(1)} %answers.1), channel_id=1, source_target_pairs={{0,8},{4,12},{8,0},{12,4},{1,9},{5,13},{9,1},{13,5},{2,10},{6,14},... | collective-permute-start | bytes 12296 | tf_op jit(solution)/shard_map/ppermute | solution.py:569
  27.1 1.3 %collective-permute-start.8 = (bf16[16,2560]{1,0:T(8,128)(2,1)S(1)}, bf16[16,2560]{1,0:T(8,128)(2,1)S(1)}, u32[]{:S(2)}, u32[]{:S(2)}) collective-permute-start(bf16[16,2560]{1,0:T(8,128)(2,1)S(1)} %merge.1.mine_ref), channel_id=1, source_target_pairs={{0,1},{1,0},{2,3},{3,2},{4,5},{5,4},{6,7},{7,6},{8,9},{9,8},{10,11... | collective-permute-start | bytes 245768 | tf_op jit(solution)/shard_map/ppermute | solution.py:569

commit v7 on v6

--- a/solution.py
+++ b/solution.py
@@ -65,7 +65,7 @@
 
 
 def pack_kernel(*refs):
-    sources, (a_ref, b_ref, up_ref), held, sems = refs[:7], refs[7:10], refs[10:17], refs[17]
+    sources, (a_ref, b_ref), held, sems = refs[:7], refs[7:9], refs[9:16], refs[16]
     copies = [
         pltpu.make_async_copy(source, target, sems.at[i])
         for i, (source, target) in enumerate(zip(sources, held))
@@ -89,7 +89,6 @@
     b_ref[:, depth // 2 + 128 : depth // 2 + 256] = split(squares)
     ups = jnp.concatenate([ku_ref[...], vu_ref[...]], 0).T.astype(BF16)
     b_ref[:, depth // 2 + 256 :] = flat(ups)
-    up_ref[...] = flat(ups)
     own = kd_ref.shape[0]
     for slot, ref in enumerate((kd_ref, vd_ref)):
         down = ref[...]
@@ -105,11 +104,10 @@
     return pl.pallas_call(
         pack_kernel,
         in_specs=[HBM] * len(operands),
-        out_specs=[VMEM] * 3,
+        out_specs=[VMEM] * 2,
         out_shape=[
             jax.ShapeDtypeStruct((16, 2 * depth), BF16),
             jax.ShapeDtypeStruct((16, depth // 2 + 256 + ups), BF16),
-            jax.ShapeDtypeStruct((16, ups), BF16),
         ],
         scratch_shapes=[pltpu.SMEM(lengths.shape, jnp.int32)]
         + [pltpu.VMEM(o.shape, o.dtype) for o in operands[1:]]
@@ -235,12 +233,12 @@
                 for i, (source, target) in enumerate(((wk_hbm, wk_ref), (wv_hbm, wv_ref)))
             ]
         )
-    steps = groups + weights
+    steps = [groups[0], groups[1] + weights[0], *weights[1:]]
     later = [[] for _ in steps]
-    later[0] = weights[:1]
-    later[1] = weights[1:3]
-    for c in range(3, chunks):
-        later[c - 1].append(weights[c])
+    later[0] = weights[1:2]
+    later[1] = weights[2:4]
+    for c in range(4, chunks):
+        later[c - 2].append(weights[c])
 
     def start(copies):
         for copy in copies:
@@ -248,6 +246,7 @@
 
     start(groups[0])
     start(groups[1])
+    start(weights[0])
     x_copy.wait()
     half = wk_hbm.shape[0] // 2
     x = x_ref[:, :half].astype(F32)
@@ -262,13 +261,8 @@
             copy.wait()
         for ahead in later[i]:
             start(ahead)
-        if i < 2:
-            attend(
-                range(i * pairs // 2, (i + 1) * pairs // 2), limit, cosine, sine,
-                q_ref, k_ref, v_ref, send_ref if i else keep_ref, None if i else qrot_ref,
-            )
-        else:
-            at = slice((i - 2) * CHUNK, (i - 1) * CHUNK)
+        if i >= 1:
+            at = slice((i - 1) * CHUNK, i * CHUNK)
             part = jnp.concatenate(
                 [
                     jnp.dot(x[:, at], ref[at], preferred_element_type=F32)
@@ -277,6 +271,11 @@
                 0,
             )
             total = part if total is None else total + part
+        if i < 2:
+            attend(
+                range(i * pairs // 2, (i + 1) * pairs // 2), limit, cosine, sine,
+                q_ref, k_ref, v_ref, send_ref if i else keep_ref, None if i else qrot_ref,
+            )
     lower, upper = total[:, : width // 2], total[:, width // 2 :]
     base_ref[:, : width // 2] = jnp.where(core == 0, lower, upper)
     base_ref[:, width // 2 :] = jnp.where(core == 0, upper, lower)
@@ -362,21 +361,25 @@
     return jnp.broadcast_to(tile[:, lane : lane + 1], tile.shape)
 
 
-def combine_part_kernel(base_ref, mine_ref, theirs_ref, *refs):
-    (*passed, out_ref), through = refs[: len(refs) // 2 + 1], refs[len(refs) // 2 + 1 :]
-    for source, target in zip(passed, through):
-        target[...] = source[...]
+def combine_part_kernel(n, base_ref, mine_ref, theirs_ref, *refs):
+    passed, refs = refs[: (len(refs) - n) // 2], refs[(len(refs) - n) // 2 :]
+    out_ref, replies, through = refs[0], refs[1:n], refs[n:]
     half = base_ref.shape[1] // 2
     own = base_ref[:, :half] + theirs_ref[:, :half].astype(F32)
     out_ref[:, :half] = own.astype(BF16)
     sums = mine_ref[:, half:].astype(F32) + theirs_ref[:, half:].astype(F32)
-    out_ref[:, half:] = split(sums[:8] + sums[8:])
-
-
-def combine_part(base, mine, theirs, *passed):
-    shapes = [mine.shape] + [p.shape for p in passed]
+    sums = split(sums[:8] + sums[8:])
+    out_ref[:, half:] = sums[:, :256]
+    for i, ref in enumerate(replies):
+        ref[...] = sums[:, 128 * (i + 2) : 128 * (i + 3)]
+    for source, target in zip(passed, through):
+        target[...] = source[...]
+
+
+def combine_part(n, base, mine, theirs, passed):
+    shapes = [(16, base.shape[1] // 2 + 256)] + [(16, 128)] * (n - 1) + [p.shape for p in passed]
     return pl.pallas_call(
-        combine_part_kernel,
+        functools.partial(combine_part_kernel, n),
         in_specs=[VMEM] * (3 + len(passed)),
         out_specs=[VMEM] * len(shapes),
         out_shape=[jax.ShapeDtypeStruct(shape, BF16) for shape in shapes],
@@ -420,25 +423,6 @@
         compiler_params=pltpu.CompilerParams(vmem_limit_bytes=32 * MEBI),
         name="combine_cache",
     )(a, b, earlier)
-
-
-def answer_kernel(at, pa_ref, pb_ref, *outs):
-    z = pa_ref[:, at:].astype(F32) + pb_ref[:, at:].astype(F32)
-    for i, ref in enumerate(outs):
-        part = z[:, 128 * (i + 1) : 128 * (i + 2)]
-        ref[...] = split(part[:8] + part[8:])
-
-
-def answers(n, part_a, part_b):
-    at = part_a.shape[1] - 128 * (n + 1)
-    return pl.pallas_call(
-        functools.partial(answer_kernel, at),
-        in_specs=[VMEM] * 2,
-        out_specs=[VMEM] * n,
-        out_shape=[jax.ShapeDtypeStruct((16, 128), BF16)] * n,
-        compiler_params=pltpu.CompilerParams(vmem_limit_bytes=32 * MEBI),
-        name="answers",
-    )(part_a, part_b)
 
 
 def merge_kernel(n, paired, width_all, *refs):
@@ -593,7 +577,7 @@
     n = len(partners)
     paired = n_dp == 4
 
-    own, tokens, own_ups = pack(lengths, hidden, norm_gain, key_down, value_down, key_up, value_up)
+    own, tokens = pack(lengths, hidden, norm_gain, key_down, value_down, key_up, value_up)
     near = to_dp(own, 1)
     sent = [to_dp(tokens, d) for d in partners]
     keep, send, base, qrot, table = local(
@@ -602,25 +586,25 @@
     received = to_tensor(send, 1)
     columns = key_up.shape[0] * 8 if paired else 0
     message, *has = rank_products(rows, depth, columns, base, table, own, near, [tokens, *sent])
-    part, own_ups = combine_part(base, message, to_tensor(message, 1), own_ups)
+    part, *rest = combine_part(n + 1, base, message, to_tensor(message, 1), has)
+    replies, has = rest[:n], rest[n:]
     if paired:
-        places = [(s, t) for s in range(n_dp) for t in range(n_tensor)]
-        perm = [
-            (s * n_tensor + t, (s ^ 1) * n_tensor + t if t % 2 == s // 2 else (s ^ 3) * n_tensor + (t ^ 1))
-            for s, t in places
-        ]
-        ups = [has[0], lax.ppermute(own_ups, ("dp", "tensor"), perm)]
+        ups = [has[0], to_dp(has[0], 1)]
     else:
-        ups = lax.all_gather(own_ups, "dp")
+        ups = lax.all_gather(tokens[:, depth // 2 + 256 :], "dp")
         ups = ups.reshape(n_dp, 16, -1, 128).transpose(0, 2, 1, 3)
         ups = ups.reshape(2, 2, 16, 16, 128).transpose(0, 1, 3, 2, 4).reshape(2, 2, 16, -1)
         ups = lax.dynamic_index_in_dim(ups, lax.axis_index("tensor") % 2, 0, keepdims=False)
         ups = [ups[0], ups[1]]
-    part_far = to_tensor(part, 2)
     cache = combine_cache(keep, received, message)
     cache_far = to_tensor(cache, 2)
-    replies = answers(n, part, part_far)
-    backs = [to_dp(reply, d) for reply, d in zip(replies, partners)]
+    part_far = to_tensor(part, 2)
+    places = [(s, t) for s in range(n_dp) for t in range(n_tensor)]
+    backs = []
+    for reply, d in zip(replies, partners):
+        for e in (0, 2):
+            perm = [(s * n_tensor + t, (s ^ d) * n_tensor + (t ^ e)) for s, t in places]
+            backs.append(lax.ppermute(reply, ("dp", "tensor"), perm))
     merged = merge(
         paired,
         float(depth * n_tensor),

time: 29.3 us -> 27.8 us (0.949)
  waiting for transfers between devices: 8.55 us -> 4.33 us
  starting transfers between devices: 9.92 us -> 12.8 us
    ppermute x8, waiting for transfers between devices: 8.54 us -> 1.65 us  [swap(): return lax.ppermute(value, axis, [(i, i ^ distance) for i in range(n)])]
    ppermute x1 -> x2, starting transfers between devices: 0.51 us -> 3.85 us  [shards(): backs.append(lax.ppermute(reply, ('dp', 'tensor'), perm))]
    ppermute x1 -> x2, waiting for transfers between devices: 0.01 us -> 2.68 us  [shards(): backs.append(lax.ppermute(reply, ('dp', 'tensor'), perm))]
    ppermute x8, starting transfers between devices: 9.4 us -> 8.91 us  [swap(): return lax.ppermute(value, axis, [(i, i ^ distance) for i in range(n)])]
  transfers between devices with their start and end apart: 9 -> 10, of which waited for: 4 -> 4; matrix products, arithmetic and copies ran while one was open for 0% -> 0% of each run, Pallas kernels for 22% -> 23%
where the time goes in v7:
time: 27.8 us; the launch traced here: 27.7 us
  starting transfers between devices  12.8 us (46%)
  Pallas kernels  9.86 us (35%)
  waiting for transfers between devices  4.33 us (16%)
  between operations  0.72 us (3%)
    ppermute x8, starting transfers between devices, swap(): return lax.ppermute(value, axis, [(i, i ^ distance) for i in range(n)])  8.91 us
    pallas_call x1, Pallas kernels, local(): pl.pallas_call(local_kernel, in_specs=[HBM] * 6, out_specs=[VMEM] * 5, ou...  5.87 us
    ppermute x2, starting transfers between devices, shards(): backs.append(lax.ppermute(reply, ('dp', 'tensor'), perm))  3.85 us
    ppermute x2, waiting for transfers between devices, shards(): backs.append(lax.ppermute(reply, ('dp', 'tensor'), perm))  2.68 us
    pallas_call x1, Pallas kernels, pack(): pl.pallas_call(pack_kernel, in_specs=[HBM] * len(operands), out_specs=[VM...  1.9 us
    ppermute x8, waiting for transfers between devices, swap(): return lax.ppermute(value, axis, [(i, i ^ distance) for i in range(n)])  1.65 us
    pallas_call x1, Pallas kernels, merge(): pl.pallas_call(functools.partial(merge_kernel, len(backs), paired, width_...  0.81 us
    pallas_call x1, Pallas kernels, place(): pl.pallas_call(place_kernel, in_specs=[VMEM] * 2, out_specs=[VMEM] * 3, o...  0.69 us
  transfers between devices with their start and end apart: 10, of which 4 were waited for; matrix products, arithmetic and copies ran while one was open for 0% of the time, Pallas kernels for 23%

profile of v7, /device:TPU:0, one launch (start us, length us, event | category | flops | bytes accessed | tf_op | source)
XLA Modules:
  0.0 27.7 jit_solution(1855449716956670839)
XLA Ops:
  0.6 1.9 %pack.1 = (bf16[16,4096]{1,0:T(8,128)(2,1)}, bf16[16,3328]{1,0:T(8,128)(2,1)}) custom-call(s32[2]{0:T(128)} %refs_0_.1, bf16[2,4,2048]{2,1,0:T(4,128)(2,1)} %refs_1_.1, bf16[2048]{0:T(1024)(128)(2,1)} %refs_2_.1, f32[16,2048]{1,0:T(8,128)} %refs_3_.1, f32[16,2048]{1,0:T(8,128)} %refs_4_.1, f32[64,256]{1,0:T(8,128)} %bitcast.2, f32[64,256]{1,0:T(8,128)} %bitcast.3), custom_call_target="tpu_custom_call" | custom-call | tf_op jit(solution)/shard_map/pack/pallas_call | solution.py:104
  2.5 3.1 %collective-permute-start = (bf16[16,4096]{1,0:T(8,128)(2,1)}, bf16[16,4096]{1,0:T(8,128)(2,1)S(1)}, u32[]{:S(2)}, u32[]{:S(2)}) collective-permute-start(bf16[16,4096]{1,0:T(8,128)(2,1)} %get-tuple-element.19.refs_2_), channel_id=1, source_target_pairs={{0,4},{4,0},{8,12},{12,8},{1,5},{5,1},{9,13},{13,9},{2,6},{6,2},{1... | collective-permute-start | bytes 393224 | tf_op jit(solution)/shard_map/ppermute | solution.py:553
  5.6 2.6 %collective-permute-start.1 = (bf16[16,3328]{1,0:T(8,128)(2,1)}, bf16[16,3328]{1,0:T(8,128)(2,1)S(1)}, u32[]{:S(2)}, u32[]{:S(2)}) collective-permute-start(bf16[16,3328]{1,0:T(8,128)(2,1)} %get-tuple-element.15.x_hbm.refs_4_), channel_id=1, source_target_pairs={{0,8},{4,12},{8,0},{12,4},{1,9},{5,13},{9,1},{13,5},{2,10},{6,14},... | collective-permute-start | bytes 319496 | tf_op jit(solution)/shard_map/ppermute | solution.py:553
  8.2 5.9 %local.1 = (bf16[16,2304]{1,0:T(8,128)(2,1)S(1)}, bf16[16,2304]{1,0:T(8,128)(2,1)S(1)}, f32[16,1024]{1,0:T(8,128)S(1)}, bf16[16,2048]{1,0:T(8,128)(2,1)S(1)}, f32[24,128]{1,0:T(8,128)S(1)}) custom-call(bf16[16,3328]{1,0:T(8,128)(2,1)} %get-tuple-element.15.x_hbm.refs_4_, bf16[2,4,8192]{2,1,0:T(4,128)(2,1)} %q_hbm.1, bf16[2,512,1024]{2,1,0:T(8,128)(2,1)} %k_hbm.1, ...), custom_call_target="tpu_custom_call" | custom-call | flops 402653184 | bytes 12582912 | tf_op jit(solution)/shard_map/local/pallas_call | solution.py:289
  14.1 0.1 collective-permute-start.4
  14.2 0.0 collective-permute-done.1.refs_5_
  14.2 0.4 %rank_products.1 = (bf16[16,896]{1,0:T(8,128)(2,1)S(1)}, bf16[16,2048]{1,0:T(8,128)(2,1)S(1)}) custom-call(f32[16,1024]{1,0:T(8,128)S(1)} %get-tuple-element.18.refs_0_.base_ref, f32[24,128]{1,0:T(8,128)S(1)} %get-tuple-element.16.refs_1_.refs_0_, bf16[16,4096]{1,0:T(8,128)(2,1)S(1)} %copy-done.1, bf16[16,4096]{1,0:T(8,128)(2,1)S(1)} %collective-permute-done.refs_3_, ...), custom_call_target="tpu_custom_call" | custom-call | tf_op jit(solution)/shard_map/rank_products/pallas_call | solution.py:350
  14.6 0.5 %collective-permute-start.2 = (bf16[16,896]{1,0:T(8,128)(2,1)S(1)}, bf16[16,896]{1,0:T(8,128)(2,1)S(1)}, u32[]{:S(2)}, u32[]{:S(2)}) collective-permute-start(bf16[16,896]{1,0:T(8,128)(2,1)S(1)} %get-tuple-element.20.mine_ref._), channel_id=1, source_target_pairs={{0,1},{1,0},{2,3},{3,2},{4,5},{5,4},{6,7},{7,6},{8,9},{9,8},{10,11... | collective-permute-start | bytes 86024 | tf_op jit(solution)/shard_map/ppermute | solution.py:553
  15.1 0.4 %collective-permute-done.4.b_ref = bf16[16,2304]{1,0:T(8,128)(2,1)S(1)} collective-permute-done((bf16[16,2304]{1,0:T(8,128)(2,1)S(1)}, bf16[16,2304]{1,0:T(8,128)(2,1)S(1)}, u32[]{:S(2)}, u32[]{:S(2)}) %collective-permute-start.4) | collective-permute-done | bytes 73760 | tf_op jit(solution)/shard_map/ppermute | solution.py:553
  15.4 0.2 combine_cache.1.refs_4_
  15.7 1.6 %collective-permute-start.5 = (bf16[16,2304]{1,0:T(8,128)(2,1)S(1)}, bf16[16,2304]{1,0:T(8,128)(2,1)S(1)}, u32[]{:S(2)}, u32[]{:S(2)}) collective-permute-start(bf16[16,2304]{1,0:T(8,128)(2,1)S(1)} %combine_cache.1.refs_4_), channel_id=1, source_target_pairs={{0,2},{1,3},{2,0},{3,1},{4,6},{5,7},{6,4},{7,5},{8,10},{9,11},{10,... | collective-permute-start | bytes 221192 | tf_op jit(solution)/shard_map/ppermute | solution.py:553
  17.2 0.0 collective-permute-done.2.theirs_ref
  17.2 0.5 %collective-permute-start.8 = (bf16[16,2048]{1,0:T(8,128)(2,1)S(1)}, bf16[16,2048]{1,0:T(8,128)(2,1)S(1)}, u32[]{:S(2)}, u32[]{:S(2)}) collective-permute-start(bf16[16,2048]{1,0:T(8,128)(2,1)S(1)} %get-tuple-element.26.refs_8_), channel_id=1, source_target_pairs={{0,4},{4,0},{8,12},{12,8},{1,5},{5,1},{9,13},{13,9},{2,6},{6,2},{1... | collective-permute-start | bytes 196616 | tf_op jit(solution)/shard_map/ppermute | solution.py:553
  17.8 0.5 %collective-permute-start.3 = (bf16[16,768]{1,0:T(8,128)(2,1)S(1)}, bf16[16,768]{1,0:T(8,128)(2,1)S(1)}, u32[]{:S(2)}, u32[]{:S(2)}) collective-permute-start(bf16[16,768]{1,0:T(8,128)(2,1)S(1)} %get-tuple-element.22.refs_2_), channel_id=1, source_target_pairs={{0,2},{1,3},{2,0},{3,1},{4,6},{5,7},{6,4},{7,5},{8,10},{9,11},{10,... | collective-permute-start | bytes 73736 | tf_op jit(solution)/shard_map/ppermute | solution.py:553
  18.3 2.0 %collective-permute-start.7 = (bf16[16,128]{1,0:T(8,128)(2,1)S(1)}, bf16[16,128]{1,0:T(8,128)(2,1)S(1)}, u32[]{:S(2)}, u32[]{:S(2)}) collective-permute-start(bf16[16,128]{1,0:T(8,128)(2,1)S(1)} %get-tuple-element.25), channel_id=1, source_target_pairs={{0,10},{1,11},{2,8},{3,9},{4,14},{5,15},{6,12},{7,13},{8,2},{9,3},... | collective-permute-start | bytes 12296 | tf_op jit(solution)/shard_map/ppermute | solution.py:607
  20.3 1.8 %collective-permute-start.6 = (bf16[16,128]{1,0:T(8,128)(2,1)S(1)}, bf16[16,128]{1,0:T(8,128)(2,1)S(1)}, u32[]{:S(2)}, u32[]{:S(2)}) collective-permute-start(bf16[16,128]{1,0:T(8,128)(2,1)S(1)} %get-tuple-element.25), channel_id=1, source_target_pairs={{0,8},{1,9},{2,10},{3,11},{4,12},{5,13},{6,14},{7,15},{8,0},{9,1},... | collective-permute-start | bytes 12296 | tf_op jit(solution)/shard_map/ppermute | solution.py:607
  22.1 1.6 %collective-permute-done.7.refs_7_ = bf16[16,128]{1,0:T(8,128)(2,1)S(1)} collective-permute-done((bf16[16,128]{1,0:T(8,128)(2,1)S(1)}, bf16[16,128]{1,0:T(8,128)(2,1)S(1)}, u32[]{:S(2)}, u32[]{:S(2)}) %collective-permute-start.7) | collective-permute-done | bytes 4128 | tf_op jit(solution)/shard_map/ppermute | solution.py:607
  23.7 1.1 %collective-permute-done.6.refs_6_ = bf16[16,128]{1,0:T(8,128)(2,1)S(1)} collective-permute-done((bf16[16,128]{1,0:T(8,128)(2,1)S(1)}, bf16[16,128]{1,0:T(8,128)(2,1)S(1)}, u32[]{:S(2)}, u32[]{:S(2)}) %collective-permute-start.6) | collective-permute-done | bytes 4128 | tf_op jit(solution)/shard_map/ppermute | solution.py:607
  24.8 0.0 collective-permute-done.5.refs_5_
  24.8 0.0 collective-permute-done.8.refs_9_
  24.8 0.8 %merge.1.mine_ref = bf16[16,2560]{1,0:T(8,128)(2,1)S(1)} custom-call(f32[24,128]{1,0:T(8,128)S(1)} %get-tuple-element.16.refs_1_.refs_0_, bf16[16,2048]{1,0:T(8,128)(2,1)S(1)} %get-tuple-element.17.refs_1_, bf16[16,768]{1,0:T(8,128)(2,1)S(1)} %get-tuple-element.22.refs_2_, bf16[16,768]{1,0:T(8,128)(2,1)S(1)} %collective-permute-done.3.refs_3_, ...), custom_call_target="tpu_custom_call" | custom-call | tf_op jit(solution)/shard_map/merge/pallas_call | solution.py:506
  25.6 0.1 collective-permute-start.9
  25.7 1.3 %collective-permute-done.9.theirs_ref = bf16[16,2560]{1,0:T(8,128)(2,1)S(1)} collective-permute-done((bf16[16,2560]{1,0:T(8,128)(2,1)S(1)}, bf16[16,2560]{1,0:T(8,128)(2,1)S(1)}, u32[]{:S(2)}, u32[]{:S(2)}) %collective-permute-start.9) | collective-permute-done | bytes 81952 | tf_op jit(solution)/shard_map/ppermute | solution.py:553
  27.0 0.7 %place.1 = (bf16[2,4,1024]{2,1,0:T(4,128)(2,1)}, bf16[2,4,1024]{2,1,0:T(4,128)(2,1)}, bf16[2,4,8192]{2,1,0:T(4,128)(2,1)}) custom-call(bf16[16,2560]{1,0:T(8,128)(2,1)S(1)} %merge.1.mine_ref, bf16[16,2560]{1,0:T(8,128)(2,1)S(1)} %collective-permute-done.9.theirs_ref), custom_call_target="tpu_custom_call" | custom-call | tf_op jit(solution)/shard_map/place/pallas_call | solution.py:538
  (7 shorter events, 0.0 us)
Async XLA Ops:
  2.5 11.7 %collective-permute-start = (bf16[16,4096]{1,0:T(8,128)(2,1)}, bf16[16,4096]{1,0:T(8,128)(2,1)S(1)}, u32[]{:S(2)}, u32[]{:S(2)}) collective-permute-start(bf16[16,4096]{1,0:T(8,128)(2,1)} %get-tuple-element.19.refs_2_), channel_id=1, source_target_pairs={{0,4},{4,0},{8,12},{12,8},{1,5},{5,1},{9,13},{13,9},{2,6},{6,2},{1... | collective-permute-start | bytes 393224 | tf_op jit(solution)/shard_map/ppermute | solution.py:553
  5.6 8.6 %copy-start = (bf16[16,3328]{1,0:T(8,128)(2,1)S(1)}, bf16[16,3328]{1,0:T(8,128)(2,1)}, u32[]{:S(2)}) copy-start(bf16[16,3328]{1,0:T(8,128)(2,1)} %get-tuple-element.15.x_hbm.refs_4_) | copy-start | bytes 319492
  5.6 8.6 %copy-start.1 = (bf16[16,4096]{1,0:T(8,128)(2,1)S(1)}, bf16[16,4096]{1,0:T(8,128)(2,1)}, u32[]{:S(2)}) copy-start(bf16[16,4096]{1,0:T(8,128)(2,1)} %get-tuple-element.19.refs_2_) | copy-start | bytes 393220
  5.6 8.5 %collective-permute-start.1 = (bf16[16,3328]{1,0:T(8,128)(2,1)}, bf16[16,3328]{1,0:T(8,128)(2,1)S(1)}, u32[]{:S(2)}, u32[]{:S(2)}) collective-permute-start(bf16[16,3328]{1,0:T(8,128)(2,1)} %get-tuple-element.15.x_hbm.refs_4_), channel_id=1, source_target_pairs={{0,8},{4,12},{8,0},{12,4},{1,9},{5,13},{9,1},{13,5},{2,10},{6,14},... | collective-permute-start | bytes 319496 | tf_op jit(solution)/shard_map/ppermute | solution.py:553
  14.1 1.3 %collective-permute-start.4 = (bf16[16,2304]{1,0:T(8,128)(2,1)S(1)}, bf16[16,2304]{1,0:T(8,128)(2,1)S(1)}, u32[]{:S(2)}, u32[]{:S(2)}) collective-permute-start(bf16[16,2304]{1,0:T(8,128)(2,1)S(1)} %get-tuple-element.24), channel_id=1, source_target_pairs={{0,1},{1,0},{2,3},{3,2},{4,5},{5,4},{6,7},{7,6},{8,9},{9,8},{10,11... | collective-permute-start | bytes 221192 | tf_op jit(solution)/shard_map/ppermute | solution.py:553
  14.6 2.6 %collective-permute-start.2 = (bf16[16,896]{1,0:T(8,128)(2,1)S(1)}, bf16[16,896]{1,0:T(8,128)(2,1)S(1)}, u32[]{:S(2)}, u32[]{:S(2)}) collective-permute-start(bf16[16,896]{1,0:T(8,128)(2,1)S(1)} %get-tuple-element.20.mine_ref._), channel_id=1, source_target_pairs={{0,1},{1,0},{2,3},{3,2},{4,5},{5,4},{6,7},{7,6},{8,9},{9,8},{10,11... | collective-permute-start | bytes 86024 | tf_op jit(solution)/shard_map/ppermute | solution.py:553
  15.7 9.2 %collective-permute-start.5 = (bf16[16,2304]{1,0:T(8,128)(2,1)S(1)}, bf16[16,2304]{1,0:T(8,128)(2,1)S(1)}, u32[]{:S(2)}, u32[]{:S(2)}) collective-permute-start(bf16[16,2304]{1,0:T(8,128)(2,1)S(1)} %combine_cache.1.refs_4_), channel_id=1, source_target_pairs={{0,2},{1,3},{2,0},{3,1},{4,6},{5,7},{6,4},{7,5},{8,10},{9,11},{10,... | collective-permute-start | bytes 221192 | tf_op jit(solution)/shard_map/ppermute | solution.py:553
  17.2 7.6 %collective-permute-start.8 = (bf16[16,2048]{1,0:T(8,128)(2,1)S(1)}, bf16[16,2048]{1,0:T(8,128)(2,1)S(1)}, u32[]{:S(2)}, u32[]{:S(2)}) collective-permute-start(bf16[16,2048]{1,0:T(8,128)(2,1)S(1)} %get-tuple-element.26.refs_8_), channel_id=1, source_target_pairs={{0,4},{4,0},{8,12},{12,8},{1,5},{5,1},{9,13},{13,9},{2,6},{6,2},{1... | collective-permute-start | bytes 196616 | tf_op jit(solution)/shard_map/ppermute | solution.py:553
  17.8 7.1 %collective-permute-start.3 = (bf16[16,768]{1,0:T(8,128)(2,1)S(1)}, bf16[16,768]{1,0:T(8,128)(2,1)S(1)}, u32[]{:S(2)}, u32[]{:S(2)}) collective-permute-start(bf16[16,768]{1,0:T(8,128)(2,1)S(1)} %get-tuple-element.22.refs_2_), channel_id=1, source_target_pairs={{0,2},{1,3},{2,0},{3,1},{4,6},{5,7},{6,4},{7,5},{8,10},{9,11},{10,... | collective-permute-start | bytes 73736 | tf_op jit(solution)/shard_map/ppermute | solution.py:553
  18.3 5.4 %collective-permute-start.7 = (bf16[16,128]{1,0:T(8,128)(2,1)S(1)}, bf16[16,128]{1,0:T(8,128)(2,1)S(1)}, u32[]{:S(2)}, u32[]{:S(2)}) collective-permute-start(bf16[16,128]{1,0:T(8,128)(2,1)S(1)} %get-tuple-element.25), channel_id=1, source_target_pairs={{0,10},{1,11},{2,8},{3,9},{4,14},{5,15},{6,12},{7,13},{8,2},{9,3},... | collective-permute-start | bytes 12296 | tf_op jit(solution)/shard_map/ppermute | solution.py:607
  20.3 4.5 %collective-permute-start.6 = (bf16[16,128]{1,0:T(8,128)(2,1)S(1)}, bf16[16,128]{1,0:T(8,128)(2,1)S(1)}, u32[]{:S(2)}, u32[]{:S(2)}) collective-permute-start(bf16[16,128]{1,0:T(8,128)(2,1)S(1)} %get-tuple-element.25), channel_id=1, source_target_pairs={{0,8},{1,9},{2,10},{3,11},{4,12},{5,13},{6,14},{7,15},{8,0},{9,1},... | collective-permute-start | bytes 12296 | tf_op jit(solution)/shard_map/ppermute | solution.py:607
  25.6 1.3 %collective-permute-start.9 = (bf16[16,2560]{1,0:T(8,128)(2,1)S(1)}, bf16[16,2560]{1,0:T(8,128)(2,1)S(1)}, u32[]{:S(2)}, u32[]{:S(2)}) collective-permute-start(bf16[16,2560]{1,0:T(8,128)(2,1)S(1)} %merge.1.mine_ref), channel_id=1, source_target_pairs={{0,1},{1,0},{2,3},{3,2},{4,5},{5,4},{6,7},{7,6},{8,9},{9,8},{10,11... | collective-permute-start | bytes 245768 | tf_op jit(solution)/shard_map/ppermute | solution.py:553

commit v8 on v7

--- a/solution.py
+++ b/solution.py
@@ -18,6 +18,7 @@
 LOWEST_TOP = -1e20
 EXPONENT = math.log2(math.e) / math.sqrt(HD)
 PAIR = GROUP * HD + 128
+UP_COLUMNS = 3584
 CHUNK = 512
 
 F32 = jnp.float32
@@ -132,9 +133,9 @@
     return jnp.cos(angle), jnp.where(lane < HD // 2, -sine, sine)
 
 
-def attend(pairs, limit, cosine, sine, q_ref, k_ref, v_ref, out_ref, qrot_ref):
+def rotated_rows(pairs, cosine, sine, q_ref, qrot_ref):
     zero = jnp.zeros((32, HD), F32)
-    scores = []
+    result = []
     for p in pairs:
         halves = [[], []]
         for e in range(2):
@@ -149,11 +150,20 @@
         mixed = [[exchanged(halves[e][g], halves[e][g + 4]) for g in range(4)] for e in range(2)]
         for s in range(2):
             rows = [jnp.concatenate([mixed[e][g][s] for g in range(4)], 0) for e in range(2)]
-            queries = jnp.concatenate(
-                [jnp.concatenate([rows[0], zero], 1), jnp.concatenate([zero, rows[1]], 1)], 0
-            ).astype(BF16)
+            result.append(
+                jnp.concatenate(
+                    [jnp.concatenate([rows[0], zero], 1), jnp.concatenate([zero, rows[1]], 1)], 0
+                ).astype(BF16)
+            )
+    return result
+
+
+def attend(pairs, limit, queries, k_ref, v_ref, wait_values, out_ref):
+    scores = []
+    for i, p in enumerate(pairs):
+        for s in range(2):
             keys = k_ref[s, :, 2 * p * HD : 2 * (p + 1) * HD]
-            score = lax.dot_general(queries, keys, NT, preferred_element_type=F32)
+            score = lax.dot_general(queries[2 * i + s], keys, NT, preferred_element_type=F32)
             place = lax.broadcasted_iota(jnp.int32, score.shape, 1)
             bound = limit[STEPS * s : STEPS * s + 1, :1].astype(jnp.int32)
             scores.append(jnp.where(place < bound, score, MASKED_SCORE))
@@ -165,6 +175,7 @@
     columns = (top, high, total - high)
     lane8 = lax.broadcasted_iota(jnp.int32, (8, 128), 1)
     numers = []
+    wait_values()
     for i, p in enumerate(pairs):
         for s in range(2):
             at = slice(64 * (2 * i + s), 64 * (2 * i + s + 1))
@@ -224,6 +235,10 @@
                 )
             )
         groups.append(copies)
+    for h in range(2):
+        groups[h][0].start()
+    for copy in groups[0][1:]:
+        copy.start()
     weights = []
     for c in range(chunks):
         at = pl.ds(c * CHUNK, CHUNK)
@@ -233,21 +248,13 @@
                 for i, (source, target) in enumerate(((wk_hbm, wk_ref), (wv_hbm, wv_ref)))
             ]
         )
-    steps = [groups[0], groups[1] + weights[0], *weights[1:]]
-    later = [[] for _ in steps]
-    later[0] = weights[1:2]
-    later[1] = weights[2:4]
-    for c in range(4, chunks):
-        later[c - 2].append(weights[c])
-
     def start(copies):
         for copy in copies:
             copy.start()
 
-    start(groups[0])
-    start(groups[1])
+    x_copy.wait()
+    start(groups[1][1:])
     start(weights[0])
-    x_copy.wait()
     half = wk_hbm.shape[0] // 2
     x = x_ref[:, :half].astype(F32)
     x = jnp.concatenate([x[:8], x[8:]], 1).astype(BF16)
@@ -255,27 +262,29 @@
     cosine, sine = tables(length)
     table_ref[...] = jnp.concatenate([joined(x_ref[:, half + 128 : half + 256]), cosine, sine], 0)
     limit = length - (lax.axis_index("tensor") * k_hbm.shape[1]).astype(F32)
+    queries = []
+    for h in range(2):
+        groups[h][0].wait()
+        own = range(h * pairs // 2, (h + 1) * pairs // 2)
+        queries.append(rotated_rows(own, cosine, sine, q_ref, None if h else qrot_ref))
+    for h, out_ref in enumerate((keep_ref, send_ref)):
+        groups[h][1].wait()
+        for copies in weights[1:2] if h == 0 else weights[2:]:
+            start(copies)
+        attend(
+            range(h * pairs // 2, (h + 1) * pairs // 2),
+            limit, queries[h], k_ref, v_ref, groups[h][2].wait, out_ref,
+        )
     total = None
-    for i, copies in enumerate(steps):
-        for copy in copies:
+    for c in range(chunks):
+        for copy in weights[c]:
             copy.wait()
-        for ahead in later[i]:
-            start(ahead)
-        if i >= 1:
-            at = slice((i - 1) * CHUNK, i * CHUNK)
-            part = jnp.concatenate(
-                [
-                    jnp.dot(x[:, at], ref[at], preferred_element_type=F32)
-                    for ref in (wk_ref, wv_ref)
-                ],
-                0,
-            )
-            total = part if total is None else total + part
-        if i < 2:
-            attend(
-                range(i * pairs // 2, (i + 1) * pairs // 2), limit, cosine, sine,
-                q_ref, k_ref, v_ref, send_ref if i else keep_ref, None if i else qrot_ref,
-            )
+        at = slice(c * CHUNK, (c + 1) * CHUNK)
+        part = jnp.concatenate(
+            [jnp.dot(x[:, at], ref[at], preferred_element_type=F32) for ref in (wk_ref, wv_ref)],
+            0,
+        )
+        total = part if total is None else total + part
     lower, upper = total[:, : width // 2], total[:, width // 2 :]
     base_ref[:, : width // 2] = jnp.where(core == 0, lower, upper)
     base_ref[:, width // 2 :] = jnp.where(core == 0, upper, lower)
@@ -339,7 +348,8 @@
     for ref in has:
         here = place // 2 == lax.axis_index("tensor") % 2
         mine, far = (token[:, depth // 2 + 256 :].astype(F32) for token in tokens[:2])
-        ref[...] = jnp.where(here, mine, far).astype(BF16)
+        ref[:, : mine.shape[1]] = jnp.where(here, mine, far).astype(BF16)
+        ref[:, mine.shape[1] :] = jnp.zeros((16, ref.shape[1] - mine.shape[1]), BF16)
 
 
 def rank_products(rows, depth, columns, base, table, own, near, tokens):
@@ -361,31 +371,28 @@
     return jnp.broadcast_to(tile[:, lane : lane + 1], tile.shape)
 
 
-def combine_part_kernel(n, base_ref, mine_ref, theirs_ref, *refs):
-    passed, refs = refs[: (len(refs) - n) // 2], refs[(len(refs) - n) // 2 :]
-    out_ref, replies, through = refs[0], refs[1:n], refs[n:]
+def combine_part_kernel(base_ref, mine_ref, theirs_ref, cache_ref, out_ref, *replies):
     half = base_ref.shape[1] // 2
     own = base_ref[:, :half] + theirs_ref[:, :half].astype(F32)
     out_ref[:, :half] = own.astype(BF16)
     sums = mine_ref[:, half:].astype(F32) + theirs_ref[:, half:].astype(F32)
     sums = split(sums[:8] + sums[8:])
-    out_ref[:, half:] = sums[:, :256]
+    out_ref[:, half : half + 256] = sums[:, :256]
+    out_ref[:, half + 256 :] = cache_ref[...]
     for i, ref in enumerate(replies):
         ref[...] = sums[:, 128 * (i + 2) : 128 * (i + 3)]
-    for source, target in zip(passed, through):
-        target[...] = source[...]
-
-
-def combine_part(n, base, mine, theirs, passed):
-    shapes = [(16, base.shape[1] // 2 + 256)] + [(16, 128)] * (n - 1) + [p.shape for p in passed]
+
+
+def combine_part(n, base, mine, theirs, cache):
+    shapes = [(16, base.shape[1] // 2 + 256 + cache.shape[1])] + [(16, 128)] * n
     return pl.pallas_call(
-        functools.partial(combine_part_kernel, n),
-        in_specs=[VMEM] * (3 + len(passed)),
+        combine_part_kernel,
+        in_specs=[VMEM] * 4,
         out_specs=[VMEM] * len(shapes),
         out_shape=[jax.ShapeDtypeStruct(shape, BF16) for shape in shapes],
         compiler_params=pltpu.CompilerParams(vmem_limit_bytes=32 * MEBI),
         name="combine_part",
-    )(base, mine, theirs, *passed)
+    )(base, mine, theirs, cache)
 
 
 def combine_cache_kernel(a_ref, b_ref, _, out_ref):
@@ -426,12 +433,13 @@
 
 
 def merge_kernel(n, paired, width_all, *refs):
-    table_ref, qrot_ref, pa_ref, pb_ref, ca_ref, cb_ref = refs[:6]
-    backs, (ua_ref, ub_ref, out_ref) = refs[6 : 6 + n], refs[6 + n :]
-    pairs = ca_ref.shape[1] // PAIR
+    table_ref, qrot_ref, pa_ref, pb_ref = refs[:4]
+    backs, (ua_ref, ub_ref, out_ref) = refs[4 : 4 + n], refs[4 + n :]
+    pairs = qrot_ref.shape[1] // (GROUP * HD)
     width = pairs * 2 * HD
     cosine, sine = table_ref[8:16], table_ref[16:]
-    sums = pa_ref[...].astype(F32) + pb_ref[...].astype(F32)
+    head = width + 256
+    sums = pa_ref[:, :head].astype(F32) + pb_ref[:, :head].astype(F32)
     tail = sums[:8, width : width + 256] + sums[8:, width : width + 256]
     squares, z = tail[:, :128], tail[:, 128:]
     for ref in backs:
@@ -442,7 +450,7 @@
     ).astype(BF16)
     adapted = []
     for ref in (ua_ref, ub_ref):
-        ups = jnp.concatenate([ref[:, i : i + 128] for i in range(0, ref.shape[1], 128)], 0)
+        ups = jnp.concatenate([ref[:, i : i + 128] for i in range(0, 16 * HD, 128)], 0)
         adapted.append(lax.dot_general(z, ups, NT, preferred_element_type=F32))
     if paired:
         even = lax.axis_index("dp") % 2 == 0
@@ -481,8 +489,8 @@
                 dot = jnp.sum(q * keys[j], 1, keepdims=True)
                 scores[j] = jnp.where(lane == g, dot, scores[j])
         scores = [jnp.where(j <= step, scores[j], MASKED_SCORE) for j in range(STEPS)]
-        end = slice(p * PAIR + GROUP * HD, (p + 1) * PAIR)
-        stats = [ref[:, end].astype(F32) for ref in (ca_ref, cb_ref)]
+        end = slice(head + p * PAIR + GROUP * HD, head + (p + 1) * PAIR)
+        stats = [ref[:, end].astype(F32) for ref in (pa_ref, pb_ref)]
         top = functools.reduce(jnp.maximum, scores + stats)
         fresh = [rounded(jnp.exp2((scores[j] - top) * EXPONENT)) for j in range(STEPS)]
         factors = [jnp.exp2(jnp.minimum(s - top, 0.0) * EXPONENT) for s in stats]
@@ -492,17 +500,17 @@
         inverse = 1.0 / denom
         coefficients = [c * inverse for c in fresh + factors]
         for g in range(GROUP):
-            at = slice(p * PAIR + g * HD, p * PAIR + (g + 1) * HD)
-            terms = values + [ref[:, at].astype(F32) for ref in (ca_ref, cb_ref)]
+            at = slice(head + p * PAIR + g * HD, head + p * PAIR + (g + 1) * HD)
+            terms = values + [ref[:, at].astype(F32) for ref in (pa_ref, pb_ref)]
             tile = jnp.zeros((16, 128), F32)
             for c, term in zip(coefficients, terms):
                 tile = tile + broadcast_lane(c, g) * term
             out_ref[:, (p * GROUP + g) * HD : (p * GROUP + g + 1) * HD] = tile.astype(BF16)
 
 
-def merge(paired, width_all, table, qrot, parts, caches, backs, ups):
-    operands = [table, qrot, *parts, *caches, *backs, *ups]
-    pairs = caches[0].shape[1] // PAIR
+def merge(paired, width_all, table, qrot, parts, backs, ups):
+    operands = [table, qrot, *parts, *backs, *ups]
+    pairs = qrot.shape[1] // (GROUP * HD)
     return pl.pallas_call(
         functools.partial(merge_kernel, len(backs), paired, width_all),
         in_specs=[VMEM] * len(operands),
@@ -584,10 +592,8 @@
         tokens, queries, key_cache, value_cache, key_weight, value_weight
     )
     received = to_tensor(send, 1)
-    columns = key_up.shape[0] * 8 if paired else 0
+    columns = UP_COLUMNS if paired else 0
     message, *has = rank_products(rows, depth, columns, base, table, own, near, [tokens, *sent])
-    part, *rest = combine_part(n + 1, base, message, to_tensor(message, 1), has)
-    replies, has = rest[:n], rest[n:]
     if paired:
         ups = [has[0], to_dp(has[0], 1)]
     else:
@@ -597,7 +603,7 @@
         ups = lax.dynamic_index_in_dim(ups, lax.axis_index("tensor") % 2, 0, keepdims=False)
         ups = [ups[0], ups[1]]
     cache = combine_cache(keep, received, message)
-    cache_far = to_tensor(cache, 2)
+    part, *replies = combine_part(n, base, message, to_tensor(message, 1), cache)
     part_far = to_tensor(part, 2)
     places = [(s, t) for s in range(n_dp) for t in range(n_tensor)]
     backs = []
@@ -611,7 +617,6 @@
         table,
         qrot,
         (part, part_far),
-        (cache, cache_far),
         backs,
         ups,
     )

time: 27.8 us -> 26.3 us (0.946)
  starting transfers between devices: 12.8 us -> 11.2 us
  waiting for transfers between devices: 4.33 us -> 4.62 us
    ppermute x2, starting transfers between devices: 3.85 us -> 2.9 us  [shards(): backs.append(lax.ppermute(reply, ('dp', 'tensor'), perm))]
    ppermute x8 -> x7, starting transfers between devices: 8.91 us -> 8.31 us  [swap(): return lax.ppermute(value, axis, [(i, i ^ distance) for i in range(n)])]
    ppermute x2, waiting for transfers between devices: 2.68 us -> 3.17 us  [shards(): backs.append(lax.ppermute(reply, ('dp', 'tensor'), perm))]
    ppermute x8 -> x7, waiting for transfers between devices: 1.65 us -> 1.45 us  [swap(): return lax.ppermute(value, axis, [(i, i ^ distance) for i in range(n)])]
  transfers between devices with their start and end apart: 10 -> 9, of which waited for: 4 -> 4; matrix products, arithmetic and copies ran while one was open for 0% -> 0% of each run, Pallas kernels for 23% -> 24%
where the time goes in v8:
time: 26.3 us; the launch traced here: 26.2 us
  starting transfers between devices  11.2 us (43%)
  Pallas kernels  9.64 us (37%)
  waiting for transfers between devices  4.62 us (18%)
  between operations  0.72 us (3%)
    ppermute x7, starting transfers between devices, swap(): return lax.ppermute(value, axis, [(i, i ^ distance) for i in range(n)])  8.31 us
    pallas_call x1, Pallas kernels, local(): pl.pallas_call(local_kernel, in_specs=[HBM] * 6, out_specs=[VMEM] * 5, ou...  5.64 us
    ppermute x2, waiting for transfers between devices, shards(): backs.append(lax.ppermute(reply, ('dp', 'tensor'), perm))  3.17 us
    ppermute x2, starting transfers between devices, shards(): backs.append(lax.ppermute(reply, ('dp', 'tensor'), perm))  2.9 us
    pallas_call x1, Pallas kernels, pack(): pl.pallas_call(pack_kernel, in_specs=[HBM] * len(operands), out_specs=[VM...  1.9 us
    ppermute x7, waiting for transfers between devices, swap(): return lax.ppermute(value, axis, [(i, i ^ distance) for i in range(n)])  1.45 us
    pallas_call x1, Pallas kernels, merge(): pl.pallas_call(functools.partial(merge_kernel, len(backs), paired, width_...  0.8 us
    pallas_call x1, Pallas kernels, place(): pl.pallas_call(place_kernel, in_specs=[VMEM] * 2, out_specs=[VMEM] * 3, o...  0.69 us
  transfers between devices with their start and end apart: 9, of which 4 were waited for; matrix products, arithmetic and copies ran while one was open for 0% of the time, Pallas kernels for 24%

profile of v8, /device:TPU:0, one launch (start us, length us, event | category | flops | bytes accessed | tf_op | source)
XLA Modules:
  0.0 26.2 jit_solution(3169446203257859223)
XLA Ops:
  0.6 1.9 %pack.1 = (bf16[16,4096]{1,0:T(8,128)(2,1)}, bf16[16,3328]{1,0:T(8,128)(2,1)}) custom-call(s32[2]{0:T(128)} %refs_0_.1, bf16[2,4,2048]{2,1,0:T(4,128)(2,1)} %refs_1_.1, bf16[2048]{0:T(1024)(128)(2,1)} %refs_2_.1, f32[16,2048]{1,0:T(8,128)} %refs_3_.1, f32[16,2048]{1,0:T(8,128)} %refs_4_.1, f32[64,256]{1,0:T(8,128)} %bitcast.2, f32[64,256]{1,0:T(8,128)} %bitcast.3), custom_call_target="tpu_custom_call" | custom-call | tf_op jit(solution)/shard_map/pack/pallas_call | solution.py:105
  2.5 3.1 %collective-permute-start = (bf16[16,4096]{1,0:T(8,128)(2,1)}, bf16[16,4096]{1,0:T(8,128)(2,1)S(1)}, u32[]{:S(2)}, u32[]{:S(2)}) collective-permute-start(bf16[16,4096]{1,0:T(8,128)(2,1)} %get-tuple-element.18.refs_2_), channel_id=1, source_target_pairs={{0,4},{4,0},{8,12},{12,8},{1,5},{5,1},{9,13},{13,9},{2,6},{6,2},{1... | collective-permute-start | bytes 393224 | tf_op jit(solution)/shard_map/ppermute | solution.py:561
  5.6 2.6 %collective-permute-start.1 = (bf16[16,3328]{1,0:T(8,128)(2,1)}, bf16[16,3328]{1,0:T(8,128)(2,1)S(1)}, u32[]{:S(2)}, u32[]{:S(2)}) collective-permute-start(bf16[16,3328]{1,0:T(8,128)(2,1)} %get-tuple-element.14.x_hbm.refs_4_), channel_id=1, source_target_pairs={{0,8},{4,12},{8,0},{12,4},{1,9},{5,13},{9,1},{13,5},{2,10},{6,14},... | collective-permute-start | bytes 319496 | tf_op jit(solution)/shard_map/ppermute | solution.py:561
  8.2 5.6 %local.1 = (bf16[16,2304]{1,0:T(8,128)(2,1)S(1)}, bf16[16,2304]{1,0:T(8,128)(2,1)S(1)}, f32[16,1024]{1,0:T(8,128)S(1)}, bf16[16,2048]{1,0:T(8,128)(2,1)S(1)}, f32[24,128]{1,0:T(8,128)S(1)}) custom-call(bf16[16,3328]{1,0:T(8,128)(2,1)} %get-tuple-element.14.x_hbm.refs_4_, bf16[2,4,8192]{2,1,0:T(4,128)(2,1)} %q_hbm.1, bf16[2,512,1024]{2,1,0:T(8,128)(2,1)} %k_hbm.1, ...), custom_call_target="tpu_custom_call" | custom-call | flops 402653184 | bytes 12582912 | tf_op jit(solution)/shard_map/local/pallas_call | solution.py:298
  13.9 0.1 collective-permute-start.3
  14.0 0.0 collective-permute-done.1.refs_5_
  14.0 0.0 collective-permute-done.refs_3_
  14.0 0.4 %rank_products.1 = (bf16[16,896]{1,0:T(8,128)(2,1)S(1)}, bf16[16,3584]{1,0:T(8,128)(2,1)S(1)}) custom-call(f32[16,1024]{1,0:T(8,128)S(1)} %get-tuple-element.17.refs_0_.base_ref, f32[24,128]{1,0:T(8,128)S(1)} %get-tuple-element.15.refs_1_.refs_0_, bf16[16,4096]{1,0:T(8,128)(2,1)S(1)} %copy-done.1, bf16[16,4096]{1,0:T(8,128)(2,1)S(1)} %collective-permute-done.refs_3_, ...), custom_call_target="tpu_custom_call" | custom-call | tf_op jit(solution)/shard_map/rank_products/pallas_call | solution.py:360
  14.4 0.5 %collective-permute-start.2 = (bf16[16,896]{1,0:T(8,128)(2,1)S(1)}, bf16[16,896]{1,0:T(8,128)(2,1)S(1)}, u32[]{:S(2)}, u32[]{:S(2)}) collective-permute-start(bf16[16,896]{1,0:T(8,128)(2,1)S(1)} %get-tuple-element.19._.mine_ref), channel_id=1, source_target_pairs={{0,1},{1,0},{2,3},{3,2},{4,5},{5,4},{6,7},{7,6},{8,9},{9,8},{10,11... | collective-permute-start | bytes 86024 | tf_op jit(solution)/shard_map/ppermute | solution.py:561
  14.8 0.4 %collective-permute-start.7 = (bf16[16,3584]{1,0:T(8,128)(2,1)S(1)}, bf16[16,3584]{1,0:T(8,128)(2,1)S(1)}, u32[]{:S(2)}, u32[]{:S(2)}) collective-permute-start(bf16[16,3584]{1,0:T(8,128)(2,1)S(1)} %get-tuple-element.24.refs_6_), channel_id=1, source_target_pairs={{0,4},{4,0},{8,12},{12,8},{1,5},{5,1},{9,13},{13,9},{2,6},{6,2},{1... | collective-permute-start | bytes 344072 | tf_op jit(solution)/shard_map/ppermute | solution.py:561
  15.3 0.0 collective-permute-done.3.b_ref
  15.3 0.2 combine_cache.1.cache_ref
  15.5 0.2 collective-permute-done.2.theirs_ref
  15.7 1.6 %collective-permute-start.4 = (bf16[16,3072]{1,0:T(8,128)(2,1)S(1)}, bf16[16,3072]{1,0:T(8,128)(2,1)S(1)}, u32[]{:S(2)}, u32[]{:S(2)}) collective-permute-start(bf16[16,3072]{1,0:T(8,128)(2,1)S(1)} %get-tuple-element.22.refs_2_), channel_id=1, source_target_pairs={{0,2},{1,3},{2,0},{3,1},{4,6},{5,7},{6,4},{7,5},{8,10},{9,11},{10,... | collective-permute-start | bytes 294920 | tf_op jit(solution)/shard_map/ppermute | solution.py:561
  17.3 1.6 %collective-permute-start.6 = (bf16[16,128]{1,0:T(8,128)(2,1)S(1)}, bf16[16,128]{1,0:T(8,128)(2,1)S(1)}, u32[]{:S(2)}, u32[]{:S(2)}) collective-permute-start(bf16[16,128]{1,0:T(8,128)(2,1)S(1)} %get-tuple-element.23), channel_id=1, source_target_pairs={{0,10},{1,11},{2,8},{3,9},{4,14},{5,15},{6,12},{7,13},{8,2},{9,3},... | collective-permute-start | bytes 12296 | tf_op jit(solution)/shard_map/ppermute | solution.py:613
  18.8 1.3 %collective-permute-start.5 = (bf16[16,128]{1,0:T(8,128)(2,1)S(1)}, bf16[16,128]{1,0:T(8,128)(2,1)S(1)}, u32[]{:S(2)}, u32[]{:S(2)}) collective-permute-start(bf16[16,128]{1,0:T(8,128)(2,1)S(1)} %get-tuple-element.23), channel_id=1, source_target_pairs={{0,8},{1,9},{2,10},{3,11},{4,12},{5,13},{6,14},{7,15},{8,0},{9,1},... | collective-permute-start | bytes 12296 | tf_op jit(solution)/shard_map/ppermute | solution.py:613
  20.2 2.5 %collective-permute-done.6.refs_5_ = bf16[16,128]{1,0:T(8,128)(2,1)S(1)} collective-permute-done((bf16[16,128]{1,0:T(8,128)(2,1)S(1)}, bf16[16,128]{1,0:T(8,128)(2,1)S(1)}, u32[]{:S(2)}, u32[]{:S(2)}) %collective-permute-start.6) | collective-permute-done | bytes 4128 | tf_op jit(solution)/shard_map/ppermute | solution.py:613
  22.7 0.7 %collective-permute-done.5.refs_4_ = bf16[16,128]{1,0:T(8,128)(2,1)S(1)} collective-permute-done((bf16[16,128]{1,0:T(8,128)(2,1)S(1)}, bf16[16,128]{1,0:T(8,128)(2,1)S(1)}, u32[]{:S(2)}, u32[]{:S(2)}) %collective-permute-start.5) | collective-permute-done | bytes 4128 | tf_op jit(solution)/shard_map/ppermute | solution.py:613
  23.3 0.0 collective-permute-done.7.refs_7_
  23.3 0.0 collective-permute-done.4.refs_3_
  23.3 0.8 %merge.1.mine_ref = bf16[16,2560]{1,0:T(8,128)(2,1)S(1)} custom-call(f32[24,128]{1,0:T(8,128)S(1)} %get-tuple-element.15.refs_1_.refs_0_, bf16[16,2048]{1,0:T(8,128)(2,1)S(1)} %get-tuple-element.16.refs_1_, bf16[16,3072]{1,0:T(8,128)(2,1)S(1)} %get-tuple-element.22.refs_2_, bf16[16,3072]{1,0:T(8,128)(2,1)S(1)} %collective-permute-done.4.refs_3_, ...), custom_call_target="tpu_custom_call" | custom-call | tf_op jit(solution)/shard_map/merge/pallas_call | solution.py:514
  24.2 0.1 collective-permute-start.8
  24.2 1.3 %collective-permute-done.8.theirs_ref = bf16[16,2560]{1,0:T(8,128)(2,1)S(1)} collective-permute-done((bf16[16,2560]{1,0:T(8,128)(2,1)S(1)}, bf16[16,2560]{1,0:T(8,128)(2,1)S(1)}, u32[]{:S(2)}, u32[]{:S(2)}) %collective-permute-start.8) | collective-permute-done | bytes 81952 | tf_op jit(solution)/shard_map/ppermute | solution.py:561
  25.5 0.7 %place.1 = (bf16[2,4,1024]{2,1,0:T(4,128)(2,1)}, bf16[2,4,1024]{2,1,0:T(4,128)(2,1)}, bf16[2,4,8192]{2,1,0:T(4,128)(2,1)}) custom-call(bf16[16,2560]{1,0:T(8,128)(2,1)S(1)} %merge.1.mine_ref, bf16[16,2560]{1,0:T(8,128)(2,1)S(1)} %collective-permute-done.8.theirs_ref), custom_call_target="tpu_custom_call" | custom-call | tf_op jit(solution)/shard_map/place/pallas_call | solution.py:546
  (5 shorter events, 0.0 us)
Async XLA Ops:
  2.5 11.4 %collective-permute-start = (bf16[16,4096]{1,0:T(8,128)(2,1)}, bf16[16,4096]{1,0:T(8,128)(2,1)S(1)}, u32[]{:S(2)}, u32[]{:S(2)}) collective-permute-start(bf16[16,4096]{1,0:T(8,128)(2,1)} %get-tuple-element.18.refs_2_), channel_id=1, source_target_pairs={{0,4},{4,0},{8,12},{12,8},{1,5},{5,1},{9,13},{13,9},{2,6},{6,2},{1... | collective-permute-start | bytes 393224 | tf_op jit(solution)/shard_map/ppermute | solution.py:561
  5.6 8.3 %copy-start = (bf16[16,3328]{1,0:T(8,128)(2,1)S(1)}, bf16[16,3328]{1,0:T(8,128)(2,1)}, u32[]{:S(2)}) copy-start(bf16[16,3328]{1,0:T(8,128)(2,1)} %get-tuple-element.14.x_hbm.refs_4_) | copy-start | bytes 319492
  5.6 8.4 %copy-start.1 = (bf16[16,4096]{1,0:T(8,128)(2,1)S(1)}, bf16[16,4096]{1,0:T(8,128)(2,1)}, u32[]{:S(2)}) copy-start(bf16[16,4096]{1,0:T(8,128)(2,1)} %get-tuple-element.18.refs_2_) | copy-start | bytes 393220
  5.6 8.3 %collective-permute-start.1 = (bf16[16,3328]{1,0:T(8,128)(2,1)}, bf16[16,3328]{1,0:T(8,128)(2,1)S(1)}, u32[]{:S(2)}, u32[]{:S(2)}) collective-permute-start(bf16[16,3328]{1,0:T(8,128)(2,1)} %get-tuple-element.14.x_hbm.refs_4_), channel_id=1, source_target_pairs={{0,8},{4,12},{8,0},{12,4},{1,9},{5,13},{9,1},{13,5},{2,10},{6,14},... | collective-permute-start | bytes 319496 | tf_op jit(solution)/shard_map/ppermute | solution.py:561
  13.9 1.4 %collective-permute-start.3 = (bf16[16,2304]{1,0:T(8,128)(2,1)S(1)}, bf16[16,2304]{1,0:T(8,128)(2,1)S(1)}, u32[]{:S(2)}, u32[]{:S(2)}) collective-permute-start(bf16[16,2304]{1,0:T(8,128)(2,1)S(1)} %get-tuple-element.21), channel_id=1, source_target_pairs={{0,1},{1,0},{2,3},{3,2},{4,5},{5,4},{6,7},{7,6},{8,9},{9,8},{10,11... | collective-permute-start | bytes 221192 | tf_op jit(solution)/shard_map/ppermute | solution.py:561
  14.4 1.3 %collective-permute-start.2 = (bf16[16,896]{1,0:T(8,128)(2,1)S(1)}, bf16[16,896]{1,0:T(8,128)(2,1)S(1)}, u32[]{:S(2)}, u32[]{:S(2)}) collective-permute-start(bf16[16,896]{1,0:T(8,128)(2,1)S(1)} %get-tuple-element.19._.mine_ref), channel_id=1, source_target_pairs={{0,1},{1,0},{2,3},{3,2},{4,5},{5,4},{6,7},{7,6},{8,9},{9,8},{10,11... | collective-permute-start | bytes 86024 | tf_op jit(solution)/shard_map/ppermute | solution.py:561
  14.8 8.5 %collective-permute-start.7 = (bf16[16,3584]{1,0:T(8,128)(2,1)S(1)}, bf16[16,3584]{1,0:T(8,128)(2,1)S(1)}, u32[]{:S(2)}, u32[]{:S(2)}) collective-permute-start(bf16[16,3584]{1,0:T(8,128)(2,1)S(1)} %get-tuple-element.24.refs_6_), channel_id=1, source_target_pairs={{0,4},{4,0},{8,12},{12,8},{1,5},{5,1},{9,13},{13,9},{2,6},{6,2},{1... | collective-permute-start | bytes 344072 | tf_op jit(solution)/shard_map/ppermute | solution.py:561
  15.7 7.6 %collective-permute-start.4 = (bf16[16,3072]{1,0:T(8,128)(2,1)S(1)}, bf16[16,3072]{1,0:T(8,128)(2,1)S(1)}, u32[]{:S(2)}, u32[]{:S(2)}) collective-permute-start(bf16[16,3072]{1,0:T(8,128)(2,1)S(1)} %get-tuple-element.22.refs_2_), channel_id=1, source_target_pairs={{0,2},{1,3},{2,0},{3,1},{4,6},{5,7},{6,4},{7,5},{8,10},{9,11},{10,... | collective-permute-start | bytes 294920 | tf_op jit(solution)/shard_map/ppermute | solution.py:561
  17.3 5.4 %collective-permute-start.6 = (bf16[16,128]{1,0:T(8,128)(2,1)S(1)}, bf16[16,128]{1,0:T(8,128)(2,1)S(1)}, u32[]{:S(2)}, u32[]{:S(2)}) collective-permute-start(bf16[16,128]{1,0:T(8,128)(2,1)S(1)} %get-tuple-element.23), channel_id=1, source_target_pairs={{0,10},{1,11},{2,8},{3,9},{4,14},{5,15},{6,12},{7,13},{8,2},{9,3},... | collective-permute-start | bytes 12296 | tf_op jit(solution)/shard_map/ppermute | solution.py:613
  18.8 4.5 %collective-permute-start.5 = (bf16[16,128]{1,0:T(8,128)(2,1)S(1)}, bf16[16,128]{1,0:T(8,128)(2,1)S(1)}, u32[]{:S(2)}, u32[]{:S(2)}) collective-permute-start(bf16[16,128]{1,0:T(8,128)(2,1)S(1)} %get-tuple-element.23), channel_id=1, source_target_pairs={{0,8},{1,9},{2,10},{3,11},{4,12},{5,13},{6,14},{7,15},{8,0},{9,1},... | collective-permute-start | bytes 12296 | tf_op jit(solution)/shard_map/ppermute | solution.py:613
  24.2 1.3 %collective-permute-start.8 = (bf16[16,2560]{1,0:T(8,128)(2,1)S(1)}, bf16[16,2560]{1,0:T(8,128)(2,1)S(1)}, u32[]{:S(2)}, u32[]{:S(2)}) collective-permute-start(bf16[16,2560]{1,0:T(8,128)(2,1)S(1)} %merge.1.mine_ref), channel_id=1, source_target_pairs={{0,1},{1,0},{2,3},{3,2},{4,5},{5,4},{6,7},{7,6},{8,9},{9,8},{10,11... | collective-permute-start | bytes 245768 | tf_op jit(solution)/shard_map/ppermute | solution.py:561

commit v9 on v8

--- a/solution.py
+++ b/solution.py
@@ -66,53 +66,67 @@
 
 
 def pack_kernel(*refs):
-    sources, (a_ref, b_ref), held, sems = refs[:7], refs[7:9], refs[9:16], refs[16]
+    sources, outs, held = refs[:7], refs[7:9], refs[9:16]
+    (a_ref, b_ref), sems, out_sems = refs[16:18], refs[18], refs[19]
     copies = [
         pltpu.make_async_copy(source, target, sems.at[i])
         for i, (source, target) in enumerate(zip(sources, held))
     ]
     for copy in copies:
         copy.start()
-    lengths_ref, x_ref, gain_ref, kd_ref, vd_ref, ku_ref, vu_ref = held
-    for copy in copies:
+    backs = [
+        pltpu.make_async_copy(source, target, out_sems.at[i])
+        for i, (source, target) in enumerate(zip((a_ref, b_ref), outs))
+    ]
+    kd_ref, vd_ref, x_ref, gain_ref, lengths_ref, ku_ref, vu_ref = held
+    own, depth = kd_ref.shape
+    for slot, ref in enumerate((kd_ref, vd_ref)):
+        copies[slot].wait()
+        down = ref[...]
+        if own < 16:
+            down = jnp.concatenate([down, jnp.zeros((16 - own, depth), F32)], 0)
+        a_ref[:, slot * depth : (slot + 1) * depth] = down.astype(BF16)
+    backs[0].start()
+    for copy in copies[2:]:
         copy.wait()
     x = jnp.concatenate([x_ref[0].astype(F32), x_ref[1].astype(F32)], 0)
-    depth = x.shape[1]
-    scaled = x * gain_ref[...].astype(F32).reshape(1, depth)
+    gain = gain_ref[...].astype(F32)
+    scaled = jnp.concatenate(
+        [x[:, i * 128 : (i + 1) * 128] * gain[i : i + 1] for i in range(depth // 128)], 1
+    )
     b_ref[:, : depth // 2] = jnp.concatenate(
         [scaled[:, : depth // 2], scaled[:, depth // 2 :]], 0
     ).astype(BF16)
     row = lax.broadcasted_iota(jnp.int32, (16, 128), 0)
-    length = jnp.where(row % 8 < STEPS, lengths_ref[0], lengths_ref[1])
+    lengths = lengths_ref[...]
+    length = jnp.where(row % 8 < STEPS, lengths[:, :1], lengths[:, 1:])
     length = jnp.where(row < 8, length // 64 * 64, length % 64)
     b_ref[:, depth // 2 : depth // 2 + 128] = length.astype(F32).astype(BF16)
     squares = jnp.broadcast_to(jnp.sum(x * x, 1, keepdims=True), (8, 128))
     b_ref[:, depth // 2 + 128 : depth // 2 + 256] = split(squares)
     ups = jnp.concatenate([ku_ref[...], vu_ref[...]], 0).T.astype(BF16)
     b_ref[:, depth // 2 + 256 :] = flat(ups)
-    own = kd_ref.shape[0]
-    for slot, ref in enumerate((kd_ref, vd_ref)):
-        down = ref[...]
-        if own < 16:
-            down = jnp.concatenate([down, jnp.zeros((16 - own, depth), F32)], 0)
-        a_ref[:, slot * depth : (slot + 1) * depth] = down.astype(BF16)
+    backs[1].start()
+    for copy in backs:
+        copy.wait()
 
 
 def pack(lengths, hidden, gain, key_down, value_down, key_up, value_up):
-    operands = [lengths, hidden, gain, key_down, value_down, key_up.T, value_up.T]
+    operands = [key_down, value_down, hidden, gain.reshape(-1, 128), lengths.reshape(1, 2)]
+    operands += [key_up.T, value_up.T]
     depth = hidden.shape[2]
     ups = key_up.shape[0] * 8
+    outs = [
+        jax.ShapeDtypeStruct((16, 2 * depth), BF16),
+        jax.ShapeDtypeStruct((16, depth // 2 + 256 + ups), BF16),
+    ]
     return pl.pallas_call(
         pack_kernel,
         in_specs=[HBM] * len(operands),
-        out_specs=[VMEM] * 2,
-        out_shape=[
-            jax.ShapeDtypeStruct((16, 2 * depth), BF16),
-            jax.ShapeDtypeStruct((16, depth // 2 + 256 + ups), BF16),
-        ],
-        scratch_shapes=[pltpu.SMEM(lengths.shape, jnp.int32)]
-        + [pltpu.VMEM(o.shape, o.dtype) for o in operands[1:]]
-        + [pltpu.SemaphoreType.DMA((len(operands),))],
+        out_specs=[HBM] * len(outs),
+        out_shape=outs,
+        scratch_shapes=[pltpu.VMEM(o.shape, o.dtype) for o in operands + outs]
+        + [pltpu.SemaphoreType.DMA((len(operands),)), pltpu.SemaphoreType.DMA((len(outs),))],
         compiler_params=pltpu.CompilerParams(vmem_limit_bytes=WHOLE_VMEM),
         name="pack",
     )(*operands)

time: 26.3 us -> 26.4 us (level)
  no operation moved by 1% of the time
where the time goes in v9:
time: 26.4 us; the launch traced here: 26.2 us
  starting transfers between devices  11.2 us (42%)
  Pallas kernels  9.66 us (37%)
  waiting for transfers between devices  4.62 us (18%)
  between operations  0.72 us (3%)
    ppermute x7, starting transfers between devices, swap(): return lax.ppermute(value, axis, [(i, i ^ distance) for i in range(n)])  8.31 us
    pallas_call x1, Pallas kernels, local(): pl.pallas_call(local_kernel, in_specs=[HBM] * 6, out_specs=[VMEM] * 5, ou...  5.64 us
    ppermute x2, waiting for transfers between devices, shards(): backs.append(lax.ppermute(reply, ('dp', 'tensor'), perm))  3.17 us
    ppermute x2, starting transfers between devices, shards(): backs.append(lax.ppermute(reply, ('dp', 'tensor'), perm))  2.9 us
    pallas_call x1, Pallas kernels, pack(): pl.pallas_call(pack_kernel, in_specs=[HBM] * len(operands), out_specs=[HB...  1.92 us
    ppermute x7, waiting for transfers between devices, swap(): return lax.ppermute(value, axis, [(i, i ^ distance) for i in range(n)])  1.45 us
    pallas_call x1, Pallas kernels, merge(): pl.pallas_call(functools.partial(merge_kernel, len(backs), paired, width_...  0.8 us
    pallas_call x1, Pallas kernels, place(): pl.pallas_call(place_kernel, in_specs=[VMEM] * 2, out_specs=[VMEM] * 3, o...  0.69 us
  transfers between devices with their start and end apart: 9, of which 4 were waited for; matrix products, arithmetic and copies ran while one was open for 0% of the time, Pallas kernels for 24%

profile of v9, /device:TPU:0, one launch (start us, length us, event | category | flops | bytes accessed | tf_op | source)
XLA Modules:
  0.0 26.2 jit_solution(17798059517048431511)
XLA Ops:
  0.6 1.9 %pack.1 = (bf16[16,4096]{1,0:T(8,128)(2,1)}, bf16[16,3328]{1,0:T(8,128)(2,1)}) custom-call(f32[16,2048]{1,0:T(8,128)} %refs_0_.1, f32[16,2048]{1,0:T(8,128)} %refs_1_.1, bf16[2,4,2048]{2,1,0:T(4,128)(2,1)} %refs_2_.1, bf16[16,128]{1,0:T(8,128)(2,1)} %bitcast.6, s32[1,2]{1,0:T(1,128)} %bitcast.7, f32[64,256]{1,0:T(8,128)} %bitcast.4, f32[64,256]{1,0:T(8,128)} %bitcast.5), custom_call_target="tpu_custom_call" | custom-call | tf_op jit(solution)/shard_map/pack/pallas_call | solution.py:123
  2.6 3.1 %collective-permute-start = (bf16[16,4096]{1,0:T(8,128)(2,1)}, bf16[16,4096]{1,0:T(8,128)(2,1)S(1)}, u32[]{:S(2)}, u32[]{:S(2)}) collective-permute-start(bf16[16,4096]{1,0:T(8,128)(2,1)} %get-tuple-element.18.refs_2_), channel_id=1, source_target_pairs={{0,4},{4,0},{8,12},{12,8},{1,5},{5,1},{9,13},{13,9},{2,6},{6,2},{1... | collective-permute-start | bytes 393224 | tf_op jit(solution)/shard_map/ppermute | solution.py:575
  5.7 2.6 %collective-permute-start.1 = (bf16[16,3328]{1,0:T(8,128)(2,1)}, bf16[16,3328]{1,0:T(8,128)(2,1)S(1)}, u32[]{:S(2)}, u32[]{:S(2)}) collective-permute-start(bf16[16,3328]{1,0:T(8,128)(2,1)} %get-tuple-element.14.x_hbm.refs_4_), channel_id=1, source_target_pairs={{0,8},{4,12},{8,0},{12,4},{1,9},{5,13},{9,1},{13,5},{2,10},{6,14},... | collective-permute-start | bytes 319496 | tf_op jit(solution)/shard_map/ppermute | solution.py:575
  8.2 5.6 %local.1 = (bf16[16,2304]{1,0:T(8,128)(2,1)S(1)}, bf16[16,2304]{1,0:T(8,128)(2,1)S(1)}, f32[16,1024]{1,0:T(8,128)S(1)}, bf16[16,2048]{1,0:T(8,128)(2,1)S(1)}, f32[24,128]{1,0:T(8,128)S(1)}) custom-call(bf16[16,3328]{1,0:T(8,128)(2,1)} %get-tuple-element.14.x_hbm.refs_4_, bf16[2,4,8192]{2,1,0:T(4,128)(2,1)} %q_hbm.1, bf16[2,512,1024]{2,1,0:T(8,128)(2,1)} %k_hbm.1, ...), custom_call_target="tpu_custom_call" | custom-call | flops 402653184 | bytes 12582912 | tf_op jit(solution)/shard_map/local/pallas_call | solution.py:312
  13.9 0.1 collective-permute-start.3
  14.0 0.0 collective-permute-done.1.refs_5_
  14.0 0.0 collective-permute-done.refs_3_
  14.0 0.4 %rank_products.1 = (bf16[16,896]{1,0:T(8,128)(2,1)S(1)}, bf16[16,3584]{1,0:T(8,128)(2,1)S(1)}) custom-call(f32[16,1024]{1,0:T(8,128)S(1)} %get-tuple-element.17.refs_0_.base_ref, f32[24,128]{1,0:T(8,128)S(1)} %get-tuple-element.15.refs_1_.refs_0_, bf16[16,4096]{1,0:T(8,128)(2,1)S(1)} %copy-done.1, bf16[16,4096]{1,0:T(8,128)(2,1)S(1)} %collective-permute-done.refs_3_, ...), custom_call_target="tpu_custom_call" | custom-call | tf_op jit(solution)/shard_map/rank_products/pallas_call | solution.py:374
  14.4 0.5 %collective-permute-start.2 = (bf16[16,896]{1,0:T(8,128)(2,1)S(1)}, bf16[16,896]{1,0:T(8,128)(2,1)S(1)}, u32[]{:S(2)}, u32[]{:S(2)}) collective-permute-start(bf16[16,896]{1,0:T(8,128)(2,1)S(1)} %get-tuple-element.19._.mine_ref), channel_id=1, source_target_pairs={{0,1},{1,0},{2,3},{3,2},{4,5},{5,4},{6,7},{7,6},{8,9},{9,8},{10,11... | collective-permute-start | bytes 86024 | tf_op jit(solution)/shard_map/ppermute | solution.py:575
  14.9 0.4 %collective-permute-start.7 = (bf16[16,3584]{1,0:T(8,128)(2,1)S(1)}, bf16[16,3584]{1,0:T(8,128)(2,1)S(1)}, u32[]{:S(2)}, u32[]{:S(2)}) collective-permute-start(bf16[16,3584]{1,0:T(8,128)(2,1)S(1)} %get-tuple-element.24.refs_6_), channel_id=1, source_target_pairs={{0,4},{4,0},{8,12},{12,8},{1,5},{5,1},{9,13},{13,9},{2,6},{6,2},{1... | collective-permute-start | bytes 344072 | tf_op jit(solution)/shard_map/ppermute | solution.py:575
  15.3 0.0 collective-permute-done.3.b_ref
  15.3 0.2 combine_cache.1.cache_ref
  15.5 0.2 collective-permute-done.2.theirs_ref
  15.7 1.6 %collective-permute-start.4 = (bf16[16,3072]{1,0:T(8,128)(2,1)S(1)}, bf16[16,3072]{1,0:T(8,128)(2,1)S(1)}, u32[]{:S(2)}, u32[]{:S(2)}) collective-permute-start(bf16[16,3072]{1,0:T(8,128)(2,1)S(1)} %get-tuple-element.22.refs_2_), channel_id=1, source_target_pairs={{0,2},{1,3},{2,0},{3,1},{4,6},{5,7},{6,4},{7,5},{8,10},{9,11},{10,... | collective-permute-start | bytes 294920 | tf_op jit(solution)/shard_map/ppermute | solution.py:575
  17.3 1.6 %collective-permute-start.6 = (bf16[16,128]{1,0:T(8,128)(2,1)S(1)}, bf16[16,128]{1,0:T(8,128)(2,1)S(1)}, u32[]{:S(2)}, u32[]{:S(2)}) collective-permute-start(bf16[16,128]{1,0:T(8,128)(2,1)S(1)} %get-tuple-element.23), channel_id=1, source_target_pairs={{0,10},{1,11},{2,8},{3,9},{4,14},{5,15},{6,12},{7,13},{8,2},{9,3},... | collective-permute-start | bytes 12296 | tf_op jit(solution)/shard_map/ppermute | solution.py:627
  18.9 1.3 %collective-permute-start.5 = (bf16[16,128]{1,0:T(8,128)(2,1)S(1)}, bf16[16,128]{1,0:T(8,128)(2,1)S(1)}, u32[]{:S(2)}, u32[]{:S(2)}) collective-permute-start(bf16[16,128]{1,0:T(8,128)(2,1)S(1)} %get-tuple-element.23), channel_id=1, source_target_pairs={{0,8},{1,9},{2,10},{3,11},{4,12},{5,13},{6,14},{7,15},{8,0},{9,1},... | collective-permute-start | bytes 12296 | tf_op jit(solution)/shard_map/ppermute | solution.py:627
  20.2 2.5 %collective-permute-done.6.refs_5_ = bf16[16,128]{1,0:T(8,128)(2,1)S(1)} collective-permute-done((bf16[16,128]{1,0:T(8,128)(2,1)S(1)}, bf16[16,128]{1,0:T(8,128)(2,1)S(1)}, u32[]{:S(2)}, u32[]{:S(2)}) %collective-permute-start.6) | collective-permute-done | bytes 4128 | tf_op jit(solution)/shard_map/ppermute | solution.py:627
  22.7 0.7 %collective-permute-done.5.refs_4_ = bf16[16,128]{1,0:T(8,128)(2,1)S(1)} collective-permute-done((bf16[16,128]{1,0:T(8,128)(2,1)S(1)}, bf16[16,128]{1,0:T(8,128)(2,1)S(1)}, u32[]{:S(2)}, u32[]{:S(2)}) %collective-permute-start.5) | collective-permute-done | bytes 4128 | tf_op jit(solution)/shard_map/ppermute | solution.py:627
  23.4 0.0 collective-permute-done.7.refs_7_
  23.4 0.0 collective-permute-done.4.refs_3_
  23.4 0.8 %merge.1.mine_ref = bf16[16,2560]{1,0:T(8,128)(2,1)S(1)} custom-call(f32[24,128]{1,0:T(8,128)S(1)} %get-tuple-element.15.refs_1_.refs_0_, bf16[16,2048]{1,0:T(8,128)(2,1)S(1)} %get-tuple-element.16.refs_1_, bf16[16,3072]{1,0:T(8,128)(2,1)S(1)} %get-tuple-element.22.refs_2_, bf16[16,3072]{1,0:T(8,128)(2,1)S(1)} %collective-permute-done.4.refs_3_, ...), custom_call_target="tpu_custom_call" | custom-call | tf_op jit(solution)/shard_map/merge/pallas_call | solution.py:528
  24.2 0.1 collective-permute-start.8
  24.3 1.3 %collective-permute-done.8.theirs_ref = bf16[16,2560]{1,0:T(8,128)(2,1)S(1)} collective-permute-done((bf16[16,2560]{1,0:T(8,128)(2,1)S(1)}, bf16[16,2560]{1,0:T(8,128)(2,1)S(1)}, u32[]{:S(2)}, u32[]{:S(2)}) %collective-permute-start.8) | collective-permute-done | bytes 81952 | tf_op jit(solution)/shard_map/ppermute | solution.py:575
  25.5 0.7 %place.1 = (bf16[2,4,1024]{2,1,0:T(4,128)(2,1)}, bf16[2,4,1024]{2,1,0:T(4,128)(2,1)}, bf16[2,4,8192]{2,1,0:T(4,128)(2,1)}) custom-call(bf16[16,2560]{1,0:T(8,128)(2,1)S(1)} %merge.1.mine_ref, bf16[16,2560]{1,0:T(8,128)(2,1)S(1)} %collective-permute-done.8.theirs_ref), custom_call_target="tpu_custom_call" | custom-call | tf_op jit(solution)/shard_map/place/pallas_call | solution.py:560
  (5 shorter events, 0.0 us)
Async XLA Ops:
  2.6 11.4 %collective-permute-start = (bf16[16,4096]{1,0:T(8,128)(2,1)}, bf16[16,4096]{1,0:T(8,128)(2,1)S(1)}, u32[]{:S(2)}, u32[]{:S(2)}) collective-permute-start(bf16[16,4096]{1,0:T(8,128)(2,1)} %get-tuple-element.18.refs_2_), channel_id=1, source_target_pairs={{0,4},{4,0},{8,12},{12,8},{1,5},{5,1},{9,13},{13,9},{2,6},{6,2},{1... | collective-permute-start | bytes 393224 | tf_op jit(solution)/shard_map/ppermute | solution.py:575
  5.7 8.3 %copy-start = (bf16[16,3328]{1,0:T(8,128)(2,1)S(1)}, bf16[16,3328]{1,0:T(8,128)(2,1)}, u32[]{:S(2)}) copy-start(bf16[16,3328]{1,0:T(8,128)(2,1)} %get-tuple-element.14.x_hbm.refs_4_) | copy-start | bytes 319492
  5.7 8.4 %copy-start.1 = (bf16[16,4096]{1,0:T(8,128)(2,1)S(1)}, bf16[16,4096]{1,0:T(8,128)(2,1)}, u32[]{:S(2)}) copy-start(bf16[16,4096]{1,0:T(8,128)(2,1)} %get-tuple-element.18.refs_2_) | copy-start | bytes 393220
  5.7 8.3 %collective-permute-start.1 = (bf16[16,3328]{1,0:T(8,128)(2,1)}, bf16[16,3328]{1,0:T(8,128)(2,1)S(1)}, u32[]{:S(2)}, u32[]{:S(2)}) collective-permute-start(bf16[16,3328]{1,0:T(8,128)(2,1)} %get-tuple-element.14.x_hbm.refs_4_), channel_id=1, source_target_pairs={{0,8},{4,12},{8,0},{12,4},{1,9},{5,13},{9,1},{13,5},{2,10},{6,14},... | collective-permute-start | bytes 319496 | tf_op jit(solution)/shard_map/ppermute | solution.py:575
  13.9 1.4 %collective-permute-start.3 = (bf16[16,2304]{1,0:T(8,128)(2,1)S(1)}, bf16[16,2304]{1,0:T(8,128)(2,1)S(1)}, u32[]{:S(2)}, u32[]{:S(2)}) collective-permute-start(bf16[16,2304]{1,0:T(8,128)(2,1)S(1)} %get-tuple-element.21), channel_id=1, source_target_pairs={{0,1},{1,0},{2,3},{3,2},{4,5},{5,4},{6,7},{7,6},{8,9},{9,8},{10,11... | collective-permute-start | bytes 221192 | tf_op jit(solution)/shard_map/ppermute | solution.py:575
  14.4 1.3 %collective-permute-start.2 = (bf16[16,896]{1,0:T(8,128)(2,1)S(1)}, bf16[16,896]{1,0:T(8,128)(2,1)S(1)}, u32[]{:S(2)}, u32[]{:S(2)}) collective-permute-start(bf16[16,896]{1,0:T(8,128)(2,1)S(1)} %get-tuple-element.19._.mine_ref), channel_id=1, source_target_pairs={{0,1},{1,0},{2,3},{3,2},{4,5},{5,4},{6,7},{7,6},{8,9},{9,8},{10,11... | collective-permute-start | bytes 86024 | tf_op jit(solution)/shard_map/ppermute | solution.py:575
  14.9 8.5 %collective-permute-start.7 = (bf16[16,3584]{1,0:T(8,128)(2,1)S(1)}, bf16[16,3584]{1,0:T(8,128)(2,1)S(1)}, u32[]{:S(2)}, u32[]{:S(2)}) collective-permute-start(bf16[16,3584]{1,0:T(8,128)(2,1)S(1)} %get-tuple-element.24.refs_6_), channel_id=1, source_target_pairs={{0,4},{4,0},{8,12},{12,8},{1,5},{5,1},{9,13},{13,9},{2,6},{6,2},{1... | collective-permute-start | bytes 344072 | tf_op jit(solution)/shard_map/ppermute | solution.py:575
  15.7 7.6 %collective-permute-start.4 = (bf16[16,3072]{1,0:T(8,128)(2,1)S(1)}, bf16[16,3072]{1,0:T(8,128)(2,1)S(1)}, u32[]{:S(2)}, u32[]{:S(2)}) collective-permute-start(bf16[16,3072]{1,0:T(8,128)(2,1)S(1)} %get-tuple-element.22.refs_2_), channel_id=1, source_target_pairs={{0,2},{1,3},{2,0},{3,1},{4,6},{5,7},{6,4},{7,5},{8,10},{9,11},{10,... | collective-permute-start | bytes 294920 | tf_op jit(solution)/shard_map/ppermute | solution.py:575
  17.3 5.4 %collective-permute-start.6 = (bf16[16,128]{1,0:T(8,128)(2,1)S(1)}, bf16[16,128]{1,0:T(8,128)(2,1)S(1)}, u32[]{:S(2)}, u32[]{:S(2)}) collective-permute-start(bf16[16,128]{1,0:T(8,128)(2,1)S(1)} %get-tuple-element.23), channel_id=1, source_target_pairs={{0,10},{1,11},{2,8},{3,9},{4,14},{5,15},{6,12},{7,13},{8,2},{9,3},... | collective-permute-start | bytes 12296 | tf_op jit(solution)/shard_map/ppermute | solution.py:627
  18.9 4.5 %collective-permute-start.5 = (bf16[16,128]{1,0:T(8,128)(2,1)S(1)}, bf16[16,128]{1,0:T(8,128)(2,1)S(1)}, u32[]{:S(2)}, u32[]{:S(2)}) collective-permute-start(bf16[16,128]{1,0:T(8,128)(2,1)S(1)} %get-tuple-element.23), channel_id=1, source_target_pairs={{0,8},{1,9},{2,10},{3,11},{4,12},{5,13},{6,14},{7,15},{8,0},{9,1},... | collective-permute-start | bytes 12296 | tf_op jit(solution)/shard_map/ppermute | solution.py:627
  24.2 1.3 %collective-permute-start.8 = (bf16[16,2560]{1,0:T(8,128)(2,1)S(1)}, bf16[16,2560]{1,0:T(8,128)(2,1)S(1)}, u32[]{:S(2)}, u32[]{:S(2)}) collective-permute-start(bf16[16,2560]{1,0:T(8,128)(2,1)S(1)} %merge.1.mine_ref), channel_id=1, source_target_pairs={{0,1},{1,0},{2,3},{3,2},{4,5},{5,4},{6,7},{7,6},{8,9},{9,8},{10,11... | collective-permute-start | bytes 245768 | tf_op jit(solution)/shard_map/ppermute | solution.py:575

commit v10 on v9

--- a/solution.py
+++ b/solution.py
@@ -66,8 +66,9 @@
 
 
 def pack_kernel(*refs):
-    sources, outs, held = refs[:7], refs[7:9], refs[9:16]
-    (a_ref, b_ref), sems, out_sems = refs[16:18], refs[18], refs[19]
+    sources, outs, held = refs[:7], refs[7:10], refs[10:17]
+    (a_ref, b_ref, own_ref), sems, out_sems = refs[17:20], refs[20], refs[21]
+    targets = [*outs[:2], outs[2].at[:, pl.ds(0, own_ref.shape[1])]]
     copies = [
         pltpu.make_async_copy(source, target, sems.at[i])
         for i, (source, target) in enumerate(zip(sources, held))
@@ -76,7 +77,7 @@
         copy.start()
     backs = [
         pltpu.make_async_copy(source, target, out_sems.at[i])
-        for i, (source, target) in enumerate(zip((a_ref, b_ref), outs))
+        for i, (source, target) in enumerate(zip((a_ref, b_ref, own_ref), targets))
     ]
     kd_ref, vd_ref, x_ref, gain_ref, lengths_ref, ku_ref, vu_ref = held
     own, depth = kd_ref.shape
@@ -94,19 +95,20 @@
     scaled = jnp.concatenate(
         [x[:, i * 128 : (i + 1) * 128] * gain[i : i + 1] for i in range(depth // 128)], 1
     )
-    b_ref[:, : depth // 2] = jnp.concatenate(
-        [scaled[:, : depth // 2], scaled[:, depth // 2 :]], 0
-    ).astype(BF16)
+    scaled = jnp.concatenate([scaled[:, : depth // 2], scaled[:, depth // 2 :]], 0).astype(BF16)
+    b_ref[:, : depth // 2] = scaled
+    ups = jnp.concatenate([ku_ref[...], vu_ref[...]], 0).T.astype(BF16)
+    b_ref[:, depth // 2 :] = flat(ups)
+    backs[1].start()
+    own_ref[:, : depth // 2] = scaled
     row = lax.broadcasted_iota(jnp.int32, (16, 128), 0)
     lengths = lengths_ref[...]
     length = jnp.where(row % 8 < STEPS, lengths[:, :1], lengths[:, 1:])
     length = jnp.where(row < 8, length // 64 * 64, length % 64)
-    b_ref[:, depth // 2 : depth // 2 + 128] = length.astype(F32).astype(BF16)
+    own_ref[:, depth // 2 : depth // 2 + 128] = length.astype(F32).astype(BF16)
     squares = jnp.broadcast_to(jnp.sum(x * x, 1, keepdims=True), (8, 128))
-    b_ref[:, depth // 2 + 128 : depth // 2 + 256] = split(squares)
-    ups = jnp.concatenate([ku_ref[...], vu_ref[...]], 0).T.astype(BF16)
-    b_ref[:, depth // 2 + 256 :] = flat(ups)
-    backs[1].start()
+    own_ref[:, depth // 2 + 128 :] = split(squares)
+    backs[2].start()
     for copy in backs:
         copy.wait()
 
@@ -118,14 +120,16 @@
     ups = key_up.shape[0] * 8
     outs = [
         jax.ShapeDtypeStruct((16, 2 * depth), BF16),
+        jax.ShapeDtypeStruct((16, depth // 2 + ups), BF16),
         jax.ShapeDtypeStruct((16, depth // 2 + 256 + ups), BF16),
     ]
+    scratch = [*operands, *outs[:2], jax.ShapeDtypeStruct((16, depth // 2 + 256), BF16)]
     return pl.pallas_call(
         pack_kernel,
         in_specs=[HBM] * len(operands),
         out_specs=[HBM] * len(outs),
         out_shape=outs,
-        scratch_shapes=[pltpu.VMEM(o.shape, o.dtype) for o in operands + outs]
+        scratch_shapes=[pltpu.VMEM(o.shape, o.dtype) for o in scratch]
         + [pltpu.SemaphoreType.DMA((len(operands),)), pltpu.SemaphoreType.DMA((len(outs),))],
         compiler_params=pltpu.CompilerParams(vmem_limit_bytes=WHOLE_VMEM),
         name="pack",
@@ -142,9 +146,24 @@
     for bit in range(6):
         factor = ROPE_BASE ** (-(2.0 * 2**bit) / HD)
         frequency = jnp.where((pair >> bit) & 1 == 1, frequency * factor, frequency)
-    angle = position * frequency
-    sine = jnp.sin(angle)
-    return jnp.cos(angle), jnp.where(lane < HD // 2, -sine, sine)
+    cosine, sine = cosine_and_sine(position * frequency)
+    return cosine, jnp.where(lane < HD // 2, -sine, sine)
+
+
+def cosine_and_sine(angle):
+    turns = jnp.floor(angle * (2.0 / math.pi) + 0.5)
+    rest = ((angle - turns * 1.5703125) - turns * 4.8351287841796875e-4) - turns * 3.1391647e-7
+    square = rest * rest
+    sine = -1.9515295891e-4 * square + 8.3321608736e-3
+    sine = (sine * square - 1.6666654611e-1) * square * rest + rest
+    cosine = 2.443315711809948e-5 * square - 1.388731625493765e-3
+    cosine = (cosine * square + 4.166664568298827e-2) * square * square - 0.5 * square + 1.0
+    quadrant = turns.astype(jnp.int32)
+    swap_them = (quadrant & 1) == 1
+    cosine, sine = jnp.where(swap_them, sine, cosine), jnp.where(swap_them, cosine, sine)
+    cosine = jnp.where(((quadrant + 1) & 2) == 2, -cosine, cosine)
+    sine = jnp.where((quadrant & 2) == 2, -sine, sine)
+    return cosine, sine
 
 
 def rotated_rows(pairs, cosine, sine, q_ref, qrot_ref):
@@ -172,7 +191,7 @@
     return result
 
 
-def attend(pairs, limit, queries, k_ref, v_ref, wait_values, out_ref):
+def attend(pairs, limit, queries, k_ref, v_ref, between, out_ref):
     scores = []
     for i, p in enumerate(pairs):
         for s in range(2):
@@ -181,6 +200,7 @@
             place = lax.broadcasted_iota(jnp.int32, score.shape, 1)
             bound = limit[STEPS * s : STEPS * s + 1, :1].astype(jnp.int32)
             scores.append(jnp.where(place < bound, score, MASKED_SCORE))
+    between()
     scores = jnp.concatenate(scores, 0)
     top = rounded(jnp.maximum(jnp.max(scores, 1, keepdims=True), LOWEST_TOP))
     weights = jnp.exp2((scores - top) * EXPONENT).astype(BF16)
@@ -189,7 +209,6 @@
     columns = (top, high, total - high)
     lane8 = lax.broadcasted_iota(jnp.int32, (8, 128), 1)
     numers = []
-    wait_values()
     for i, p in enumerate(pairs):
         for s in range(2):
             at = slice(64 * (2 * i + s), 64 * (2 * i + s + 1))
@@ -232,7 +251,7 @@
     chunks = wk_hbm.shape[0] // CHUNK
     width = wk_hbm.shape[1]
     core = lax.axis_index("tensor") % 2
-    x_copy = pltpu.make_async_copy(x_hbm, x_ref, x_sem)
+    x_copy = pltpu.make_async_copy(x_hbm.at[:, pl.ds(0, x_ref.shape[1])], x_ref, x_sem)
     x_copy.start()
     groups = []
     for h in range(2):
@@ -281,24 +300,47 @@
         groups[h][0].wait()
         own = range(h * pairs // 2, (h + 1) * pairs // 2)
         queries.append(rotated_rows(own, cosine, sine, q_ref, None if h else qrot_ref))
+    parts = []
+
+    def project(chunk_ids):
+        for c in chunk_ids:
+            for copy in weights[c]:
+                copy.wait()
+        for c in chunk_ids:
+            at = slice(c * CHUNK, (c + 1) * CHUNK)
+            parts.append(
+                jnp.concatenate(
+                    [
+                        jnp.dot(x[:, at], ref[at], preferred_element_type=F32)
+                        for ref in (wk_ref, wv_ref)
+                    ],
+                    0,
+                )
+            )
+
+    early = range(chunks // 2)
+
+    def between(h):
+        groups[h][2].wait()
+        start(weights[chunks // 2 + h])
+        if h:
+            project(early)
+
     for h, out_ref in enumerate((keep_ref, send_ref)):
         groups[h][1].wait()
-        for copies in weights[1:2] if h == 0 else weights[2:]:
-            start(copies)
+        if h == 0:
+            for copies in weights[1 : chunks // 2]:
+                start(copies)
+        else:
+            for copies in weights[chunks // 2 + 2 :]:
+                start(copies)
         attend(
             range(h * pairs // 2, (h + 1) * pairs // 2),
-            limit, queries[h], k_ref, v_ref, groups[h][2].wait, out_ref,
+            limit, queries[h], k_ref, v_ref, functools.partial(between, h), out_ref,
         )
-    total = None
-    for c in range(chunks):
-        for copy in weights[c]:
-            copy.wait()
-        at = slice(c * CHUNK, (c + 1) * CHUNK)
-        part = jnp.concatenate(
-            [jnp.dot(x[:, at], ref[at], preferred_element_type=F32) for ref in (wk_ref, wv_ref)],
-            0,
-        )
-        total = part if total is None else total + part
+    for c in range(chunks // 2, chunks):
+        project([c])
+    total = functools.reduce(jnp.add, parts)
     lower, upper = total[:, : width // 2], total[:, width // 2 :]
     base_ref[:, : width // 2] = jnp.where(core == 0, lower, upper)
     base_ref[:, width // 2 :] = jnp.where(core == 0, upper, lower)
@@ -320,7 +362,8 @@
             jax.ShapeDtypeStruct((16, pairs // 2 * GROUP * HD), BF16),
             jax.ShapeDtypeStruct((24, 128), F32),
         ],
-        scratch_shapes=[pltpu.VMEM(o.shape, BF16) for o in operands]
+        scratch_shapes=[pltpu.VMEM((16, depth // 2 + 256), BF16)]
+        + [pltpu.VMEM(o.shape, BF16) for o in operands[1:]]
         + [
             pltpu.SemaphoreType.DMA,
             pltpu.SemaphoreType.DMA((2,)),
@@ -361,7 +404,7 @@
         out_ref[:, at : at + 128] = split(z[8 * i : 8 * i + 8])
     for ref in has:
         here = place // 2 == lax.axis_index("tensor") % 2
-        mine, far = (token[:, depth // 2 + 256 :].astype(F32) for token in tokens[:2])
+        mine, far = (token[:, depth // 2 :].astype(F32) for token in tokens[:2])
         ref[:, : mine.shape[1]] = jnp.where(here, mine, far).astype(BF16)
         ref[:, mine.shape[1] :] = jnp.zeros((16, ref.shape[1] - mine.shape[1]), BF16)
 
@@ -599,19 +642,21 @@
     n = len(partners)
     paired = n_dp == 4
 
-    own, tokens = pack(lengths, hidden, norm_gain, key_down, value_down, key_up, value_up)
-    near = to_dp(own, 1)
+    down, tokens, own = pack(
+        lengths, hidden, norm_gain, key_down, value_down, key_up, value_up
+    )
+    near = to_dp(down, 1)
     sent = [to_dp(tokens, d) for d in partners]
     keep, send, base, qrot, table = local(
-        tokens, queries, key_cache, value_cache, key_weight, value_weight
+        own, queries, key_cache, value_cache, key_weight, value_weight
     )
     received = to_tensor(send, 1)
     columns = UP_COLUMNS if paired else 0
-    message, *has = rank_products(rows, depth, columns, base, table, own, near, [tokens, *sent])
+    message, *has = rank_products(rows, depth, columns, base, table, down, near, [tokens, *sent])
     if paired:
         ups = [has[0], to_dp(has[0], 1)]
     else:
-        ups = lax.all_gather(tokens[:, depth // 2 + 256 :], "dp")
+        ups = lax.all_gather(tokens[:, depth // 2 :], "dp")
         ups = ups.reshape(n_dp, 16, -1, 128).transpose(0, 2, 1, 3)
         ups = ups.reshape(2, 2, 16, 16, 128).transpose(0, 1, 3, 2, 4).reshape(2, 2, 16, -1)
         ups = lax.dynamic_index_in_dim(ups, lax.axis_index("tensor") % 2, 0, keepdims=False)

time: 26.4 us -> 26.1 us (0.989)
  no operation moved by 1% of the time
where the time goes in v10:
time: 26.1 us; the launch traced here: 25.9 us
  starting transfers between devices  11.2 us (43%)
  Pallas kernels  9.5 us (36%)
  waiting for transfers between devices  4.46 us (17%)
  between operations  0.72 us (3%)
    ppermute x7, starting transfers between devices, swap(): return lax.ppermute(value, axis, [(i, i ^ distance) for i in range(n)])  8.31 us
    pallas_call x1, Pallas kernels, local(): pl.pallas_call(local_kernel, in_specs=[HBM] * 6, out_specs=[VMEM] * 5, ou...  5.53 us
    ppermute x2, waiting for transfers between devices, shards(): backs.append(lax.ppermute(reply, ('dp', 'tensor'), perm))  3.02 us
    ppermute x2, starting transfers between devices, shards(): backs.append(lax.ppermute(reply, ('dp', 'tensor'), perm))  2.9 us
    pallas_call x1, Pallas kernels, pack(): pl.pallas_call(pack_kernel, in_specs=[HBM] * len(operands), out_specs=[HB...  1.88 us
    ppermute x7, waiting for transfers between devices, swap(): return lax.ppermute(value, axis, [(i, i ^ distance) for i in range(n)])  1.45 us
    pallas_call x1, Pallas kernels, merge(): pl.pallas_call(functools.partial(merge_kernel, len(backs), paired, width_...  0.8 us
    pallas_call x1, Pallas kernels, place(): pl.pallas_call(place_kernel, in_specs=[VMEM] * 2, out_specs=[VMEM] * 3, o...  0.69 us
  transfers between devices with their start and end apart: 9, of which 4 were waited for; matrix products, arithmetic and copies ran while one was open for 0% of the time, Pallas kernels for 24%

profile of v10, /device:TPU:0, one launch (start us, length us, event | category | flops | bytes accessed | tf_op | source)
XLA Modules:
  0.0 25.9 jit_solution(9232842983079594093)
XLA Ops:
  0.6 1.9 %pack.1 = (bf16[16,4096]{1,0:T(8,128)(2,1)}, bf16[16,3072]{1,0:T(8,128)(2,1)}, bf16[16,3328]{1,0:T(8,128)(2,1)}) custom-call(f32[16,2048]{1,0:T(8,128)} %refs_0_.1, f32[16,2048]{1,0:T(8,128)} %refs_1_.1, bf16[2,4,2048]{2,1,0:T(4,128)(2,1)} %refs_2_.1, bf16[16,128]{1,0:T(8,128)(2,1)} %bitcast.6, s32[1,2]{1,0:T(1,128)} %bitcast.7, f32[64,256]{1,0:T(8,128)} %bitcast.4, ...), custom_call_target="tpu_custom_call" | custom-call | tf_op jit(solution)/shard_map/pack/pallas_call | solution.py:127
  2.5 3.1 %collective-permute-start = (bf16[16,4096]{1,0:T(8,128)(2,1)}, bf16[16,4096]{1,0:T(8,128)(2,1)S(1)}, u32[]{:S(2)}, u32[]{:S(2)}) collective-permute-start(bf16[16,4096]{1,0:T(8,128)(2,1)} %get-tuple-element.19.refs_2_), channel_id=1, source_target_pairs={{0,4},{4,0},{8,12},{12,8},{1,5},{5,1},{9,13},{13,9},{2,6},{6,2},{1... | collective-permute-start | bytes 393224 | tf_op jit(solution)/shard_map/ppermute | solution.py:618
  5.6 2.6 %collective-permute-start.1 = (bf16[16,3072]{1,0:T(8,128)(2,1)}, bf16[16,3072]{1,0:T(8,128)(2,1)S(1)}, u32[]{:S(2)}, u32[]{:S(2)}) collective-permute-start(bf16[16,3072]{1,0:T(8,128)(2,1)} %get-tuple-element.20.refs_4_), channel_id=1, source_target_pairs={{0,8},{4,12},{8,0},{12,4},{1,9},{5,13},{9,1},{13,5},{2,10},{6,14},... | collective-permute-start | bytes 294920 | tf_op jit(solution)/shard_map/ppermute | solution.py:618
  8.2 5.5 %local.1 = (bf16[16,2304]{1,0:T(8,128)(2,1)S(1)}, bf16[16,2304]{1,0:T(8,128)(2,1)S(1)}, f32[16,1024]{1,0:T(8,128)S(1)}, bf16[16,2048]{1,0:T(8,128)(2,1)S(1)}, f32[24,128]{1,0:T(8,128)S(1)}) custom-call(bf16[16,3328]{1,0:T(8,128)(2,1)} %get-tuple-element.15.x_hbm, bf16[2,4,8192]{2,1,0:T(4,128)(2,1)} %q_hbm.1, bf16[2,512,1024]{2,1,0:T(8,128)(2,1)} %k_hbm.1, ...), custom_call_target="tpu_custom_call" | custom-call | flops 402653184 | bytes 12582912 | tf_op jit(solution)/shard_map/local/pallas_call | solution.py:354
  13.7 0.1 collective-permute-start.3
  13.8 0.0 collective-permute-done.1.refs_5_
  13.8 0.0 collective-permute-done.refs_3_
  13.9 0.4 %rank_products.1 = (bf16[16,896]{1,0:T(8,128)(2,1)S(1)}, bf16[16,3584]{1,0:T(8,128)(2,1)S(1)}) custom-call(f32[16,1024]{1,0:T(8,128)S(1)} %get-tuple-element.18.refs_0_.base_ref, f32[24,128]{1,0:T(8,128)S(1)} %get-tuple-element.16.refs_1_.refs_0_, bf16[16,4096]{1,0:T(8,128)(2,1)S(1)} %copy-done, bf16[16,4096]{1,0:T(8,128)(2,1)S(1)} %collective-permute-done.refs_3_, ...), custom_call_target="tpu_custom_call" | custom-call | tf_op jit(solution)/shard_map/rank_products/pallas_call | solution.py:417
  14.2 0.5 %collective-permute-start.2 = (bf16[16,896]{1,0:T(8,128)(2,1)S(1)}, bf16[16,896]{1,0:T(8,128)(2,1)S(1)}, u32[]{:S(2)}, u32[]{:S(2)}) collective-permute-start(bf16[16,896]{1,0:T(8,128)(2,1)S(1)} %get-tuple-element.21._.mine_ref), channel_id=1, source_target_pairs={{0,1},{1,0},{2,3},{3,2},{4,5},{5,4},{6,7},{7,6},{8,9},{9,8},{10,11... | collective-permute-start | bytes 86024 | tf_op jit(solution)/shard_map/ppermute | solution.py:618
  14.7 0.4 %collective-permute-start.7 = (bf16[16,3584]{1,0:T(8,128)(2,1)S(1)}, bf16[16,3584]{1,0:T(8,128)(2,1)S(1)}, u32[]{:S(2)}, u32[]{:S(2)}) collective-permute-start(bf16[16,3584]{1,0:T(8,128)(2,1)S(1)} %get-tuple-element.26.refs_6_), channel_id=1, source_target_pairs={{0,4},{4,0},{8,12},{12,8},{1,5},{5,1},{9,13},{13,9},{2,6},{6,2},{1... | collective-permute-start | bytes 344072 | tf_op jit(solution)/shard_map/ppermute | solution.py:618
  15.2 0.0 collective-permute-done.3.b_ref
  15.2 0.2 combine_cache.1.cache_ref
  15.4 0.2 collective-permute-done.2.theirs_ref
  15.6 1.6 %collective-permute-start.4 = (bf16[16,3072]{1,0:T(8,128)(2,1)S(1)}, bf16[16,3072]{1,0:T(8,128)(2,1)S(1)}, u32[]{:S(2)}, u32[]{:S(2)}) collective-permute-start(bf16[16,3072]{1,0:T(8,128)(2,1)S(1)} %get-tuple-element.24.refs_2_), channel_id=1, source_target_pairs={{0,2},{1,3},{2,0},{3,1},{4,6},{5,7},{6,4},{7,5},{8,10},{9,11},{10,... | collective-permute-start | bytes 294920 | tf_op jit(solution)/shard_map/ppermute | solution.py:618
  17.1 1.4 %collective-permute-start.6 = (bf16[16,128]{1,0:T(8,128)(2,1)S(1)}, bf16[16,128]{1,0:T(8,128)(2,1)S(1)}, u32[]{:S(2)}, u32[]{:S(2)}) collective-permute-start(bf16[16,128]{1,0:T(8,128)(2,1)S(1)} %get-tuple-element.25), channel_id=1, source_target_pairs={{0,10},{1,11},{2,8},{3,9},{4,14},{5,15},{6,12},{7,13},{8,2},{9,3},... | collective-permute-start | bytes 12296 | tf_op jit(solution)/shard_map/ppermute | solution.py:672
  18.5 1.5 %collective-permute-start.5 = (bf16[16,128]{1,0:T(8,128)(2,1)S(1)}, bf16[16,128]{1,0:T(8,128)(2,1)S(1)}, u32[]{:S(2)}, u32[]{:S(2)}) collective-permute-start(bf16[16,128]{1,0:T(8,128)(2,1)S(1)} %get-tuple-element.25), channel_id=1, source_target_pairs={{0,8},{1,9},{2,10},{3,11},{4,12},{5,13},{6,14},{7,15},{8,0},{9,1},... | collective-permute-start | bytes 12296 | tf_op jit(solution)/shard_map/ppermute | solution.py:672
  20.0 2.5 %collective-permute-done.6.refs_5_ = bf16[16,128]{1,0:T(8,128)(2,1)S(1)} collective-permute-done((bf16[16,128]{1,0:T(8,128)(2,1)S(1)}, bf16[16,128]{1,0:T(8,128)(2,1)S(1)}, u32[]{:S(2)}, u32[]{:S(2)}) %collective-permute-start.6) | collective-permute-done | bytes 4128 | tf_op jit(solution)/shard_map/ppermute | solution.py:672
  22.5 0.5 %collective-permute-done.5.refs_4_ = bf16[16,128]{1,0:T(8,128)(2,1)S(1)} collective-permute-done((bf16[16,128]{1,0:T(8,128)(2,1)S(1)}, bf16[16,128]{1,0:T(8,128)(2,1)S(1)}, u32[]{:S(2)}, u32[]{:S(2)}) %collective-permute-start.5) | collective-permute-done | bytes 4128 | tf_op jit(solution)/shard_map/ppermute | solution.py:672
  23.0 0.0 collective-permute-done.7.refs_7_
  23.1 0.0 collective-permute-done.4.refs_3_
  23.1 0.8 %merge.1.mine_ref = bf16[16,2560]{1,0:T(8,128)(2,1)S(1)} custom-call(f32[24,128]{1,0:T(8,128)S(1)} %get-tuple-element.16.refs_1_.refs_0_, bf16[16,2048]{1,0:T(8,128)(2,1)S(1)} %get-tuple-element.17.refs_1_, bf16[16,3072]{1,0:T(8,128)(2,1)S(1)} %get-tuple-element.24.refs_2_, bf16[16,3072]{1,0:T(8,128)(2,1)S(1)} %collective-permute-done.4.refs_3_, ...), custom_call_target="tpu_custom_call" | custom-call | tf_op jit(solution)/shard_map/merge/pallas_call | solution.py:571
  23.9 0.1 collective-permute-start.8
  23.9 1.3 %collective-permute-done.8.theirs_ref = bf16[16,2560]{1,0:T(8,128)(2,1)S(1)} collective-permute-done((bf16[16,2560]{1,0:T(8,128)(2,1)S(1)}, bf16[16,2560]{1,0:T(8,128)(2,1)S(1)}, u32[]{:S(2)}, u32[]{:S(2)}) %collective-permute-start.8) | collective-permute-done | bytes 81952 | tf_op jit(solution)/shard_map/ppermute | solution.py:618
  25.2 0.7 %place.1 = (bf16[2,4,1024]{2,1,0:T(4,128)(2,1)}, bf16[2,4,1024]{2,1,0:T(4,128)(2,1)}, bf16[2,4,8192]{2,1,0:T(4,128)(2,1)}) custom-call(bf16[16,2560]{1,0:T(8,128)(2,1)S(1)} %merge.1.mine_ref, bf16[16,2560]{1,0:T(8,128)(2,1)S(1)} %collective-permute-done.8.theirs_ref), custom_call_target="tpu_custom_call" | custom-call | tf_op jit(solution)/shard_map/place/pallas_call | solution.py:603
  (5 shorter events, 0.0 us)
Async XLA Ops:
  2.5 11.3 %collective-permute-start = (bf16[16,4096]{1,0:T(8,128)(2,1)}, bf16[16,4096]{1,0:T(8,128)(2,1)S(1)}, u32[]{:S(2)}, u32[]{:S(2)}) collective-permute-start(bf16[16,4096]{1,0:T(8,128)(2,1)} %get-tuple-element.19.refs_2_), channel_id=1, source_target_pairs={{0,4},{4,0},{8,12},{12,8},{1,5},{5,1},{9,13},{13,9},{2,6},{6,2},{1... | collective-permute-start | bytes 393224 | tf_op jit(solution)/shard_map/ppermute | solution.py:618
  5.6 8.2 %collective-permute-start.1 = (bf16[16,3072]{1,0:T(8,128)(2,1)}, bf16[16,3072]{1,0:T(8,128)(2,1)S(1)}, u32[]{:S(2)}, u32[]{:S(2)}) collective-permute-start(bf16[16,3072]{1,0:T(8,128)(2,1)} %get-tuple-element.20.refs_4_), channel_id=1, source_target_pairs={{0,8},{4,12},{8,0},{12,4},{1,9},{5,13},{9,1},{13,5},{2,10},{6,14},... | collective-permute-start | bytes 294920 | tf_op jit(solution)/shard_map/ppermute | solution.py:618
  8.2 5.6 %copy-start = (bf16[16,4096]{1,0:T(8,128)(2,1)S(1)}, bf16[16,4096]{1,0:T(8,128)(2,1)}, u32[]{:S(2)}) copy-start(bf16[16,4096]{1,0:T(8,128)(2,1)} %get-tuple-element.19.refs_2_) | copy-start | bytes 393220
  8.2 5.7 %copy-start.1 = (bf16[16,3072]{1,0:T(8,128)(2,1)S(1)}, bf16[16,3072]{1,0:T(8,128)(2,1)}, u32[]{:S(2)}) copy-start(bf16[16,3072]{1,0:T(8,128)(2,1)} %get-tuple-element.20.refs_4_) | copy-start | bytes 294916
  13.7 1.4 %collective-permute-start.3 = (bf16[16,2304]{1,0:T(8,128)(2,1)S(1)}, bf16[16,2304]{1,0:T(8,128)(2,1)S(1)}, u32[]{:S(2)}, u32[]{:S(2)}) collective-permute-start(bf16[16,2304]{1,0:T(8,128)(2,1)S(1)} %get-tuple-element.23), channel_id=1, source_target_pairs={{0,1},{1,0},{2,3},{3,2},{4,5},{5,4},{6,7},{7,6},{8,9},{9,8},{10,11... | collective-permute-start | bytes 221192 | tf_op jit(solution)/shard_map/ppermute | solution.py:618
  14.2 1.3 %collective-permute-start.2 = (bf16[16,896]{1,0:T(8,128)(2,1)S(1)}, bf16[16,896]{1,0:T(8,128)(2,1)S(1)}, u32[]{:S(2)}, u32[]{:S(2)}) collective-permute-start(bf16[16,896]{1,0:T(8,128)(2,1)S(1)} %get-tuple-element.21._.mine_ref), channel_id=1, source_target_pairs={{0,1},{1,0},{2,3},{3,2},{4,5},{5,4},{6,7},{7,6},{8,9},{9,8},{10,11... | collective-permute-start | bytes 86024 | tf_op jit(solution)/shard_map/ppermute | solution.py:618
  14.7 8.3 %collective-permute-start.7 = (bf16[16,3584]{1,0:T(8,128)(2,1)S(1)}, bf16[16,3584]{1,0:T(8,128)(2,1)S(1)}, u32[]{:S(2)}, u32[]{:S(2)}) collective-permute-start(bf16[16,3584]{1,0:T(8,128)(2,1)S(1)} %get-tuple-element.26.refs_6_), channel_id=1, source_target_pairs={{0,4},{4,0},{8,12},{12,8},{1,5},{5,1},{9,13},{13,9},{2,6},{6,2},{1... | collective-permute-start | bytes 344072 | tf_op jit(solution)/shard_map/ppermute | solution.py:618
  15.6 7.5 %collective-permute-start.4 = (bf16[16,3072]{1,0:T(8,128)(2,1)S(1)}, bf16[16,3072]{1,0:T(8,128)(2,1)S(1)}, u32[]{:S(2)}, u32[]{:S(2)}) collective-permute-start(bf16[16,3072]{1,0:T(8,128)(2,1)S(1)} %get-tuple-element.24.refs_2_), channel_id=1, source_target_pairs={{0,2},{1,3},{2,0},{3,1},{4,6},{5,7},{6,4},{7,5},{8,10},{9,11},{10,... | collective-permute-start | bytes 294920 | tf_op jit(solution)/shard_map/ppermute | solution.py:618
  17.1 5.4 %collective-permute-start.6 = (bf16[16,128]{1,0:T(8,128)(2,1)S(1)}, bf16[16,128]{1,0:T(8,128)(2,1)S(1)}, u32[]{:S(2)}, u32[]{:S(2)}) collective-permute-start(bf16[16,128]{1,0:T(8,128)(2,1)S(1)} %get-tuple-element.25), channel_id=1, source_target_pairs={{0,10},{1,11},{2,8},{3,9},{4,14},{5,15},{6,12},{7,13},{8,2},{9,3},... | collective-permute-start | bytes 12296 | tf_op jit(solution)/shard_map/ppermute | solution.py:672
  18.5 4.5 %collective-permute-start.5 = (bf16[16,128]{1,0:T(8,128)(2,1)S(1)}, bf16[16,128]{1,0:T(8,128)(2,1)S(1)}, u32[]{:S(2)}, u32[]{:S(2)}) collective-permute-start(bf16[16,128]{1,0:T(8,128)(2,1)S(1)} %get-tuple-element.25), channel_id=1, source_target_pairs={{0,8},{1,9},{2,10},{3,11},{4,12},{5,13},{6,14},{7,15},{8,0},{9,1},... | collective-permute-start | bytes 12296 | tf_op jit(solution)/shard_map/ppermute | solution.py:672
  23.9 1.3 %collective-permute-start.8 = (bf16[16,2560]{1,0:T(8,128)(2,1)S(1)}, bf16[16,2560]{1,0:T(8,128)(2,1)S(1)}, u32[]{:S(2)}, u32[]{:S(2)}) collective-permute-start(bf16[16,2560]{1,0:T(8,128)(2,1)S(1)} %merge.1.mine_ref), channel_id=1, source_target_pairs={{0,1},{1,0},{2,3},{3,2},{4,5},{5,4},{6,7},{7,6},{8,9},{9,8},{10,11... | collective-permute-start | bytes 245768 | tf_op jit(solution)/shard_map/ppermute | solution.py:618

commit v11 on v10

--- a/solution.py
+++ b/solution.py
@@ -191,15 +191,13 @@
     return result
 
 
-def attend(pairs, limit, queries, k_ref, v_ref, between, out_ref):
+def attend(pairs, masks, queries, k_ref, v_ref, between, out_ref):
     scores = []
     for i, p in enumerate(pairs):
         for s in range(2):
             keys = k_ref[s, :, 2 * p * HD : 2 * (p + 1) * HD]
             score = lax.dot_general(queries[2 * i + s], keys, NT, preferred_element_type=F32)
-            place = lax.broadcasted_iota(jnp.int32, score.shape, 1)
-            bound = limit[STEPS * s : STEPS * s + 1, :1].astype(jnp.int32)
-            scores.append(jnp.where(place < bound, score, MASKED_SCORE))
+            scores.append(score + jnp.concatenate([masks[s]] * (score.shape[0] // 8), 0))
     between()
     scores = jnp.concatenate(scores, 0)
     top = rounded(jnp.maximum(jnp.max(scores, 1, keepdims=True), LOWEST_TOP))
@@ -295,6 +293,10 @@
     cosine, sine = tables(length)
     table_ref[...] = jnp.concatenate([joined(x_ref[:, half + 128 : half + 256]), cosine, sine], 0)
     limit = length - (lax.axis_index("tensor") * k_hbm.shape[1]).astype(F32)
+    place = lax.broadcasted_iota(jnp.int32, (8, k_hbm.shape[1]), 1).astype(F32)
+    masks = [
+        jnp.where(place < limit[STEPS * s : STEPS * s + 1, :1], 0.0, MASKED_SCORE) for s in range(2)
+    ]
     queries = []
     for h in range(2):
         groups[h][0].wait()
@@ -302,44 +304,32 @@
         queries.append(rotated_rows(own, cosine, sine, q_ref, None if h else qrot_ref))
     parts = []
 
-    def project(chunk_ids):
-        for c in chunk_ids:
-            for copy in weights[c]:
-                copy.wait()
-        for c in chunk_ids:
-            at = slice(c * CHUNK, (c + 1) * CHUNK)
-            parts.append(
-                jnp.concatenate(
-                    [
-                        jnp.dot(x[:, at], ref[at], preferred_element_type=F32)
-                        for ref in (wk_ref, wv_ref)
-                    ],
-                    0,
-                )
-            )
-
-    early = range(chunks // 2)
+    def project(c):
+        at = slice(c * CHUNK, (c + 1) * CHUNK)
+        halves = []
+        for copy, ref in zip(weights[c], (wk_ref, wv_ref)):
+            copy.wait()
+            halves.append(jnp.dot(x[:, at], ref[at], preferred_element_type=F32))
+        parts.append(jnp.concatenate(halves, 0))
 
     def between(h):
         groups[h][2].wait()
-        start(weights[chunks // 2 + h])
-        if h:
-            project(early)
+        if h == 0:
+            start(weights[chunks // 2])
+        else:
+            for c in range(chunks // 2):
+                project(c)
 
     for h, out_ref in enumerate((keep_ref, send_ref)):
         groups[h][1].wait()
-        if h == 0:
-            for copies in weights[1 : chunks // 2]:
-                start(copies)
-        else:
-            for copies in weights[chunks // 2 + 2 :]:
-                start(copies)
+        for copies in weights[chunks // 2 + 1 :] if h else weights[1 : chunks // 2]:
+            start(copies)
         attend(
             range(h * pairs // 2, (h + 1) * pairs // 2),
-            limit, queries[h], k_ref, v_ref, functools.partial(between, h), out_ref,
+            masks, queries[h], k_ref, v_ref, functools.partial(between, h), out_ref,
         )
     for c in range(chunks // 2, chunks):
-        project([c])
+        project(c)
     total = functools.reduce(jnp.add, parts)
     lower, upper = total[:, : width // 2], total[:, width // 2 :]
     base_ref[:, : width // 2] = jnp.where(core == 0, lower, upper)

time: 26.1 us -> 26.1 us (level)
  transfers between devices with their start and end apart: 9 -> 9, of which waited for: 4 -> 4; matrix products, arithmetic and copies ran while one was open for 0% -> 0% of each run, Pallas kernels for 24% -> 23%
where the time goes in v11:
time: 26.1 us; the launch traced here: 25.9 us
  starting transfers between devices  11.2 us (43%)
  Pallas kernels  9.36 us (36%)
  waiting for transfers between devices  4.6 us (18%)
  between operations  0.72 us (3%)
    ppermute x7, starting transfers between devices, swap(): return lax.ppermute(value, axis, [(i, i ^ distance) for i in range(n)])  8.31 us
    pallas_call x1, Pallas kernels, local(): pl.pallas_call(local_kernel, in_specs=[HBM] * 6, out_specs=[VMEM] * 5, ou...  5.39 us
    ppermute x2, waiting for transfers between devices, shards(): backs.append(lax.ppermute(reply, ('dp', 'tensor'), perm))  3.16 us
    ppermute x2, starting transfers between devices, shards(): backs.append(lax.ppermute(reply, ('dp', 'tensor'), perm))  2.9 us
    pallas_call x1, Pallas kernels, pack(): pl.pallas_call(pack_kernel, in_specs=[HBM] * len(operands), out_specs=[HB...  1.88 us
    ppermute x7, waiting for transfers between devices, swap(): return lax.ppermute(value, axis, [(i, i ^ distance) for i in range(n)])  1.45 us
    pallas_call x1, Pallas kernels, merge(): pl.pallas_call(functools.partial(merge_kernel, len(backs), paired, width_...  0.8 us
    pallas_call x1, Pallas kernels, place(): pl.pallas_call(place_kernel, in_specs=[VMEM] * 2, out_specs=[VMEM] * 3, o...  0.69 us
  transfers between devices with their start and end apart: 9, of which 4 were waited for; matrix products, arithmetic and copies ran while one was open for 0% of the time, Pallas kernels for 23%

profile of v11, /device:TPU:0, one launch (start us, length us, event | category | flops | bytes accessed | tf_op | source)
XLA Modules:
  0.0 25.9 jit_solution(17864367527803364370)
XLA Ops:
  0.6 1.9 %pack.1 = (bf16[16,4096]{1,0:T(8,128)(2,1)}, bf16[16,3072]{1,0:T(8,128)(2,1)}, bf16[16,3328]{1,0:T(8,128)(2,1)}) custom-call(f32[16,2048]{1,0:T(8,128)} %refs_0_.1, f32[16,2048]{1,0:T(8,128)} %refs_1_.1, bf16[2,4,2048]{2,1,0:T(4,128)(2,1)} %refs_2_.1, bf16[16,128]{1,0:T(8,128)(2,1)} %bitcast.6, s32[1,2]{1,0:T(1,128)} %bitcast.7, f32[64,256]{1,0:T(8,128)} %bitcast.4, ...), custom_call_target="tpu_custom_call" | custom-call | tf_op jit(solution)/shard_map/pack/pallas_call | solution.py:127
  2.5 3.1 %collective-permute-start = (bf16[16,4096]{1,0:T(8,128)(2,1)}, bf16[16,4096]{1,0:T(8,128)(2,1)S(1)}, u32[]{:S(2)}, u32[]{:S(2)}) collective-permute-start(bf16[16,4096]{1,0:T(8,128)(2,1)} %get-tuple-element.19.refs_2_), channel_id=1, source_target_pairs={{0,4},{4,0},{8,12},{12,8},{1,5},{5,1},{9,13},{13,9},{2,6},{6,2},{1... | collective-permute-start | bytes 393224 | tf_op jit(solution)/shard_map/ppermute | solution.py:608
  5.6 2.6 %collective-permute-start.1 = (bf16[16,3072]{1,0:T(8,128)(2,1)}, bf16[16,3072]{1,0:T(8,128)(2,1)S(1)}, u32[]{:S(2)}, u32[]{:S(2)}) collective-permute-start(bf16[16,3072]{1,0:T(8,128)(2,1)} %get-tuple-element.20.refs_4_), channel_id=1, source_target_pairs={{0,8},{4,12},{8,0},{12,4},{1,9},{5,13},{9,1},{13,5},{2,10},{6,14},... | collective-permute-start | bytes 294920 | tf_op jit(solution)/shard_map/ppermute | solution.py:608
  8.2 5.4 %local.1 = (bf16[16,2304]{1,0:T(8,128)(2,1)S(1)}, bf16[16,2304]{1,0:T(8,128)(2,1)S(1)}, f32[16,1024]{1,0:T(8,128)S(1)}, bf16[16,2048]{1,0:T(8,128)(2,1)S(1)}, f32[24,128]{1,0:T(8,128)S(1)}) custom-call(bf16[16,3328]{1,0:T(8,128)(2,1)} %get-tuple-element.15.x_hbm, bf16[2,4,8192]{2,1,0:T(4,128)(2,1)} %q_hbm.1, bf16[2,512,1024]{2,1,0:T(8,128)(2,1)} %k_hbm.1, ...), custom_call_target="tpu_custom_call" | custom-call | flops 402653184 | bytes 12582912 | tf_op jit(solution)/shard_map/local/pallas_call | solution.py:344
  13.6 0.1 collective-permute-start.3
  13.7 0.0 collective-permute-done.1.refs_5_
  13.7 0.0 collective-permute-done.refs_3_
  13.7 0.4 %rank_products.1 = (bf16[16,896]{1,0:T(8,128)(2,1)S(1)}, bf16[16,3584]{1,0:T(8,128)(2,1)S(1)}) custom-call(f32[16,1024]{1,0:T(8,128)S(1)} %get-tuple-element.18.refs_0_.base_ref, f32[24,128]{1,0:T(8,128)S(1)} %get-tuple-element.16.refs_1_.refs_0_, bf16[16,4096]{1,0:T(8,128)(2,1)S(1)} %copy-done, bf16[16,4096]{1,0:T(8,128)(2,1)S(1)} %collective-permute-done.refs_3_, ...), custom_call_target="tpu_custom_call" | custom-call | tf_op jit(solution)/shard_map/rank_products/pallas_call | solution.py:407
  14.1 0.5 %collective-permute-start.2 = (bf16[16,896]{1,0:T(8,128)(2,1)S(1)}, bf16[16,896]{1,0:T(8,128)(2,1)S(1)}, u32[]{:S(2)}, u32[]{:S(2)}) collective-permute-start(bf16[16,896]{1,0:T(8,128)(2,1)S(1)} %get-tuple-element.21._.mine_ref), channel_id=1, source_target_pairs={{0,1},{1,0},{2,3},{3,2},{4,5},{5,4},{6,7},{7,6},{8,9},{9,8},{10,11... | collective-permute-start | bytes 86024 | tf_op jit(solution)/shard_map/ppermute | solution.py:608
  14.6 0.4 %collective-permute-start.7 = (bf16[16,3584]{1,0:T(8,128)(2,1)S(1)}, bf16[16,3584]{1,0:T(8,128)(2,1)S(1)}, u32[]{:S(2)}, u32[]{:S(2)}) collective-permute-start(bf16[16,3584]{1,0:T(8,128)(2,1)S(1)} %get-tuple-element.26.refs_6_), channel_id=1, source_target_pairs={{0,4},{4,0},{8,12},{12,8},{1,5},{5,1},{9,13},{13,9},{2,6},{6,2},{1... | collective-permute-start | bytes 344072 | tf_op jit(solution)/shard_map/ppermute | solution.py:608
  15.0 0.0 collective-permute-done.3.b_ref
  15.0 0.2 combine_cache.1.cache_ref
  15.2 0.2 collective-permute-done.2.theirs_ref
  15.4 1.6 %collective-permute-start.4 = (bf16[16,3072]{1,0:T(8,128)(2,1)S(1)}, bf16[16,3072]{1,0:T(8,128)(2,1)S(1)}, u32[]{:S(2)}, u32[]{:S(2)}) collective-permute-start(bf16[16,3072]{1,0:T(8,128)(2,1)S(1)} %get-tuple-element.24.refs_2_), channel_id=1, source_target_pairs={{0,2},{1,3},{2,0},{3,1},{4,6},{5,7},{6,4},{7,5},{8,10},{9,11},{10,... | collective-permute-start | bytes 294920 | tf_op jit(solution)/shard_map/ppermute | solution.py:608
  17.0 1.5 %collective-permute-start.6 = (bf16[16,128]{1,0:T(8,128)(2,1)S(1)}, bf16[16,128]{1,0:T(8,128)(2,1)S(1)}, u32[]{:S(2)}, u32[]{:S(2)}) collective-permute-start(bf16[16,128]{1,0:T(8,128)(2,1)S(1)} %get-tuple-element.25), channel_id=1, source_target_pairs={{0,10},{1,11},{2,8},{3,9},{4,14},{5,15},{6,12},{7,13},{8,2},{9,3},... | collective-permute-start | bytes 12296 | tf_op jit(solution)/shard_map/ppermute | solution.py:662
  18.5 1.4 %collective-permute-start.5 = (bf16[16,128]{1,0:T(8,128)(2,1)S(1)}, bf16[16,128]{1,0:T(8,128)(2,1)S(1)}, u32[]{:S(2)}, u32[]{:S(2)}) collective-permute-start(bf16[16,128]{1,0:T(8,128)(2,1)S(1)} %get-tuple-element.25), channel_id=1, source_target_pairs={{0,8},{1,9},{2,10},{3,11},{4,12},{5,13},{6,14},{7,15},{8,0},{9,1},... | collective-permute-start | bytes 12296 | tf_op jit(solution)/shard_map/ppermute | solution.py:662
  19.9 2.5 %collective-permute-done.6.refs_5_ = bf16[16,128]{1,0:T(8,128)(2,1)S(1)} collective-permute-done((bf16[16,128]{1,0:T(8,128)(2,1)S(1)}, bf16[16,128]{1,0:T(8,128)(2,1)S(1)}, u32[]{:S(2)}, u32[]{:S(2)}) %collective-permute-start.6) | collective-permute-done | bytes 4128 | tf_op jit(solution)/shard_map/ppermute | solution.py:662
  22.4 0.6 %collective-permute-done.5.refs_4_ = bf16[16,128]{1,0:T(8,128)(2,1)S(1)} collective-permute-done((bf16[16,128]{1,0:T(8,128)(2,1)S(1)}, bf16[16,128]{1,0:T(8,128)(2,1)S(1)}, u32[]{:S(2)}, u32[]{:S(2)}) %collective-permute-start.5) | collective-permute-done | bytes 4128 | tf_op jit(solution)/shard_map/ppermute | solution.py:662
  23.0 0.0 collective-permute-done.7.refs_7_
  23.1 0.0 collective-permute-done.4.refs_3_
  23.1 0.8 %merge.1.mine_ref = bf16[16,2560]{1,0:T(8,128)(2,1)S(1)} custom-call(f32[24,128]{1,0:T(8,128)S(1)} %get-tuple-element.16.refs_1_.refs_0_, bf16[16,2048]{1,0:T(8,128)(2,1)S(1)} %get-tuple-element.17.refs_1_, bf16[16,3072]{1,0:T(8,128)(2,1)S(1)} %get-tuple-element.24.refs_2_, bf16[16,3072]{1,0:T(8,128)(2,1)S(1)} %collective-permute-done.4.refs_3_, ...), custom_call_target="tpu_custom_call" | custom-call | tf_op jit(solution)/shard_map/merge/pallas_call | solution.py:561
  23.9 0.1 collective-permute-start.8
  23.9 1.3 %collective-permute-done.8.theirs_ref = bf16[16,2560]{1,0:T(8,128)(2,1)S(1)} collective-permute-done((bf16[16,2560]{1,0:T(8,128)(2,1)S(1)}, bf16[16,2560]{1,0:T(8,128)(2,1)S(1)}, u32[]{:S(2)}, u32[]{:S(2)}) %collective-permute-start.8) | collective-permute-done | bytes 81952 | tf_op jit(solution)/shard_map/ppermute | solution.py:608
  25.2 0.7 %place.1 = (bf16[2,4,1024]{2,1,0:T(4,128)(2,1)}, bf16[2,4,1024]{2,1,0:T(4,128)(2,1)}, bf16[2,4,8192]{2,1,0:T(4,128)(2,1)}) custom-call(bf16[16,2560]{1,0:T(8,128)(2,1)S(1)} %merge.1.mine_ref, bf16[16,2560]{1,0:T(8,128)(2,1)S(1)} %collective-permute-done.8.theirs_ref), custom_call_target="tpu_custom_call" | custom-call | tf_op jit(solution)/shard_map/place/pallas_call | solution.py:593
  (5 shorter events, 0.0 us)
Async XLA Ops:
  2.5 11.2 %collective-permute-start = (bf16[16,4096]{1,0:T(8,128)(2,1)}, bf16[16,4096]{1,0:T(8,128)(2,1)S(1)}, u32[]{:S(2)}, u32[]{:S(2)}) collective-permute-start(bf16[16,4096]{1,0:T(8,128)(2,1)} %get-tuple-element.19.refs_2_), channel_id=1, source_target_pairs={{0,4},{4,0},{8,12},{12,8},{1,5},{5,1},{9,13},{13,9},{2,6},{6,2},{1... | collective-permute-start | bytes 393224 | tf_op jit(solution)/shard_map/ppermute | solution.py:608
  5.6 8.1 %collective-permute-start.1 = (bf16[16,3072]{1,0:T(8,128)(2,1)}, bf16[16,3072]{1,0:T(8,128)(2,1)S(1)}, u32[]{:S(2)}, u32[]{:S(2)}) collective-permute-start(bf16[16,3072]{1,0:T(8,128)(2,1)} %get-tuple-element.20.refs_4_), channel_id=1, source_target_pairs={{0,8},{4,12},{8,0},{12,4},{1,9},{5,13},{9,1},{13,5},{2,10},{6,14},... | collective-permute-start | bytes 294920 | tf_op jit(solution)/shard_map/ppermute | solution.py:608
  8.2 5.5 %copy-start = (bf16[16,4096]{1,0:T(8,128)(2,1)S(1)}, bf16[16,4096]{1,0:T(8,128)(2,1)}, u32[]{:S(2)}) copy-start(bf16[16,4096]{1,0:T(8,128)(2,1)} %get-tuple-element.19.refs_2_) | copy-start | bytes 393220
  8.2 5.5 %copy-start.1 = (bf16[16,3072]{1,0:T(8,128)(2,1)S(1)}, bf16[16,3072]{1,0:T(8,128)(2,1)}, u32[]{:S(2)}) copy-start(bf16[16,3072]{1,0:T(8,128)(2,1)} %get-tuple-element.20.refs_4_) | copy-start | bytes 294916
  13.6 1.4 %collective-permute-start.3 = (bf16[16,2304]{1,0:T(8,128)(2,1)S(1)}, bf16[16,2304]{1,0:T(8,128)(2,1)S(1)}, u32[]{:S(2)}, u32[]{:S(2)}) collective-permute-start(bf16[16,2304]{1,0:T(8,128)(2,1)S(1)} %get-tuple-element.23), channel_id=1, source_target_pairs={{0,1},{1,0},{2,3},{3,2},{4,5},{5,4},{6,7},{7,6},{8,9},{9,8},{10,11... | collective-permute-start | bytes 221192 | tf_op jit(solution)/shard_map/ppermute | solution.py:608
  14.1 1.3 %collective-permute-start.2 = (bf16[16,896]{1,0:T(8,128)(2,1)S(1)}, bf16[16,896]{1,0:T(8,128)(2,1)S(1)}, u32[]{:S(2)}, u32[]{:S(2)}) collective-permute-start(bf16[16,896]{1,0:T(8,128)(2,1)S(1)} %get-tuple-element.21._.mine_ref), channel_id=1, source_target_pairs={{0,1},{1,0},{2,3},{3,2},{4,5},{5,4},{6,7},{7,6},{8,9},{9,8},{10,11... | collective-permute-start | bytes 86024 | tf_op jit(solution)/shard_map/ppermute | solution.py:608
  14.6 8.5 %collective-permute-start.7 = (bf16[16,3584]{1,0:T(8,128)(2,1)S(1)}, bf16[16,3584]{1,0:T(8,128)(2,1)S(1)}, u32[]{:S(2)}, u32[]{:S(2)}) collective-permute-start(bf16[16,3584]{1,0:T(8,128)(2,1)S(1)} %get-tuple-element.26.refs_6_), channel_id=1, source_target_pairs={{0,4},{4,0},{8,12},{12,8},{1,5},{5,1},{9,13},{13,9},{2,6},{6,2},{1... | collective-permute-start | bytes 344072 | tf_op jit(solution)/shard_map/ppermute | solution.py:608
  15.4 7.6 %collective-permute-start.4 = (bf16[16,3072]{1,0:T(8,128)(2,1)S(1)}, bf16[16,3072]{1,0:T(8,128)(2,1)S(1)}, u32[]{:S(2)}, u32[]{:S(2)}) collective-permute-start(bf16[16,3072]{1,0:T(8,128)(2,1)S(1)} %get-tuple-element.24.refs_2_), channel_id=1, source_target_pairs={{0,2},{1,3},{2,0},{3,1},{4,6},{5,7},{6,4},{7,5},{8,10},{9,11},{10,... | collective-permute-start | bytes 294920 | tf_op jit(solution)/shard_map/ppermute | solution.py:608
  17.0 5.4 %collective-permute-start.6 = (bf16[16,128]{1,0:T(8,128)(2,1)S(1)}, bf16[16,128]{1,0:T(8,128)(2,1)S(1)}, u32[]{:S(2)}, u32[]{:S(2)}) collective-permute-start(bf16[16,128]{1,0:T(8,128)(2,1)S(1)} %get-tuple-element.25), channel_id=1, source_target_pairs={{0,10},{1,11},{2,8},{3,9},{4,14},{5,15},{6,12},{7,13},{8,2},{9,3},... | collective-permute-start | bytes 12296 | tf_op jit(solution)/shard_map/ppermute | solution.py:662
  18.5 4.5 %collective-permute-start.5 = (bf16[16,128]{1,0:T(8,128)(2,1)S(1)}, bf16[16,128]{1,0:T(8,128)(2,1)S(1)}, u32[]{:S(2)}, u32[]{:S(2)}) collective-permute-start(bf16[16,128]{1,0:T(8,128)(2,1)S(1)} %get-tuple-element.25), channel_id=1, source_target_pairs={{0,8},{1,9},{2,10},{3,11},{4,12},{5,13},{6,14},{7,15},{8,0},{9,1},... | collective-permute-start | bytes 12296 | tf_op jit(solution)/shard_map/ppermute | solution.py:662
  23.9 1.3 %collective-permute-start.8 = (bf16[16,2560]{1,0:T(8,128)(2,1)S(1)}, bf16[16,2560]{1,0:T(8,128)(2,1)S(1)}, u32[]{:S(2)}, u32[]{:S(2)}) collective-permute-start(bf16[16,2560]{1,0:T(8,128)(2,1)S(1)} %merge.1.mine_ref), channel_id=1, source_target_pairs={{0,1},{1,0},{2,3},{3,2},{4,5},{5,4},{6,7},{7,6},{8,9},{9,8},{10,11... | collective-permute-start | bytes 245768 | tf_op jit(solution)/shard_map/ppermute | solution.py:608

commit v12 on v11

--- a/solution.py
+++ b/solution.py
@@ -380,12 +380,17 @@
         part = ref[:, : depth // 2].astype(F32)
         x.append(jnp.concatenate([part[:8], part[8:]], 1))
     x = jnp.concatenate(x, 0).astype(BF16)
-    fill = jnp.zeros((RANK - 16, depth), BF16)
+    down = jnp.concatenate(
+        [ref[:, at : at + depth] for at in (0, depth) for ref in (own_ref, near_ref)], 0
+    )
+    products = lax.dot_general(x, down, NT, preferred_element_type=F32)
+    products = jnp.concatenate([products, jnp.zeros_like(products)], 1)
+    lane = lax.broadcasted_iota(jnp.int32, products.shape, 1)
     z = None
-    for ref, at in ((own_ref, place), (near_ref, place ^ 1)):
-        down = jnp.concatenate([ref[:, :depth], fill, ref[:, depth:], fill], 0)
-        part = lax.dot_general(x, down, NT, preferred_element_type=F32)
-        part = pltpu.roll(part, at * rows, 1)
+    for i in range(4):
+        part = jnp.where(lane // 16 == i, products, 0.0)
+        column = (place ^ (i % 2)) * rows + i // 2 * RANK
+        part = pltpu.roll(part, (column + 128 - 16 * i) % 128, 1)
         z = part if z is None else z + part
     out_ref[:, :half] = base_ref[:, half:].astype(BF16)
     out_ref[:, half : half + 128] = split(table_ref[:8])

time: 26.1 us -> 26 us (level)
  no operation moved by 1% of the time
where the time goes in v12:
time: 26 us; the launch traced here: 25.8 us
  starting transfers between devices  11.2 us (43%)
  Pallas kernels  9.26 us (36%)
  waiting for transfers between devices  4.6 us (18%)
  between operations  0.72 us (3%)
    ppermute x7, starting transfers between devices, swap(): return lax.ppermute(value, axis, [(i, i ^ distance) for i in range(n)])  8.31 us
    pallas_call x1, Pallas kernels, local(): pl.pallas_call(local_kernel, in_specs=[HBM] * 6, out_specs=[VMEM] * 5, ou...  5.39 us
    ppermute x2, waiting for transfers between devices, shards(): backs.append(lax.ppermute(reply, ('dp', 'tensor'), perm))  3.15 us
    ppermute x2, starting transfers between devices, shards(): backs.append(lax.ppermute(reply, ('dp', 'tensor'), perm))  2.9 us
    pallas_call x1, Pallas kernels, pack(): pl.pallas_call(pack_kernel, in_specs=[HBM] * len(operands), out_specs=[HB...  1.88 us
    ppermute x7, waiting for transfers between devices, swap(): return lax.ppermute(value, axis, [(i, i ^ distance) for i in range(n)])  1.45 us
    pallas_call x1, Pallas kernels, merge(): pl.pallas_call(functools.partial(merge_kernel, len(backs), paired, width_...  0.8 us
    pallas_call x1, Pallas kernels, place(): pl.pallas_call(place_kernel, in_specs=[VMEM] * 2, out_specs=[VMEM] * 3, o...  0.69 us
  transfers between devices with their start and end apart: 9, of which 4 were waited for; matrix products, arithmetic and copies ran while one was open for 0% of the time, Pallas kernels for 23%

profile of v12, /device:TPU:0, one launch (start us, length us, event | category | flops | bytes accessed | tf_op | source)
XLA Modules:
  0.0 25.8 jit_solution(7100662873708792291)
XLA Ops:
  0.6 1.9 %pack.1 = (bf16[16,4096]{1,0:T(8,128)(2,1)}, bf16[16,3072]{1,0:T(8,128)(2,1)}, bf16[16,3328]{1,0:T(8,128)(2,1)}) custom-call(f32[16,2048]{1,0:T(8,128)} %refs_0_.1, f32[16,2048]{1,0:T(8,128)} %refs_1_.1, bf16[2,4,2048]{2,1,0:T(4,128)(2,1)} %refs_2_.1, bf16[16,128]{1,0:T(8,128)(2,1)} %bitcast.6, s32[1,2]{1,0:T(1,128)} %bitcast.7, f32[64,256]{1,0:T(8,128)} %bitcast.4, ...), custom_call_target="tpu_custom_call" | custom-call | tf_op jit(solution)/shard_map/pack/pallas_call | solution.py:127
  2.5 3.1 %collective-permute-start = (bf16[16,4096]{1,0:T(8,128)(2,1)}, bf16[16,4096]{1,0:T(8,128)(2,1)S(1)}, u32[]{:S(2)}, u32[]{:S(2)}) collective-permute-start(bf16[16,4096]{1,0:T(8,128)(2,1)} %get-tuple-element.19.refs_2_), channel_id=1, source_target_pairs={{0,4},{4,0},{8,12},{12,8},{1,5},{5,1},{9,13},{13,9},{2,6},{6,2},{1... | collective-permute-start | bytes 393224 | tf_op jit(solution)/shard_map/ppermute | solution.py:613
  5.6 2.6 %collective-permute-start.1 = (bf16[16,3072]{1,0:T(8,128)(2,1)}, bf16[16,3072]{1,0:T(8,128)(2,1)S(1)}, u32[]{:S(2)}, u32[]{:S(2)}) collective-permute-start(bf16[16,3072]{1,0:T(8,128)(2,1)} %get-tuple-element.20.refs_4_), channel_id=1, source_target_pairs={{0,8},{4,12},{8,0},{12,4},{1,9},{5,13},{9,1},{13,5},{2,10},{6,14},... | collective-permute-start | bytes 294920 | tf_op jit(solution)/shard_map/ppermute | solution.py:613
  8.2 5.4 %local.1 = (bf16[16,2304]{1,0:T(8,128)(2,1)S(1)}, bf16[16,2304]{1,0:T(8,128)(2,1)S(1)}, f32[16,1024]{1,0:T(8,128)S(1)}, bf16[16,2048]{1,0:T(8,128)(2,1)S(1)}, f32[24,128]{1,0:T(8,128)S(1)}) custom-call(bf16[16,3328]{1,0:T(8,128)(2,1)} %get-tuple-element.15.x_hbm, bf16[2,4,8192]{2,1,0:T(4,128)(2,1)} %q_hbm.1, bf16[2,512,1024]{2,1,0:T(8,128)(2,1)} %k_hbm.1, ...), custom_call_target="tpu_custom_call" | custom-call | flops 402653184 | bytes 12582912 | tf_op jit(solution)/shard_map/local/pallas_call | solution.py:344
  13.6 0.1 collective-permute-start.3
  13.7 0.0 collective-permute-done.1.refs_5_
  13.7 0.0 collective-permute-done.refs_3_
  13.7 0.3 rank_products.1
  14.0 0.5 %collective-permute-start.2 = (bf16[16,896]{1,0:T(8,128)(2,1)S(1)}, bf16[16,896]{1,0:T(8,128)(2,1)S(1)}, u32[]{:S(2)}, u32[]{:S(2)}) collective-permute-start(bf16[16,896]{1,0:T(8,128)(2,1)S(1)} %get-tuple-element.21._.mine_ref), channel_id=1, source_target_pairs={{0,1},{1,0},{2,3},{3,2},{4,5},{5,4},{6,7},{7,6},{8,9},{9,8},{10,11... | collective-permute-start | bytes 86024 | tf_op jit(solution)/shard_map/ppermute | solution.py:613
  14.5 0.4 %collective-permute-start.7 = (bf16[16,3584]{1,0:T(8,128)(2,1)S(1)}, bf16[16,3584]{1,0:T(8,128)(2,1)S(1)}, u32[]{:S(2)}, u32[]{:S(2)}) collective-permute-start(bf16[16,3584]{1,0:T(8,128)(2,1)S(1)} %get-tuple-element.26.refs_6_), channel_id=1, source_target_pairs={{0,4},{4,0},{8,12},{12,8},{1,5},{5,1},{9,13},{13,9},{2,6},{6,2},{1... | collective-permute-start | bytes 344072 | tf_op jit(solution)/shard_map/ppermute | solution.py:613
  14.9 0.0 collective-permute-done.3.b_ref
  14.9 0.2 combine_cache.1.cache_ref
  15.2 0.2 collective-permute-done.2.theirs_ref
  15.3 1.6 %collective-permute-start.4 = (bf16[16,3072]{1,0:T(8,128)(2,1)S(1)}, bf16[16,3072]{1,0:T(8,128)(2,1)S(1)}, u32[]{:S(2)}, u32[]{:S(2)}) collective-permute-start(bf16[16,3072]{1,0:T(8,128)(2,1)S(1)} %get-tuple-element.24.refs_2_), channel_id=1, source_target_pairs={{0,2},{1,3},{2,0},{3,1},{4,6},{5,7},{6,4},{7,5},{8,10},{9,11},{10,... | collective-permute-start | bytes 294920 | tf_op jit(solution)/shard_map/ppermute | solution.py:613
  16.9 1.5 %collective-permute-start.6 = (bf16[16,128]{1,0:T(8,128)(2,1)S(1)}, bf16[16,128]{1,0:T(8,128)(2,1)S(1)}, u32[]{:S(2)}, u32[]{:S(2)}) collective-permute-start(bf16[16,128]{1,0:T(8,128)(2,1)S(1)} %get-tuple-element.25), channel_id=1, source_target_pairs={{0,10},{1,11},{2,8},{3,9},{4,14},{5,15},{6,12},{7,13},{8,2},{9,3},... | collective-permute-start | bytes 12296 | tf_op jit(solution)/shard_map/ppermute | solution.py:667
  18.4 1.4 %collective-permute-start.5 = (bf16[16,128]{1,0:T(8,128)(2,1)S(1)}, bf16[16,128]{1,0:T(8,128)(2,1)S(1)}, u32[]{:S(2)}, u32[]{:S(2)}) collective-permute-start(bf16[16,128]{1,0:T(8,128)(2,1)S(1)} %get-tuple-element.25), channel_id=1, source_target_pairs={{0,8},{1,9},{2,10},{3,11},{4,12},{5,13},{6,14},{7,15},{8,0},{9,1},... | collective-permute-start | bytes 12296 | tf_op jit(solution)/shard_map/ppermute | solution.py:667
  19.8 2.5 %collective-permute-done.6.refs_5_ = bf16[16,128]{1,0:T(8,128)(2,1)S(1)} collective-permute-done((bf16[16,128]{1,0:T(8,128)(2,1)S(1)}, bf16[16,128]{1,0:T(8,128)(2,1)S(1)}, u32[]{:S(2)}, u32[]{:S(2)}) %collective-permute-start.6) | collective-permute-done | bytes 4128 | tf_op jit(solution)/shard_map/ppermute | solution.py:667
  22.3 0.6 %collective-permute-done.5.refs_4_ = bf16[16,128]{1,0:T(8,128)(2,1)S(1)} collective-permute-done((bf16[16,128]{1,0:T(8,128)(2,1)S(1)}, bf16[16,128]{1,0:T(8,128)(2,1)S(1)}, u32[]{:S(2)}, u32[]{:S(2)}) %collective-permute-start.5) | collective-permute-done | bytes 4128 | tf_op jit(solution)/shard_map/ppermute | solution.py:667
  23.0 0.0 collective-permute-done.7.refs_7_
  23.0 0.0 collective-permute-done.4.refs_3_
  23.0 0.8 %merge.1.mine_ref = bf16[16,2560]{1,0:T(8,128)(2,1)S(1)} custom-call(f32[24,128]{1,0:T(8,128)S(1)} %get-tuple-element.16.refs_1_.refs_0_, bf16[16,2048]{1,0:T(8,128)(2,1)S(1)} %get-tuple-element.17.refs_1_, bf16[16,3072]{1,0:T(8,128)(2,1)S(1)} %get-tuple-element.24.refs_2_, bf16[16,3072]{1,0:T(8,128)(2,1)S(1)} %collective-permute-done.4.refs_3_, ...), custom_call_target="tpu_custom_call" | custom-call | tf_op jit(solution)/shard_map/merge/pallas_call | solution.py:566
  23.8 0.1 collective-permute-start.8
  23.8 1.3 %collective-permute-done.8.theirs_ref = bf16[16,2560]{1,0:T(8,128)(2,1)S(1)} collective-permute-done((bf16[16,2560]{1,0:T(8,128)(2,1)S(1)}, bf16[16,2560]{1,0:T(8,128)(2,1)S(1)}, u32[]{:S(2)}, u32[]{:S(2)}) %collective-permute-start.8) | collective-permute-done | bytes 81952 | tf_op jit(solution)/shard_map/ppermute | solution.py:613
  25.1 0.7 %place.1 = (bf16[2,4,1024]{2,1,0:T(4,128)(2,1)}, bf16[2,4,1024]{2,1,0:T(4,128)(2,1)}, bf16[2,4,8192]{2,1,0:T(4,128)(2,1)}) custom-call(bf16[16,2560]{1,0:T(8,128)(2,1)S(1)} %merge.1.mine_ref, bf16[16,2560]{1,0:T(8,128)(2,1)S(1)} %collective-permute-done.8.theirs_ref), custom_call_target="tpu_custom_call" | custom-call | tf_op jit(solution)/shard_map/place/pallas_call | solution.py:598
  (5 shorter events, 0.0 us)
Async XLA Ops:
  2.5 11.2 %collective-permute-start = (bf16[16,4096]{1,0:T(8,128)(2,1)}, bf16[16,4096]{1,0:T(8,128)(2,1)S(1)}, u32[]{:S(2)}, u32[]{:S(2)}) collective-permute-start(bf16[16,4096]{1,0:T(8,128)(2,1)} %get-tuple-element.19.refs_2_), channel_id=1, source_target_pairs={{0,4},{4,0},{8,12},{12,8},{1,5},{5,1},{9,13},{13,9},{2,6},{6,2},{1... | collective-permute-start | bytes 393224 | tf_op jit(solution)/shard_map/ppermute | solution.py:613
  5.6 8.1 %collective-permute-start.1 = (bf16[16,3072]{1,0:T(8,128)(2,1)}, bf16[16,3072]{1,0:T(8,128)(2,1)S(1)}, u32[]{:S(2)}, u32[]{:S(2)}) collective-permute-start(bf16[16,3072]{1,0:T(8,128)(2,1)} %get-tuple-element.20.refs_4_), channel_id=1, source_target_pairs={{0,8},{4,12},{8,0},{12,4},{1,9},{5,13},{9,1},{13,5},{2,10},{6,14},... | collective-permute-start | bytes 294920 | tf_op jit(solution)/shard_map/ppermute | solution.py:613
  8.2 5.5 %copy-start = (bf16[16,4096]{1,0:T(8,128)(2,1)S(1)}, bf16[16,4096]{1,0:T(8,128)(2,1)}, u32[]{:S(2)}) copy-start(bf16[16,4096]{1,0:T(8,128)(2,1)} %get-tuple-element.19.refs_2_) | copy-start | bytes 393220
  8.2 5.5 %copy-start.1 = (bf16[16,3072]{1,0:T(8,128)(2,1)S(1)}, bf16[16,3072]{1,0:T(8,128)(2,1)}, u32[]{:S(2)}) copy-start(bf16[16,3072]{1,0:T(8,128)(2,1)} %get-tuple-element.20.refs_4_) | copy-start | bytes 294916
  13.6 1.3 %collective-permute-start.3 = (bf16[16,2304]{1,0:T(8,128)(2,1)S(1)}, bf16[16,2304]{1,0:T(8,128)(2,1)S(1)}, u32[]{:S(2)}, u32[]{:S(2)}) collective-permute-start(bf16[16,2304]{1,0:T(8,128)(2,1)S(1)} %get-tuple-element.23), channel_id=1, source_target_pairs={{0,1},{1,0},{2,3},{3,2},{4,5},{5,4},{6,7},{7,6},{8,9},{9,8},{10,11... | collective-permute-start | bytes 221192 | tf_op jit(solution)/shard_map/ppermute | solution.py:613
  14.0 1.3 %collective-permute-start.2 = (bf16[16,896]{1,0:T(8,128)(2,1)S(1)}, bf16[16,896]{1,0:T(8,128)(2,1)S(1)}, u32[]{:S(2)}, u32[]{:S(2)}) collective-permute-start(bf16[16,896]{1,0:T(8,128)(2,1)S(1)} %get-tuple-element.21._.mine_ref), channel_id=1, source_target_pairs={{0,1},{1,0},{2,3},{3,2},{4,5},{5,4},{6,7},{7,6},{8,9},{9,8},{10,11... | collective-permute-start | bytes 86024 | tf_op jit(solution)/shard_map/ppermute | solution.py:613
  14.5 8.5 %collective-permute-start.7 = (bf16[16,3584]{1,0:T(8,128)(2,1)S(1)}, bf16[16,3584]{1,0:T(8,128)(2,1)S(1)}, u32[]{:S(2)}, u32[]{:S(2)}) collective-permute-start(bf16[16,3584]{1,0:T(8,128)(2,1)S(1)} %get-tuple-element.26.refs_6_), channel_id=1, source_target_pairs={{0,4},{4,0},{8,12},{12,8},{1,5},{5,1},{9,13},{13,9},{2,6},{6,2},{1... | collective-permute-start | bytes 344072 | tf_op jit(solution)/shard_map/ppermute | solution.py:613
  15.3 7.6 %collective-permute-start.4 = (bf16[16,3072]{1,0:T(8,128)(2,1)S(1)}, bf16[16,3072]{1,0:T(8,128)(2,1)S(1)}, u32[]{:S(2)}, u32[]{:S(2)}) collective-permute-start(bf16[16,3072]{1,0:T(8,128)(2,1)S(1)} %get-tuple-element.24.refs_2_), channel_id=1, source_target_pairs={{0,2},{1,3},{2,0},{3,1},{4,6},{5,7},{6,4},{7,5},{8,10},{9,11},{10,... | collective-permute-start | bytes 294920 | tf_op jit(solution)/shard_map/ppermute | solution.py:613
  16.9 5.4 %collective-permute-start.6 = (bf16[16,128]{1,0:T(8,128)(2,1)S(1)}, bf16[16,128]{1,0:T(8,128)(2,1)S(1)}, u32[]{:S(2)}, u32[]{:S(2)}) collective-permute-start(bf16[16,128]{1,0:T(8,128)(2,1)S(1)} %get-tuple-element.25), channel_id=1, source_target_pairs={{0,10},{1,11},{2,8},{3,9},{4,14},{5,15},{6,12},{7,13},{8,2},{9,3},... | collective-permute-start | bytes 12296 | tf_op jit(solution)/shard_map/ppermute | solution.py:667
  18.4 4.5 %collective-permute-start.5 = (bf16[16,128]{1,0:T(8,128)(2,1)S(1)}, bf16[16,128]{1,0:T(8,128)(2,1)S(1)}, u32[]{:S(2)}, u32[]{:S(2)}) collective-permute-start(bf16[16,128]{1,0:T(8,128)(2,1)S(1)} %get-tuple-element.25), channel_id=1, source_target_pairs={{0,8},{1,9},{2,10},{3,11},{4,12},{5,13},{6,14},{7,15},{8,0},{9,1},... | collective-permute-start | bytes 12296 | tf_op jit(solution)/shard_map/ppermute | solution.py:667
  23.8 1.3 %collective-permute-start.8 = (bf16[16,2560]{1,0:T(8,128)(2,1)S(1)}, bf16[16,2560]{1,0:T(8,128)(2,1)S(1)}, u32[]{:S(2)}, u32[]{:S(2)}) collective-permute-start(bf16[16,2560]{1,0:T(8,128)(2,1)S(1)} %merge.1.mine_ref), channel_id=1, source_target_pairs={{0,1},{1,0},{2,3},{3,2},{4,5},{5,4},{6,7},{7,6},{8,9},{9,8},{10,11... | collective-permute-start | bytes 245768 | tf_op jit(solution)/shard_map/ppermute | solution.py:613

commit v13 on v12

--- a/solution.py
+++ b/solution.py
@@ -19,7 +19,7 @@
 EXPONENT = math.log2(math.e) / math.sqrt(HD)
 PAIR = GROUP * HD + 128
 UP_COLUMNS = 3584
-CHUNK = 512
+CHUNK = 256
 
 F32 = jnp.float32
 BF16 = jnp.bfloat16
@@ -285,7 +285,8 @@
 
     x_copy.wait()
     start(groups[1][1:])
-    start(weights[0])
+    for copies in weights[: chunks // 4]:
+        start(copies)
     half = wk_hbm.shape[0] // 2
     x = x_ref[:, :half].astype(F32)
     x = jnp.concatenate([x[:8], x[8:]], 1).astype(BF16)
@@ -315,14 +316,15 @@
     def between(h):
         groups[h][2].wait()
         if h == 0:
-            start(weights[chunks // 2])
+            for copies in weights[chunks // 2 : 3 * chunks // 4]:
+                start(copies)
         else:
             for c in range(chunks // 2):
                 project(c)
 
     for h, out_ref in enumerate((keep_ref, send_ref)):
         groups[h][1].wait()
-        for copies in weights[chunks // 2 + 1 :] if h else weights[1 : chunks // 2]:
+        for copies in weights[3 * chunks // 4 :] if h else weights[chunks // 4 : chunks // 2]:
             start(copies)
         attend(
             range(h * pairs // 2, (h + 1) * pairs // 2),

time: 26 us -> 26 us (level)
  no operation moved by 1% of the time
where the time goes in v13:
time: 26 us; the launch traced here: 25.8 us
  starting transfers between devices  11.2 us (43%)
  Pallas kernels  9.27 us (36%)
  waiting for transfers between devices  4.6 us (18%)
  between operations  0.72 us (3%)
    ppermute x7, starting transfers between devices, swap(): return lax.ppermute(value, axis, [(i, i ^ distance) for i in range(n)])  8.31 us
    pallas_call x1, Pallas kernels, local(): pl.pallas_call(local_kernel, in_specs=[HBM] * 6, out_specs=[VMEM] * 5, ou...  5.4 us
    ppermute x2, waiting for transfers between devices, shards(): backs.append(lax.ppermute(reply, ('dp', 'tensor'), perm))  3.15 us
    ppermute x2, starting transfers between devices, shards(): backs.append(lax.ppermute(reply, ('dp', 'tensor'), perm))  2.9 us
    pallas_call x1, Pallas kernels, pack(): pl.pallas_call(pack_kernel, in_specs=[HBM] * len(operands), out_specs=[HB...  1.88 us
    ppermute x7, waiting for transfers between devices, swap(): return lax.ppermute(value, axis, [(i, i ^ distance) for i in range(n)])  1.45 us
    pallas_call x1, Pallas kernels, merge(): pl.pallas_call(functools.partial(merge_kernel, len(backs), paired, width_...  0.8 us
    pallas_call x1, Pallas kernels, place(): pl.pallas_call(place_kernel, in_specs=[VMEM] * 2, out_specs=[VMEM] * 3, o...  0.69 us
  transfers between devices with their start and end apart: 9, of which 4 were waited for; matrix products, arithmetic and copies ran while one was open for 0% of the time, Pallas kernels for 23%

profile of v13, /device:TPU:0, one launch (start us, length us, event | category | flops | bytes accessed | tf_op | source)
XLA Modules:
  0.0 25.8 jit_solution(3861525824504815648)
XLA Ops:
  0.6 1.9 %pack.1 = (bf16[16,4096]{1,0:T(8,128)(2,1)}, bf16[16,3072]{1,0:T(8,128)(2,1)}, bf16[16,3328]{1,0:T(8,128)(2,1)}) custom-call(f32[16,2048]{1,0:T(8,128)} %refs_0_.1, f32[16,2048]{1,0:T(8,128)} %refs_1_.1, bf16[2,4,2048]{2,1,0:T(4,128)(2,1)} %refs_2_.1, bf16[16,128]{1,0:T(8,128)(2,1)} %bitcast.6, s32[1,2]{1,0:T(1,128)} %bitcast.7, f32[64,256]{1,0:T(8,128)} %bitcast.4, ...), custom_call_target="tpu_custom_call" | custom-call | tf_op jit(solution)/shard_map/pack/pallas_call | solution.py:127
  2.5 3.1 %collective-permute-start = (bf16[16,4096]{1,0:T(8,128)(2,1)}, bf16[16,4096]{1,0:T(8,128)(2,1)S(1)}, u32[]{:S(2)}, u32[]{:S(2)}) collective-permute-start(bf16[16,4096]{1,0:T(8,128)(2,1)} %get-tuple-element.19.refs_2_), channel_id=1, source_target_pairs={{0,4},{4,0},{8,12},{12,8},{1,5},{5,1},{9,13},{13,9},{2,6},{6,2},{1... | collective-permute-start | bytes 393224 | tf_op jit(solution)/shard_map/ppermute | solution.py:615
  5.6 2.6 %collective-permute-start.1 = (bf16[16,3072]{1,0:T(8,128)(2,1)}, bf16[16,3072]{1,0:T(8,128)(2,1)S(1)}, u32[]{:S(2)}, u32[]{:S(2)}) collective-permute-start(bf16[16,3072]{1,0:T(8,128)(2,1)} %get-tuple-element.20.refs_4_), channel_id=1, source_target_pairs={{0,8},{4,12},{8,0},{12,4},{1,9},{5,13},{9,1},{13,5},{2,10},{6,14},... | collective-permute-start | bytes 294920 | tf_op jit(solution)/shard_map/ppermute | solution.py:615
  8.2 5.4 %local.1 = (bf16[16,2304]{1,0:T(8,128)(2,1)S(1)}, bf16[16,2304]{1,0:T(8,128)(2,1)S(1)}, f32[16,1024]{1,0:T(8,128)S(1)}, bf16[16,2048]{1,0:T(8,128)(2,1)S(1)}, f32[24,128]{1,0:T(8,128)S(1)}) custom-call(bf16[16,3328]{1,0:T(8,128)(2,1)} %get-tuple-element.15.x_hbm, bf16[2,4,8192]{2,1,0:T(4,128)(2,1)} %q_hbm.1, bf16[2,512,1024]{2,1,0:T(8,128)(2,1)} %k_hbm.1, ...), custom_call_target="tpu_custom_call" | custom-call | flops 402653184 | bytes 12582912 | tf_op jit(solution)/shard_map/local/pallas_call | solution.py:346
  13.6 0.1 collective-permute-start.3
  13.7 0.0 collective-permute-done.1.refs_5_
  13.7 0.0 collective-permute-done.refs_3_
  13.7 0.3 rank_products.1
  14.0 0.5 %collective-permute-start.2 = (bf16[16,896]{1,0:T(8,128)(2,1)S(1)}, bf16[16,896]{1,0:T(8,128)(2,1)S(1)}, u32[]{:S(2)}, u32[]{:S(2)}) collective-permute-start(bf16[16,896]{1,0:T(8,128)(2,1)S(1)} %get-tuple-element.21._.mine_ref), channel_id=1, source_target_pairs={{0,1},{1,0},{2,3},{3,2},{4,5},{5,4},{6,7},{7,6},{8,9},{9,8},{10,11... | collective-permute-start | bytes 86024 | tf_op jit(solution)/shard_map/ppermute | solution.py:615
  14.5 0.4 %collective-permute-start.7 = (bf16[16,3584]{1,0:T(8,128)(2,1)S(1)}, bf16[16,3584]{1,0:T(8,128)(2,1)S(1)}, u32[]{:S(2)}, u32[]{:S(2)}) collective-permute-start(bf16[16,3584]{1,0:T(8,128)(2,1)S(1)} %get-tuple-element.26.refs_6_), channel_id=1, source_target_pairs={{0,4},{4,0},{8,12},{12,8},{1,5},{5,1},{9,13},{13,9},{2,6},{6,2},{1... | collective-permute-start | bytes 344072 | tf_op jit(solution)/shard_map/ppermute | solution.py:615
  14.9 0.0 collective-permute-done.3.b_ref
  14.9 0.2 combine_cache.1.cache_ref
  15.2 0.2 collective-permute-done.2.theirs_ref
  15.3 1.6 %collective-permute-start.4 = (bf16[16,3072]{1,0:T(8,128)(2,1)S(1)}, bf16[16,3072]{1,0:T(8,128)(2,1)S(1)}, u32[]{:S(2)}, u32[]{:S(2)}) collective-permute-start(bf16[16,3072]{1,0:T(8,128)(2,1)S(1)} %get-tuple-element.24.refs_2_), channel_id=1, source_target_pairs={{0,2},{1,3},{2,0},{3,1},{4,6},{5,7},{6,4},{7,5},{8,10},{9,11},{10,... | collective-permute-start | bytes 294920 | tf_op jit(solution)/shard_map/ppermute | solution.py:615
  16.9 1.5 %collective-permute-start.6 = (bf16[16,128]{1,0:T(8,128)(2,1)S(1)}, bf16[16,128]{1,0:T(8,128)(2,1)S(1)}, u32[]{:S(2)}, u32[]{:S(2)}) collective-permute-start(bf16[16,128]{1,0:T(8,128)(2,1)S(1)} %get-tuple-element.25), channel_id=1, source_target_pairs={{0,10},{1,11},{2,8},{3,9},{4,14},{5,15},{6,12},{7,13},{8,2},{9,3},... | collective-permute-start | bytes 12296 | tf_op jit(solution)/shard_map/ppermute | solution.py:669
  18.4 1.4 %collective-permute-start.5 = (bf16[16,128]{1,0:T(8,128)(2,1)S(1)}, bf16[16,128]{1,0:T(8,128)(2,1)S(1)}, u32[]{:S(2)}, u32[]{:S(2)}) collective-permute-start(bf16[16,128]{1,0:T(8,128)(2,1)S(1)} %get-tuple-element.25), channel_id=1, source_target_pairs={{0,8},{1,9},{2,10},{3,11},{4,12},{5,13},{6,14},{7,15},{8,0},{9,1},... | collective-permute-start | bytes 12296 | tf_op jit(solution)/shard_map/ppermute | solution.py:669
  19.8 2.5 %collective-permute-done.6.refs_5_ = bf16[16,128]{1,0:T(8,128)(2,1)S(1)} collective-permute-done((bf16[16,128]{1,0:T(8,128)(2,1)S(1)}, bf16[16,128]{1,0:T(8,128)(2,1)S(1)}, u32[]{:S(2)}, u32[]{:S(2)}) %collective-permute-start.6) | collective-permute-done | bytes 4128 | tf_op jit(solution)/shard_map/ppermute | solution.py:669
  22.3 0.6 %collective-permute-done.5.refs_4_ = bf16[16,128]{1,0:T(8,128)(2,1)S(1)} collective-permute-done((bf16[16,128]{1,0:T(8,128)(2,1)S(1)}, bf16[16,128]{1,0:T(8,128)(2,1)S(1)}, u32[]{:S(2)}, u32[]{:S(2)}) %collective-permute-start.5) | collective-permute-done | bytes 4128 | tf_op jit(solution)/shard_map/ppermute | solution.py:669
  23.0 0.0 collective-permute-done.7.refs_7_
  23.0 0.0 collective-permute-done.4.refs_3_
  23.0 0.8 %merge.1.mine_ref = bf16[16,2560]{1,0:T(8,128)(2,1)S(1)} custom-call(f32[24,128]{1,0:T(8,128)S(1)} %get-tuple-element.16.refs_1_.refs_0_, bf16[16,2048]{1,0:T(8,128)(2,1)S(1)} %get-tuple-element.17.refs_1_, bf16[16,3072]{1,0:T(8,128)(2,1)S(1)} %get-tuple-element.24.refs_2_, bf16[16,3072]{1,0:T(8,128)(2,1)S(1)} %collective-permute-done.4.refs_3_, ...), custom_call_target="tpu_custom_call" | custom-call | tf_op jit(solution)/shard_map/merge/pallas_call | solution.py:568
  23.8 0.1 collective-permute-start.8
  23.8 1.3 %collective-permute-done.8.theirs_ref = bf16[16,2560]{1,0:T(8,128)(2,1)S(1)} collective-permute-done((bf16[16,2560]{1,0:T(8,128)(2,1)S(1)}, bf16[16,2560]{1,0:T(8,128)(2,1)S(1)}, u32[]{:S(2)}, u32[]{:S(2)}) %collective-permute-start.8) | collective-permute-done | bytes 81952 | tf_op jit(solution)/shard_map/ppermute | solution.py:615
  25.1 0.7 %place.1 = (bf16[2,4,1024]{2,1,0:T(4,128)(2,1)}, bf16[2,4,1024]{2,1,0:T(4,128)(2,1)}, bf16[2,4,8192]{2,1,0:T(4,128)(2,1)}) custom-call(bf16[16,2560]{1,0:T(8,128)(2,1)S(1)} %merge.1.mine_ref, bf16[16,2560]{1,0:T(8,128)(2,1)S(1)} %collective-permute-done.8.theirs_ref), custom_call_target="tpu_custom_call" | custom-call | tf_op jit(solution)/shard_map/place/pallas_call | solution.py:600
  (5 shorter events, 0.0 us)
Async XLA Ops:
  2.5 11.2 %collective-permute-start = (bf16[16,4096]{1,0:T(8,128)(2,1)}, bf16[16,4096]{1,0:T(8,128)(2,1)S(1)}, u32[]{:S(2)}, u32[]{:S(2)}) collective-permute-start(bf16[16,4096]{1,0:T(8,128)(2,1)} %get-tuple-element.19.refs_2_), channel_id=1, source_target_pairs={{0,4},{4,0},{8,12},{12,8},{1,5},{5,1},{9,13},{13,9},{2,6},{6,2},{1... | collective-permute-start | bytes 393224 | tf_op jit(solution)/shard_map/ppermute | solution.py:615
  5.6 8.1 %collective-permute-start.1 = (bf16[16,3072]{1,0:T(8,128)(2,1)}, bf16[16,3072]{1,0:T(8,128)(2,1)S(1)}, u32[]{:S(2)}, u32[]{:S(2)}) collective-permute-start(bf16[16,3072]{1,0:T(8,128)(2,1)} %get-tuple-element.20.refs_4_), channel_id=1, source_target_pairs={{0,8},{4,12},{8,0},{12,4},{1,9},{5,13},{9,1},{13,5},{2,10},{6,14},... | collective-permute-start | bytes 294920 | tf_op jit(solution)/shard_map/ppermute | solution.py:615
  8.2 5.5 %copy-start = (bf16[16,4096]{1,0:T(8,128)(2,1)S(1)}, bf16[16,4096]{1,0:T(8,128)(2,1)}, u32[]{:S(2)}) copy-start(bf16[16,4096]{1,0:T(8,128)(2,1)} %get-tuple-element.19.refs_2_) | copy-start | bytes 393220
  8.2 5.5 %copy-start.1 = (bf16[16,3072]{1,0:T(8,128)(2,1)S(1)}, bf16[16,3072]{1,0:T(8,128)(2,1)}, u32[]{:S(2)}) copy-start(bf16[16,3072]{1,0:T(8,128)(2,1)} %get-tuple-element.20.refs_4_) | copy-start | bytes 294916
  13.6 1.3 %collective-permute-start.3 = (bf16[16,2304]{1,0:T(8,128)(2,1)S(1)}, bf16[16,2304]{1,0:T(8,128)(2,1)S(1)}, u32[]{:S(2)}, u32[]{:S(2)}) collective-permute-start(bf16[16,2304]{1,0:T(8,128)(2,1)S(1)} %get-tuple-element.23), channel_id=1, source_target_pairs={{0,1},{1,0},{2,3},{3,2},{4,5},{5,4},{6,7},{7,6},{8,9},{9,8},{10,11... | collective-permute-start | bytes 221192 | tf_op jit(solution)/shard_map/ppermute | solution.py:615
  14.0 1.3 %collective-permute-start.2 = (bf16[16,896]{1,0:T(8,128)(2,1)S(1)}, bf16[16,896]{1,0:T(8,128)(2,1)S(1)}, u32[]{:S(2)}, u32[]{:S(2)}) collective-permute-start(bf16[16,896]{1,0:T(8,128)(2,1)S(1)} %get-tuple-element.21._.mine_ref), channel_id=1, source_target_pairs={{0,1},{1,0},{2,3},{3,2},{4,5},{5,4},{6,7},{7,6},{8,9},{9,8},{10,11... | collective-permute-start | bytes 86024 | tf_op jit(solution)/shard_map/ppermute | solution.py:615
  14.5 8.5 %collective-permute-start.7 = (bf16[16,3584]{1,0:T(8,128)(2,1)S(1)}, bf16[16,3584]{1,0:T(8,128)(2,1)S(1)}, u32[]{:S(2)}, u32[]{:S(2)}) collective-permute-start(bf16[16,3584]{1,0:T(8,128)(2,1)S(1)} %get-tuple-element.26.refs_6_), channel_id=1, source_target_pairs={{0,4},{4,0},{8,12},{12,8},{1,5},{5,1},{9,13},{13,9},{2,6},{6,2},{1... | collective-permute-start | bytes 344072 | tf_op jit(solution)/shard_map/ppermute | solution.py:615
  15.3 7.6 %collective-permute-start.4 = (bf16[16,3072]{1,0:T(8,128)(2,1)S(1)}, bf16[16,3072]{1,0:T(8,128)(2,1)S(1)}, u32[]{:S(2)}, u32[]{:S(2)}) collective-permute-start(bf16[16,3072]{1,0:T(8,128)(2,1)S(1)} %get-tuple-element.24.refs_2_), channel_id=1, source_target_pairs={{0,2},{1,3},{2,0},{3,1},{4,6},{5,7},{6,4},{7,5},{8,10},{9,11},{10,... | collective-permute-start | bytes 294920 | tf_op jit(solution)/shard_map/ppermute | solution.py:615
  16.9 5.4 %collective-permute-start.6 = (bf16[16,128]{1,0:T(8,128)(2,1)S(1)}, bf16[16,128]{1,0:T(8,128)(2,1)S(1)}, u32[]{:S(2)}, u32[]{:S(2)}) collective-permute-start(bf16[16,128]{1,0:T(8,128)(2,1)S(1)} %get-tuple-element.25), channel_id=1, source_target_pairs={{0,10},{1,11},{2,8},{3,9},{4,14},{5,15},{6,12},{7,13},{8,2},{9,3},... | collective-permute-start | bytes 12296 | tf_op jit(solution)/shard_map/ppermute | solution.py:669
  18.4 4.5 %collective-permute-start.5 = (bf16[16,128]{1,0:T(8,128)(2,1)S(1)}, bf16[16,128]{1,0:T(8,128)(2,1)S(1)}, u32[]{:S(2)}, u32[]{:S(2)}) collective-permute-start(bf16[16,128]{1,0:T(8,128)(2,1)S(1)} %get-tuple-element.25), channel_id=1, source_target_pairs={{0,8},{1,9},{2,10},{3,11},{4,12},{5,13},{6,14},{7,15},{8,0},{9,1},... | collective-permute-start | bytes 12296 | tf_op jit(solution)/shard_map/ppermute | solution.py:669
  23.8 1.3 %collective-permute-start.8 = (bf16[16,2560]{1,0:T(8,128)(2,1)S(1)}, bf16[16,2560]{1,0:T(8,128)(2,1)S(1)}, u32[]{:S(2)}, u32[]{:S(2)}) collective-permute-start(bf16[16,2560]{1,0:T(8,128)(2,1)S(1)} %merge.1.mine_ref), channel_id=1, source_target_pairs={{0,1},{1,0},{2,3},{3,2},{4,5},{5,4},{6,7},{7,6},{8,9},{9,8},{10,11... | collective-permute-start | bytes 245768 | tf_op jit(solution)/shard_map/ppermute | solution.py:615

commit v14 on v13

--- a/solution.py
+++ b/solution.py
@@ -18,7 +18,7 @@
 LOWEST_TOP = -1e20
 EXPONENT = math.log2(math.e) / math.sqrt(HD)
 PAIR = GROUP * HD + 128
-UP_COLUMNS = 3584
+UP_COLUMNS = 3200
 CHUNK = 256
 
 F32 = jnp.float32

time: 26 us -> 26 us (level)
  no operation moved by 1% of the time
where the time goes in v14:
time: 26 us; the launch traced here: 25.8 us
  starting transfers between devices  11.2 us (43%)
  Pallas kernels  9.27 us (36%)
  waiting for transfers between devices  4.6 us (18%)
  between operations  0.72 us (3%)
    ppermute x7, starting transfers between devices, swap(): return lax.ppermute(value, axis, [(i, i ^ distance) for i in range(n)])  8.31 us
    pallas_call x1, Pallas kernels, local(): pl.pallas_call(local_kernel, in_specs=[HBM] * 6, out_specs=[VMEM] * 5, ou...  5.4 us
    ppermute x2, waiting for transfers between devices, shards(): backs.append(lax.ppermute(reply, ('dp', 'tensor'), perm))  3.15 us
    ppermute x2, starting transfers between devices, shards(): backs.append(lax.ppermute(reply, ('dp', 'tensor'), perm))  2.9 us
    pallas_call x1, Pallas kernels, pack(): pl.pallas_call(pack_kernel, in_specs=[HBM] * len(operands), out_specs=[HB...  1.88 us
    ppermute x7, waiting for transfers between devices, swap(): return lax.ppermute(value, axis, [(i, i ^ distance) for i in range(n)])  1.45 us
    pallas_call x1, Pallas kernels, merge(): pl.pallas_call(functools.partial(merge_kernel, len(backs), paired, width_...  0.8 us
    pallas_call x1, Pallas kernels, place(): pl.pallas_call(place_kernel, in_specs=[VMEM] * 2, out_specs=[VMEM] * 3, o...  0.69 us
  transfers between devices with their start and end apart: 9, of which 4 were waited for; matrix products, arithmetic and copies ran while one was open for 0% of the time, Pallas kernels for 23%

profile of v14, /device:TPU:0, one launch (start us, length us, event | category | flops | bytes accessed | tf_op | source)
XLA Modules:
  0.0 25.8 jit_solution(9007882900273443772)
XLA Ops:
  0.6 1.9 %pack.1 = (bf16[16,4096]{1,0:T(8,128)(2,1)}, bf16[16,3072]{1,0:T(8,128)(2,1)}, bf16[16,3328]{1,0:T(8,128)(2,1)}) custom-call(f32[16,2048]{1,0:T(8,128)} %refs_0_.1, f32[16,2048]{1,0:T(8,128)} %refs_1_.1, bf16[2,4,2048]{2,1,0:T(4,128)(2,1)} %refs_2_.1, bf16[16,128]{1,0:T(8,128)(2,1)} %bitcast.6, s32[1,2]{1,0:T(1,128)} %bitcast.7, f32[64,256]{1,0:T(8,128)} %bitcast.4, ...), custom_call_target="tpu_custom_call" | custom-call | tf_op jit(solution)/shard_map/pack/pallas_call | solution.py:127
  2.5 3.1 %collective-permute-start = (bf16[16,4096]{1,0:T(8,128)(2,1)}, bf16[16,4096]{1,0:T(8,128)(2,1)S(1)}, u32[]{:S(2)}, u32[]{:S(2)}) collective-permute-start(bf16[16,4096]{1,0:T(8,128)(2,1)} %get-tuple-element.19.refs_2_), channel_id=1, source_target_pairs={{0,4},{4,0},{8,12},{12,8},{1,5},{5,1},{9,13},{13,9},{2,6},{6,2},{1... | collective-permute-start | bytes 393224 | tf_op jit(solution)/shard_map/ppermute | solution.py:615
  5.6 2.6 %collective-permute-start.1 = (bf16[16,3072]{1,0:T(8,128)(2,1)}, bf16[16,3072]{1,0:T(8,128)(2,1)S(1)}, u32[]{:S(2)}, u32[]{:S(2)}) collective-permute-start(bf16[16,3072]{1,0:T(8,128)(2,1)} %get-tuple-element.20.refs_4_), channel_id=1, source_target_pairs={{0,8},{4,12},{8,0},{12,4},{1,9},{5,13},{9,1},{13,5},{2,10},{6,14},... | collective-permute-start | bytes 294920 | tf_op jit(solution)/shard_map/ppermute | solution.py:615
  8.2 5.4 %local.1 = (bf16[16,2304]{1,0:T(8,128)(2,1)S(1)}, bf16[16,2304]{1,0:T(8,128)(2,1)S(1)}, f32[16,1024]{1,0:T(8,128)S(1)}, bf16[16,2048]{1,0:T(8,128)(2,1)S(1)}, f32[24,128]{1,0:T(8,128)S(1)}) custom-call(bf16[16,3328]{1,0:T(8,128)(2,1)} %get-tuple-element.15.x_hbm, bf16[2,4,8192]{2,1,0:T(4,128)(2,1)} %q_hbm.1, bf16[2,512,1024]{2,1,0:T(8,128)(2,1)} %k_hbm.1, ...), custom_call_target="tpu_custom_call" | custom-call | flops 402653184 | bytes 12582912 | tf_op jit(solution)/shard_map/local/pallas_call | solution.py:346
  13.6 0.1 collective-permute-start.3
  13.7 0.0 collective-permute-done.1.refs_5_
  13.7 0.0 collective-permute-done.refs_3_
  13.7 0.3 rank_products.1
  14.0 0.5 %collective-permute-start.2 = (bf16[16,896]{1,0:T(8,128)(2,1)S(1)}, bf16[16,896]{1,0:T(8,128)(2,1)S(1)}, u32[]{:S(2)}, u32[]{:S(2)}) collective-permute-start(bf16[16,896]{1,0:T(8,128)(2,1)S(1)} %get-tuple-element.21._.mine_ref), channel_id=1, source_target_pairs={{0,1},{1,0},{2,3},{3,2},{4,5},{5,4},{6,7},{7,6},{8,9},{9,8},{10,11... | collective-permute-start | bytes 86024 | tf_op jit(solution)/shard_map/ppermute | solution.py:615
  14.5 0.4 %collective-permute-start.7 = (bf16[16,3200]{1,0:T(8,128)(2,1)S(1)}, bf16[16,3200]{1,0:T(8,128)(2,1)S(1)}, u32[]{:S(2)}, u32[]{:S(2)}) collective-permute-start(bf16[16,3200]{1,0:T(8,128)(2,1)S(1)} %get-tuple-element.26.refs_6_), channel_id=1, source_target_pairs={{0,4},{4,0},{8,12},{12,8},{1,5},{5,1},{9,13},{13,9},{2,6},{6,2},{1... | collective-permute-start | bytes 307208 | tf_op jit(solution)/shard_map/ppermute | solution.py:615
  14.9 0.0 collective-permute-done.3.b_ref
  14.9 0.2 combine_cache.1.cache_ref
  15.2 0.2 collective-permute-done.2.theirs_ref
  15.3 1.6 %collective-permute-start.4 = (bf16[16,3072]{1,0:T(8,128)(2,1)S(1)}, bf16[16,3072]{1,0:T(8,128)(2,1)S(1)}, u32[]{:S(2)}, u32[]{:S(2)}) collective-permute-start(bf16[16,3072]{1,0:T(8,128)(2,1)S(1)} %get-tuple-element.24.refs_2_), channel_id=1, source_target_pairs={{0,2},{1,3},{2,0},{3,1},{4,6},{5,7},{6,4},{7,5},{8,10},{9,11},{10,... | collective-permute-start | bytes 294920 | tf_op jit(solution)/shard_map/ppermute | solution.py:615
  16.9 1.5 %collective-permute-start.6 = (bf16[16,128]{1,0:T(8,128)(2,1)S(1)}, bf16[16,128]{1,0:T(8,128)(2,1)S(1)}, u32[]{:S(2)}, u32[]{:S(2)}) collective-permute-start(bf16[16,128]{1,0:T(8,128)(2,1)S(1)} %get-tuple-element.25), channel_id=1, source_target_pairs={{0,10},{1,11},{2,8},{3,9},{4,14},{5,15},{6,12},{7,13},{8,2},{9,3},... | collective-permute-start | bytes 12296 | tf_op jit(solution)/shard_map/ppermute | solution.py:669
  18.4 1.4 %collective-permute-start.5 = (bf16[16,128]{1,0:T(8,128)(2,1)S(1)}, bf16[16,128]{1,0:T(8,128)(2,1)S(1)}, u32[]{:S(2)}, u32[]{:S(2)}) collective-permute-start(bf16[16,128]{1,0:T(8,128)(2,1)S(1)} %get-tuple-element.25), channel_id=1, source_target_pairs={{0,8},{1,9},{2,10},{3,11},{4,12},{5,13},{6,14},{7,15},{8,0},{9,1},... | collective-permute-start | bytes 12296 | tf_op jit(solution)/shard_map/ppermute | solution.py:669
  19.8 2.5 %collective-permute-done.6.refs_5_ = bf16[16,128]{1,0:T(8,128)(2,1)S(1)} collective-permute-done((bf16[16,128]{1,0:T(8,128)(2,1)S(1)}, bf16[16,128]{1,0:T(8,128)(2,1)S(1)}, u32[]{:S(2)}, u32[]{:S(2)}) %collective-permute-start.6) | collective-permute-done | bytes 4128 | tf_op jit(solution)/shard_map/ppermute | solution.py:669
  22.3 0.6 %collective-permute-done.5.refs_4_ = bf16[16,128]{1,0:T(8,128)(2,1)S(1)} collective-permute-done((bf16[16,128]{1,0:T(8,128)(2,1)S(1)}, bf16[16,128]{1,0:T(8,128)(2,1)S(1)}, u32[]{:S(2)}, u32[]{:S(2)}) %collective-permute-start.5) | collective-permute-done | bytes 4128 | tf_op jit(solution)/shard_map/ppermute | solution.py:669
  23.0 0.0 collective-permute-done.7.refs_7_
  23.0 0.0 collective-permute-done.4.refs_3_
  23.0 0.8 %merge.1.mine_ref = bf16[16,2560]{1,0:T(8,128)(2,1)S(1)} custom-call(f32[24,128]{1,0:T(8,128)S(1)} %get-tuple-element.16.refs_1_.refs_0_, bf16[16,2048]{1,0:T(8,128)(2,1)S(1)} %get-tuple-element.17.refs_1_, bf16[16,3072]{1,0:T(8,128)(2,1)S(1)} %get-tuple-element.24.refs_2_, bf16[16,3072]{1,0:T(8,128)(2,1)S(1)} %collective-permute-done.4.refs_3_, ...), custom_call_target="tpu_custom_call" | custom-call | tf_op jit(solution)/shard_map/merge/pallas_call | solution.py:568
  23.8 0.1 collective-permute-start.8
  23.8 1.3 %collective-permute-done.8.theirs_ref = bf16[16,2560]{1,0:T(8,128)(2,1)S(1)} collective-permute-done((bf16[16,2560]{1,0:T(8,128)(2,1)S(1)}, bf16[16,2560]{1,0:T(8,128)(2,1)S(1)}, u32[]{:S(2)}, u32[]{:S(2)}) %collective-permute-start.8) | collective-permute-done | bytes 81952 | tf_op jit(solution)/shard_map/ppermute | solution.py:615
  25.1 0.7 %place.1 = (bf16[2,4,1024]{2,1,0:T(4,128)(2,1)}, bf16[2,4,1024]{2,1,0:T(4,128)(2,1)}, bf16[2,4,8192]{2,1,0:T(4,128)(2,1)}) custom-call(bf16[16,2560]{1,0:T(8,128)(2,1)S(1)} %merge.1.mine_ref, bf16[16,2560]{1,0:T(8,128)(2,1)S(1)} %collective-permute-done.8.theirs_ref), custom_call_target="tpu_custom_call" | custom-call | tf_op jit(solution)/shard_map/place/pallas_call | solution.py:600
  (5 shorter events, 0.0 us)
Async XLA Ops:
  2.5 11.2 %collective-permute-start = (bf16[16,4096]{1,0:T(8,128)(2,1)}, bf16[16,4096]{1,0:T(8,128)(2,1)S(1)}, u32[]{:S(2)}, u32[]{:S(2)}) collective-permute-start(bf16[16,4096]{1,0:T(8,128)(2,1)} %get-tuple-element.19.refs_2_), channel_id=1, source_target_pairs={{0,4},{4,0},{8,12},{12,8},{1,5},{5,1},{9,13},{13,9},{2,6},{6,2},{1... | collective-permute-start | bytes 393224 | tf_op jit(solution)/shard_map/ppermute | solution.py:615
  5.6 8.1 %collective-permute-start.1 = (bf16[16,3072]{1,0:T(8,128)(2,1)}, bf16[16,3072]{1,0:T(8,128)(2,1)S(1)}, u32[]{:S(2)}, u32[]{:S(2)}) collective-permute-start(bf16[16,3072]{1,0:T(8,128)(2,1)} %get-tuple-element.20.refs_4_), channel_id=1, source_target_pairs={{0,8},{4,12},{8,0},{12,4},{1,9},{5,13},{9,1},{13,5},{2,10},{6,14},... | collective-permute-start | bytes 294920 | tf_op jit(solution)/shard_map/ppermute | solution.py:615
  8.2 5.5 %copy-start = (bf16[16,4096]{1,0:T(8,128)(2,1)S(1)}, bf16[16,4096]{1,0:T(8,128)(2,1)}, u32[]{:S(2)}) copy-start(bf16[16,4096]{1,0:T(8,128)(2,1)} %get-tuple-element.19.refs_2_) | copy-start | bytes 393220
  8.2 5.5 %copy-start.1 = (bf16[16,3072]{1,0:T(8,128)(2,1)S(1)}, bf16[16,3072]{1,0:T(8,128)(2,1)}, u32[]{:S(2)}) copy-start(bf16[16,3072]{1,0:T(8,128)(2,1)} %get-tuple-element.20.refs_4_) | copy-start | bytes 294916
  13.6 1.3 %collective-permute-start.3 = (bf16[16,2304]{1,0:T(8,128)(2,1)S(1)}, bf16[16,2304]{1,0:T(8,128)(2,1)S(1)}, u32[]{:S(2)}, u32[]{:S(2)}) collective-permute-start(bf16[16,2304]{1,0:T(8,128)(2,1)S(1)} %get-tuple-element.23), channel_id=1, source_target_pairs={{0,1},{1,0},{2,3},{3,2},{4,5},{5,4},{6,7},{7,6},{8,9},{9,8},{10,11... | collective-permute-start | bytes 221192 | tf_op jit(solution)/shard_map/ppermute | solution.py:615
  14.0 1.3 %collective-permute-start.2 = (bf16[16,896]{1,0:T(8,128)(2,1)S(1)}, bf16[16,896]{1,0:T(8,128)(2,1)S(1)}, u32[]{:S(2)}, u32[]{:S(2)}) collective-permute-start(bf16[16,896]{1,0:T(8,128)(2,1)S(1)} %get-tuple-element.21._.mine_ref), channel_id=1, source_target_pairs={{0,1},{1,0},{2,3},{3,2},{4,5},{5,4},{6,7},{7,6},{8,9},{9,8},{10,11... | collective-permute-start | bytes 86024 | tf_op jit(solution)/shard_map/ppermute | solution.py:615
  14.5 8.5 %collective-permute-start.7 = (bf16[16,3200]{1,0:T(8,128)(2,1)S(1)}, bf16[16,3200]{1,0:T(8,128)(2,1)S(1)}, u32[]{:S(2)}, u32[]{:S(2)}) collective-permute-start(bf16[16,3200]{1,0:T(8,128)(2,1)S(1)} %get-tuple-element.26.refs_6_), channel_id=1, source_target_pairs={{0,4},{4,0},{8,12},{12,8},{1,5},{5,1},{9,13},{13,9},{2,6},{6,2},{1... | collective-permute-start | bytes 307208 | tf_op jit(solution)/shard_map/ppermute | solution.py:615
  15.3 7.6 %collective-permute-start.4 = (bf16[16,3072]{1,0:T(8,128)(2,1)S(1)}, bf16[16,3072]{1,0:T(8,128)(2,1)S(1)}, u32[]{:S(2)}, u32[]{:S(2)}) collective-permute-start(bf16[16,3072]{1,0:T(8,128)(2,1)S(1)} %get-tuple-element.24.refs_2_), channel_id=1, source_target_pairs={{0,2},{1,3},{2,0},{3,1},{4,6},{5,7},{6,4},{7,5},{8,10},{9,11},{10,... | collective-permute-start | bytes 294920 | tf_op jit(solution)/shard_map/ppermute | solution.py:615
  16.9 5.4 %collective-permute-start.6 = (bf16[16,128]{1,0:T(8,128)(2,1)S(1)}, bf16[16,128]{1,0:T(8,128)(2,1)S(1)}, u32[]{:S(2)}, u32[]{:S(2)}) collective-permute-start(bf16[16,128]{1,0:T(8,128)(2,1)S(1)} %get-tuple-element.25), channel_id=1, source_target_pairs={{0,10},{1,11},{2,8},{3,9},{4,14},{5,15},{6,12},{7,13},{8,2},{9,3},... | collective-permute-start | bytes 12296 | tf_op jit(solution)/shard_map/ppermute | solution.py:669
  18.4 4.5 %collective-permute-start.5 = (bf16[16,128]{1,0:T(8,128)(2,1)S(1)}, bf16[16,128]{1,0:T(8,128)(2,1)S(1)}, u32[]{:S(2)}, u32[]{:S(2)}) collective-permute-start(bf16[16,128]{1,0:T(8,128)(2,1)S(1)} %get-tuple-element.25), channel_id=1, source_target_pairs={{0,8},{1,9},{2,10},{3,11},{4,12},{5,13},{6,14},{7,15},{8,0},{9,1},... | collective-permute-start | bytes 12296 | tf_op jit(solution)/shard_map/ppermute | solution.py:669
  23.8 1.3 %collective-permute-start.8 = (bf16[16,2560]{1,0:T(8,128)(2,1)S(1)}, bf16[16,2560]{1,0:T(8,128)(2,1)S(1)}, u32[]{:S(2)}, u32[]{:S(2)}) collective-permute-start(bf16[16,2560]{1,0:T(8,128)(2,1)S(1)} %merge.1.mine_ref), channel_id=1, source_target_pairs={{0,1},{1,0},{2,3},{3,2},{4,5},{5,4},{6,7},{7,6},{8,9},{9,8},{10,11... | collective-permute-start | bytes 245768 | tf_op jit(solution)/shard_map/ppermute | solution.py:615

commit v15 on v13

--- a/solution.py
+++ b/solution.py
@@ -512,7 +512,6 @@
         adapted = [jnp.where(even, a, b), jnp.where(even, b, a)]
     total = sums[:, :width] + jnp.concatenate(adapted, 1)
     scale = lax.rsqrt(squares / width_all + EPSILON)
-    lane = lax.broadcasted_iota(jnp.int32, (16, 128), 1)
     step = lax.broadcasted_iota(jnp.int32, (16, 128), 0) % STEPS
     first = first_rows((8, 128))
 
@@ -536,29 +535,33 @@
             out_ref[:, start : start + HD] = fresh.astype(BF16)
         keys = [of_step(new_keys, j) for j in range(STEPS)]
         values = [of_step(new_values, j) for j in range(STEPS)]
-        scores = [jnp.zeros((16, 128), F32) for _ in range(STEPS)]
-        for g in range(GROUP):
-            q = qrot_ref[:, (p * GROUP + g) * HD : (p * GROUP + g + 1) * HD].astype(F32)
-            for j in range(STEPS):
-                dot = jnp.sum(q * keys[j], 1, keepdims=True)
-                scores[j] = jnp.where(lane == g, dot, scores[j])
-        scores = [jnp.where(j <= step, scores[j], MASKED_SCORE) for j in range(STEPS)]
         end = slice(head + p * PAIR + GROUP * HD, head + (p + 1) * PAIR)
         stats = [ref[:, end].astype(F32) for ref in (pa_ref, pb_ref)]
-        top = functools.reduce(jnp.maximum, scores + stats)
-        fresh = [rounded(jnp.exp2((scores[j] - top) * EXPONENT)) for j in range(STEPS)]
-        factors = [jnp.exp2(jnp.minimum(s - top, 0.0) * EXPONENT) for s in stats]
-        denom = functools.reduce(jnp.add, fresh)
-        for factor, s in zip(factors, stats):
-            denom = denom + factor * totals(s)
-        inverse = 1.0 / denom
-        coefficients = [c * inverse for c in fresh + factors]
+        sums_of = [totals(tile) for tile in stats]
         for g in range(GROUP):
+            tops = [broadcast_lane(tile, g) for tile in stats]
+            weights = [broadcast_lane(tile, g) for tile in sums_of]
+            q = qrot_ref[:, (p * GROUP + g) * HD : (p * GROUP + g + 1) * HD].astype(F32)
+            scores = [
+                jnp.where(
+                    j <= step,
+                    jnp.broadcast_to(jnp.sum(q * keys[j], 1, keepdims=True), (16, 128)),
+                    MASKED_SCORE,
+                )
+                for j in range(STEPS)
+            ]
+            top = functools.reduce(jnp.maximum, scores + tops)
+            fresh = [rounded(jnp.exp2((score - top) * EXPONENT)) for score in scores]
+            factors = [jnp.exp2((tile - top) * EXPONENT) for tile in tops]
+            denom = functools.reduce(jnp.add, fresh)
+            for factor, weight in zip(factors, weights):
+                denom = denom + factor * weight
             at = slice(head + p * PAIR + g * HD, head + p * PAIR + (g + 1) * HD)
             terms = values + [ref[:, at].astype(F32) for ref in (pa_ref, pb_ref)]
             tile = jnp.zeros((16, 128), F32)
-            for c, term in zip(coefficients, terms):
-                tile = tile + broadcast_lane(c, g) * term
+            for c, term in zip(fresh + factors, terms):
+                tile = tile + c * term
+            tile = tile * (1.0 / denom)
             out_ref[:, (p * GROUP + g) * HD : (p * GROUP + g + 1) * HD] = tile.astype(BF16)
 
 

time: 26 us -> 26 us (level)
  no operation moved by 1% of the time
where the time goes in v15:
time: 26 us; the launch traced here: 25.9 us
  starting transfers between devices  11.2 us (43%)
  Pallas kernels  9.35 us (36%)
  waiting for transfers between devices  4.6 us (18%)
  between operations  0.72 us (3%)
    ppermute x7, starting transfers between devices, swap(): return lax.ppermute(value, axis, [(i, i ^ distance) for i in range(n)])  8.31 us
    pallas_call x1, Pallas kernels, local(): pl.pallas_call(local_kernel, in_specs=[HBM] * 6, out_specs=[VMEM] * 5, ou...  5.4 us
    ppermute x2, waiting for transfers between devices, shards(): backs.append(lax.ppermute(reply, ('dp', 'tensor'), perm))  3.15 us
    ppermute x2, starting transfers between devices, shards(): backs.append(lax.ppermute(reply, ('dp', 'tensor'), perm))  2.9 us
    pallas_call x1, Pallas kernels, pack(): pl.pallas_call(pack_kernel, in_specs=[HBM] * len(operands), out_specs=[HB...  1.88 us
    ppermute x7, waiting for transfers between devices, swap(): return lax.ppermute(value, axis, [(i, i ^ distance) for i in range(n)])  1.45 us
    pallas_call x1, Pallas kernels, merge(): pl.pallas_call(functools.partial(merge_kernel, len(backs), paired, width_...  0.89 us
    pallas_call x1, Pallas kernels, place(): pl.pallas_call(place_kernel, in_specs=[VMEM] * 2, out_specs=[VMEM] * 3, o...  0.69 us
  transfers between devices with their start and end apart: 9, of which 4 were waited for; matrix products, arithmetic and copies ran while one was open for 0% of the time, Pallas kernels for 23%

profile of v15, /device:TPU:0, one launch (start us, length us, event | category | flops | bytes accessed | tf_op | source)
XLA Modules:
  0.0 25.9 jit_solution(14692342498696790294)
XLA Ops:
  0.6 1.9 %pack.1 = (bf16[16,4096]{1,0:T(8,128)(2,1)}, bf16[16,3072]{1,0:T(8,128)(2,1)}, bf16[16,3328]{1,0:T(8,128)(2,1)}) custom-call(f32[16,2048]{1,0:T(8,128)} %refs_0_.1, f32[16,2048]{1,0:T(8,128)} %refs_1_.1, bf16[2,4,2048]{2,1,0:T(4,128)(2,1)} %refs_2_.1, bf16[16,128]{1,0:T(8,128)(2,1)} %bitcast.6, s32[1,2]{1,0:T(1,128)} %bitcast.7, f32[64,256]{1,0:T(8,128)} %bitcast.4, ...), custom_call_target="tpu_custom_call" | custom-call | tf_op jit(solution)/shard_map/pack/pallas_call | solution.py:127
  2.5 3.1 %collective-permute-start = (bf16[16,4096]{1,0:T(8,128)(2,1)}, bf16[16,4096]{1,0:T(8,128)(2,1)S(1)}, u32[]{:S(2)}, u32[]{:S(2)}) collective-permute-start(bf16[16,4096]{1,0:T(8,128)(2,1)} %get-tuple-element.19.refs_2_), channel_id=1, source_target_pairs={{0,4},{4,0},{8,12},{12,8},{1,5},{5,1},{9,13},{13,9},{2,6},{6,2},{1... | collective-permute-start | bytes 393224 | tf_op jit(solution)/shard_map/ppermute | solution.py:618
  5.6 2.6 %collective-permute-start.1 = (bf16[16,3072]{1,0:T(8,128)(2,1)}, bf16[16,3072]{1,0:T(8,128)(2,1)S(1)}, u32[]{:S(2)}, u32[]{:S(2)}) collective-permute-start(bf16[16,3072]{1,0:T(8,128)(2,1)} %get-tuple-element.20.refs_4_), channel_id=1, source_target_pairs={{0,8},{4,12},{8,0},{12,4},{1,9},{5,13},{9,1},{13,5},{2,10},{6,14},... | collective-permute-start | bytes 294920 | tf_op jit(solution)/shard_map/ppermute | solution.py:618
  8.2 5.4 %local.1 = (bf16[16,2304]{1,0:T(8,128)(2,1)S(1)}, bf16[16,2304]{1,0:T(8,128)(2,1)S(1)}, f32[16,1024]{1,0:T(8,128)S(1)}, bf16[16,2048]{1,0:T(8,128)(2,1)S(1)}, f32[24,128]{1,0:T(8,128)S(1)}) custom-call(bf16[16,3328]{1,0:T(8,128)(2,1)} %get-tuple-element.15.x_hbm, bf16[2,4,8192]{2,1,0:T(4,128)(2,1)} %q_hbm.1, bf16[2,512,1024]{2,1,0:T(8,128)(2,1)} %k_hbm.1, ...), custom_call_target="tpu_custom_call" | custom-call | flops 402653184 | bytes 12582912 | tf_op jit(solution)/shard_map/local/pallas_call | solution.py:346
  13.6 0.1 collective-permute-start.3
  13.7 0.0 collective-permute-done.1.refs_5_
  13.7 0.0 collective-permute-done.refs_3_
  13.7 0.3 rank_products.1
  14.0 0.5 %collective-permute-start.2 = (bf16[16,896]{1,0:T(8,128)(2,1)S(1)}, bf16[16,896]{1,0:T(8,128)(2,1)S(1)}, u32[]{:S(2)}, u32[]{:S(2)}) collective-permute-start(bf16[16,896]{1,0:T(8,128)(2,1)S(1)} %get-tuple-element.21._.mine_ref), channel_id=1, source_target_pairs={{0,1},{1,0},{2,3},{3,2},{4,5},{5,4},{6,7},{7,6},{8,9},{9,8},{10,11... | collective-permute-start | bytes 86024 | tf_op jit(solution)/shard_map/ppermute | solution.py:618
  14.5 0.4 %collective-permute-start.7 = (bf16[16,3584]{1,0:T(8,128)(2,1)S(1)}, bf16[16,3584]{1,0:T(8,128)(2,1)S(1)}, u32[]{:S(2)}, u32[]{:S(2)}) collective-permute-start(bf16[16,3584]{1,0:T(8,128)(2,1)S(1)} %get-tuple-element.26.refs_6_), channel_id=1, source_target_pairs={{0,4},{4,0},{8,12},{12,8},{1,5},{5,1},{9,13},{13,9},{2,6},{6,2},{1... | collective-permute-start | bytes 344072 | tf_op jit(solution)/shard_map/ppermute | solution.py:618
  14.9 0.0 collective-permute-done.3.b_ref
  14.9 0.2 combine_cache.1.cache_ref
  15.2 0.2 collective-permute-done.2.theirs_ref
  15.3 1.6 %collective-permute-start.4 = (bf16[16,3072]{1,0:T(8,128)(2,1)S(1)}, bf16[16,3072]{1,0:T(8,128)(2,1)S(1)}, u32[]{:S(2)}, u32[]{:S(2)}) collective-permute-start(bf16[16,3072]{1,0:T(8,128)(2,1)S(1)} %get-tuple-element.24.refs_2_), channel_id=1, source_target_pairs={{0,2},{1,3},{2,0},{3,1},{4,6},{5,7},{6,4},{7,5},{8,10},{9,11},{10,... | collective-permute-start | bytes 294920 | tf_op jit(solution)/shard_map/ppermute | solution.py:618
  16.9 1.5 %collective-permute-start.6 = (bf16[16,128]{1,0:T(8,128)(2,1)S(1)}, bf16[16,128]{1,0:T(8,128)(2,1)S(1)}, u32[]{:S(2)}, u32[]{:S(2)}) collective-permute-start(bf16[16,128]{1,0:T(8,128)(2,1)S(1)} %get-tuple-element.25), channel_id=1, source_target_pairs={{0,10},{1,11},{2,8},{3,9},{4,14},{5,15},{6,12},{7,13},{8,2},{9,3},... | collective-permute-start | bytes 12296 | tf_op jit(solution)/shard_map/ppermute | solution.py:672
  18.4 1.4 %collective-permute-start.5 = (bf16[16,128]{1,0:T(8,128)(2,1)S(1)}, bf16[16,128]{1,0:T(8,128)(2,1)S(1)}, u32[]{:S(2)}, u32[]{:S(2)}) collective-permute-start(bf16[16,128]{1,0:T(8,128)(2,1)S(1)} %get-tuple-element.25), channel_id=1, source_target_pairs={{0,8},{1,9},{2,10},{3,11},{4,12},{5,13},{6,14},{7,15},{8,0},{9,1},... | collective-permute-start | bytes 12296 | tf_op jit(solution)/shard_map/ppermute | solution.py:672
  19.8 2.5 %collective-permute-done.6.refs_5_ = bf16[16,128]{1,0:T(8,128)(2,1)S(1)} collective-permute-done((bf16[16,128]{1,0:T(8,128)(2,1)S(1)}, bf16[16,128]{1,0:T(8,128)(2,1)S(1)}, u32[]{:S(2)}, u32[]{:S(2)}) %collective-permute-start.6) | collective-permute-done | bytes 4128 | tf_op jit(solution)/shard_map/ppermute | solution.py:672
  22.3 0.6 %collective-permute-done.5.refs_4_ = bf16[16,128]{1,0:T(8,128)(2,1)S(1)} collective-permute-done((bf16[16,128]{1,0:T(8,128)(2,1)S(1)}, bf16[16,128]{1,0:T(8,128)(2,1)S(1)}, u32[]{:S(2)}, u32[]{:S(2)}) %collective-permute-start.5) | collective-permute-done | bytes 4128 | tf_op jit(solution)/shard_map/ppermute | solution.py:672
  23.0 0.0 collective-permute-done.7.refs_7_
  23.0 0.0 collective-permute-done.4.refs_3_
  23.0 0.9 %merge.1.mine_ref = bf16[16,2560]{1,0:T(8,128)(2,1)S(1)} custom-call(f32[24,128]{1,0:T(8,128)S(1)} %get-tuple-element.16.refs_1_.refs_0_, bf16[16,2048]{1,0:T(8,128)(2,1)S(1)} %get-tuple-element.17.refs_1_, bf16[16,3072]{1,0:T(8,128)(2,1)S(1)} %get-tuple-element.24.refs_2_, bf16[16,3072]{1,0:T(8,128)(2,1)S(1)} %collective-permute-done.4.refs_3_, ...), custom_call_target="tpu_custom_call" | custom-call | tf_op jit(solution)/shard_map/merge/pallas_call | solution.py:571
  23.9 0.1 collective-permute-start.8
  23.9 1.3 %collective-permute-done.8.theirs_ref = bf16[16,2560]{1,0:T(8,128)(2,1)S(1)} collective-permute-done((bf16[16,2560]{1,0:T(8,128)(2,1)S(1)}, bf16[16,2560]{1,0:T(8,128)(2,1)S(1)}, u32[]{:S(2)}, u32[]{:S(2)}) %collective-permute-start.8) | collective-permute-done | bytes 81952 | tf_op jit(solution)/shard_map/ppermute | solution.py:618
  25.2 0.7 %place.1 = (bf16[2,4,1024]{2,1,0:T(4,128)(2,1)}, bf16[2,4,1024]{2,1,0:T(4,128)(2,1)}, bf16[2,4,8192]{2,1,0:T(4,128)(2,1)}) custom-call(bf16[16,2560]{1,0:T(8,128)(2,1)S(1)} %merge.1.mine_ref, bf16[16,2560]{1,0:T(8,128)(2,1)S(1)} %collective-permute-done.8.theirs_ref), custom_call_target="tpu_custom_call" | custom-call | tf_op jit(solution)/shard_map/place/pallas_call | solution.py:603
  (5 shorter events, 0.0 us)
Async XLA Ops:
  2.5 11.2 %collective-permute-start = (bf16[16,4096]{1,0:T(8,128)(2,1)}, bf16[16,4096]{1,0:T(8,128)(2,1)S(1)}, u32[]{:S(2)}, u32[]{:S(2)}) collective-permute-start(bf16[16,4096]{1,0:T(8,128)(2,1)} %get-tuple-element.19.refs_2_), channel_id=1, source_target_pairs={{0,4},{4,0},{8,12},{12,8},{1,5},{5,1},{9,13},{13,9},{2,6},{6,2},{1... | collective-permute-start | bytes 393224 | tf_op jit(solution)/shard_map/ppermute | solution.py:618
  5.6 8.1 %collective-permute-start.1 = (bf16[16,3072]{1,0:T(8,128)(2,1)}, bf16[16,3072]{1,0:T(8,128)(2,1)S(1)}, u32[]{:S(2)}, u32[]{:S(2)}) collective-permute-start(bf16[16,3072]{1,0:T(8,128)(2,1)} %get-tuple-element.20.refs_4_), channel_id=1, source_target_pairs={{0,8},{4,12},{8,0},{12,4},{1,9},{5,13},{9,1},{13,5},{2,10},{6,14},... | collective-permute-start | bytes 294920 | tf_op jit(solution)/shard_map/ppermute | solution.py:618
  8.2 5.5 %copy-start = (bf16[16,4096]{1,0:T(8,128)(2,1)S(1)}, bf16[16,4096]{1,0:T(8,128)(2,1)}, u32[]{:S(2)}) copy-start(bf16[16,4096]{1,0:T(8,128)(2,1)} %get-tuple-element.19.refs_2_) | copy-start | bytes 393220
  8.2 5.5 %copy-start.1 = (bf16[16,3072]{1,0:T(8,128)(2,1)S(1)}, bf16[16,3072]{1,0:T(8,128)(2,1)}, u32[]{:S(2)}) copy-start(bf16[16,3072]{1,0:T(8,128)(2,1)} %get-tuple-element.20.refs_4_) | copy-start | bytes 294916
  13.6 1.3 %collective-permute-start.3 = (bf16[16,2304]{1,0:T(8,128)(2,1)S(1)}, bf16[16,2304]{1,0:T(8,128)(2,1)S(1)}, u32[]{:S(2)}, u32[]{:S(2)}) collective-permute-start(bf16[16,2304]{1,0:T(8,128)(2,1)S(1)} %get-tuple-element.23), channel_id=1, source_target_pairs={{0,1},{1,0},{2,3},{3,2},{4,5},{5,4},{6,7},{7,6},{8,9},{9,8},{10,11... | collective-permute-start | bytes 221192 | tf_op jit(solution)/shard_map/ppermute | solution.py:618
  14.0 1.3 %collective-permute-start.2 = (bf16[16,896]{1,0:T(8,128)(2,1)S(1)}, bf16[16,896]{1,0:T(8,128)(2,1)S(1)}, u32[]{:S(2)}, u32[]{:S(2)}) collective-permute-start(bf16[16,896]{1,0:T(8,128)(2,1)S(1)} %get-tuple-element.21._.mine_ref), channel_id=1, source_target_pairs={{0,1},{1,0},{2,3},{3,2},{4,5},{5,4},{6,7},{7,6},{8,9},{9,8},{10,11... | collective-permute-start | bytes 86024 | tf_op jit(solution)/shard_map/ppermute | solution.py:618
  14.5 8.5 %collective-permute-start.7 = (bf16[16,3584]{1,0:T(8,128)(2,1)S(1)}, bf16[16,3584]{1,0:T(8,128)(2,1)S(1)}, u32[]{:S(2)}, u32[]{:S(2)}) collective-permute-start(bf16[16,3584]{1,0:T(8,128)(2,1)S(1)} %get-tuple-element.26.refs_6_), channel_id=1, source_target_pairs={{0,4},{4,0},{8,12},{12,8},{1,5},{5,1},{9,13},{13,9},{2,6},{6,2},{1... | collective-permute-start | bytes 344072 | tf_op jit(solution)/shard_map/ppermute | solution.py:618
  15.3 7.6 %collective-permute-start.4 = (bf16[16,3072]{1,0:T(8,128)(2,1)S(1)}, bf16[16,3072]{1,0:T(8,128)(2,1)S(1)}, u32[]{:S(2)}, u32[]{:S(2)}) collective-permute-start(bf16[16,3072]{1,0:T(8,128)(2,1)S(1)} %get-tuple-element.24.refs_2_), channel_id=1, source_target_pairs={{0,2},{1,3},{2,0},{3,1},{4,6},{5,7},{6,4},{7,5},{8,10},{9,11},{10,... | collective-permute-start | bytes 294920 | tf_op jit(solution)/shard_map/ppermute | solution.py:618
  16.9 5.4 %collective-permute-start.6 = (bf16[16,128]{1,0:T(8,128)(2,1)S(1)}, bf16[16,128]{1,0:T(8,128)(2,1)S(1)}, u32[]{:S(2)}, u32[]{:S(2)}) collective-permute-start(bf16[16,128]{1,0:T(8,128)(2,1)S(1)} %get-tuple-element.25), channel_id=1, source_target_pairs={{0,10},{1,11},{2,8},{3,9},{4,14},{5,15},{6,12},{7,13},{8,2},{9,3},... | collective-permute-start | bytes 12296 | tf_op jit(solution)/shard_map/ppermute | solution.py:672
  18.4 4.5 %collective-permute-start.5 = (bf16[16,128]{1,0:T(8,128)(2,1)S(1)}, bf16[16,128]{1,0:T(8,128)(2,1)S(1)}, u32[]{:S(2)}, u32[]{:S(2)}) collective-permute-start(bf16[16,128]{1,0:T(8,128)(2,1)S(1)} %get-tuple-element.25), channel_id=1, source_target_pairs={{0,8},{1,9},{2,10},{3,11},{4,12},{5,13},{6,14},{7,15},{8,0},{9,1},... | collective-permute-start | bytes 12296 | tf_op jit(solution)/shard_map/ppermute | solution.py:672
  23.9 1.3 %collective-permute-start.8 = (bf16[16,2560]{1,0:T(8,128)(2,1)S(1)}, bf16[16,2560]{1,0:T(8,128)(2,1)S(1)}, u32[]{:S(2)}, u32[]{:S(2)}) collective-permute-start(bf16[16,2560]{1,0:T(8,128)(2,1)S(1)} %merge.1.mine_ref), channel_id=1, source_target_pairs={{0,1},{1,0},{2,3},{3,2},{4,5},{5,4},{6,7},{7,6},{8,9},{9,8},{10,11... | collective-permute-start | bytes 245768 | tf_op jit(solution)/shard_map/ppermute | solution.py:618

commit v16 on v13

--- a/solution.py
+++ b/solution.py
@@ -486,14 +486,47 @@
     )(a, b, earlier)
 
 
+def blend_kernel(pairs, pa_ref, pb_ref, sums_ref, numer_ref, stats_ref):
+    head = sums_ref.shape[1]
+    sums_ref[...] = pa_ref[:, :head].astype(F32) + pb_ref[:, :head].astype(F32)
+    for p in range(pairs):
+        end = slice(head + p * PAIR + GROUP * HD, head + (p + 1) * PAIR)
+        a, b = pa_ref[:, end].astype(F32), pb_ref[:, end].astype(F32)
+        top = jnp.maximum(a, b)
+        fa = jnp.exp2(jnp.minimum(a - top, 0.0) * EXPONENT)
+        fb = jnp.exp2(jnp.minimum(b - top, 0.0) * EXPONENT)
+        stats_ref[:, 2 * p * 128 : (2 * p + 1) * 128] = top
+        stats_ref[:, (2 * p + 1) * 128 : (2 * p + 2) * 128] = fa * totals(a) + fb * totals(b)
+        for g in range(GROUP):
+            at = slice(head + p * PAIR + g * HD, head + p * PAIR + (g + 1) * HD)
+            numer_ref[:, (p * GROUP + g) * HD : (p * GROUP + g + 1) * HD] = broadcast_lane(
+                fa, g
+            ) * pa_ref[:, at].astype(F32) + broadcast_lane(fb, g) * pb_ref[:, at].astype(F32)
+
+
+def blend(pairs, part_a, part_b):
+    head = part_a.shape[1] - pairs * PAIR
+    return pl.pallas_call(
+        functools.partial(blend_kernel, pairs),
+        in_specs=[VMEM] * 2,
+        out_specs=[VMEM] * 3,
+        out_shape=[
+            jax.ShapeDtypeStruct((16, head), F32),
+            jax.ShapeDtypeStruct((16, pairs * GROUP * HD), F32),
+            jax.ShapeDtypeStruct((16, pairs * 256), F32),
+        ],
+        compiler_params=pltpu.CompilerParams(vmem_limit_bytes=32 * MEBI),
+        name="blend",
+    )(part_a, part_b)
+
+
 def merge_kernel(n, paired, width_all, *refs):
-    table_ref, qrot_ref, pa_ref, pb_ref = refs[:4]
-    backs, (ua_ref, ub_ref, out_ref) = refs[4 : 4 + n], refs[4 + n :]
+    table_ref, qrot_ref, sums_ref, numer_ref, stats_ref = refs[:5]
+    backs, (ua_ref, ub_ref, out_ref) = refs[5 : 5 + n], refs[5 + n :]
     pairs = qrot_ref.shape[1] // (GROUP * HD)
     width = pairs * 2 * HD
     cosine, sine = table_ref[8:16], table_ref[16:]
-    head = width + 256
-    sums = pa_ref[:, :head].astype(F32) + pb_ref[:, :head].astype(F32)
+    sums = sums_ref[...]
     tail = sums[:8, width : width + 256] + sums[8:, width : width + 256]
     squares, z = tail[:, :128], tail[:, 128:]
     for ref in backs:
@@ -543,23 +576,19 @@
                 dot = jnp.sum(q * keys[j], 1, keepdims=True)
                 scores[j] = jnp.where(lane == g, dot, scores[j])
         scores = [jnp.where(j <= step, scores[j], MASKED_SCORE) for j in range(STEPS)]
-        end = slice(head + p * PAIR + GROUP * HD, head + (p + 1) * PAIR)
-        stats = [ref[:, end].astype(F32) for ref in (pa_ref, pb_ref)]
-        top = functools.reduce(jnp.maximum, scores + stats)
+        cached = stats_ref[:, 2 * p * 128 : (2 * p + 1) * 128]
+        top = functools.reduce(jnp.maximum, [*scores, cached])
         fresh = [rounded(jnp.exp2((scores[j] - top) * EXPONENT)) for j in range(STEPS)]
-        factors = [jnp.exp2(jnp.minimum(s - top, 0.0) * EXPONENT) for s in stats]
-        denom = functools.reduce(jnp.add, fresh)
-        for factor, s in zip(factors, stats):
-            denom = denom + factor * totals(s)
-        inverse = 1.0 / denom
-        coefficients = [c * inverse for c in fresh + factors]
+        factor = jnp.exp2(jnp.minimum(cached - top, 0.0) * EXPONENT)
+        denom = factor * stats_ref[:, (2 * p + 1) * 128 : (2 * p + 2) * 128]
+        inverse = 1.0 / functools.reduce(jnp.add, fresh, denom)
+        coefficients = [c * inverse for c in (*fresh, factor)]
         for g in range(GROUP):
-            at = slice(head + p * PAIR + g * HD, head + p * PAIR + (g + 1) * HD)
-            terms = values + [ref[:, at].astype(F32) for ref in (pa_ref, pb_ref)]
+            at = slice((p * GROUP + g) * HD, (p * GROUP + g + 1) * HD)
             tile = jnp.zeros((16, 128), F32)
-            for c, term in zip(coefficients, terms):
+            for c, term in zip(coefficients, [*values, numer_ref[:, at]]):
                 tile = tile + broadcast_lane(c, g) * term
-            out_ref[:, (p * GROUP + g) * HD : (p * GROUP + g + 1) * HD] = tile.astype(BF16)
+            out_ref[:, at] = tile.astype(BF16)
 
 
 def merge(paired, width_all, table, qrot, parts, backs, ups):
@@ -672,7 +701,7 @@
         float(depth * n_tensor),
         table,
         qrot,
-        (part, part_far),
+        blend(width // (4 * HD), part, part_far),
         backs,
         ups,
     )

time: 26 us -> 25.9 us (level)
    ppermute x2, waiting for transfers between devices: 3.15 us -> 2.31 us  [shards(): backs.append(lax.ppermute(reply, ('dp', 'tensor'), perm))]
    ppermute x7, waiting for transfers between devices: 1.45 us -> 2.1 us  [swap(): return lax.ppermute(value, axis, [(i, i ^ distance) for i in range(n)])]
  transfers between devices with their start and end apart: 9 -> 9, of which waited for: 4 -> 5; matrix products, arithmetic and copies ran while one was open for 0% -> 0% of each run, Pallas kernels for 23% -> 24%
where the time goes in v16:
time: 25.9 us; the launch traced here: 25.7 us
  starting transfers between devices  11.2 us (43%)
  Pallas kernels  9.4 us (36%)
  waiting for transfers between devices  4.42 us (17%)
  between operations  0.72 us (3%)
    ppermute x7, starting transfers between devices, swap(): return lax.ppermute(value, axis, [(i, i ^ distance) for i in range(n)])  8.31 us
    pallas_call x1, Pallas kernels, local(): pl.pallas_call(local_kernel, in_specs=[HBM] * 6, out_specs=[VMEM] * 5, ou...  5.4 us
    ppermute x2, starting transfers between devices, shards(): backs.append(lax.ppermute(reply, ('dp', 'tensor'), perm))  2.9 us
    ppermute x2, waiting for transfers between devices, shards(): backs.append(lax.ppermute(reply, ('dp', 'tensor'), perm))  2.31 us
    ppermute x7, waiting for transfers between devices, swap(): return lax.ppermute(value, axis, [(i, i ^ distance) for i in range(n)])  2.1 us
    pallas_call x1, Pallas kernels, pack(): pl.pallas_call(pack_kernel, in_specs=[HBM] * len(operands), out_specs=[HB...  1.88 us
    pallas_call x1, Pallas kernels, merge(): pl.pallas_call(functools.partial(merge_kernel, len(backs), paired, width_...  0.75 us
    pallas_call x1, Pallas kernels, place(): pl.pallas_call(place_kernel, in_specs=[VMEM] * 2, out_specs=[VMEM] * 3, o...  0.69 us
  transfers between devices with their start and end apart: 9, of which 5 were waited for; matrix products, arithmetic and copies ran while one was open for 0% of the time, Pallas kernels for 24%

profile of v16, /device:TPU:0, one launch (start us, length us, event | category | flops | bytes accessed | tf_op | source)
XLA Modules:
  0.0 25.7 jit_solution(17111793630090348738)
XLA Ops:
  0.6 1.9 %pack.1 = (bf16[16,4096]{1,0:T(8,128)(2,1)}, bf16[16,3072]{1,0:T(8,128)(2,1)}, bf16[16,3328]{1,0:T(8,128)(2,1)}) custom-call(f32[16,2048]{1,0:T(8,128)} %refs_0_.1, f32[16,2048]{1,0:T(8,128)} %refs_1_.1, bf16[2,4,2048]{2,1,0:T(4,128)(2,1)} %refs_2_.1, bf16[16,128]{1,0:T(8,128)(2,1)} %bitcast.6, s32[1,2]{1,0:T(1,128)} %bitcast.7, f32[64,256]{1,0:T(8,128)} %bitcast.4, ...), custom_call_target="tpu_custom_call" | custom-call | tf_op jit(solution)/shard_map/pack/pallas_call | solution.py:127
  2.5 3.1 %collective-permute-start = (bf16[16,4096]{1,0:T(8,128)(2,1)}, bf16[16,4096]{1,0:T(8,128)(2,1)S(1)}, u32[]{:S(2)}, u32[]{:S(2)}) collective-permute-start(bf16[16,4096]{1,0:T(8,128)(2,1)} %get-tuple-element.22.refs_2_), channel_id=1, source_target_pairs={{0,4},{4,0},{8,12},{12,8},{1,5},{5,1},{9,13},{13,9},{2,6},{6,2},{1... | collective-permute-start | bytes 393224 | tf_op jit(solution)/shard_map/ppermute | solution.py:644
  5.6 2.6 %collective-permute-start.1 = (bf16[16,3072]{1,0:T(8,128)(2,1)}, bf16[16,3072]{1,0:T(8,128)(2,1)S(1)}, u32[]{:S(2)}, u32[]{:S(2)}) collective-permute-start(bf16[16,3072]{1,0:T(8,128)(2,1)} %get-tuple-element.23.refs_4_), channel_id=1, source_target_pairs={{0,8},{4,12},{8,0},{12,4},{1,9},{5,13},{9,1},{13,5},{2,10},{6,14},... | collective-permute-start | bytes 294920 | tf_op jit(solution)/shard_map/ppermute | solution.py:644
  8.2 5.4 %local.1 = (bf16[16,2304]{1,0:T(8,128)(2,1)S(1)}, bf16[16,2304]{1,0:T(8,128)(2,1)S(1)}, f32[16,1024]{1,0:T(8,128)S(1)}, bf16[16,2048]{1,0:T(8,128)(2,1)S(1)}, f32[24,128]{1,0:T(8,128)S(1)}) custom-call(bf16[16,3328]{1,0:T(8,128)(2,1)} %get-tuple-element.18.x_hbm, bf16[2,4,8192]{2,1,0:T(4,128)(2,1)} %q_hbm.1, bf16[2,512,1024]{2,1,0:T(8,128)(2,1)} %k_hbm.1, ...), custom_call_target="tpu_custom_call" | custom-call | flops 402653184 | bytes 12582912 | tf_op jit(solution)/shard_map/local/pallas_call | solution.py:346
  13.6 0.1 collective-permute-start.3
  13.7 0.0 collective-permute-done.1.refs_5_
  13.7 0.0 collective-permute-done.refs_3_
  13.7 0.3 %rank_products.1 = (bf16[16,896]{1,0:T(8,128)(2,1)S(1)}, bf16[16,3584]{1,0:T(8,128)(2,1)S(1)}) custom-call(f32[16,1024]{1,0:T(8,128)S(1)} %get-tuple-element.21.refs_0_.base_ref, f32[24,128]{1,0:T(8,128)S(1)} %get-tuple-element.19.refs_1_.refs_0_, bf16[16,4096]{1,0:T(8,128)(2,1)S(1)} %copy-done, bf16[16,4096]{1,0:T(8,128)(2,1)S(1)} %collective-permute-done.refs_3_, ...), custom_call_target="tpu_custom_call" | custom-call | tf_op jit(solution)/shard_map/rank_products/pallas_call | solution.py:414
  14.0 0.5 %collective-permute-start.2 = (bf16[16,896]{1,0:T(8,128)(2,1)S(1)}, bf16[16,896]{1,0:T(8,128)(2,1)S(1)}, u32[]{:S(2)}, u32[]{:S(2)}) collective-permute-start(bf16[16,896]{1,0:T(8,128)(2,1)S(1)} %get-tuple-element.24._.mine_ref), channel_id=1, source_target_pairs={{0,1},{1,0},{2,3},{3,2},{4,5},{5,4},{6,7},{7,6},{8,9},{9,8},{10,11... | collective-permute-start | bytes 86024 | tf_op jit(solution)/shard_map/ppermute | solution.py:644
  14.5 0.4 %collective-permute-start.7 = (bf16[16,3584]{1,0:T(8,128)(2,1)S(1)}, bf16[16,3584]{1,0:T(8,128)(2,1)S(1)}, u32[]{:S(2)}, u32[]{:S(2)}) collective-permute-start(bf16[16,3584]{1,0:T(8,128)(2,1)S(1)} %get-tuple-element.32.refs_7_), channel_id=1, source_target_pairs={{0,4},{4,0},{8,12},{12,8},{1,5},{5,1},{9,13},{13,9},{2,6},{6,2},{1... | collective-permute-start | bytes 344072 | tf_op jit(solution)/shard_map/ppermute | solution.py:644
  14.9 0.0 collective-permute-done.3.b_ref
  14.9 0.2 combine_cache.1.cache_ref
  15.2 0.2 collective-permute-done.2.theirs_ref
  15.3 1.6 %collective-permute-start.4 = (bf16[16,3072]{1,0:T(8,128)(2,1)S(1)}, bf16[16,3072]{1,0:T(8,128)(2,1)S(1)}, u32[]{:S(2)}, u32[]{:S(2)}) collective-permute-start(bf16[16,3072]{1,0:T(8,128)(2,1)S(1)} %get-tuple-element.27.pa_ref), channel_id=1, source_target_pairs={{0,2},{1,3},{2,0},{3,1},{4,6},{5,7},{6,4},{7,5},{8,10},{9,11},{10,... | collective-permute-start | bytes 294920 | tf_op jit(solution)/shard_map/ppermute | solution.py:644
  16.9 1.5 %collective-permute-start.6 = (bf16[16,128]{1,0:T(8,128)(2,1)S(1)}, bf16[16,128]{1,0:T(8,128)(2,1)S(1)}, u32[]{:S(2)}, u32[]{:S(2)}) collective-permute-start(bf16[16,128]{1,0:T(8,128)(2,1)S(1)} %get-tuple-element.31), channel_id=1, source_target_pairs={{0,10},{1,11},{2,8},{3,9},{4,14},{5,15},{6,12},{7,13},{8,2},{9,3},... | collective-permute-start | bytes 12296 | tf_op jit(solution)/shard_map/ppermute | solution.py:698
  18.4 1.4 %collective-permute-start.5 = (bf16[16,128]{1,0:T(8,128)(2,1)S(1)}, bf16[16,128]{1,0:T(8,128)(2,1)S(1)}, u32[]{:S(2)}, u32[]{:S(2)}) collective-permute-start(bf16[16,128]{1,0:T(8,128)(2,1)S(1)} %get-tuple-element.31), channel_id=1, source_target_pairs={{0,8},{1,9},{2,10},{3,11},{4,12},{5,13},{6,14},{7,15},{8,0},{9,1},... | collective-permute-start | bytes 12296 | tf_op jit(solution)/shard_map/ppermute | solution.py:698
  19.8 0.7 %collective-permute-done.4.pb_ref = bf16[16,3072]{1,0:T(8,128)(2,1)S(1)} collective-permute-done((bf16[16,3072]{1,0:T(8,128)(2,1)S(1)}, bf16[16,3072]{1,0:T(8,128)(2,1)S(1)}, u32[]{:S(2)}, u32[]{:S(2)}) %collective-permute-start.4) | collective-permute-done | bytes 98336 | tf_op jit(solution)/shard_map/ppermute | solution.py:644
  20.5 0.2 blend.1
  20.6 1.7 %collective-permute-done.6.refs_6_ = bf16[16,128]{1,0:T(8,128)(2,1)S(1)} collective-permute-done((bf16[16,128]{1,0:T(8,128)(2,1)S(1)}, bf16[16,128]{1,0:T(8,128)(2,1)S(1)}, u32[]{:S(2)}, u32[]{:S(2)}) %collective-permute-start.6) | collective-permute-done | bytes 4128 | tf_op jit(solution)/shard_map/ppermute | solution.py:698
  22.3 0.6 %collective-permute-done.5.refs_5_ = bf16[16,128]{1,0:T(8,128)(2,1)S(1)} collective-permute-done((bf16[16,128]{1,0:T(8,128)(2,1)S(1)}, bf16[16,128]{1,0:T(8,128)(2,1)S(1)}, u32[]{:S(2)}, u32[]{:S(2)}) %collective-permute-start.5) | collective-permute-done | bytes 4128 | tf_op jit(solution)/shard_map/ppermute | solution.py:698
  23.0 0.8 %merge.1.mine_ref = bf16[16,2560]{1,0:T(8,128)(2,1)S(1)} custom-call(f32[24,128]{1,0:T(8,128)S(1)} %get-tuple-element.19.refs_1_.refs_0_, bf16[16,2048]{1,0:T(8,128)(2,1)S(1)} %get-tuple-element.20.refs_1_, f32[16,768]{1,0:T(8,128)S(1)} %get-tuple-element.28.refs_2_, f32[16,2048]{1,0:T(8,128)S(1)} %get-tuple-element.29.refs_3_, ...), custom_call_target="tpu_custom_call" | custom-call | tf_op jit(solution)/shard_map/merge/pallas_call | solution.py:597
  23.7 0.1 collective-permute-start.8
  23.8 1.3 %collective-permute-done.8.theirs_ref = bf16[16,2560]{1,0:T(8,128)(2,1)S(1)} collective-permute-done((bf16[16,2560]{1,0:T(8,128)(2,1)S(1)}, bf16[16,2560]{1,0:T(8,128)(2,1)S(1)}, u32[]{:S(2)}, u32[]{:S(2)}) %collective-permute-start.8) | collective-permute-done | bytes 81952 | tf_op jit(solution)/shard_map/ppermute | solution.py:644
  25.1 0.7 %place.1 = (bf16[2,4,1024]{2,1,0:T(4,128)(2,1)}, bf16[2,4,1024]{2,1,0:T(4,128)(2,1)}, bf16[2,4,8192]{2,1,0:T(4,128)(2,1)}) custom-call(bf16[16,2560]{1,0:T(8,128)(2,1)S(1)} %merge.1.mine_ref, bf16[16,2560]{1,0:T(8,128)(2,1)S(1)} %collective-permute-done.8.theirs_ref), custom_call_target="tpu_custom_call" | custom-call | tf_op jit(solution)/shard_map/place/pallas_call | solution.py:629
  (6 shorter events, 0.0 us)
Async XLA Ops:
  2.5 11.2 %collective-permute-start = (bf16[16,4096]{1,0:T(8,128)(2,1)}, bf16[16,4096]{1,0:T(8,128)(2,1)S(1)}, u32[]{:S(2)}, u32[]{:S(2)}) collective-permute-start(bf16[16,4096]{1,0:T(8,128)(2,1)} %get-tuple-element.22.refs_2_), channel_id=1, source_target_pairs={{0,4},{4,0},{8,12},{12,8},{1,5},{5,1},{9,13},{13,9},{2,6},{6,2},{1... | collective-permute-start | bytes 393224 | tf_op jit(solution)/shard_map/ppermute | solution.py:644
  5.6 8.1 %collective-permute-start.1 = (bf16[16,3072]{1,0:T(8,128)(2,1)}, bf16[16,3072]{1,0:T(8,128)(2,1)S(1)}, u32[]{:S(2)}, u32[]{:S(2)}) collective-permute-start(bf16[16,3072]{1,0:T(8,128)(2,1)} %get-tuple-element.23.refs_4_), channel_id=1, source_target_pairs={{0,8},{4,12},{8,0},{12,4},{1,9},{5,13},{9,1},{13,5},{2,10},{6,14},... | collective-permute-start | bytes 294920 | tf_op jit(solution)/shard_map/ppermute | solution.py:644
  8.2 5.5 %copy-start = (bf16[16,4096]{1,0:T(8,128)(2,1)S(1)}, bf16[16,4096]{1,0:T(8,128)(2,1)}, u32[]{:S(2)}) copy-start(bf16[16,4096]{1,0:T(8,128)(2,1)} %get-tuple-element.22.refs_2_) | copy-start | bytes 393220
  8.2 5.5 %copy-start.1 = (bf16[16,3072]{1,0:T(8,128)(2,1)S(1)}, bf16[16,3072]{1,0:T(8,128)(2,1)}, u32[]{:S(2)}) copy-start(bf16[16,3072]{1,0:T(8,128)(2,1)} %get-tuple-element.23.refs_4_) | copy-start | bytes 294916
  13.6 1.3 %collective-permute-start.3 = (bf16[16,2304]{1,0:T(8,128)(2,1)S(1)}, bf16[16,2304]{1,0:T(8,128)(2,1)S(1)}, u32[]{:S(2)}, u32[]{:S(2)}) collective-permute-start(bf16[16,2304]{1,0:T(8,128)(2,1)S(1)} %get-tuple-element.26), channel_id=1, source_target_pairs={{0,1},{1,0},{2,3},{3,2},{4,5},{5,4},{6,7},{7,6},{8,9},{9,8},{10,11... | collective-permute-start | bytes 221192 | tf_op jit(solution)/shard_map/ppermute | solution.py:644
  14.0 1.3 %collective-permute-start.2 = (bf16[16,896]{1,0:T(8,128)(2,1)S(1)}, bf16[16,896]{1,0:T(8,128)(2,1)S(1)}, u32[]{:S(2)}, u32[]{:S(2)}) collective-permute-start(bf16[16,896]{1,0:T(8,128)(2,1)S(1)} %get-tuple-element.24._.mine_ref), channel_id=1, source_target_pairs={{0,1},{1,0},{2,3},{3,2},{4,5},{5,4},{6,7},{7,6},{8,9},{9,8},{10,11... | collective-permute-start | bytes 86024 | tf_op jit(solution)/shard_map/ppermute | solution.py:644
  14.5 8.5 %collective-permute-start.7 = (bf16[16,3584]{1,0:T(8,128)(2,1)S(1)}, bf16[16,3584]{1,0:T(8,128)(2,1)S(1)}, u32[]{:S(2)}, u32[]{:S(2)}) collective-permute-start(bf16[16,3584]{1,0:T(8,128)(2,1)S(1)} %get-tuple-element.32.refs_7_), channel_id=1, source_target_pairs={{0,4},{4,0},{8,12},{12,8},{1,5},{5,1},{9,13},{13,9},{2,6},{6,2},{1... | collective-permute-start | bytes 344072 | tf_op jit(solution)/shard_map/ppermute | solution.py:644
  15.3 5.1 %collective-permute-start.4 = (bf16[16,3072]{1,0:T(8,128)(2,1)S(1)}, bf16[16,3072]{1,0:T(8,128)(2,1)S(1)}, u32[]{:S(2)}, u32[]{:S(2)}) collective-permute-start(bf16[16,3072]{1,0:T(8,128)(2,1)S(1)} %get-tuple-element.27.pa_ref), channel_id=1, source_target_pairs={{0,2},{1,3},{2,0},{3,1},{4,6},{5,7},{6,4},{7,5},{8,10},{9,11},{10,... | collective-permute-start | bytes 294920 | tf_op jit(solution)/shard_map/ppermute | solution.py:644
  16.9 5.4 %collective-permute-start.6 = (bf16[16,128]{1,0:T(8,128)(2,1)S(1)}, bf16[16,128]{1,0:T(8,128)(2,1)S(1)}, u32[]{:S(2)}, u32[]{:S(2)}) collective-permute-start(bf16[16,128]{1,0:T(8,128)(2,1)S(1)} %get-tuple-element.31), channel_id=1, source_target_pairs={{0,10},{1,11},{2,8},{3,9},{4,14},{5,15},{6,12},{7,13},{8,2},{9,3},... | collective-permute-start | bytes 12296 | tf_op jit(solution)/shard_map/ppermute | solution.py:698
  18.4 4.5 %collective-permute-start.5 = (bf16[16,128]{1,0:T(8,128)(2,1)S(1)}, bf16[16,128]{1,0:T(8,128)(2,1)S(1)}, u32[]{:S(2)}, u32[]{:S(2)}) collective-permute-start(bf16[16,128]{1,0:T(8,128)(2,1)S(1)} %get-tuple-element.31), channel_id=1, source_target_pairs={{0,8},{1,9},{2,10},{3,11},{4,12},{5,13},{6,14},{7,15},{8,0},{9,1},... | collective-permute-start | bytes 12296 | tf_op jit(solution)/shard_map/ppermute | solution.py:698
  23.7 1.3 %collective-permute-start.8 = (bf16[16,2560]{1,0:T(8,128)(2,1)S(1)}, bf16[16,2560]{1,0:T(8,128)(2,1)S(1)}, u32[]{:S(2)}, u32[]{:S(2)}) collective-permute-start(bf16[16,2560]{1,0:T(8,128)(2,1)S(1)} %merge.1.mine_ref), channel_id=1, source_target_pairs={{0,1},{1,0},{2,3},{3,2},{4,5},{5,4},{6,7},{7,6},{8,9},{9,8},{10,11... | collective-permute-start | bytes 245768 | tf_op jit(solution)/shard_map/ppermute | solution.py:644

commit v17 on v16

--- a/solution.py
+++ b/solution.py
@@ -486,8 +486,14 @@
     )(a, b, earlier)
 
 
-def blend_kernel(pairs, pa_ref, pb_ref, sums_ref, numer_ref, stats_ref):
+def blend_kernel(pairs, paired, pa_ref, pb_ref, ua_ref, ub_ref, *refs):
+    sums_ref, numer_ref, stats_ref, first_ref, second_ref = refs
     head = sums_ref.shape[1]
+    size = first_ref.shape[1]
+    a, b = ua_ref[:, :size].astype(F32), ub_ref[:, :size].astype(F32)
+    even = lax.axis_index("dp") % 2 == 0 if paired else True
+    first_ref[...] = jnp.where(even, a, b).astype(BF16)
+    second_ref[...] = jnp.where(even, b, a).astype(BF16)
     sums_ref[...] = pa_ref[:, :head].astype(F32) + pb_ref[:, :head].astype(F32)
     for p in range(pairs):
         end = slice(head + p * PAIR + GROUP * HD, head + (p + 1) * PAIR)
@@ -504,25 +510,27 @@
             ) * pa_ref[:, at].astype(F32) + broadcast_lane(fb, g) * pb_ref[:, at].astype(F32)
 
 
-def blend(pairs, part_a, part_b):
+def blend(pairs, paired, part_a, part_b, ups):
     head = part_a.shape[1] - pairs * PAIR
     return pl.pallas_call(
-        functools.partial(blend_kernel, pairs),
-        in_specs=[VMEM] * 2,
-        out_specs=[VMEM] * 3,
+        functools.partial(blend_kernel, pairs, paired),
+        in_specs=[VMEM] * 4,
+        out_specs=[VMEM] * 5,
         out_shape=[
             jax.ShapeDtypeStruct((16, head), F32),
             jax.ShapeDtypeStruct((16, pairs * GROUP * HD), F32),
             jax.ShapeDtypeStruct((16, pairs * 256), F32),
+            jax.ShapeDtypeStruct((16, 16 * HD), BF16),
+            jax.ShapeDtypeStruct((16, 16 * HD), BF16),
         ],
         compiler_params=pltpu.CompilerParams(vmem_limit_bytes=32 * MEBI),
         name="blend",
-    )(part_a, part_b)
-
-
-def merge_kernel(n, paired, width_all, *refs):
+    )(part_a, part_b, *ups)
+
+
+def merge_kernel(n, p, width_all, *refs):
     table_ref, qrot_ref, sums_ref, numer_ref, stats_ref = refs[:5]
-    backs, (ua_ref, ub_ref, out_ref) = refs[5 : 5 + n], refs[5 + n :]
+    backs, (up_ref, out_ref) = refs[5 : 5 + n], refs[5 + n :]
     pairs = qrot_ref.shape[1] // (GROUP * HD)
     width = pairs * 2 * HD
     cosine, sine = table_ref[8:16], table_ref[16:]
@@ -535,15 +543,10 @@
     z = jnp.concatenate(
         [jnp.where(lane8 < RANK, z, 0.0), jnp.where(lane8 < RANK, 0.0, z)], 0
     ).astype(BF16)
-    adapted = []
-    for ref in (ua_ref, ub_ref):
-        ups = jnp.concatenate([ref[:, i : i + 128] for i in range(0, 16 * HD, 128)], 0)
-        adapted.append(lax.dot_general(z, ups, NT, preferred_element_type=F32))
-    if paired:
-        even = lax.axis_index("dp") % 2 == 0
-        a, b = adapted
-        adapted = [jnp.where(even, a, b), jnp.where(even, b, a)]
-    total = sums[:, :width] + jnp.concatenate(adapted, 1)
+    ups = jnp.concatenate([up_ref[:, i : i + 128] for i in range(0, 16 * HD, 128)], 0)
+    total = sums[:, 2 * p * HD : 2 * (p + 1) * HD] + lax.dot_general(
+        z, ups, NT, preferred_element_type=F32
+    )
     scale = lax.rsqrt(squares / width_all + EPSILON)
     lane = lax.broadcasted_iota(jnp.int32, (16, 128), 1)
     step = lax.broadcasted_iota(jnp.int32, (16, 128), 0) % STEPS
@@ -558,77 +561,76 @@
             0,
         )
 
-    for p in range(pairs):
-        new_keys, new_values = [], []
-        for e in range(2):
-            at = slice((2 * p + e) * HD, (2 * p + e + 1) * HD)
-            new_keys.append(rounded(rotated(total[:8, at] * scale, cosine, sine)))
-            new_values.append(rounded(total[8:, at] * scale))
-            fresh = jnp.concatenate([new_keys[e], new_values[e]], 0)
-            start = pairs * GROUP * HD + (2 * p + e) * HD
-            out_ref[:, start : start + HD] = fresh.astype(BF16)
-        keys = [of_step(new_keys, j) for j in range(STEPS)]
-        values = [of_step(new_values, j) for j in range(STEPS)]
-        scores = [jnp.zeros((16, 128), F32) for _ in range(STEPS)]
-        for g in range(GROUP):
-            q = qrot_ref[:, (p * GROUP + g) * HD : (p * GROUP + g + 1) * HD].astype(F32)
-            for j in range(STEPS):
-                dot = jnp.sum(q * keys[j], 1, keepdims=True)
-                scores[j] = jnp.where(lane == g, dot, scores[j])
-        scores = [jnp.where(j <= step, scores[j], MASKED_SCORE) for j in range(STEPS)]
-        cached = stats_ref[:, 2 * p * 128 : (2 * p + 1) * 128]
-        top = functools.reduce(jnp.maximum, [*scores, cached])
-        fresh = [rounded(jnp.exp2((scores[j] - top) * EXPONENT)) for j in range(STEPS)]
-        factor = jnp.exp2(jnp.minimum(cached - top, 0.0) * EXPONENT)
-        denom = factor * stats_ref[:, (2 * p + 1) * 128 : (2 * p + 2) * 128]
-        inverse = 1.0 / functools.reduce(jnp.add, fresh, denom)
-        coefficients = [c * inverse for c in (*fresh, factor)]
-        for g in range(GROUP):
-            at = slice((p * GROUP + g) * HD, (p * GROUP + g + 1) * HD)
-            tile = jnp.zeros((16, 128), F32)
-            for c, term in zip(coefficients, [*values, numer_ref[:, at]]):
-                tile = tile + broadcast_lane(c, g) * term
-            out_ref[:, at] = tile.astype(BF16)
-
-
-def merge(paired, width_all, table, qrot, parts, backs, ups):
-    operands = [table, qrot, *parts, *backs, *ups]
-    pairs = qrot.shape[1] // (GROUP * HD)
+    new_keys, new_values = [], []
+    for e in range(2):
+        at = slice(e * HD, (e + 1) * HD)
+        new_keys.append(rounded(rotated(total[:8, at] * scale, cosine, sine)))
+        new_values.append(rounded(total[8:, at] * scale))
+        fresh = jnp.concatenate([new_keys[e], new_values[e]], 0)
+        start = GROUP * HD + e * HD
+        out_ref[:, start : start + HD] = fresh.astype(BF16)
+    keys = [of_step(new_keys, j) for j in range(STEPS)]
+    values = [of_step(new_values, j) for j in range(STEPS)]
+    scores = [jnp.zeros((16, 128), F32) for _ in range(STEPS)]
+    for g in range(GROUP):
+        q = qrot_ref[:, (p * GROUP + g) * HD : (p * GROUP + g + 1) * HD].astype(F32)
+        for j in range(STEPS):
+            dot = jnp.sum(q * keys[j], 1, keepdims=True)
+            scores[j] = jnp.where(lane == g, dot, scores[j])
+    scores = [jnp.where(j <= step, scores[j], MASKED_SCORE) for j in range(STEPS)]
+    cached = stats_ref[:, 2 * p * 128 : (2 * p + 1) * 128]
+    top = functools.reduce(jnp.maximum, [*scores, cached])
+    fresh = [rounded(jnp.exp2((scores[j] - top) * EXPONENT)) for j in range(STEPS)]
+    factor = jnp.exp2(jnp.minimum(cached - top, 0.0) * EXPONENT)
+    denom = factor * stats_ref[:, (2 * p + 1) * 128 : (2 * p + 2) * 128]
+    inverse = 1.0 / functools.reduce(jnp.add, fresh, denom)
+    coefficients = [c * inverse for c in (*fresh, factor)]
+    for g in range(GROUP):
+        at = slice((p * GROUP + g) * HD, (p * GROUP + g + 1) * HD)
+        tile = jnp.zeros((16, 128), F32)
+        for c, term in zip(coefficients, [*values, numer_ref[:, at]]):
+            tile = tile + broadcast_lane(c, g) * term
+        out_ref[:, g * HD : (g + 1) * HD] = tile.astype(BF16)
+    if out_ref.shape[1] > (GROUP + 2) * HD:
+        out_ref[:, (GROUP + 2) * HD :] = jnp.zeros((16, HD), BF16)
+
+
+def merge(p, width_all, table, qrot, blended, backs, ups):
+    operands = [table, qrot, *blended, *backs, ups]
     return pl.pallas_call(
-        functools.partial(merge_kernel, len(backs), paired, width_all),
+        functools.partial(merge_kernel, len(backs), p, width_all),
         in_specs=[VMEM] * len(operands),
         out_specs=VMEM,
-        out_shape=jax.ShapeDtypeStruct((16, pairs * (GROUP + 2) * HD), BF16),
+        out_shape=jax.ShapeDtypeStruct((16, (GROUP + 2 + (p == 0)) * HD), BF16),
         compiler_params=pltpu.CompilerParams(vmem_limit_bytes=32 * MEBI),
         name="merge",
     )(*operands)
 
 
-def place_kernel(mine_ref, theirs_ref, keys_out, values_out, out_ref):
-    pairs = mine_ref.shape[1] // ((GROUP + 2) * HD)
-    for c, ref in enumerate((mine_ref, theirs_ref)):
-        for p in range(pairs):
-            pair = pair_at(c * pairs + p)
-            tiles = ref[:, p * GROUP * HD : (p + 1) * GROUP * HD].astype(F32)
-            size = GROUP * HD
-            for e in range(2):
-                at = pl.ds(pl.multiple_of((2 * pair + e) * size, size), size)
-                for s in range(2):
-                    rows = slice(8 * e + 4 * s, 8 * e + 4 * s + 4)
-                    out_ref[s, :, at] = tiles[rows].astype(BF16)
-            start = pairs * GROUP * HD + p * 2 * HD
-            fresh = ref[:, start : start + 2 * HD].astype(F32)
-            at = pl.ds(pl.multiple_of(pair * 2 * HD, 2 * HD), 2 * HD)
-            for i, out in enumerate((keys_out, values_out)):
-                for s in range(2):
-                    rows = slice(8 * i + 4 * s, 8 * i + 4 * s + 4)
-                    out[s, :, at] = fresh[rows].astype(BF16)
-
-
-def place(width, mine, theirs):
+def place_kernel(*refs):
+    pairs = (len(refs) - 3) // 2
+    keys_out, values_out, out_ref = refs[2 * pairs :]
+    for i, ref in enumerate(refs[: 2 * pairs]):
+        pair = pair_at(i)
+        size = GROUP * HD
+        tiles = ref[:, :size].astype(F32)
+        for e in range(2):
+            at = pl.ds(pl.multiple_of((2 * pair + e) * size, size), size)
+            for s in range(2):
+                rows = slice(8 * e + 4 * s, 8 * e + 4 * s + 4)
+                out_ref[s, :, at] = tiles[rows].astype(BF16)
+        fresh = ref[:, size : size + 2 * HD].astype(F32)
+        at = pl.ds(pl.multiple_of(pair * 2 * HD, 2 * HD), 2 * HD)
+        for i, out in enumerate((keys_out, values_out)):
+            for s in range(2):
+                rows = slice(8 * i + 4 * s, 8 * i + 4 * s + 4)
+                out[s, :, at] = fresh[rows].astype(BF16)
+
+
+def place(width, *results):
     return pl.pallas_call(
         place_kernel,
-        in_specs=[VMEM] * 2,
+        in_specs=[VMEM] * len(results),
         out_specs=[VMEM] * 3,
         out_shape=[
             jax.ShapeDtypeStruct((2, STEPS, width), BF16),
@@ -637,7 +639,7 @@
         ],
         compiler_params=pltpu.CompilerParams(vmem_limit_bytes=32 * MEBI),
         name="place",
-    )(mine, theirs)
+    )(*results)
 
 
 def swap(value, axis, n, distance):
@@ -696,16 +698,13 @@
         for e in (0, 2):
             perm = [(s * n_tensor + t, (s ^ d) * n_tensor + (t ^ e)) for s, t in places]
             backs.append(lax.ppermute(reply, ("dp", "tensor"), perm))
-    merged = merge(
-        paired,
-        float(depth * n_tensor),
-        table,
-        qrot,
-        blend(width // (4 * HD), part, part_far),
-        backs,
-        ups,
-    )
-    return place(width, merged, to_tensor(merged, 1))
+    pairs = width // (4 * HD)
+    *blended, first, second = blend(pairs, paired, part, part_far, ups)
+    mine = [
+        merge(p, float(depth * n_tensor), table, qrot, blended, backs, up)
+        for p, up in enumerate((first, second))
+    ]
+    return place(width, *mine, *[to_tensor(result, 1) for result in mine])
 
 
 def solution(mesh):

time: 25.9 us -> 26.6 us (1.027)
  starting transfers between devices: 11.2 us -> 11.8 us
  Pallas kernels: 9.4 us -> 9.9 us
  waiting for transfers between devices: 4.42 us -> 4.01 us
    ppermute x7 -> x8, starting transfers between devices: 8.31 us -> 8.87 us  [swap(): return lax.ppermute(value, axis, [(i, i ^ distance) for i in range(n)])]
    pallas_call x3 -> x4, Pallas kernels: 1.62 us -> 2.12 us  [the longest x2 1.24 us: merge(): pl.pallas_call(functools.partial(merge_kernel, len(backs), p, width_all),...]
    ppermute x7 -> x8, waiting for transfers between devices: 2.1 us -> 1.71 us  [swap(): return lax.ppermute(value, axis, [(i, i ^ distance) for i in range(n)])]
  transfers between devices with their start and end apart: 9 -> 10, of which waited for: 5 -> 5; matrix products, arithmetic and copies ran while one was open for 0% -> 0% of each run, Pallas kernels for 24% -> 25%
where the time goes in v17:
time: 26.6 us; the launch traced here: 26.4 us
  starting transfers between devices  11.8 us (44%)
  Pallas kernels  9.9 us (37%)
  waiting for transfers between devices  4.01 us (15%)
  between operations  0.73 us (3%)
    ppermute x8, starting transfers between devices, swap(): return lax.ppermute(value, axis, [(i, i ^ distance) for i in range(n)])  8.87 us
    pallas_call x1, Pallas kernels, local(): pl.pallas_call(local_kernel, in_specs=[HBM] * 6, out_specs=[VMEM] * 5, ou...  5.4 us
    ppermute x2, starting transfers between devices, shards(): backs.append(lax.ppermute(reply, ('dp', 'tensor'), perm))  2.9 us
    ppermute x2, waiting for transfers between devices, shards(): backs.append(lax.ppermute(reply, ('dp', 'tensor'), perm))  2.3 us
    pallas_call x1, Pallas kernels, pack(): pl.pallas_call(pack_kernel, in_specs=[HBM] * len(operands), out_specs=[HB...  1.88 us
    ppermute x8, waiting for transfers between devices, swap(): return lax.ppermute(value, axis, [(i, i ^ distance) for i in range(n)])  1.71 us
    pallas_call x2, Pallas kernels, merge(): pl.pallas_call(functools.partial(merge_kernel, len(backs), p, width_all),...  1.24 us
    pallas_call x1, Pallas kernels, place(): pl.pallas_call(place_kernel, in_specs=[VMEM] * len(results), out_specs=[V...  0.69 us
  transfers between devices with their start and end apart: 10, of which 5 were waited for; matrix products, arithmetic and copies ran while one was open for 0% of the time, Pallas kernels for 25%

profile of v17, /device:TPU:0, one launch (start us, length us, event | category | flops | bytes accessed | tf_op | source)
XLA Modules:
  0.0 26.4 jit_solution(12189031425161946562)
XLA Ops:
  0.6 1.9 %pack.1 = (bf16[16,4096]{1,0:T(8,128)(2,1)}, bf16[16,3072]{1,0:T(8,128)(2,1)}, bf16[16,3328]{1,0:T(8,128)(2,1)}) custom-call(f32[16,2048]{1,0:T(8,128)} %refs_0_.1, f32[16,2048]{1,0:T(8,128)} %refs_1_.1, bf16[2,4,2048]{2,1,0:T(4,128)(2,1)} %refs_2_.1, bf16[16,128]{1,0:T(8,128)(2,1)} %bitcast.6, s32[1,2]{1,0:T(1,128)} %bitcast.7, f32[64,256]{1,0:T(8,128)} %bitcast.4, ...), custom_call_target="tpu_custom_call" | custom-call | tf_op jit(solution)/shard_map/pack/pallas_call | solution.py:127
  2.5 3.1 %collective-permute-start = (bf16[16,4096]{1,0:T(8,128)(2,1)}, bf16[16,4096]{1,0:T(8,128)(2,1)S(1)}, u32[]{:S(2)}, u32[]{:S(2)}) collective-permute-start(bf16[16,4096]{1,0:T(8,128)(2,1)} %get-tuple-element.24.refs_2_), channel_id=1, source_target_pairs={{0,4},{4,0},{8,12},{12,8},{1,5},{5,1},{9,13},{13,9},{2,6},{6,2},{1... | collective-permute-start | bytes 393224 | tf_op jit(solution)/shard_map/ppermute | solution.py:646
  5.6 2.6 %collective-permute-start.1 = (bf16[16,3072]{1,0:T(8,128)(2,1)}, bf16[16,3072]{1,0:T(8,128)(2,1)S(1)}, u32[]{:S(2)}, u32[]{:S(2)}) collective-permute-start(bf16[16,3072]{1,0:T(8,128)(2,1)} %get-tuple-element.25.refs_4_), channel_id=1, source_target_pairs={{0,8},{4,12},{8,0},{12,4},{1,9},{5,13},{9,1},{13,5},{2,10},{6,14},... | collective-permute-start | bytes 294920 | tf_op jit(solution)/shard_map/ppermute | solution.py:646
  8.2 5.4 %local.1 = (bf16[16,2304]{1,0:T(8,128)(2,1)S(1)}, bf16[16,2304]{1,0:T(8,128)(2,1)S(1)}, f32[16,1024]{1,0:T(8,128)S(1)}, bf16[16,2048]{1,0:T(8,128)(2,1)S(1)}, f32[24,128]{1,0:T(8,128)S(1)}) custom-call(bf16[16,3328]{1,0:T(8,128)(2,1)} %get-tuple-element.20.x_hbm, bf16[2,4,8192]{2,1,0:T(4,128)(2,1)} %q_hbm.1, bf16[2,512,1024]{2,1,0:T(8,128)(2,1)} %k_hbm.1, ...), custom_call_target="tpu_custom_call" | custom-call | flops 402653184 | bytes 12582912 | tf_op jit(solution)/shard_map/local/pallas_call | solution.py:346
  13.6 0.1 collective-permute-start.3
  13.7 0.3 rank_products.1
  14.0 0.5 %collective-permute-start.2 = (bf16[16,896]{1,0:T(8,128)(2,1)S(1)}, bf16[16,896]{1,0:T(8,128)(2,1)S(1)}, u32[]{:S(2)}, u32[]{:S(2)}) collective-permute-start(bf16[16,896]{1,0:T(8,128)(2,1)S(1)} %get-tuple-element.26._.mine_ref), channel_id=1, source_target_pairs={{0,1},{1,0},{2,3},{3,2},{4,5},{5,4},{6,7},{7,6},{8,9},{9,8},{10,11... | collective-permute-start | bytes 86024 | tf_op jit(solution)/shard_map/ppermute | solution.py:646
  14.5 0.4 %collective-permute-start.5 = (bf16[16,3584]{1,0:T(8,128)(2,1)S(1)}, bf16[16,3584]{1,0:T(8,128)(2,1)S(1)}, u32[]{:S(2)}, u32[]{:S(2)}) collective-permute-start(bf16[16,3584]{1,0:T(8,128)(2,1)S(1)} %get-tuple-element.30.ua_ref), channel_id=1, source_target_pairs={{0,4},{4,0},{8,12},{12,8},{1,5},{5,1},{9,13},{13,9},{2,6},{6,2},{1... | collective-permute-start | bytes 344072 | tf_op jit(solution)/shard_map/ppermute | solution.py:646
  14.9 0.0 collective-permute-done.3.b_ref
  14.9 0.2 combine_cache.1.cache_ref
  15.2 0.2 collective-permute-done.2.theirs_ref
  15.4 1.6 %collective-permute-start.4 = (bf16[16,3072]{1,0:T(8,128)(2,1)S(1)}, bf16[16,3072]{1,0:T(8,128)(2,1)S(1)}, u32[]{:S(2)}, u32[]{:S(2)}) collective-permute-start(bf16[16,3072]{1,0:T(8,128)(2,1)S(1)} %get-tuple-element.29.pa_ref), channel_id=1, source_target_pairs={{0,2},{1,3},{2,0},{3,1},{4,6},{5,7},{6,4},{7,5},{8,10},{9,11},{10,... | collective-permute-start | bytes 294920 | tf_op jit(solution)/shard_map/ppermute | solution.py:646
  16.9 1.5 %collective-permute-start.7 = (bf16[16,128]{1,0:T(8,128)(2,1)S(1)}, bf16[16,128]{1,0:T(8,128)(2,1)S(1)}, u32[]{:S(2)}, u32[]{:S(2)}) collective-permute-start(bf16[16,128]{1,0:T(8,128)(2,1)S(1)} %get-tuple-element.34), channel_id=1, source_target_pairs={{0,10},{1,11},{2,8},{3,9},{4,14},{5,15},{6,12},{7,13},{8,2},{9,3},... | collective-permute-start | bytes 12296 | tf_op jit(solution)/shard_map/ppermute | solution.py:700
  18.4 1.4 %collective-permute-start.6 = (bf16[16,128]{1,0:T(8,128)(2,1)S(1)}, bf16[16,128]{1,0:T(8,128)(2,1)S(1)}, u32[]{:S(2)}, u32[]{:S(2)}) collective-permute-start(bf16[16,128]{1,0:T(8,128)(2,1)S(1)} %get-tuple-element.34), channel_id=1, source_target_pairs={{0,8},{1,9},{2,10},{3,11},{4,12},{5,13},{6,14},{7,15},{8,0},{9,1},... | collective-permute-start | bytes 12296 | tf_op jit(solution)/shard_map/ppermute | solution.py:700
  19.8 0.7 %collective-permute-done.4.pb_ref = bf16[16,3072]{1,0:T(8,128)(2,1)S(1)} collective-permute-done((bf16[16,3072]{1,0:T(8,128)(2,1)S(1)}, bf16[16,3072]{1,0:T(8,128)(2,1)S(1)}, u32[]{:S(2)}, u32[]{:S(2)}) %collective-permute-start.4) | collective-permute-done | bytes 98336 | tf_op jit(solution)/shard_map/ppermute | solution.py:646
  20.5 0.2 blend.1
  20.7 1.7 %collective-permute-done.7.refs_6_ = bf16[16,128]{1,0:T(8,128)(2,1)S(1)} collective-permute-done((bf16[16,128]{1,0:T(8,128)(2,1)S(1)}, bf16[16,128]{1,0:T(8,128)(2,1)S(1)}, u32[]{:S(2)}, u32[]{:S(2)}) %collective-permute-start.7) | collective-permute-done | bytes 4128 | tf_op jit(solution)/shard_map/ppermute | solution.py:700
  22.3 0.6 %collective-permute-done.6.refs_5_ = bf16[16,128]{1,0:T(8,128)(2,1)S(1)} collective-permute-done((bf16[16,128]{1,0:T(8,128)(2,1)S(1)}, bf16[16,128]{1,0:T(8,128)(2,1)S(1)}, u32[]{:S(2)}, u32[]{:S(2)}) %collective-permute-start.6) | collective-permute-done | bytes 4128 | tf_op jit(solution)/shard_map/ppermute | solution.py:700
  23.0 0.6 %merge.2.refs_0_ = bf16[16,1408]{1,0:T(8,128)(2,1)S(1)} custom-call(f32[24,128]{1,0:T(8,128)S(1)} %get-tuple-element.21.refs_1_.refs_0_, bf16[16,2048]{1,0:T(8,128)(2,1)S(1)} %get-tuple-element.22.refs_1_, f32[16,768]{1,0:T(8,128)S(1)} %get-tuple-element.31.refs_2_, f32[16,2048]{1,0:T(8,128)S(1)} %get-tuple-element.32.refs_3_, ...), custom_call_target="tpu_custom_call" | custom-call | tf_op jit(solution)/shard_map/merge/pallas_call | solution.py:600
  23.6 0.1 collective-permute-start.8
  23.7 0.6 %merge.3.refs_1_ = bf16[16,1280]{1,0:T(8,128)(2,1)S(1)} custom-call(f32[24,128]{1,0:T(8,128)S(1)} %get-tuple-element.21.refs_1_.refs_0_, bf16[16,2048]{1,0:T(8,128)(2,1)S(1)} %get-tuple-element.22.refs_1_, f32[16,768]{1,0:T(8,128)S(1)} %get-tuple-element.31.refs_2_, f32[16,2048]{1,0:T(8,128)S(1)} %get-tuple-element.32.refs_3_, ...), custom_call_target="tpu_custom_call" | custom-call | tf_op jit(solution)/shard_map/merge/pallas_call | solution.py:600
  24.3 0.6 %collective-permute-start.9 = (bf16[16,1280]{1,0:T(8,128)(2,1)S(1)}, bf16[16,1280]{1,0:T(8,128)(2,1)S(1)}, u32[]{:S(2)}, u32[]{:S(2)}) collective-permute-start(bf16[16,1280]{1,0:T(8,128)(2,1)S(1)} %merge.3.refs_1_), channel_id=1, source_target_pairs={{0,1},{1,0},{2,3},{3,2},{4,5},{5,4},{6,7},{7,6},{8,9},{9,8},{10,11... | collective-permute-start | bytes 122888 | tf_op jit(solution)/shard_map/ppermute | solution.py:646
  24.8 0.9 %collective-permute-done.9.refs_3_ = bf16[16,1280]{1,0:T(8,128)(2,1)S(1)} collective-permute-done((bf16[16,1280]{1,0:T(8,128)(2,1)S(1)}, bf16[16,1280]{1,0:T(8,128)(2,1)S(1)}, u32[]{:S(2)}, u32[]{:S(2)}) %collective-permute-start.9) | collective-permute-done | bytes 40992 | tf_op jit(solution)/shard_map/ppermute | solution.py:646
  25.7 0.7 %place.1 = (bf16[2,4,1024]{2,1,0:T(4,128)(2,1)}, bf16[2,4,1024]{2,1,0:T(4,128)(2,1)}, bf16[2,4,8192]{2,1,0:T(4,128)(2,1)}) custom-call(bf16[16,1408]{1,0:T(8,128)(2,1)S(1)} %merge.2.refs_0_, bf16[16,1280]{1,0:T(8,128)(2,1)S(1)} %merge.3.refs_1_, bf16[16,1408]{1,0:T(8,128)(2,1)S(1)} %collective-permute-done.8.refs_2_, ...), custom_call_target="tpu_custom_call" | custom-call | tf_op jit(solution)/shard_map/place/pallas_call | solution.py:631
  (9 shorter events, 0.0 us)
Async XLA Ops:
  2.5 11.2 %collective-permute-start = (bf16[16,4096]{1,0:T(8,128)(2,1)}, bf16[16,4096]{1,0:T(8,128)(2,1)S(1)}, u32[]{:S(2)}, u32[]{:S(2)}) collective-permute-start(bf16[16,4096]{1,0:T(8,128)(2,1)} %get-tuple-element.24.refs_2_), channel_id=1, source_target_pairs={{0,4},{4,0},{8,12},{12,8},{1,5},{5,1},{9,13},{13,9},{2,6},{6,2},{1... | collective-permute-start | bytes 393224 | tf_op jit(solution)/shard_map/ppermute | solution.py:646
  5.6 8.1 %collective-permute-start.1 = (bf16[16,3072]{1,0:T(8,128)(2,1)}, bf16[16,3072]{1,0:T(8,128)(2,1)S(1)}, u32[]{:S(2)}, u32[]{:S(2)}) collective-permute-start(bf16[16,3072]{1,0:T(8,128)(2,1)} %get-tuple-element.25.refs_4_), channel_id=1, source_target_pairs={{0,8},{4,12},{8,0},{12,4},{1,9},{5,13},{9,1},{13,5},{2,10},{6,14},... | collective-permute-start | bytes 294920 | tf_op jit(solution)/shard_map/ppermute | solution.py:646
  8.2 5.5 %copy-start = (bf16[16,4096]{1,0:T(8,128)(2,1)S(1)}, bf16[16,4096]{1,0:T(8,128)(2,1)}, u32[]{:S(2)}) copy-start(bf16[16,4096]{1,0:T(8,128)(2,1)} %get-tuple-element.24.refs_2_) | copy-start | bytes 393220
  8.2 5.5 %copy-start.1 = (bf16[16,3072]{1,0:T(8,128)(2,1)S(1)}, bf16[16,3072]{1,0:T(8,128)(2,1)}, u32[]{:S(2)}) copy-start(bf16[16,3072]{1,0:T(8,128)(2,1)} %get-tuple-element.25.refs_4_) | copy-start | bytes 294916
  13.6 1.3 %collective-permute-start.3 = (bf16[16,2304]{1,0:T(8,128)(2,1)S(1)}, bf16[16,2304]{1,0:T(8,128)(2,1)S(1)}, u32[]{:S(2)}, u32[]{:S(2)}) collective-permute-start(bf16[16,2304]{1,0:T(8,128)(2,1)S(1)} %get-tuple-element.28), channel_id=1, source_target_pairs={{0,1},{1,0},{2,3},{3,2},{4,5},{5,4},{6,7},{7,6},{8,9},{9,8},{10,11... | collective-permute-start | bytes 221192 | tf_op jit(solution)/shard_map/ppermute | solution.py:646
  14.0 1.3 %collective-permute-start.2 = (bf16[16,896]{1,0:T(8,128)(2,1)S(1)}, bf16[16,896]{1,0:T(8,128)(2,1)S(1)}, u32[]{:S(2)}, u32[]{:S(2)}) collective-permute-start(bf16[16,896]{1,0:T(8,128)(2,1)S(1)} %get-tuple-element.26._.mine_ref), channel_id=1, source_target_pairs={{0,1},{1,0},{2,3},{3,2},{4,5},{5,4},{6,7},{7,6},{8,9},{9,8},{10,11... | collective-permute-start | bytes 86024 | tf_op jit(solution)/shard_map/ppermute | solution.py:646
  14.5 5.3 %collective-permute-start.5 = (bf16[16,3584]{1,0:T(8,128)(2,1)S(1)}, bf16[16,3584]{1,0:T(8,128)(2,1)S(1)}, u32[]{:S(2)}, u32[]{:S(2)}) collective-permute-start(bf16[16,3584]{1,0:T(8,128)(2,1)S(1)} %get-tuple-element.30.ua_ref), channel_id=1, source_target_pairs={{0,4},{4,0},{8,12},{12,8},{1,5},{5,1},{9,13},{13,9},{2,6},{6,2},{1... | collective-permute-start | bytes 344072 | tf_op jit(solution)/shard_map/ppermute | solution.py:646
  15.4 5.1 %collective-permute-start.4 = (bf16[16,3072]{1,0:T(8,128)(2,1)S(1)}, bf16[16,3072]{1,0:T(8,128)(2,1)S(1)}, u32[]{:S(2)}, u32[]{:S(2)}) collective-permute-start(bf16[16,3072]{1,0:T(8,128)(2,1)S(1)} %get-tuple-element.29.pa_ref), channel_id=1, source_target_pairs={{0,2},{1,3},{2,0},{3,1},{4,6},{5,7},{6,4},{7,5},{8,10},{9,11},{10,... | collective-permute-start | bytes 294920 | tf_op jit(solution)/shard_map/ppermute | solution.py:646
  16.9 5.4 %collective-permute-start.7 = (bf16[16,128]{1,0:T(8,128)(2,1)S(1)}, bf16[16,128]{1,0:T(8,128)(2,1)S(1)}, u32[]{:S(2)}, u32[]{:S(2)}) collective-permute-start(bf16[16,128]{1,0:T(8,128)(2,1)S(1)} %get-tuple-element.34), channel_id=1, source_target_pairs={{0,10},{1,11},{2,8},{3,9},{4,14},{5,15},{6,12},{7,13},{8,2},{9,3},... | collective-permute-start | bytes 12296 | tf_op jit(solution)/shard_map/ppermute | solution.py:700
  18.4 4.5 %collective-permute-start.6 = (bf16[16,128]{1,0:T(8,128)(2,1)S(1)}, bf16[16,128]{1,0:T(8,128)(2,1)S(1)}, u32[]{:S(2)}, u32[]{:S(2)}) collective-permute-start(bf16[16,128]{1,0:T(8,128)(2,1)S(1)} %get-tuple-element.34), channel_id=1, source_target_pairs={{0,8},{1,9},{2,10},{3,11},{4,12},{5,13},{6,14},{7,15},{8,0},{9,1},... | collective-permute-start | bytes 12296 | tf_op jit(solution)/shard_map/ppermute | solution.py:700
  23.6 2.1 %collective-permute-start.8 = (bf16[16,1408]{1,0:T(8,128)(2,1)S(1)}, bf16[16,1408]{1,0:T(8,128)(2,1)S(1)}, u32[]{:S(2)}, u32[]{:S(2)}) collective-permute-start(bf16[16,1408]{1,0:T(8,128)(2,1)S(1)} %merge.2.refs_0_), channel_id=1, source_target_pairs={{0,1},{1,0},{2,3},{3,2},{4,5},{5,4},{6,7},{7,6},{8,9},{9,8},{10,11... | collective-permute-start | bytes 135176 | tf_op jit(solution)/shard_map/ppermute | solution.py:646
  24.3 1.4 %collective-permute-start.9 = (bf16[16,1280]{1,0:T(8,128)(2,1)S(1)}, bf16[16,1280]{1,0:T(8,128)(2,1)S(1)}, u32[]{:S(2)}, u32[]{:S(2)}) collective-permute-start(bf16[16,1280]{1,0:T(8,128)(2,1)S(1)} %merge.3.refs_1_), channel_id=1, source_target_pairs={{0,1},{1,0},{2,3},{3,2},{4,5},{5,4},{6,7},{7,6},{8,9},{9,8},{10,11... | collective-permute-start | bytes 122888 | tf_op jit(solution)/shard_map/ppermute | solution.py:646

commit v18 on v13

--- a/solution.py
+++ b/solution.py
@@ -191,7 +191,7 @@
     return result
 
 
-def attend(pairs, masks, queries, k_ref, v_ref, between, out_ref):
+def attend(pairs, masks, queries, k_ref, v_ref, between, out_refs):
     scores = []
     for i, p in enumerate(pairs):
         for s in range(2):
@@ -213,6 +213,7 @@
             values = v_ref[s, :, 2 * p * HD : 2 * (p + 1) * HD]
             numers.append(jnp.dot(weights[at], values, preferred_element_type=F32))
     for i, p in enumerate(pairs):
+        out_ref, place = out_refs[2 * i // len(pairs)], i % (len(pairs) // 2) * PAIR
         outs, ends = [[], []], []
         for e in range(2):
             back, stats = [], []
@@ -231,9 +232,9 @@
             a, b = exchanged(*stats)
             ends.append(jnp.where(lane8 % 8 < 4, a, pltpu.roll(b, 4, 1)))
         for g in range(GROUP):
-            at = slice(i * PAIR + g * HD, i * PAIR + (g + 1) * HD)
+            at = slice(place + g * HD, place + (g + 1) * HD)
             out_ref[:, at] = jnp.concatenate([outs[0][g], outs[1][g]], 0).astype(BF16)
-        out_ref[:, i * PAIR + GROUP * HD : (i + 1) * PAIR] = jnp.concatenate(ends, 0).astype(BF16)
+        out_ref[:, place + GROUP * HD : place + PAIR] = jnp.concatenate(ends, 0).astype(BF16)
 
 
 def pair_at(i):
@@ -313,23 +314,21 @@
             halves.append(jnp.dot(x[:, at], ref[at], preferred_element_type=F32))
         parts.append(jnp.concatenate(halves, 0))
 
-    def between(h):
-        groups[h][2].wait()
-        if h == 0:
-            for copies in weights[chunks // 2 : 3 * chunks // 4]:
-                start(copies)
-        else:
-            for c in range(chunks // 2):
-                project(c)
-
-    for h, out_ref in enumerate((keep_ref, send_ref)):
+    def between():
+        for copies in weights[chunks // 2 :]:
+            start(copies)
+        for h in range(2):
+            groups[h][2].wait()
+        for c in range(chunks // 2):
+            project(c)
+
+    for h in range(2):
         groups[h][1].wait()
-        for copies in weights[3 * chunks // 4 :] if h else weights[chunks // 4 : chunks // 2]:
-            start(copies)
-        attend(
-            range(h * pairs // 2, (h + 1) * pairs // 2),
-            masks, queries[h], k_ref, v_ref, functools.partial(between, h), out_ref,
-        )
+    for copies in weights[chunks // 4 : chunks // 2]:
+        start(copies)
+    attend(
+        range(pairs), masks, queries[0] + queries[1], k_ref, v_ref, between, (keep_ref, send_ref)
+    )
     for c in range(chunks // 2, chunks):
         project(c)
     total = functools.reduce(jnp.add, parts)

time: 26 us -> 26 us (level)
  waiting for transfers between devices: 4.6 us -> 4.14 us
  Pallas kernels: 9.27 us -> 9.72 us
    pallas_call x1, Pallas kernels: 5.4 us -> 5.85 us  [local(): pl.pallas_call(local_kernel, in_specs=[HBM] * 6, out_specs=[VMEM] * 5, ou...]
    ppermute x2, waiting for transfers between devices: 3.15 us -> 2.7 us  [shards(): backs.append(lax.ppermute(reply, ('dp', 'tensor'), perm))]
  transfers between devices with their start and end apart: 9 -> 9, of which waited for: 4 -> 4; matrix products, arithmetic and copies ran while one was open for 0% -> 0% of each run, Pallas kernels for 23% -> 25%
where the time goes in v18:
time: 26 us; the launch traced here: 25.8 us
  starting transfers between devices  11.2 us (43%)
  Pallas kernels  9.72 us (37%)
  waiting for transfers between devices  4.14 us (16%)
  between operations  0.72 us (3%)
    ppermute x7, starting transfers between devices, swap(): return lax.ppermute(value, axis, [(i, i ^ distance) for i in range(n)])  8.32 us
    pallas_call x1, Pallas kernels, local(): pl.pallas_call(local_kernel, in_specs=[HBM] * 6, out_specs=[VMEM] * 5, ou...  5.85 us
    ppermute x2, starting transfers between devices, shards(): backs.append(lax.ppermute(reply, ('dp', 'tensor'), perm))  2.89 us
    ppermute x2, waiting for transfers between devices, shards(): backs.append(lax.ppermute(reply, ('dp', 'tensor'), perm))  2.7 us
    pallas_call x1, Pallas kernels, pack(): pl.pallas_call(pack_kernel, in_specs=[HBM] * len(operands), out_specs=[HB...  1.88 us
    ppermute x7, waiting for transfers between devices, swap(): return lax.ppermute(value, axis, [(i, i ^ distance) for i in range(n)])  1.45 us
    pallas_call x1, Pallas kernels, merge(): pl.pallas_call(functools.partial(merge_kernel, len(backs), paired, width_...  0.8 us
    pallas_call x1, Pallas kernels, place(): pl.pallas_call(place_kernel, in_specs=[VMEM] * 2, out_specs=[VMEM] * 3, o...  0.69 us
  transfers between devices with their start and end apart: 9, of which 4 were waited for; matrix products, arithmetic and copies ran while one was open for 0% of the time, Pallas kernels for 25%

profile of v18, /device:TPU:0, one launch (start us, length us, event | category | flops | bytes accessed | tf_op | source)
XLA Modules:
  0.0 25.8 jit_solution(5162108773338252321)
XLA Ops:
  0.6 1.9 %pack.1 = (bf16[16,4096]{1,0:T(8,128)(2,1)}, bf16[16,3072]{1,0:T(8,128)(2,1)}, bf16[16,3328]{1,0:T(8,128)(2,1)}) custom-call(f32[16,2048]{1,0:T(8,128)} %refs_0_.1, f32[16,2048]{1,0:T(8,128)} %refs_1_.1, bf16[2,4,2048]{2,1,0:T(4,128)(2,1)} %refs_2_.1, bf16[16,128]{1,0:T(8,128)(2,1)} %bitcast.6, s32[1,2]{1,0:T(1,128)} %bitcast.7, f32[64,256]{1,0:T(8,128)} %bitcast.4, ...), custom_call_target="tpu_custom_call" | custom-call | tf_op jit(solution)/shard_map/pack/pallas_call | solution.py:127
  2.5 3.1 %collective-permute-start = (bf16[16,4096]{1,0:T(8,128)(2,1)}, bf16[16,4096]{1,0:T(8,128)(2,1)S(1)}, u32[]{:S(2)}, u32[]{:S(2)}) collective-permute-start(bf16[16,4096]{1,0:T(8,128)(2,1)} %get-tuple-element.19.refs_2_), channel_id=1, source_target_pairs={{0,4},{4,0},{8,12},{12,8},{1,5},{5,1},{9,13},{13,9},{2,6},{6,2},{1... | collective-permute-start | bytes 393224 | tf_op jit(solution)/shard_map/ppermute | solution.py:614
  5.6 2.6 %collective-permute-start.1 = (bf16[16,3072]{1,0:T(8,128)(2,1)}, bf16[16,3072]{1,0:T(8,128)(2,1)S(1)}, u32[]{:S(2)}, u32[]{:S(2)}) collective-permute-start(bf16[16,3072]{1,0:T(8,128)(2,1)} %get-tuple-element.20.refs_4_), channel_id=1, source_target_pairs={{0,8},{4,12},{8,0},{12,4},{1,9},{5,13},{9,1},{13,5},{2,10},{6,14},... | collective-permute-start | bytes 294920 | tf_op jit(solution)/shard_map/ppermute | solution.py:614
  8.2 5.8 %local.1 = (bf16[16,2304]{1,0:T(8,128)(2,1)S(1)}, bf16[16,2304]{1,0:T(8,128)(2,1)S(1)}, f32[16,1024]{1,0:T(8,128)S(1)}, bf16[16,2048]{1,0:T(8,128)(2,1)S(1)}, f32[24,128]{1,0:T(8,128)S(1)}) custom-call(bf16[16,3328]{1,0:T(8,128)(2,1)} %get-tuple-element.15.x_hbm, bf16[2,4,8192]{2,1,0:T(4,128)(2,1)} %q_hbm.1, bf16[2,512,1024]{2,1,0:T(8,128)(2,1)} %k_hbm.1, ...), custom_call_target="tpu_custom_call" | custom-call | flops 402653184 | bytes 12582912 | tf_op jit(solution)/shard_map/local/pallas_call | solution.py:345
  14.1 0.1 collective-permute-start.3
  14.1 0.0 collective-permute-done.1.refs_5_
  14.1 0.0 collective-permute-done.refs_3_
  14.2 0.3 rank_products.1
  14.4 0.5 %collective-permute-start.2 = (bf16[16,896]{1,0:T(8,128)(2,1)S(1)}, bf16[16,896]{1,0:T(8,128)(2,1)S(1)}, u32[]{:S(2)}, u32[]{:S(2)}) collective-permute-start(bf16[16,896]{1,0:T(8,128)(2,1)S(1)} %get-tuple-element.21._.mine_ref), channel_id=1, source_target_pairs={{0,1},{1,0},{2,3},{3,2},{4,5},{5,4},{6,7},{7,6},{8,9},{9,8},{10,11... | collective-permute-start | bytes 86024 | tf_op jit(solution)/shard_map/ppermute | solution.py:614
  14.9 0.4 %collective-permute-start.7 = (bf16[16,3584]{1,0:T(8,128)(2,1)S(1)}, bf16[16,3584]{1,0:T(8,128)(2,1)S(1)}, u32[]{:S(2)}, u32[]{:S(2)}) collective-permute-start(bf16[16,3584]{1,0:T(8,128)(2,1)S(1)} %get-tuple-element.26.refs_6_), channel_id=1, source_target_pairs={{0,4},{4,0},{8,12},{12,8},{1,5},{5,1},{9,13},{13,9},{2,6},{6,2},{1... | collective-permute-start | bytes 344072 | tf_op jit(solution)/shard_map/ppermute | solution.py:614
  15.4 0.0 collective-permute-done.3.b_ref
  15.4 0.2 combine_cache.1.cache_ref
  15.6 0.2 collective-permute-done.2.theirs_ref
  15.8 1.6 %collective-permute-start.4 = (bf16[16,3072]{1,0:T(8,128)(2,1)S(1)}, bf16[16,3072]{1,0:T(8,128)(2,1)S(1)}, u32[]{:S(2)}, u32[]{:S(2)}) collective-permute-start(bf16[16,3072]{1,0:T(8,128)(2,1)S(1)} %get-tuple-element.24.refs_2_), channel_id=1, source_target_pairs={{0,2},{1,3},{2,0},{3,1},{4,6},{5,7},{6,4},{7,5},{8,10},{9,11},{10,... | collective-permute-start | bytes 294920 | tf_op jit(solution)/shard_map/ppermute | solution.py:614
  17.4 1.1 %collective-permute-start.6 = (bf16[16,128]{1,0:T(8,128)(2,1)S(1)}, bf16[16,128]{1,0:T(8,128)(2,1)S(1)}, u32[]{:S(2)}, u32[]{:S(2)}) collective-permute-start(bf16[16,128]{1,0:T(8,128)(2,1)S(1)} %get-tuple-element.25), channel_id=1, source_target_pairs={{0,10},{1,11},{2,8},{3,9},{4,14},{5,15},{6,12},{7,13},{8,2},{9,3},... | collective-permute-start | bytes 12296 | tf_op jit(solution)/shard_map/ppermute | solution.py:668
  18.4 1.8 %collective-permute-start.5 = (bf16[16,128]{1,0:T(8,128)(2,1)S(1)}, bf16[16,128]{1,0:T(8,128)(2,1)S(1)}, u32[]{:S(2)}, u32[]{:S(2)}) collective-permute-start(bf16[16,128]{1,0:T(8,128)(2,1)S(1)} %get-tuple-element.25), channel_id=1, source_target_pairs={{0,8},{1,9},{2,10},{3,11},{4,12},{5,13},{6,14},{7,15},{8,0},{9,1},... | collective-permute-start | bytes 12296 | tf_op jit(solution)/shard_map/ppermute | solution.py:668
  20.3 2.5 %collective-permute-done.6.refs_5_ = bf16[16,128]{1,0:T(8,128)(2,1)S(1)} collective-permute-done((bf16[16,128]{1,0:T(8,128)(2,1)S(1)}, bf16[16,128]{1,0:T(8,128)(2,1)S(1)}, u32[]{:S(2)}, u32[]{:S(2)}) %collective-permute-start.6) | collective-permute-done | bytes 4128 | tf_op jit(solution)/shard_map/ppermute | solution.py:668
  22.8 0.2 collective-permute-done.5.refs_4_
  23.0 0.0 collective-permute-done.7.refs_7_
  23.0 0.0 collective-permute-done.4.refs_3_
  23.0 0.8 %merge.1.mine_ref = bf16[16,2560]{1,0:T(8,128)(2,1)S(1)} custom-call(f32[24,128]{1,0:T(8,128)S(1)} %get-tuple-element.16.refs_1_.refs_0_, bf16[16,2048]{1,0:T(8,128)(2,1)S(1)} %get-tuple-element.17.refs_1_, bf16[16,3072]{1,0:T(8,128)(2,1)S(1)} %get-tuple-element.24.refs_2_, bf16[16,3072]{1,0:T(8,128)(2,1)S(1)} %collective-permute-done.4.refs_3_, ...), custom_call_target="tpu_custom_call" | custom-call | tf_op jit(solution)/shard_map/merge/pallas_call | solution.py:567
  23.8 0.1 collective-permute-start.8
  23.8 1.3 %collective-permute-done.8.theirs_ref = bf16[16,2560]{1,0:T(8,128)(2,1)S(1)} collective-permute-done((bf16[16,2560]{1,0:T(8,128)(2,1)S(1)}, bf16[16,2560]{1,0:T(8,128)(2,1)S(1)}, u32[]{:S(2)}, u32[]{:S(2)}) %collective-permute-start.8) | collective-permute-done | bytes 81952 | tf_op jit(solution)/shard_map/ppermute | solution.py:614
  25.1 0.7 %place.1 = (bf16[2,4,1024]{2,1,0:T(4,128)(2,1)}, bf16[2,4,1024]{2,1,0:T(4,128)(2,1)}, bf16[2,4,8192]{2,1,0:T(4,128)(2,1)}) custom-call(bf16[16,2560]{1,0:T(8,128)(2,1)S(1)} %merge.1.mine_ref, bf16[16,2560]{1,0:T(8,128)(2,1)S(1)} %collective-permute-done.8.theirs_ref), custom_call_target="tpu_custom_call" | custom-call | tf_op jit(solution)/shard_map/place/pallas_call | solution.py:599
  (5 shorter events, 0.0 us)
Async XLA Ops:
  2.5 11.6 %collective-permute-start = (bf16[16,4096]{1,0:T(8,128)(2,1)}, bf16[16,4096]{1,0:T(8,128)(2,1)S(1)}, u32[]{:S(2)}, u32[]{:S(2)}) collective-permute-start(bf16[16,4096]{1,0:T(8,128)(2,1)} %get-tuple-element.19.refs_2_), channel_id=1, source_target_pairs={{0,4},{4,0},{8,12},{12,8},{1,5},{5,1},{9,13},{13,9},{2,6},{6,2},{1... | collective-permute-start | bytes 393224 | tf_op jit(solution)/shard_map/ppermute | solution.py:614
  5.6 8.5 %collective-permute-start.1 = (bf16[16,3072]{1,0:T(8,128)(2,1)}, bf16[16,3072]{1,0:T(8,128)(2,1)S(1)}, u32[]{:S(2)}, u32[]{:S(2)}) collective-permute-start(bf16[16,3072]{1,0:T(8,128)(2,1)} %get-tuple-element.20.refs_4_), channel_id=1, source_target_pairs={{0,8},{4,12},{8,0},{12,4},{1,9},{5,13},{9,1},{13,5},{2,10},{6,14},... | collective-permute-start | bytes 294920 | tf_op jit(solution)/shard_map/ppermute | solution.py:614
  8.2 6.0 %copy-start = (bf16[16,4096]{1,0:T(8,128)(2,1)S(1)}, bf16[16,4096]{1,0:T(8,128)(2,1)}, u32[]{:S(2)}) copy-start(bf16[16,4096]{1,0:T(8,128)(2,1)} %get-tuple-element.19.refs_2_) | copy-start | bytes 393220
  8.2 6.0 %copy-start.1 = (bf16[16,3072]{1,0:T(8,128)(2,1)S(1)}, bf16[16,3072]{1,0:T(8,128)(2,1)}, u32[]{:S(2)}) copy-start(bf16[16,3072]{1,0:T(8,128)(2,1)} %get-tuple-element.20.refs_4_) | copy-start | bytes 294916
  14.1 1.3 %collective-permute-start.3 = (bf16[16,2304]{1,0:T(8,128)(2,1)S(1)}, bf16[16,2304]{1,0:T(8,128)(2,1)S(1)}, u32[]{:S(2)}, u32[]{:S(2)}) collective-permute-start(bf16[16,2304]{1,0:T(8,128)(2,1)S(1)} %get-tuple-element.23), channel_id=1, source_target_pairs={{0,1},{1,0},{2,3},{3,2},{4,5},{5,4},{6,7},{7,6},{8,9},{9,8},{10,11... | collective-permute-start | bytes 221192 | tf_op jit(solution)/shard_map/ppermute | solution.py:614
  14.4 1.3 %collective-permute-start.2 = (bf16[16,896]{1,0:T(8,128)(2,1)S(1)}, bf16[16,896]{1,0:T(8,128)(2,1)S(1)}, u32[]{:S(2)}, u32[]{:S(2)}) collective-permute-start(bf16[16,896]{1,0:T(8,128)(2,1)S(1)} %get-tuple-element.21._.mine_ref), channel_id=1, source_target_pairs={{0,1},{1,0},{2,3},{3,2},{4,5},{5,4},{6,7},{7,6},{8,9},{9,8},{10,11... | collective-permute-start | bytes 86024 | tf_op jit(solution)/shard_map/ppermute | solution.py:614
  14.9 8.0 %collective-permute-start.7 = (bf16[16,3584]{1,0:T(8,128)(2,1)S(1)}, bf16[16,3584]{1,0:T(8,128)(2,1)S(1)}, u32[]{:S(2)}, u32[]{:S(2)}) collective-permute-start(bf16[16,3584]{1,0:T(8,128)(2,1)S(1)} %get-tuple-element.26.refs_6_), channel_id=1, source_target_pairs={{0,4},{4,0},{8,12},{12,8},{1,5},{5,1},{9,13},{13,9},{2,6},{6,2},{1... | collective-permute-start | bytes 344072 | tf_op jit(solution)/shard_map/ppermute | solution.py:614
  15.8 7.2 %collective-permute-start.4 = (bf16[16,3072]{1,0:T(8,128)(2,1)S(1)}, bf16[16,3072]{1,0:T(8,128)(2,1)S(1)}, u32[]{:S(2)}, u32[]{:S(2)}) collective-permute-start(bf16[16,3072]{1,0:T(8,128)(2,1)S(1)} %get-tuple-element.24.refs_2_), channel_id=1, source_target_pairs={{0,2},{1,3},{2,0},{3,1},{4,6},{5,7},{6,4},{7,5},{8,10},{9,11},{10,... | collective-permute-start | bytes 294920 | tf_op jit(solution)/shard_map/ppermute | solution.py:614
  17.4 5.4 %collective-permute-start.6 = (bf16[16,128]{1,0:T(8,128)(2,1)S(1)}, bf16[16,128]{1,0:T(8,128)(2,1)S(1)}, u32[]{:S(2)}, u32[]{:S(2)}) collective-permute-start(bf16[16,128]{1,0:T(8,128)(2,1)S(1)} %get-tuple-element.25), channel_id=1, source_target_pairs={{0,10},{1,11},{2,8},{3,9},{4,14},{5,15},{6,12},{7,13},{8,2},{9,3},... | collective-permute-start | bytes 12296 | tf_op jit(solution)/shard_map/ppermute | solution.py:668
  18.4 4.5 %collective-permute-start.5 = (bf16[16,128]{1,0:T(8,128)(2,1)S(1)}, bf16[16,128]{1,0:T(8,128)(2,1)S(1)}, u32[]{:S(2)}, u32[]{:S(2)}) collective-permute-start(bf16[16,128]{1,0:T(8,128)(2,1)S(1)} %get-tuple-element.25), channel_id=1, source_target_pairs={{0,8},{1,9},{2,10},{3,11},{4,12},{5,13},{6,14},{7,15},{8,0},{9,1},... | collective-permute-start | bytes 12296 | tf_op jit(solution)/shard_map/ppermute | solution.py:668
  23.8 1.3 %collective-permute-start.8 = (bf16[16,2560]{1,0:T(8,128)(2,1)S(1)}, bf16[16,2560]{1,0:T(8,128)(2,1)S(1)}, u32[]{:S(2)}, u32[]{:S(2)}) collective-permute-start(bf16[16,2560]{1,0:T(8,128)(2,1)S(1)} %merge.1.mine_ref), channel_id=1, source_target_pairs={{0,1},{1,0},{2,3},{3,2},{4,5},{5,4},{6,7},{7,6},{8,9},{9,8},{10,11... | collective-permute-start | bytes 245768 | tf_op jit(solution)/shard_map/ppermute | solution.py:614

commit v19 on v13

--- a/solution.py
+++ b/solution.py
@@ -266,10 +266,9 @@
                 )
             )
         groups.append(copies)
+    groups[0][1].start()
     for h in range(2):
         groups[h][0].start()
-    for copy in groups[0][1:]:
-        copy.start()
     weights = []
     for c in range(chunks):
         at = pl.ds(c * CHUNK, CHUNK)
@@ -284,6 +283,7 @@
             copy.start()
 
     x_copy.wait()
+    groups[0][2].start()
     start(groups[1][1:])
     for copies in weights[: chunks // 4]:
         start(copies)

time: 26 us -> 26 us (level)
  waiting for transfers between devices: 4.6 us -> 4.28 us
  Pallas kernels: 9.27 us -> 9.58 us
    pallas_call x1, Pallas kernels: 5.4 us -> 5.71 us  [local(): pl.pallas_call(local_kernel, in_specs=[HBM] * 6, out_specs=[VMEM] * 5, ou...]
    ppermute x2, waiting for transfers between devices: 3.15 us -> 2.84 us  [shards(): backs.append(lax.ppermute(reply, ('dp', 'tensor'), perm))]
  transfers between devices with their start and end apart: 9 -> 9, of which waited for: 4 -> 4; matrix products, arithmetic and copies ran while one was open for 0% -> 0% of each run, Pallas kernels for 23% -> 24%
where the time goes in v19:
time: 26 us; the launch traced here: 25.8 us
  starting transfers between devices  11.2 us (43%)
  Pallas kernels  9.58 us (37%)
  waiting for transfers between devices  4.28 us (16%)
  between operations  0.72 us (3%)
    ppermute x7, starting transfers between devices, swap(): return lax.ppermute(value, axis, [(i, i ^ distance) for i in range(n)])  8.31 us
    pallas_call x1, Pallas kernels, local(): pl.pallas_call(local_kernel, in_specs=[HBM] * 6, out_specs=[VMEM] * 5, ou...  5.71 us
    ppermute x2, starting transfers between devices, shards(): backs.append(lax.ppermute(reply, ('dp', 'tensor'), perm))  2.9 us
    ppermute x2, waiting for transfers between devices, shards(): backs.append(lax.ppermute(reply, ('dp', 'tensor'), perm))  2.84 us
    pallas_call x1, Pallas kernels, pack(): pl.pallas_call(pack_kernel, in_specs=[HBM] * len(operands), out_specs=[HB...  1.88 us
    ppermute x7, waiting for transfers between devices, swap(): return lax.ppermute(value, axis, [(i, i ^ distance) for i in range(n)])  1.45 us
    pallas_call x1, Pallas kernels, merge(): pl.pallas_call(functools.partial(merge_kernel, len(backs), paired, width_...  0.8 us
    pallas_call x1, Pallas kernels, place(): pl.pallas_call(place_kernel, in_specs=[VMEM] * 2, out_specs=[VMEM] * 3, o...  0.69 us
  transfers between devices with their start and end apart: 9, of which 4 were waited for; matrix products, arithmetic and copies ran while one was open for 0% of the time, Pallas kernels for 24%

profile of v19, /device:TPU:0, one launch (start us, length us, event | category | flops | bytes accessed | tf_op | source)
XLA Modules:
  0.0 25.8 jit_solution(2730272064869613085)
XLA Ops:
  0.6 1.9 %pack.1 = (bf16[16,4096]{1,0:T(8,128)(2,1)}, bf16[16,3072]{1,0:T(8,128)(2,1)}, bf16[16,3328]{1,0:T(8,128)(2,1)}) custom-call(f32[16,2048]{1,0:T(8,128)} %refs_0_.1, f32[16,2048]{1,0:T(8,128)} %refs_1_.1, bf16[2,4,2048]{2,1,0:T(4,128)(2,1)} %refs_2_.1, bf16[16,128]{1,0:T(8,128)(2,1)} %bitcast.6, s32[1,2]{1,0:T(1,128)} %bitcast.7, f32[64,256]{1,0:T(8,128)} %bitcast.4, ...), custom_call_target="tpu_custom_call" | custom-call | tf_op jit(solution)/shard_map/pack/pallas_call | solution.py:127
  2.5 3.1 %collective-permute-start = (bf16[16,4096]{1,0:T(8,128)(2,1)}, bf16[16,4096]{1,0:T(8,128)(2,1)S(1)}, u32[]{:S(2)}, u32[]{:S(2)}) collective-permute-start(bf16[16,4096]{1,0:T(8,128)(2,1)} %get-tuple-element.19.refs_2_), channel_id=1, source_target_pairs={{0,4},{4,0},{8,12},{12,8},{1,5},{5,1},{9,13},{13,9},{2,6},{6,2},{1... | collective-permute-start | bytes 393224 | tf_op jit(solution)/shard_map/ppermute | solution.py:615
  5.6 2.6 %collective-permute-start.1 = (bf16[16,3072]{1,0:T(8,128)(2,1)}, bf16[16,3072]{1,0:T(8,128)(2,1)S(1)}, u32[]{:S(2)}, u32[]{:S(2)}) collective-permute-start(bf16[16,3072]{1,0:T(8,128)(2,1)} %get-tuple-element.20.refs_4_), channel_id=1, source_target_pairs={{0,8},{4,12},{8,0},{12,4},{1,9},{5,13},{9,1},{13,5},{2,10},{6,14},... | collective-permute-start | bytes 294920 | tf_op jit(solution)/shard_map/ppermute | solution.py:615
  8.2 5.7 %local.1 = (bf16[16,2304]{1,0:T(8,128)(2,1)S(1)}, bf16[16,2304]{1,0:T(8,128)(2,1)S(1)}, f32[16,1024]{1,0:T(8,128)S(1)}, bf16[16,2048]{1,0:T(8,128)(2,1)S(1)}, f32[24,128]{1,0:T(8,128)S(1)}) custom-call(bf16[16,3328]{1,0:T(8,128)(2,1)} %get-tuple-element.15.x_hbm, bf16[2,4,8192]{2,1,0:T(4,128)(2,1)} %q_hbm.1, bf16[2,512,1024]{2,1,0:T(8,128)(2,1)} %k_hbm.1, ...), custom_call_target="tpu_custom_call" | custom-call | flops 402653184 | bytes 12582912 | tf_op jit(solution)/shard_map/local/pallas_call | solution.py:346
  13.9 0.1 collective-permute-start.3
  14.0 0.0 collective-permute-done.1.refs_5_
  14.0 0.0 collective-permute-done.refs_3_
  14.0 0.3 rank_products.1
  14.3 0.5 %collective-permute-start.2 = (bf16[16,896]{1,0:T(8,128)(2,1)S(1)}, bf16[16,896]{1,0:T(8,128)(2,1)S(1)}, u32[]{:S(2)}, u32[]{:S(2)}) collective-permute-start(bf16[16,896]{1,0:T(8,128)(2,1)S(1)} %get-tuple-element.21._.mine_ref), channel_id=1, source_target_pairs={{0,1},{1,0},{2,3},{3,2},{4,5},{5,4},{6,7},{7,6},{8,9},{9,8},{10,11... | collective-permute-start | bytes 86024 | tf_op jit(solution)/shard_map/ppermute | solution.py:615
  14.8 0.4 %collective-permute-start.7 = (bf16[16,3584]{1,0:T(8,128)(2,1)S(1)}, bf16[16,3584]{1,0:T(8,128)(2,1)S(1)}, u32[]{:S(2)}, u32[]{:S(2)}) collective-permute-start(bf16[16,3584]{1,0:T(8,128)(2,1)S(1)} %get-tuple-element.26.refs_6_), channel_id=1, source_target_pairs={{0,4},{4,0},{8,12},{12,8},{1,5},{5,1},{9,13},{13,9},{2,6},{6,2},{1... | collective-permute-start | bytes 344072 | tf_op jit(solution)/shard_map/ppermute | solution.py:615
  15.2 0.0 collective-permute-done.3.b_ref
  15.3 0.2 combine_cache.1.cache_ref
  15.5 0.2 collective-permute-done.2.theirs_ref
  15.7 1.6 %collective-permute-start.4 = (bf16[16,3072]{1,0:T(8,128)(2,1)S(1)}, bf16[16,3072]{1,0:T(8,128)(2,1)S(1)}, u32[]{:S(2)}, u32[]{:S(2)}) collective-permute-start(bf16[16,3072]{1,0:T(8,128)(2,1)S(1)} %get-tuple-element.24.refs_2_), channel_id=1, source_target_pairs={{0,2},{1,3},{2,0},{3,1},{4,6},{5,7},{6,4},{7,5},{8,10},{9,11},{10,... | collective-permute-start | bytes 294920 | tf_op jit(solution)/shard_map/ppermute | solution.py:615
  17.2 1.2 %collective-permute-start.6 = (bf16[16,128]{1,0:T(8,128)(2,1)S(1)}, bf16[16,128]{1,0:T(8,128)(2,1)S(1)}, u32[]{:S(2)}, u32[]{:S(2)}) collective-permute-start(bf16[16,128]{1,0:T(8,128)(2,1)S(1)} %get-tuple-element.25), channel_id=1, source_target_pairs={{0,10},{1,11},{2,8},{3,9},{4,14},{5,15},{6,12},{7,13},{8,2},{9,3},... | collective-permute-start | bytes 12296 | tf_op jit(solution)/shard_map/ppermute | solution.py:669
  18.4 1.7 %collective-permute-start.5 = (bf16[16,128]{1,0:T(8,128)(2,1)S(1)}, bf16[16,128]{1,0:T(8,128)(2,1)S(1)}, u32[]{:S(2)}, u32[]{:S(2)}) collective-permute-start(bf16[16,128]{1,0:T(8,128)(2,1)S(1)} %get-tuple-element.25), channel_id=1, source_target_pairs={{0,8},{1,9},{2,10},{3,11},{4,12},{5,13},{6,14},{7,15},{8,0},{9,1},... | collective-permute-start | bytes 12296 | tf_op jit(solution)/shard_map/ppermute | solution.py:669
  20.1 2.5 %collective-permute-done.6.refs_5_ = bf16[16,128]{1,0:T(8,128)(2,1)S(1)} collective-permute-done((bf16[16,128]{1,0:T(8,128)(2,1)S(1)}, bf16[16,128]{1,0:T(8,128)(2,1)S(1)}, u32[]{:S(2)}, u32[]{:S(2)}) %collective-permute-start.6) | collective-permute-done | bytes 4128 | tf_op jit(solution)/shard_map/ppermute | solution.py:669
  22.6 0.3 %collective-permute-done.5.refs_4_ = bf16[16,128]{1,0:T(8,128)(2,1)S(1)} collective-permute-done((bf16[16,128]{1,0:T(8,128)(2,1)S(1)}, bf16[16,128]{1,0:T(8,128)(2,1)S(1)}, u32[]{:S(2)}, u32[]{:S(2)}) %collective-permute-start.5) | collective-permute-done | bytes 4128 | tf_op jit(solution)/shard_map/ppermute | solution.py:669
  23.0 0.0 collective-permute-done.7.refs_7_
  23.0 0.0 collective-permute-done.4.refs_3_
  23.0 0.8 %merge.1.mine_ref = bf16[16,2560]{1,0:T(8,128)(2,1)S(1)} custom-call(f32[24,128]{1,0:T(8,128)S(1)} %get-tuple-element.16.refs_1_.refs_0_, bf16[16,2048]{1,0:T(8,128)(2,1)S(1)} %get-tuple-element.17.refs_1_, bf16[16,3072]{1,0:T(8,128)(2,1)S(1)} %get-tuple-element.24.refs_2_, bf16[16,3072]{1,0:T(8,128)(2,1)S(1)} %collective-permute-done.4.refs_3_, ...), custom_call_target="tpu_custom_call" | custom-call | tf_op jit(solution)/shard_map/merge/pallas_call | solution.py:568
  23.8 0.1 collective-permute-start.8
  23.8 1.3 %collective-permute-done.8.theirs_ref = bf16[16,2560]{1,0:T(8,128)(2,1)S(1)} collective-permute-done((bf16[16,2560]{1,0:T(8,128)(2,1)S(1)}, bf16[16,2560]{1,0:T(8,128)(2,1)S(1)}, u32[]{:S(2)}, u32[]{:S(2)}) %collective-permute-start.8) | collective-permute-done | bytes 81952 | tf_op jit(solution)/shard_map/ppermute | solution.py:615
  25.1 0.7 %place.1 = (bf16[2,4,1024]{2,1,0:T(4,128)(2,1)}, bf16[2,4,1024]{2,1,0:T(4,128)(2,1)}, bf16[2,4,8192]{2,1,0:T(4,128)(2,1)}) custom-call(bf16[16,2560]{1,0:T(8,128)(2,1)S(1)} %merge.1.mine_ref, bf16[16,2560]{1,0:T(8,128)(2,1)S(1)} %collective-permute-done.8.theirs_ref), custom_call_target="tpu_custom_call" | custom-call | tf_op jit(solution)/shard_map/place/pallas_call | solution.py:600
  (5 shorter events, 0.0 us)
Async XLA Ops:
  2.5 11.5 %collective-permute-start = (bf16[16,4096]{1,0:T(8,128)(2,1)}, bf16[16,4096]{1,0:T(8,128)(2,1)S(1)}, u32[]{:S(2)}, u32[]{:S(2)}) collective-permute-start(bf16[16,4096]{1,0:T(8,128)(2,1)} %get-tuple-element.19.refs_2_), channel_id=1, source_target_pairs={{0,4},{4,0},{8,12},{12,8},{1,5},{5,1},{9,13},{13,9},{2,6},{6,2},{1... | collective-permute-start | bytes 393224 | tf_op jit(solution)/shard_map/ppermute | solution.py:615
  5.6 8.4 %collective-permute-start.1 = (bf16[16,3072]{1,0:T(8,128)(2,1)}, bf16[16,3072]{1,0:T(8,128)(2,1)S(1)}, u32[]{:S(2)}, u32[]{:S(2)}) collective-permute-start(bf16[16,3072]{1,0:T(8,128)(2,1)} %get-tuple-element.20.refs_4_), channel_id=1, source_target_pairs={{0,8},{4,12},{8,0},{12,4},{1,9},{5,13},{9,1},{13,5},{2,10},{6,14},... | collective-permute-start | bytes 294920 | tf_op jit(solution)/shard_map/ppermute | solution.py:615
  8.2 5.8 %copy-start = (bf16[16,4096]{1,0:T(8,128)(2,1)S(1)}, bf16[16,4096]{1,0:T(8,128)(2,1)}, u32[]{:S(2)}) copy-start(bf16[16,4096]{1,0:T(8,128)(2,1)} %get-tuple-element.19.refs_2_) | copy-start | bytes 393220
  8.2 5.8 %copy-start.1 = (bf16[16,3072]{1,0:T(8,128)(2,1)S(1)}, bf16[16,3072]{1,0:T(8,128)(2,1)}, u32[]{:S(2)}) copy-start(bf16[16,3072]{1,0:T(8,128)(2,1)} %get-tuple-element.20.refs_4_) | copy-start | bytes 294916
  13.9 1.3 %collective-permute-start.3 = (bf16[16,2304]{1,0:T(8,128)(2,1)S(1)}, bf16[16,2304]{1,0:T(8,128)(2,1)S(1)}, u32[]{:S(2)}, u32[]{:S(2)}) collective-permute-start(bf16[16,2304]{1,0:T(8,128)(2,1)S(1)} %get-tuple-element.23), channel_id=1, source_target_pairs={{0,1},{1,0},{2,3},{3,2},{4,5},{5,4},{6,7},{7,6},{8,9},{9,8},{10,11... | collective-permute-start | bytes 221192 | tf_op jit(solution)/shard_map/ppermute | solution.py:615
  14.3 1.3 %collective-permute-start.2 = (bf16[16,896]{1,0:T(8,128)(2,1)S(1)}, bf16[16,896]{1,0:T(8,128)(2,1)S(1)}, u32[]{:S(2)}, u32[]{:S(2)}) collective-permute-start(bf16[16,896]{1,0:T(8,128)(2,1)S(1)} %get-tuple-element.21._.mine_ref), channel_id=1, source_target_pairs={{0,1},{1,0},{2,3},{3,2},{4,5},{5,4},{6,7},{7,6},{8,9},{9,8},{10,11... | collective-permute-start | bytes 86024 | tf_op jit(solution)/shard_map/ppermute | solution.py:615
  14.8 8.2 %collective-permute-start.7 = (bf16[16,3584]{1,0:T(8,128)(2,1)S(1)}, bf16[16,3584]{1,0:T(8,128)(2,1)S(1)}, u32[]{:S(2)}, u32[]{:S(2)}) collective-permute-start(bf16[16,3584]{1,0:T(8,128)(2,1)S(1)} %get-tuple-element.26.refs_6_), channel_id=1, source_target_pairs={{0,4},{4,0},{8,12},{12,8},{1,5},{5,1},{9,13},{13,9},{2,6},{6,2},{1... | collective-permute-start | bytes 344072 | tf_op jit(solution)/shard_map/ppermute | solution.py:615
  15.7 7.3 %collective-permute-start.4 = (bf16[16,3072]{1,0:T(8,128)(2,1)S(1)}, bf16[16,3072]{1,0:T(8,128)(2,1)S(1)}, u32[]{:S(2)}, u32[]{:S(2)}) collective-permute-start(bf16[16,3072]{1,0:T(8,128)(2,1)S(1)} %get-tuple-element.24.refs_2_), channel_id=1, source_target_pairs={{0,2},{1,3},{2,0},{3,1},{4,6},{5,7},{6,4},{7,5},{8,10},{9,11},{10,... | collective-permute-start | bytes 294920 | tf_op jit(solution)/shard_map/ppermute | solution.py:615
  17.2 5.4 %collective-permute-start.6 = (bf16[16,128]{1,0:T(8,128)(2,1)S(1)}, bf16[16,128]{1,0:T(8,128)(2,1)S(1)}, u32[]{:S(2)}, u32[]{:S(2)}) collective-permute-start(bf16[16,128]{1,0:T(8,128)(2,1)S(1)} %get-tuple-element.25), channel_id=1, source_target_pairs={{0,10},{1,11},{2,8},{3,9},{4,14},{5,15},{6,12},{7,13},{8,2},{9,3},... | collective-permute-start | bytes 12296 | tf_op jit(solution)/shard_map/ppermute | solution.py:669
  18.4 4.5 %collective-permute-start.5 = (bf16[16,128]{1,0:T(8,128)(2,1)S(1)}, bf16[16,128]{1,0:T(8,128)(2,1)S(1)}, u32[]{:S(2)}, u32[]{:S(2)}) collective-permute-start(bf16[16,128]{1,0:T(8,128)(2,1)S(1)} %get-tuple-element.25), channel_id=1, source_target_pairs={{0,8},{1,9},{2,10},{3,11},{4,12},{5,13},{6,14},{7,15},{8,0},{9,1},... | collective-permute-start | bytes 12296 | tf_op jit(solution)/shard_map/ppermute | solution.py:669
  23.8 1.3 %collective-permute-start.8 = (bf16[16,2560]{1,0:T(8,128)(2,1)S(1)}, bf16[16,2560]{1,0:T(8,128)(2,1)S(1)}, u32[]{:S(2)}, u32[]{:S(2)}) collective-permute-start(bf16[16,2560]{1,0:T(8,128)(2,1)S(1)} %merge.1.mine_ref), channel_id=1, source_target_pairs={{0,1},{1,0},{2,3},{3,2},{4,5},{5,4},{6,7},{7,6},{8,9},{9,8},{10,11... | collective-permute-start | bytes 245768 | tf_op jit(solution)/shard_map/ppermute | solution.py:615
